TPU v7x, 128 devices: a whole 4x4x4 slice. The times are simulated.
128 devices in a mesh: ga: 16 (over z, y_hi, core), ba: 8 (over y_lo, x).
Axes of the slice: x: 4, y: 4 (y_hi: 2, y_lo: 2; y = y_hi * 2 + y_lo), z: 4, core: 2. Of those that a mesh axis runs over, the one named last changes fastest.
Arguments:
- psi_val: bfloat16 [32, 32768], P('ba', 'ga'), may hold values from -6 to 6
- psi_con: bfloat16 [64, 32768], P(None, 'ga'), may hold values from -6 to 6
- e_val: float32 [32], P('ba'), may hold values from -12 to -1
- e_con: float32 [64], replicated, may hold values from 1 to 20
- occ: int32 [32], P('ba'), may hold values 0 or 1
- omega: float32 [8], replicated, may hold values from 0.5 to 20
- g_index: int32 [6144], replicated, may hold values from 0 to 16383
Outputs:
- chi: float32 [8, 6144, 6144], P('ba', 'ga')
All inputs are finite; a program needn't handle non-finite values. No bound on the sum of `occ` on one device may be relied on, other than what follows from the above.
Results may differ from a plain program's by a relative error of at most 0.0058.
Values may be sent and summed in bfloat16 or wider, within the bound.
No kernel may reach another device: no remote copies, remote signals or barrier semaphores. Data moves between devices by JAX's collectives and lax.ppermute only.
A program may use at most 128 MiB of HBM per device.

v0:
```python
import math

import jax
import jax.numpy as jnp
from jax import lax
from jax.sharding import PartitionSpec as P

NV = 32
NC = 64


def cosine_table(kvals, positions, grid_total, norm_factor):
    phase = kvals[:, None] * positions[None, :] % grid_total
    return (jnp.cos(phase.astype(jnp.float32) * (2.0 * math.pi / grid_total)) * norm_factor).astype(
        jnp.bfloat16
    )


def on_device(psi_val, psi_con, e_val, e_con, occ, omega, g_index):
    val_local = psi_val.shape[0]
    con_count = psi_con.shape[0]
    grid_local = psi_val.shape[1]
    ga_count = lax.axis_size("ga")
    grid_total = grid_local * ga_count
    norm_factor = math.sqrt(2.0 / grid_total)
    density = (
        psi_val.astype(jnp.float32)[:, None, :] * psi_con.astype(jnp.float32)[None, :, :]
    ).astype(jnp.bfloat16)
    density = density.reshape(val_local * con_count, grid_local)
    positions = lax.axis_index("ga") * grid_local + jnp.arange(grid_local, dtype=jnp.int32)
    table = cosine_table(g_index, positions, grid_total, norm_factor)
    rho = lax.psum_scatter(
        lax.dot_general(
            table, density, (((1,), (1,)), ((), ())), preferred_element_type=jnp.float32
        ),
        "ga",
        scatter_dimension=0,
        tiled=True,
    )
    delta = e_con[None, :] - e_val[:, None]
    occf = occ.astype(jnp.float32)[:, None]
    root = jnp.sqrt(
        4.0
        * occf[None]
        * delta[None]
        / (delta[None] * delta[None] + omega[:, None, None] * omega[:, None, None])
        / math.sqrt(NV * NC)
    )
    root = root.reshape(omega.shape[0], val_local * con_count)
    scaled = (rho[None, :, :] * root[:, None, :]).astype(jnp.bfloat16)
    mine = lax.all_to_all(scaled, "ba", split_axis=0, concat_axis=2, tiled=True)
    return -jnp.einsum(
        "fgp,fhp->fgh",
        mine,
        lax.all_gather(mine, "ga", axis=1, tiled=True),
        preferred_element_type=jnp.float32,
    )


def solution(mesh):
    placed = (P("ba", "ga"), P(None, "ga"), P("ba"), P(), P("ba"), P(), P())
    return jax.shard_map(
        on_device, mesh=mesh, in_specs=placed, out_specs=P("ba", "ga", None), check_vma=False
    )
```

profile of v0, /device:TPU:1, one launch (start us, length us, event | category | flops | bytes accessed | tf_op | source)
XLA Modules:
  0.0 502.0 jit_solution(7156083581893055618)
XLA Ops:
  6.5 0.0 reduce-scatter.2.cloned.1.call-start
  6.5 0.7 convert_element_type.27
  7.3 1.0 convert_element_type.28
  8.3 0.2 multiply_convert_fusion.1
  8.4 0.0 copy-start.2
  8.4 0.0 copy-start
  8.4 0.0 copy-start.3
  8.5 0.0 copy-start.1
  8.5 190.5 %fusion.8 = f32[6144,256]{1,0:T(8,128)} fusion(bf16[256,2048]{1,0:T(8,128)(2,1)S(1)} %bitcast.20, s32[2048]{0:T(1024)S(1)} %iota_add_fusion, s32[6144]{0:T(1024)} %param.13), kind=kOutput, calls=%fused_computation.13 | convolution fusion | flops 6643777536 | bytes 7372800 | tf_op jit(solution)/shard_map/dot_general | solution.py:33
  199.0 0.0 reduce-scatter.2.cloned.1.call-update
  199.0 0.0 all-gather.2.cloned.1.call-start
  199.0 0.0 copy-done.2
  199.1 0.0 copy-done
  199.1 0.1 sub.25
  199.2 0.0 copy-done.3
  199.2 0.0 copy-done.1
  199.2 0.1 broadcast_reduce_fusion
  199.3 0.1 sub.27
  199.4 0.1 mul.101
  199.4 0.1 multiply_sqrt_fusion
  199.5 91.6 %reduce-scatter.2.cloned.1.call-done = f32[384,256]{1,0:T(8,128)} async-done(((f32[6144,256]{1,0:T(8,128)}), f32[384,256]{1,0:T(8,128)}) %reduce-scatter.2.cloned.1.call-update) | async-done | bytes 393232 | tf_op jit(solution)/shard_map/reduce_scatter | solution.py:32
  291.1 1.2 copy.8
  292.3 0.3 multiply_convert_fusion
  292.6 22.9 %all_to_all.18 = bf16[8,384,256]{1,2,0:T(8,128)(2,1)} all-to-all(bf16[8,384,256]{1,2,0:T(8,128)(2,1)S(1)} %multiply_convert_fusion), channel_id=1, replica_groups=mesh['ga'=16,'ba'=8] {'ba'}, dimensions={0} | all-to-all | bytes 3145728 | tf_op jit(solution)/shard_map/all_to_all | solution.py:51
  315.6 0.0 all-gather.2.cloned.1.call-update
  315.6 162.1 %all-gather.2.cloned.1.call-done = bf16[1,6144,2048]{1,2,0:T(8,128)(2,1)} async-done(((bf16[1,384,2048]{1,2,0:T(8,128)(2,1)}), bf16[1,6144,2048]{1,2,0:T(8,128)(2,1)}) %all-gather.2.cloned.1.call-update) | async-done | bytes 25165840 | tf_op jit(solution)/shard_map/all_gather | solution.py:55
  477.7 17.5 %negate_bitcast_fusion = f32[1,384,6144]{2,1,0:T(8,128)} fusion(bf16[384,2048]{0,1:T(8,128)(2,1)} %bitcast.19, bf16[1,6144,2048]{1,2,0:T(8,128)(2,1)} %all-gather.2.cloned.1.call-done), kind=kOutput, calls=%fused_computation.14 | convolution fusion | flops 9666035712 | bytes 36175872 | tf_op jit(solution)/shard_map/fgp,fhp->fgh/dot_general | solution.py:52
  (5 shorter events, 0.0 us)
Async XLA Ops:
  6.5 284.6 %reduce-scatter.2.cloned.1.call-start = ((), (), s32[]{:S(2)}) async-start(), calls=%async_computation.2 | async-start | bytes 6684672 | tf_op jit(solution)/shard_map/reduce_scatter | solution.py:32
  8.4 190.6 %copy-start.2 = (f32[8]{0:T(128)S(1)}, f32[8]{0:T(128)}, u32[]{:S(2)}) copy-start(f32[8]{0:T(128)} %param.12) | copy-start | bytes 100
  8.4 190.6 %copy-start = (f32[64]{0:T(128)S(1)}, f32[64]{0:T(128)}, u32[]{:S(2)}) copy-start(f32[64]{0:T(128)} %param.10) | copy-start | bytes 772
  8.4 190.7 %copy-start.3 = (s32[4]{0:T(128)S(1)}, s32[4]{0:T(128)}, u32[]{:S(2)}) copy-start(s32[4]{0:T(128)} %param.11) | copy-start | bytes 52
  8.5 190.7 %copy-start.1 = (f32[4]{0:T(128)S(1)}, f32[4]{0:T(128)}, u32[]{:S(2)}) copy-start(f32[4]{0:T(128)} %param.9) | copy-start | bytes 52
  199.0 278.7 %all-gather.2.cloned.1.call-start = ((), (), s32[]{:S(2)}) async-start(), calls=%async_computation.3 | async-start | bytes 26738688 | tf_op jit(solution)/shard_map/all_gather | solution.py:55
Sparse Core Ops, SparseCore 0:
  199.1 91.9 reduce-scatter.1
  315.7 161.9 all-gather.1
where the time goes:
time: 502 us
  waiting for transfers between devices  254 us (51%)
  matrix products  208 us (41%)
  blocking collectives  22.9 us (5%)
  between operations  13.5 us (3%)
    dot_general x1, matrix products, on_device(): lax.dot_general(table, density, (((1,), (1,)), ((), ())), preferred_eleme...  190 us
    all_gather x1, waiting for transfers between devices, on_device(): lax.all_gather(mine, 'ga', axis=1, tiled=True)  162 us
    reduce_scatter x1, waiting for transfers between devices, on_device(): lax.psum_scatter(lax.dot_general(table, density, (((1,), (1,)), ((), ()))...  91.6 us
    all_to_all x1, blocking collectives, on_device(): mine = lax.all_to_all(scaled, 'ba', split_axis=0, concat_axis=2, tiled=True)  22.9 us
    dot_general x1, matrix products, on_device(): jnp.einsum('fgp,fhp->fgh', mine, lax.all_gather(mine, 'ga', axis=1, tiled...  17.5 us
  transfers between devices with their start and end apart: 2, of which 2 were waited for; matrix products, arithmetic and copies ran while one was open for 0% of the time, Pallas kernels for 0%

commit v1 on v0

v1 whole, which is shorter than its diff:
```python
import functools
import math

import jax
import jax.numpy as jnp
import numpy as np
from jax import lax
from jax.experimental import pallas as pl
from jax.experimental.pallas import tpu as pltpu
from jax.sharding import PartitionSpec as P

NV = 32
NC = 64
N = 32768
NA = 128
NB = 256
NG = 6144
LANES = 128
PAIRS = 16
PARTS = (2048, 2048, 2176)
BLOCK = 512
AXES = ("z", "y", "x")
ORDERS = (("x", "y", "z"), ("y", "z", "x"), ("z", "x", "y"))
STRIDES = tuple({o[0]: 16, o[1]: 64, o[2]: 256} for o in ORDERS)


def split_bf16(a):
    hi = a.astype(np.float32).astype(jnp.bfloat16)
    lo = (a - hi.astype(np.float64)).astype(np.float32).astype(jnp.bfloat16)
    return hi, lo


def dft_constants():
    k1 = np.arange(NA)[:, None]
    ang = 2.0 * math.pi * ((k1 * np.arange(NA)[None, :]) % NA) / NA
    fh, fl = split_bf16(np.concatenate([np.cos(ang), np.sin(ang)], 0))
    first = np.concatenate([fh, fl], 1)
    tw = 2.0 * math.pi * ((k1 * np.arange(NB)[None, :]) % N) / N
    norm = math.sqrt(2.0 / N)
    tcos = (np.cos(tw) * norm).astype(np.float32)
    tsin = (np.sin(tw) * norm).astype(np.float32)
    b2 = 2.0 * math.pi * ((np.arange(NB)[:, None] * np.arange(NA)[None, :]) % NB) / NB
    sh, sl = split_bf16(np.concatenate([np.cos(b2), -np.sin(b2)], 0))
    second = np.concatenate([sh, sl, sh], 0)
    return first, tcos, tsin, second


def rho_kernel(psi, gidx, meta, first, tcos, tsin, second, out0, out1, out2, spec):
    bands = [psi[:, i].astype(jnp.float32).reshape(NA, NB) for i in range(8)]
    ca = tcos[...]
    sa = tsin[...]
    for p in range(PAIRS):
        d = (bands[p // 4] * bands[4 + p % 4]).astype(jnp.bfloat16)
        y = jnp.dot(first[...], jnp.concatenate([d, d], 0), preferred_element_type=jnp.float32)
        a, b = y[:NA], y[NA:]
        uv = jnp.concatenate([a * ca - b * sa, a * sa + b * ca], 1)
        hi = uv.astype(jnp.bfloat16)
        lo = (uv - hi.astype(jnp.float32)).astype(jnp.bfloat16)
        x = jnp.dot(
            jnp.concatenate([hi, hi, lo], 1), second[...], preferred_element_type=jnp.float32
        ).astype(jnp.bfloat16)
        spec[p * 64 : p * 64 + 64, 0:128] = x[:64]
        spec[p * 64 : p * 64 + 64, 128:256] = x[64:]
    width = 256
    base = 0
    for out, cols in ((out0, 2048), (out1, 2048), (out2, 2048)):

        def pick(i, carry, out=out, base=base):
            g = gidx[:, pl.ds(pl.multiple_of(base + i * width, width), width)]
            k1 = lax.bitwise_and(g, 127)
            k2 = lax.shift_right_logical(g, 7)
            kk = lax.shift_right_logical(k1, 6) * 128 + k2
            hot = jnp.where(
                lax.broadcasted_iota(jnp.int32, (256, width), 0) == kk, 1.0, 0.0
            ).astype(jnp.bfloat16)
            o = jnp.dot(spec[...], hot, preferred_element_type=jnp.float32)
            m = lax.broadcasted_iota(jnp.int32, (64, width), 0) == lax.bitwise_and(k1, 63)
            picked = jnp.sum(jnp.where(m[None], o.reshape(PAIRS, 64, width), 0.0), axis=1)
            out[:, pl.ds(pl.multiple_of(i * width, width), width)] = picked.astype(jnp.bfloat16)
            return carry

        lax.fori_loop(0, cols // width, pick, 0)
        base += cols
    out2[:, 2048:2176] = meta[...]


def rho_parts(psi, gidx, meta):
    first, tcos, tsin, second = dft_constants()
    vm = pl.BlockSpec(memory_space=pltpu.VMEM)
    return pl.pallas_call(
        rho_kernel,
        out_shape=[jax.ShapeDtypeStruct((PAIRS, c), jnp.bfloat16) for c in PARTS],
        in_specs=[vm] * 7,
        out_specs=[vm] * 3,
        scratch_shapes=[pltpu.VMEM((PAIRS * 64, 256), jnp.bfloat16)],
        compiler_params=pltpu.CompilerParams(vmem_limit_bytes=32 * 1024 * 1024),
        name="rho_pairs",
    )(psi, gidx, meta, *(jnp.asarray(c) for c in (first, tcos, tsin, second)))


def device_index(z, y, x, c):
    return (z * 4 + (y >> 1) * 2 + c) * 8 + (y & 1) * 4 + x


@functools.cache
def ring_pairs(axis, way):
    pairs = []
    for z in range(4):
        for y in range(4):
            for x in range(4):
                for c in range(2):
                    to = {"z": z, "y": y, "x": x}
                    to[axis] = (to[axis] + (way if c == 0 else -way)) % 4
                    pairs.append((device_index(z, y, x, c), device_index(to["z"], to["y"], to["x"], c)))
    return tuple(pairs)


@functools.cache
def core_pairs():
    return tuple(
        (device_index(z, y, x, c), device_index(z, y, x, 1 - c))
        for z in range(4) for y in range(4) for x in range(4) for c in range(2)
    )


def send(a, pairs):
    return lax.ppermute(a, ("ga", "ba"), pairs)


def ring_gather(a, axis):
    near = send(a, ring_pairs(axis, 1))
    other = send(a, ring_pairs(axis, -1))
    far = send(near, ring_pairs(axis, 1))
    return [a, near, other, far]


def chi_kernel(*refs):
    place, omega = refs[0], refs[1]
    pieces = [[refs[2 + t * 8 + q] for q in range(8)] for t in range(3)]
    out = refs[26]
    raw, meta, weight, left, left_t, right, result, sem_raw, sem_meta, sem_right, sem_out = refs[27:]
    block0 = place[0] * 3

    def right_copies(t, i, slot):
        return [
            pltpu.make_async_copy(
                pieces[t][q].at[:, pl.ds(pl.multiple_of(i * BLOCK, BLOCK), BLOCK)],
                right.at[slot, pl.ds(q * 256, 256), :],
                sem_right.at[slot, q],
            )
            for q in range(8)
        ]

    def raw_copy(e, t, q):
        lane = (block0 + e - 16 * t) * LANES
        return pltpu.make_async_copy(
            pieces[t][q].at[:, pl.ds(pl.multiple_of(lane, LANES), LANES)],
            raw.at[e, pl.ds(q * 256, 256), :],
            sem_raw.at[e, q],
        )

    meta_copies = [
        pltpu.make_async_copy(
            pieces[2][q].at[:, pl.ds(2048, LANES)], meta.at[pl.ds(q * 256, 256), :], sem_meta.at[q]
        )
        for q in range(8)
    ]
    for copy in meta_copies:
        copy.start()
    for e in range(3):
        for t in range(3):

            @pl.when((block0 + e) // 16 == t)
            def _(e=e, t=t):
                for q in range(8):
                    raw_copy(e, t, q).start()

    for copy in right_copies(0, 0, 0):
        copy.start()

    for copy in meta_copies:
        copy.wait()
    w2 = omega[0] * omega[0]
    for q in range(8):
        m = meta[q * 256 : q * 256 + 256, :].astype(jnp.float32)
        delta = m[:, 0:1] + m[:, 1:2] + m[:, 2:3]
        w = -4.0 * m[:, 3:4] * delta / (delta * delta + w2) / math.sqrt(NV * NC)
        weight[q * 256 : q * 256 + 256, :] = jnp.broadcast_to(w, (256, LANES))

    for e in range(3):
        for t in range(3):

            @pl.when((block0 + e) // 16 == t)
            def _(e=e, t=t):
                for q in range(8):
                    raw_copy(e, t, q).wait()

        part = (block0 + e) // 16
        sz, sy, sx = (
            jnp.where(part == 0, STRIDES[0][a], jnp.where(part == 1, STRIDES[1][a], STRIDES[2][a]))
            for a in AXES
        )

        def reorder(n, carry, e=e, sz=sz, sy=sy, sx=sx):
            z, y, x = n // 16, (n // 4) % 4, n % 4
            for core in range(2):
                src = pl.multiple_of(core * 1024 + z * sz + y * sy + x * sx, 16)
                wsrc = pl.multiple_of(
                    core * 1024 + z * STRIDES[2]["z"] + y * STRIDES[2]["y"] + x * STRIDES[2]["x"], 16
                )
                dst = pl.multiple_of(core * 1024 + n * 16, 16)
                left[pl.ds(dst, 16), e * LANES : (e + 1) * LANES] = (
                    raw[e, pl.ds(src, 16), :].astype(jnp.float32) * weight[pl.ds(wsrc, 16), :]
                ).astype(jnp.bfloat16)
            return carry

        lax.fori_loop(0, 64, reorder, 0, unroll=4)

    for t in range(3):
        first, second, last = ORDERS[t]
        for core in range(2):
            for d3 in range(4):
                rows = []
                for d2 in range(4):
                    for d1 in range(4):
                        at = {first: d1, second: d2, last: d3}
                        src = core * 1024 + sum(STRIDES[0][a] * at[a] for a in AXES)
                        rows.append(left[src : src + 16, :])
                block = jnp.concatenate(rows, 0)
                k = core * 1024 + d3 * 256
                left_t[t, :, k : k + 256] = block.T

    steps = 2048 // BLOCK
    for t in range(3):

        def step(i, carry, t=t):
            n = t * steps + i
            slot = lax.rem(n, 2)
            for copy in right_copies(t, i, slot):
                copy.wait()

            @pl.when(i < steps - 1)
            def _():
                for copy in right_copies(t, i + 1, 1 - slot):
                    copy.start()

            if t < 2:

                @pl.when(i == steps - 1)
                def _():
                    for copy in right_copies(t + 1, 0, 1 - slot):
                        copy.start()

            def out_copy(n):
                s = lax.rem(n, 2)
                return pltpu.make_async_copy(
                    result.at[s],
                    out.at[:, pl.ds(pl.multiple_of(n * BLOCK, BLOCK), BLOCK)],
                    sem_out.at[s],
                )

            @pl.when(n >= 2)
            def _():
                out_copy(n - 2).wait()

            result[slot] = jnp.dot(left_t[t], right[slot], preferred_element_type=jnp.float32)
            out_copy(n).start()
            return carry

        lax.fori_loop(0, steps, step, 0)
    for n in (3 * steps - 2, 3 * steps - 1):
        pltpu.make_async_copy(
            result.at[n % 2], out.at[:, pl.ds(n * BLOCK, BLOCK)], sem_out.at[n % 2]
        ).wait()


def chi_rows(place, omega, pieces):
    smem = pl.BlockSpec(memory_space=pltpu.SMEM)
    hbm = pl.BlockSpec(memory_space=pl.ANY)
    return pl.pallas_call(
        chi_kernel,
        out_shape=jax.ShapeDtypeStruct((384, NG), jnp.float32),
        in_specs=[smem, smem] + [hbm] * 24,
        out_specs=hbm,
        scratch_shapes=[
            pltpu.VMEM((3, 2048, LANES), jnp.bfloat16),
            pltpu.VMEM((2048, LANES), jnp.bfloat16),
            pltpu.VMEM((2048, LANES), jnp.float32),
            pltpu.VMEM((2048, 384), jnp.bfloat16),
            pltpu.VMEM((3, 384, 2048), jnp.bfloat16),
            pltpu.VMEM((2, 2048, BLOCK), jnp.bfloat16),
            pltpu.VMEM((2, 384, BLOCK), jnp.float32),
            pltpu.SemaphoreType.DMA((3, 8)),
            pltpu.SemaphoreType.DMA((8,)),
            pltpu.SemaphoreType.DMA((2, 8)),
            pltpu.SemaphoreType.DMA((2,)),
        ],
        compiler_params=pltpu.CompilerParams(vmem_limit_bytes=32 * 1024 * 1024),
        cost_estimate=pl.CostEstimate(
            flops=2 * 384 * NG * 2048, bytes_accessed=35 * 1024 * 1024, transcendentals=0
        ),
        name="chi_rows",
    )(place, omega, *pieces)


def on_device(psi_val, psi_con, e_val, e_con, occ, omega, g_index):
    ga = lax.axis_index("ga")
    ba = lax.axis_index("ba")
    con = psi_con.reshape(16, 4, 8, NB)
    val = jnp.broadcast_to(psi_val.reshape(1, 4, 8, NB), (16, 4, 8, NB))
    psi = lax.all_to_all(jnp.concatenate([val, con], 1), "ga", 0, 0, tiled=True)

    delta = (lax.dynamic_slice(e_con, (ga * 4,), (4,))[None, :] - e_val[:, None]).reshape(PAIRS)
    taken = jnp.broadcast_to(occ.astype(jnp.float32)[:, None], (4, 4)).reshape(PAIRS)
    d1 = lax.reduce_precision(delta, 8, 7)
    d2 = lax.reduce_precision(delta - d1, 8, 7)
    d3 = delta - d1 - d2
    meta = jnp.stack([d1, d2, d3, taken], 1).astype(jnp.bfloat16)
    meta = jnp.pad(meta, ((0, 0), (0, LANES - 4)))

    parts = rho_parts(psi, g_index.reshape(1, NG), meta)

    pieces = []
    for t in range(3):
        first, second, last = ORDERS[t]
        a = jnp.concatenate(ring_gather(parts[t], first), 0)
        a = jnp.concatenate(ring_gather(a, second), 0)
        mine = ring_gather(a, last)
        pieces += mine + [send(b, core_pairs()) for b in mine]

    place = ga.astype(jnp.int32).reshape(1)
    mine_omega = lax.dynamic_slice(omega, (ba,), (1,))
    return chi_rows(place, mine_omega, pieces)[None]


def solution(mesh):
    placed = (P("ba", "ga"), P(None, "ga"), P("ba"), P(), P("ba"), P(), P())
    return jax.shard_map(
        on_device, mesh=mesh, in_specs=placed, out_specs=P("ba", "ga", None), check_vma=False
    )
```

time: 502 us -> 196 us (0.39)
  matrix products: 208 us -> 0 us
  waiting for transfers between devices: 254 us -> 58 us
  starting transfers between devices: 0.04 us -> 70 us
  Pallas kernels: 0 us -> 37.6 us
  local copies, waits for them, and re-layouts: 1.52 us -> 27.5 us
  blocking collectives: 22.9 us -> 0 us
  between operations: 13.5 us -> 0.51 us
    dot_general x2 -> x0, matrix products: 208 us -> none  [the longest x1 190 us: on_device(): lax.dot_general(table, density, (((1,), (1,)), ((), ())), preferred_eleme...]
    all_gather x1 -> x0, waiting for transfers between devices: 162 us -> none  [on_device(): lax.all_gather(mine, 'ga', axis=1, tiled=True)]
    reduce_scatter x1 -> x0, waiting for transfers between devices: 91.6 us -> none  [on_device(): lax.psum_scatter(lax.dot_general(table, density, (((1,), (1,)), ((), ()))...]
    ppermute x0 -> x39, starting transfers between devices: none -> 60.5 us  [send(): return lax.ppermute(a, ('ga', 'ba'), pairs)]
    ppermute x0 -> x39, waiting for transfers between devices: none -> 47.2 us  [send(): return lax.ppermute(a, ('ga', 'ba'), pairs)]
    pallas_call x0 -> x2, Pallas kernels: none -> 37.6 us  [the longest x1 25.4 us: chi_rows(): pl.pallas_call(chi_kernel, out_shape=jax.ShapeDtypeStruct((384, NG), jnp....]
    unnamed x8 -> x78, local copies, waits for them, and re-layouts: 0.03 us -> 26.3 us
    all_to_all x1 -> x0, blocking collectives: 22.9 us -> none  [on_device(): mine = lax.all_to_all(scaled, 'ba', split_axis=0, concat_axis=2, tiled=True)]
  transfers between devices with their start and end apart: 2 -> 40, of which waited for: 2 -> 12; matrix products, arithmetic and copies ran while one was open for 0% -> 1% of each run, Pallas kernels for 0% -> 0%
where the time goes in v1:
time: 196 us; the launch traced here: 194 us
  starting transfers between devices  70 us (36%)
  waiting for transfers between devices  58 us (30%)
  Pallas kernels  37.6 us (19%)
  local copies, waits for them, and re-layouts  27.5 us (14%)
    ppermute x39, starting transfers between devices, send(): return lax.ppermute(a, ('ga', 'ba'), pairs)  60.5 us
    ppermute x39, waiting for transfers between devices, send(): return lax.ppermute(a, ('ga', 'ba'), pairs)  47.2 us
    unnamed x78, local copies, waits for them, and re-layouts  26.3 us
    pallas_call x1, Pallas kernels, chi_rows(): pl.pallas_call(chi_kernel, out_shape=jax.ShapeDtypeStruct((384, NG), jnp....  25.4 us
    pallas_call x1, Pallas kernels, rho_parts(): pl.pallas_call(rho_kernel, out_shape=[jax.ShapeDtypeStruct((PAIRS, c), jn...  12.2 us
    all_to_all x1, waiting for transfers between devices, on_device(): psi = lax.all_to_all(jnp.concatenate([val, con], 1), 'ga', 0, 0, tiled=True)  10.8 us
    all_to_all x1, starting transfers between devices, on_device(): psi = lax.all_to_all(jnp.concatenate([val, con], 1), 'ga', 0, 0, tiled=True)  9.46 us
  transfers between devices with their start and end apart: 40, of which 12 were waited for; matrix products, arithmetic and copies ran while one was open for 1% of the time, Pallas kernels for 0%

profile of v1, /device:TPU:1, one launch (start us, length us, event | category | flops | bytes accessed | tf_op | source)
XLA Modules:
  0.0 194.5 jit_solution(9885981182420183399)
XLA Ops:
  2.7 9.5 %all-to-all-start = ((bf16[16,8,8,256]{3,2,1,0:T(8,128)(2,1)}), bf16[16,8,8,256]{3,2,1,0:T(8,128)(2,1)S(1)}, u32[]{:S(2)}, u32[]{:S(2)}) async-start(bf16[16,8,8,256]{3,2,1,0:T(8,128)(2,1)} %pad_maximum_fusion), calls=%async_computation | async-start | bytes 1048576 | tf_op jit(solution)/shard_map/all_to_all | solution.py:311
  12.7 10.8 %all-to-all-done.psi = bf16[16,8,8,256]{3,2,1,0:T(8,128)(2,1)S(1)} async-done(((bf16[16,8,8,256]{3,2,1,0:T(8,128)(2,1)}), bf16[16,8,8,256]{3,2,1,0:T(8,128)(2,1)S(1)}, u32[]{:S(2)}, u32[]{:S(2)}) %all-to-all-start) | async-done | bytes 524320 | tf_op jit(solution)/shard_map/all_to_all | solution.py:311
  23.5 12.2 %rho_pairs.1 = (bf16[16,2048]{1,0:T(8,128)(2,1)S(1)}, bf16[16,2048]{1,0:T(8,128)(2,1)S(1)}, bf16[16,2176]{1,0:T(8,128)(2,1)S(1)}) custom-call(bf16[16,8,8,256]{3,2,1,0:T(8,128)(2,1)S(1)} %all-to-all-done.psi, s32[1,6144]{1,0:T(1,128)S(1)} %bitcast.10, bf16[16,128]{1,0:T(8,128)(2,1)S(1)} %pad.4.meta, bf16[256,256]{1,0:T(8,128)(2,1)S(1)} %copy-done.3, ...), custom_call_target="tpu_custom_call" | custom-call | tf_op jit(solution)/shard_map/rho_pairs/pallas_call | solution.py:90
  36.9 1.5 collective-permute-start
  38.8 2.3 %collective-permute-start.13 = (bf16[16,2048]{1,0:T(8,128)(2,1)S(1)}, bf16[16,2048]{1,0:T(8,128)(2,1)S(1)}, u32[]{:S(2)}, u32[]{:S(2)}) collective-permute-start(bf16[16,2048]{1,0:T(8,128)(2,1)S(1)} %get-tuple-element.9), channel_id=1, source_target_pairs={{0,4},{8,28},{1,5},{9,29},{2,6},{10,30},{3,7},{11,31},{4,16},{12,8... | collective-permute-start | bytes 196616 | tf_op jit(solution)/shard_map/ppermute | solution.py:127
  41.1 2.7 %collective-permute-start.26 = (bf16[16,2176]{1,0:T(8,128)(2,1)S(1)}, bf16[16,2176]{1,0:T(8,128)(2,1)S(1)}, u32[]{:S(2)}, u32[]{:S(2)}) collective-permute-start(bf16[16,2176]{1,0:T(8,128)(2,1)S(1)} %get-tuple-element.10), channel_id=1, source_target_pairs={{0,32},{8,104},{1,33},{9,105},{2,34},{10,106},{3,35},{11,107},{4,3... | collective-permute-start | bytes 208904 | tf_op jit(solution)/shard_map/ppermute | solution.py:127
  43.9 1.3 collective-permute-start.2
  45.3 1.5 collective-permute-start.15
  46.8 1.4 collective-permute-start.28
  50.6 3.0 %collective-permute-done.3 = bf16[64,2048]{1,0:T(8,128)(2,1)S(1)} collective-permute-done((bf16[64,2048]{1,0:T(8,128)(2,1)S(1)}, bf16[64,2048]{1,0:T(8,128)(2,1)S(1)}, u32[]{:S(2)}, u32[]{:S(2)}) %collective-permute-start.3) | collective-permute-done | bytes 262176 | tf_op jit(solution)/shard_map/ppermute | solution.py:127
  53.6 2.3 %collective-permute-start.5 = (bf16[64,2048]{1,0:T(8,128)(2,1)S(1)}, bf16[64,2048]{1,0:T(8,128)(2,1)S(1)}, u32[]{:S(2)}, u32[]{:S(2)}) collective-permute-start(bf16[64,2048]{1,0:T(8,128)(2,1)S(1)} %collective-permute-done.3), channel_id=1, source_target_pairs={{0,4},{8,28},{1,5},{9,29},{2,6},{10,30},{3,7},{11,31},{4,16},{12,8... | collective-permute-start | bytes 786440 | tf_op jit(solution)/shard_map/ppermute | solution.py:127
  56.1 4.8 %collective-permute-done.5 = bf16[64,2048]{1,0:T(8,128)(2,1)S(1)} collective-permute-done((bf16[64,2048]{1,0:T(8,128)(2,1)S(1)}, bf16[64,2048]{1,0:T(8,128)(2,1)S(1)}, u32[]{:S(2)}, u32[]{:S(2)}) %collective-permute-start.5) | collective-permute-done | bytes 262176 | tf_op jit(solution)/shard_map/ppermute | solution.py:127
  61.0 5.9 %collective-permute-start.9 = (bf16[256,2048]{1,0:T(8,128)(2,1)S(1)}, bf16[256,2048]{1,0:T(8,128)(2,1)S(1)}, u32[]{:S(2)}, u32[]{:S(2)}) collective-permute-start(bf16[256,2048]{1,0:T(8,128)(2,1)S(1)} %constant_dynamic-update-slice_fusion.4.refs_2_), channel_id=1, source_target_pairs={{0,8},{8,0},{1,9},{9,1},{2,10},{10,2},{3,11},{11,3},{4,12},{12,4},... | collective-permute-start | bytes 3145736 | tf_op jit(solution)/shard_map/ppermute | solution.py:127
  66.8 2.3 %collective-permute-start.29 = (bf16[64,2176]{1,0:T(8,128)(2,1)S(1)}, bf16[64,2176]{1,0:T(8,128)(2,1)S(1)}, u32[]{:S(2)}, u32[]{:S(2)}) collective-permute-start(bf16[64,2176]{1,0:T(8,128)(2,1)S(1)} %get-tuple-element.11), channel_id=1, source_target_pairs={{0,1},{8,11},{1,2},{9,8},{2,3},{10,9},{3,0},{11,10},{4,5},{12,15},... | collective-permute-start | bytes 835592 | tf_op jit(solution)/shard_map/ppermute | solution.py:127
  69.6 2.3 %collective-permute-start.18 = (bf16[64,2048]{1,0:T(8,128)(2,1)S(1)}, bf16[64,2048]{1,0:T(8,128)(2,1)S(1)}, u32[]{:S(2)}, u32[]{:S(2)}) collective-permute-start(bf16[64,2048]{1,0:T(8,128)(2,1)S(1)} %collective-permute-done.16), channel_id=1, source_target_pairs={{0,32},{8,104},{1,33},{9,105},{2,34},{10,106},{3,35},{11,107},{4,3... | collective-permute-start | bytes 786440 | tf_op jit(solution)/shard_map/ppermute | solution.py:127
  72.7 3.1 %collective-permute-start.31 = (bf16[64,2176]{1,0:T(8,128)(2,1)S(1)}, bf16[64,2176]{1,0:T(8,128)(2,1)S(1)}, u32[]{:S(2)}, u32[]{:S(2)}) collective-permute-start(bf16[64,2176]{1,0:T(8,128)(2,1)S(1)} %collective-permute-done.29), channel_id=1, source_target_pairs={{0,1},{8,11},{1,2},{9,8},{2,3},{10,9},{3,0},{11,10},{4,5},{12,15},... | collective-permute-start | bytes 835592 | tf_op jit(solution)/shard_map/ppermute | solution.py:127
  77.0 1.9 collective-permute-start.6
  78.9 1.4 collective-permute-start.22
  81.6 2.4 %collective-permute-start.19 = (bf16[256,2048]{1,0:T(8,128)(2,1)S(1)}, bf16[256,2048]{1,0:T(8,128)(2,1)S(1)}, u32[]{:S(2)}, u32[]{:S(2)}) collective-permute-start(bf16[256,2048]{1,0:T(8,128)(2,1)S(1)} %constant_dynamic-update-slice_fusion.15.refs_10_), channel_id=1, source_target_pairs={{0,1},{8,11},{1,2},{9,8},{2,3},{10,9},{3,0},{11,10},{4,5},{12,15},... | collective-permute-start | bytes 3145736 | tf_op jit(solution)/shard_map/ppermute | solution.py:127
  84.1 13.4 %collective-permute-done.7.refs_4_ = bf16[256,2048]{1,0:T(8,128)(2,1)S(1)} collective-permute-done((bf16[256,2048]{1,0:T(8,128)(2,1)S(1)}, bf16[256,2048]{1,0:T(8,128)(2,1)S(1)}, u32[]{:S(2)}, u32[]{:S(2)}) %collective-permute-start.7) | collective-permute-done | bytes 1048608 | tf_op jit(solution)/shard_map/ppermute | solution.py:127
  97.5 4.4 %collective-permute-done.6.refs_3_ = bf16[256,2048]{1,0:T(8,128)(2,1)S(1)} collective-permute-done((bf16[256,2048]{1,0:T(8,128)(2,1)S(1)}, bf16[256,2048]{1,0:T(8,128)(2,1)S(1)}, u32[]{:S(2)}, u32[]{:S(2)}) %collective-permute-start.6) | collective-permute-done | bytes 1048608 | tf_op jit(solution)/shard_map/ppermute | solution.py:127
  103.7 3.7 %collective-permute-start.11 = (bf16[256,2048]{1,0:T(8,128)(2,1)S(1)}, bf16[256,2048]{1,0:T(8,128)(2,1)S(1)}, u32[]{:S(2)}, u32[]{:S(2)}) collective-permute-start(bf16[256,2048]{1,0:T(8,128)(2,1)S(1)} %collective-permute-done.7.refs_4_), channel_id=1, source_target_pairs={{0,8},{8,0},{1,9},{9,1},{2,10},{10,2},{3,11},{11,3},{4,12},{12,4},... | collective-permute-start | bytes 3145736 | tf_op jit(solution)/shard_map/ppermute | solution.py:127
  108.3 9.1 %collective-permute-done.32.refs_19_ = bf16[256,2176]{1,0:T(8,128)(2,1)} collective-permute-done((bf16[256,2176]{1,0:T(8,128)(2,1)S(1)}, bf16[256,2176]{1,0:T(8,128)(2,1)}, u32[]{:S(2)}, u32[]{:S(2)}) %collective-permute-start.32) | collective-permute-done | bytes 1114144 | tf_op jit(solution)/shard_map/ppermute | solution.py:127
  118.4 3.5 %collective-permute-start.8 = (bf16[256,2048]{1,0:T(8,128)(2,1)S(1)}, bf16[256,2048]{1,0:T(8,128)(2,1)}, u32[]{:S(2)}, u32[]{:S(2)}) collective-permute-start(bf16[256,2048]{1,0:T(8,128)(2,1)S(1)} %collective-permute-done.6.refs_3_), channel_id=1, source_target_pairs={{0,32},{8,104},{1,33},{9,105},{2,34},{10,106},{3,35},{11,107},{4,3... | collective-permute-start | bytes 3145736 | tf_op jit(solution)/shard_map/ppermute | solution.py:127
  122.9 7.1 %collective-permute-done.33.refs_20_ = bf16[256,2176]{1,0:T(8,128)(2,1)} collective-permute-done((bf16[256,2176]{1,0:T(8,128)(2,1)S(1)}, bf16[256,2176]{1,0:T(8,128)(2,1)}, u32[]{:S(2)}, u32[]{:S(2)}) %collective-permute-start.33) | collective-permute-done | bytes 1114144 | tf_op jit(solution)/shard_map/ppermute | solution.py:127
  130.0 1.4 collective-permute-start.24
  134.3 3.0 %collective-permute-start.21 = (bf16[256,2048]{1,0:T(8,128)(2,1)S(1)}, bf16[256,2048]{1,0:T(8,128)(2,1)}, u32[]{:S(2)}, u32[]{:S(2)}) collective-permute-start(bf16[256,2048]{1,0:T(8,128)(2,1)S(1)} %collective-permute-done.19.refs_11_), channel_id=1, source_target_pairs={{0,1},{8,11},{1,2},{9,8},{2,3},{10,9},{3,0},{11,10},{4,5},{12,15},... | collective-permute-start | bytes 3145736 | tf_op jit(solution)/shard_map/ppermute | solution.py:127
  138.3 8.2 %collective-permute-start.37 = (bf16[256,2176]{1,0:T(8,128)(2,1)}, bf16[256,2176]{1,0:T(8,128)(2,1)}, u32[]{:S(2)}, u32[]{:S(2)}) collective-permute-start(bf16[256,2176]{1,0:T(8,128)(2,1)} %collective-permute-done.33.refs_20_), channel_id=1, source_target_pairs={{0,8},{8,0},{1,9},{9,1},{2,10},{10,2},{3,11},{11,3},{4,12},{12,4},... | collective-permute-start | bytes 3342344 | tf_op jit(solution)/shard_map/ppermute | solution.py:127
  149.5 1.5 collective-permute-start.25
  151.6 2.3 %collective-permute-done.12.refs_9_ = bf16[256,2048]{1,0:T(8,128)(2,1)} collective-permute-done((bf16[256,2048]{1,0:T(8,128)(2,1)}, bf16[256,2048]{1,0:T(8,128)(2,1)}, u32[]{:S(2)}, u32[]{:S(2)}) %collective-permute-start.12) | collective-permute-done | bytes 1048608 | tf_op jit(solution)/shard_map/ppermute | solution.py:127
  153.9 1.5 collective-permute-done.25.refs_17_
  168.9 25.4 %chi_rows.1 = f32[384,6144]{1,0:T(8,128)} custom-call(s32[1]{0:T(128)} %bitcast.refs_0_, f32[1]{0:T(128)} %dynamic_slice.6.refs_1_, bf16[256,2048]{1,0:T(8,128)(2,1)S(1)} %constant_dynamic-update-slice_fusion.4.refs_2_, bf16[256,2048]{1,0:T(8,128)(2,1)S(1)} %copy-done.12, bf16[256,2048]{1,0:T(8,128)(2,1)S(1)} %copy-done.10, ...), custom_call_target="tpu_custom_call" | custom-call | flops 9663676416 | bytes 36700160 | tf_op jit(solution)/shard_map/chi_rows/pallas_call | solution.py:280
  (147 shorter events, 37.2 us)
Async XLA Ops:
  2.7 20.8 %all-to-all-start = ((bf16[16,8,8,256]{3,2,1,0:T(8,128)(2,1)}), bf16[16,8,8,256]{3,2,1,0:T(8,128)(2,1)S(1)}, u32[]{:S(2)}, u32[]{:S(2)}) async-start(bf16[16,8,8,256]{3,2,1,0:T(8,128)(2,1)} %pad_maximum_fusion), calls=%async_computation | async-start | bytes 1048576 | tf_op jit(solution)/shard_map/all_to_all | solution.py:311
  35.7 9.6 %collective-permute-start.1 = (bf16[16,2048]{1,0:T(8,128)(2,1)S(1)}, bf16[16,2048]{1,0:T(8,128)(2,1)S(1)}, u32[]{:S(2)}, u32[]{:S(2)}) collective-permute-start(bf16[16,2048]{1,0:T(8,128)(2,1)S(1)} %get-tuple-element.8), channel_id=1, source_target_pairs={{0,3},{8,9},{1,0},{9,10},{2,1},{10,11},{3,2},{11,8},{4,7},{12,13},... | collective-permute-start | bytes 196616 | tf_op jit(solution)/shard_map/ppermute | solution.py:127
  38.4 8.4 %collective-permute-start.14 = (bf16[16,2048]{1,0:T(8,128)(2,1)S(1)}, bf16[16,2048]{1,0:T(8,128)(2,1)S(1)}, u32[]{:S(2)}, u32[]{:S(2)}) collective-permute-start(bf16[16,2048]{1,0:T(8,128)(2,1)S(1)} %get-tuple-element.9), channel_id=1, source_target_pairs={{0,20},{8,12},{1,21},{9,13},{2,22},{10,14},{3,23},{11,15},{4,0},{1... | collective-permute-start | bytes 196616 | tf_op jit(solution)/shard_map/ppermute | solution.py:127
  41.1 8.0 %collective-permute-start.27 = (bf16[16,2176]{1,0:T(8,128)(2,1)S(1)}, bf16[16,2176]{1,0:T(8,128)(2,1)S(1)}, u32[]{:S(2)}, u32[]{:S(2)}) collective-permute-start(bf16[16,2176]{1,0:T(8,128)(2,1)S(1)} %get-tuple-element.10), channel_id=1, source_target_pairs={{0,96},{8,40},{1,97},{9,41},{2,98},{10,42},{3,99},{11,43},{4,100},... | collective-permute-start | bytes 208904 | tf_op jit(solution)/shard_map/ppermute | solution.py:127
  46.8 20.0 %collective-permute-start.28 = (bf16[16,2176]{1,0:T(8,128)(2,1)S(1)}, bf16[16,2176]{1,0:T(8,128)(2,1)S(1)}, u32[]{:S(2)}, u32[]{:S(2)}) collective-permute-start(bf16[16,2176]{1,0:T(8,128)(2,1)S(1)} %collective-permute-done.26), channel_id=1, source_target_pairs={{0,32},{8,104},{1,33},{9,105},{2,34},{10,106},{3,35},{11,107},{4,3... | collective-permute-start | bytes 208904 | tf_op jit(solution)/shard_map/ppermute | solution.py:127
  49.1 7.0 %collective-permute-start.4 = (bf16[64,2048]{1,0:T(8,128)(2,1)S(1)}, bf16[64,2048]{1,0:T(8,128)(2,1)S(1)}, u32[]{:S(2)}, u32[]{:S(2)}) collective-permute-start(bf16[64,2048]{1,0:T(8,128)(2,1)S(1)} %get-tuple-element.27), channel_id=1, source_target_pairs={{0,20},{8,12},{1,21},{9,13},{2,22},{10,14},{3,23},{11,15},{4,0},{1... | collective-permute-start | bytes 786440 | tf_op jit(solution)/shard_map/ppermute | solution.py:127
  49.9 19.7 %collective-permute-start.16 = (bf16[64,2048]{1,0:T(8,128)(2,1)S(1)}, bf16[64,2048]{1,0:T(8,128)(2,1)S(1)}, u32[]{:S(2)}, u32[]{:S(2)}) collective-permute-start(bf16[64,2048]{1,0:T(8,128)(2,1)S(1)} %get-tuple-element.19), channel_id=1, source_target_pairs={{0,32},{8,104},{1,33},{9,105},{2,34},{10,106},{3,35},{11,107},{4,3... | collective-permute-start | bytes 786440 | tf_op jit(solution)/shard_map/ppermute | solution.py:127
  53.6 7.4 %collective-permute-start.5 = (bf16[64,2048]{1,0:T(8,128)(2,1)S(1)}, bf16[64,2048]{1,0:T(8,128)(2,1)S(1)}, u32[]{:S(2)}, u32[]{:S(2)}) collective-permute-start(bf16[64,2048]{1,0:T(8,128)(2,1)S(1)} %collective-permute-done.3), channel_id=1, source_target_pairs={{0,4},{8,28},{1,5},{9,29},{2,6},{10,30},{3,7},{11,31},{4,16},{12,8... | collective-permute-start | bytes 786440 | tf_op jit(solution)/shard_map/ppermute | solution.py:127
  61.0 19.6 %collective-permute-start.9 = (bf16[256,2048]{1,0:T(8,128)(2,1)S(1)}, bf16[256,2048]{1,0:T(8,128)(2,1)S(1)}, u32[]{:S(2)}, u32[]{:S(2)}) collective-permute-start(bf16[256,2048]{1,0:T(8,128)(2,1)S(1)} %constant_dynamic-update-slice_fusion.4.refs_2_), channel_id=1, source_target_pairs={{0,8},{8,0},{1,9},{9,1},{2,10},{10,2},{3,11},{11,3},{4,12},{12,4},... | collective-permute-start | bytes 3145736 | tf_op jit(solution)/shard_map/ppermute | solution.py:127
  66.8 5.8 %collective-permute-start.29 = (bf16[64,2176]{1,0:T(8,128)(2,1)S(1)}, bf16[64,2176]{1,0:T(8,128)(2,1)S(1)}, u32[]{:S(2)}, u32[]{:S(2)}) collective-permute-start(bf16[64,2176]{1,0:T(8,128)(2,1)S(1)} %get-tuple-element.11), channel_id=1, source_target_pairs={{0,1},{8,11},{1,2},{9,8},{2,3},{10,9},{3,0},{11,10},{4,5},{12,15},... | collective-permute-start | bytes 835592 | tf_op jit(solution)/shard_map/ppermute | solution.py:127
  69.2 6.6 %collective-permute-start.17 = (bf16[64,2048]{1,0:T(8,128)(2,1)S(1)}, bf16[64,2048]{1,0:T(8,128)(2,1)S(1)}, u32[]{:S(2)}, u32[]{:S(2)}) collective-permute-start(bf16[64,2048]{1,0:T(8,128)(2,1)S(1)} %get-tuple-element.19), channel_id=1, source_target_pairs={{0,96},{8,40},{1,97},{9,41},{2,98},{10,42},{3,99},{11,43},{4,100},... | collective-permute-start | bytes 786440 | tf_op jit(solution)/shard_map/ppermute | solution.py:127
  69.6 9.3 %collective-permute-start.30 = (bf16[64,2176]{1,0:T(8,128)(2,1)S(1)}, bf16[64,2176]{1,0:T(8,128)(2,1)S(1)}, u32[]{:S(2)}, u32[]{:S(2)}) collective-permute-start(bf16[64,2176]{1,0:T(8,128)(2,1)S(1)} %get-tuple-element.11), channel_id=1, source_target_pairs={{0,3},{8,9},{1,0},{9,10},{2,1},{10,11},{3,2},{11,8},{4,7},{12,13},... | collective-permute-start | bytes 835592 | tf_op jit(solution)/shard_map/ppermute | solution.py:127
  69.6 7.4 %collective-permute-start.18 = (bf16[64,2048]{1,0:T(8,128)(2,1)S(1)}, bf16[64,2048]{1,0:T(8,128)(2,1)S(1)}, u32[]{:S(2)}, u32[]{:S(2)}) collective-permute-start(bf16[64,2048]{1,0:T(8,128)(2,1)S(1)} %collective-permute-done.16), channel_id=1, source_target_pairs={{0,32},{8,104},{1,33},{9,105},{2,34},{10,106},{3,35},{11,107},{4,3... | collective-permute-start | bytes 786440 | tf_op jit(solution)/shard_map/ppermute | solution.py:127
  72.7 7.7 %collective-permute-start.31 = (bf16[64,2176]{1,0:T(8,128)(2,1)S(1)}, bf16[64,2176]{1,0:T(8,128)(2,1)S(1)}, u32[]{:S(2)}, u32[]{:S(2)}) collective-permute-start(bf16[64,2176]{1,0:T(8,128)(2,1)S(1)} %collective-permute-done.29), channel_id=1, source_target_pairs={{0,1},{8,11},{1,2},{9,8},{2,3},{10,9},{3,0},{11,10},{4,5},{12,15},... | collective-permute-start | bytes 835592 | tf_op jit(solution)/shard_map/ppermute | solution.py:127
  75.8 21.6 %collective-permute-start.7 = (bf16[256,2048]{1,0:T(8,128)(2,1)S(1)}, bf16[256,2048]{1,0:T(8,128)(2,1)S(1)}, u32[]{:S(2)}, u32[]{:S(2)}) collective-permute-start(bf16[256,2048]{1,0:T(8,128)(2,1)S(1)} %constant_dynamic-update-slice_fusion.4.refs_2_), channel_id=1, source_target_pairs={{0,96},{8,40},{1,97},{9,41},{2,98},{10,42},{3,99},{11,43},{4,100},... | collective-permute-start | bytes 3145736 | tf_op jit(solution)/shard_map/ppermute | solution.py:127
  77.0 24.8 %collective-permute-start.6 = (bf16[256,2048]{1,0:T(8,128)(2,1)S(1)}, bf16[256,2048]{1,0:T(8,128)(2,1)S(1)}, u32[]{:S(2)}, u32[]{:S(2)}) collective-permute-start(bf16[256,2048]{1,0:T(8,128)(2,1)S(1)} %constant_dynamic-update-slice_fusion.4.refs_2_), channel_id=1, source_target_pairs={{0,32},{8,104},{1,33},{9,105},{2,34},{10,106},{3,35},{11,107},{4,3... | collective-permute-start | bytes 3145736 | tf_op jit(solution)/shard_map/ppermute | solution.py:127
  78.9 23.8 %collective-permute-start.22 = (bf16[256,2048]{1,0:T(8,128)(2,1)S(1)}, bf16[256,2048]{1,0:T(8,128)(2,1)S(1)}, u32[]{:S(2)}, u32[]{:S(2)}) collective-permute-start(bf16[256,2048]{1,0:T(8,128)(2,1)S(1)} %constant_dynamic-update-slice_fusion.15.refs_10_), channel_id=1, source_target_pairs={{0,8},{8,0},{1,9},{9,1},{2,10},{10,2},{3,11},{11,3},{4,12},{12,4},... | collective-permute-start | bytes 3145736 | tf_op jit(solution)/shard_map/ppermute | solution.py:127
  80.3 23.3 %collective-permute-start.20 = (bf16[256,2048]{1,0:T(8,128)(2,1)S(1)}, bf16[256,2048]{1,0:T(8,128)(2,1)S(1)}, u32[]{:S(2)}, u32[]{:S(2)}) collective-permute-start(bf16[256,2048]{1,0:T(8,128)(2,1)S(1)} %constant_dynamic-update-slice_fusion.15.refs_10_), channel_id=1, source_target_pairs={{0,3},{8,9},{1,0},{9,10},{2,1},{10,11},{3,2},{11,8},{4,7},{12,13},... | collective-permute-start | bytes 3145736 | tf_op jit(solution)/shard_map/ppermute | solution.py:127
  81.6 26.8 %collective-permute-start.19 = (bf16[256,2048]{1,0:T(8,128)(2,1)S(1)}, bf16[256,2048]{1,0:T(8,128)(2,1)S(1)}, u32[]{:S(2)}, u32[]{:S(2)}) collective-permute-start(bf16[256,2048]{1,0:T(8,128)(2,1)S(1)} %constant_dynamic-update-slice_fusion.15.refs_10_), channel_id=1, source_target_pairs={{0,1},{8,11},{1,2},{9,8},{2,3},{10,9},{3,0},{11,10},{4,5},{12,15},... | collective-permute-start | bytes 3145736 | tf_op jit(solution)/shard_map/ppermute | solution.py:127
  97.5 19.9 %collective-permute-start.32 = (bf16[256,2176]{1,0:T(8,128)(2,1)S(1)}, bf16[256,2176]{1,0:T(8,128)(2,1)}, u32[]{:S(2)}, u32[]{:S(2)}) collective-permute-start(bf16[256,2176]{1,0:T(8,128)(2,1)S(1)} %constant_dynamic-update-slice_fusion.26.refs_18_), channel_id=1, source_target_pairs={{0,4},{8,28},{1,5},{9,29},{2,6},{10,30},{3,7},{11,31},{4,16},{12,8... | collective-permute-start | bytes 3342344 | tf_op jit(solution)/shard_map/ppermute | solution.py:127
  101.9 15.5 %collective-permute-start.35 = (bf16[256,2176]{1,0:T(8,128)(2,1)S(1)}, bf16[256,2176]{1,0:T(8,128)(2,1)S(1)}, u32[]{:S(2)}, u32[]{:S(2)}) collective-permute-start(bf16[256,2176]{1,0:T(8,128)(2,1)S(1)} %constant_dynamic-update-slice_fusion.26.refs_18_), channel_id=1, source_target_pairs={{0,8},{8,0},{1,9},{9,1},{2,10},{10,2},{3,11},{11,3},{4,12},{12,4},... | collective-permute-start | bytes 3342344 | tf_op jit(solution)/shard_map/ppermute | solution.py:127
  103.7 26.3 %collective-permute-start.33 = (bf16[256,2176]{1,0:T(8,128)(2,1)S(1)}, bf16[256,2176]{1,0:T(8,128)(2,1)}, u32[]{:S(2)}, u32[]{:S(2)}) collective-permute-start(bf16[256,2176]{1,0:T(8,128)(2,1)S(1)} %constant_dynamic-update-slice_fusion.26.refs_18_), channel_id=1, source_target_pairs={{0,20},{8,12},{1,21},{9,13},{2,22},{10,14},{3,23},{11,15},{4,0},{1... | collective-permute-start | bytes 3342344 | tf_op jit(solution)/shard_map/ppermute | solution.py:127
  103.7 28.7 %collective-permute-start.11 = (bf16[256,2048]{1,0:T(8,128)(2,1)S(1)}, bf16[256,2048]{1,0:T(8,128)(2,1)S(1)}, u32[]{:S(2)}, u32[]{:S(2)}) collective-permute-start(bf16[256,2048]{1,0:T(8,128)(2,1)S(1)} %collective-permute-done.7.refs_4_), channel_id=1, source_target_pairs={{0,8},{8,0},{1,9},{9,1},{2,10},{10,2},{3,11},{11,3},{4,12},{12,4},... | collective-permute-start | bytes 3145736 | tf_op jit(solution)/shard_map/ppermute | solution.py:127
  108.3 25.0 %collective-permute-start.10 = (bf16[256,2048]{1,0:T(8,128)(2,1)S(1)}, bf16[256,2048]{1,0:T(8,128)(2,1)S(1)}, u32[]{:S(2)}, u32[]{:S(2)}) collective-permute-start(bf16[256,2048]{1,0:T(8,128)(2,1)S(1)} %collective-permute-done.6.refs_3_), channel_id=1, source_target_pairs={{0,8},{8,0},{1,9},{9,1},{2,10},{10,2},{3,11},{11,3},{4,12},{12,4},... | collective-permute-start | bytes 3145736 | tf_op jit(solution)/shard_map/ppermute | solution.py:127
  117.4 30.1 %collective-permute-start.34 = (bf16[256,2176]{1,0:T(8,128)(2,1)}, bf16[256,2176]{1,0:T(8,128)(2,1)}, u32[]{:S(2)}, u32[]{:S(2)}) collective-permute-start(bf16[256,2176]{1,0:T(8,128)(2,1)} %collective-permute-done.32.refs_19_), channel_id=1, source_target_pairs={{0,4},{8,28},{1,5},{9,29},{2,6},{10,30},{3,7},{11,31},{4,16},{12,8... | collective-permute-start | bytes 3342344 | tf_op jit(solution)/shard_map/ppermute | solution.py:127
  118.4 19.9 %collective-permute-start.8 = (bf16[256,2048]{1,0:T(8,128)(2,1)S(1)}, bf16[256,2048]{1,0:T(8,128)(2,1)}, u32[]{:S(2)}, u32[]{:S(2)}) collective-permute-start(bf16[256,2048]{1,0:T(8,128)(2,1)S(1)} %collective-permute-done.6.refs_3_), channel_id=1, source_target_pairs={{0,32},{8,104},{1,33},{9,105},{2,34},{10,106},{3,35},{11,107},{4,3... | collective-permute-start | bytes 3145736 | tf_op jit(solution)/shard_map/ppermute | solution.py:127
  130.0 16.5 %collective-permute-start.24 = (bf16[256,2048]{1,0:T(8,128)(2,1)S(1)}, bf16[256,2048]{1,0:T(8,128)(2,1)S(1)}, u32[]{:S(2)}, u32[]{:S(2)}) collective-permute-start(bf16[256,2048]{1,0:T(8,128)(2,1)S(1)} %collective-permute-done.20.refs_12_), channel_id=1, source_target_pairs={{0,8},{8,0},{1,9},{9,1},{2,10},{10,2},{3,11},{11,3},{4,12},{12,4},... | collective-permute-start | bytes 3145736 | tf_op jit(solution)/shard_map/ppermute | solution.py:127
  133.3 14.7 %collective-permute-start.23 = (bf16[256,2048]{1,0:T(8,128)(2,1)S(1)}, bf16[256,2048]{1,0:T(8,128)(2,1)S(1)}, u32[]{:S(2)}, u32[]{:S(2)}) collective-permute-start(bf16[256,2048]{1,0:T(8,128)(2,1)S(1)} %collective-permute-done.19.refs_11_), channel_id=1, source_target_pairs={{0,8},{8,0},{1,9},{9,1},{2,10},{10,2},{3,11},{11,3},{4,12},{12,4},... | collective-permute-start | bytes 3145736 | tf_op jit(solution)/shard_map/ppermute | solution.py:127
  134.3 15.2 %collective-permute-start.21 = (bf16[256,2048]{1,0:T(8,128)(2,1)S(1)}, bf16[256,2048]{1,0:T(8,128)(2,1)}, u32[]{:S(2)}, u32[]{:S(2)}) collective-permute-start(bf16[256,2048]{1,0:T(8,128)(2,1)S(1)} %collective-permute-done.19.refs_11_), channel_id=1, source_target_pairs={{0,1},{8,11},{1,2},{9,8},{2,3},{10,9},{3,0},{11,10},{4,5},{12,15},... | collective-permute-start | bytes 3145736 | tf_op jit(solution)/shard_map/ppermute | solution.py:127
  138.3 13.3 %collective-permute-start.37 = (bf16[256,2176]{1,0:T(8,128)(2,1)}, bf16[256,2176]{1,0:T(8,128)(2,1)}, u32[]{:S(2)}, u32[]{:S(2)}) collective-permute-start(bf16[256,2176]{1,0:T(8,128)(2,1)} %collective-permute-done.33.refs_20_), channel_id=1, source_target_pairs={{0,8},{8,0},{1,9},{9,1},{2,10},{10,2},{3,11},{11,3},{4,12},{12,4},... | collective-permute-start | bytes 3342344 | tf_op jit(solution)/shard_map/ppermute | solution.py:127
  147.5 7.9 %collective-permute-start.38 = (bf16[256,2176]{1,0:T(8,128)(2,1)}, bf16[256,2176]{1,0:T(8,128)(2,1)}, u32[]{:S(2)}, u32[]{:S(2)}) collective-permute-start(bf16[256,2176]{1,0:T(8,128)(2,1)} %collective-permute-done.34.refs_21_), channel_id=1, source_target_pairs={{0,8},{8,0},{1,9},{9,1},{2,10},{10,2},{3,11},{11,3},{4,12},{12,4},... | collective-permute-start | bytes 3342344 | tf_op jit(solution)/shard_map/ppermute | solution.py:127
  149.5 5.8 %collective-permute-start.25 = (bf16[256,2048]{1,0:T(8,128)(2,1)}, bf16[256,2048]{1,0:T(8,128)(2,1)}, u32[]{:S(2)}, u32[]{:S(2)}) collective-permute-start(bf16[256,2048]{1,0:T(8,128)(2,1)} %collective-permute-done.21.refs_13_), channel_id=1, source_target_pairs={{0,8},{8,0},{1,9},{9,1},{2,10},{10,2},{3,11},{11,3},{4,12},{12,4},... | collective-permute-start | bytes 3145736 | tf_op jit(solution)/shard_map/ppermute | solution.py:127
  (39 other events, 277.7 us)

commit v2 on v0

v2 whole, which is shorter than its diff:
```python
import functools
import math

import jax
import jax.numpy as jnp
import numpy as np
from jax import lax
from jax.experimental import pallas as pl
from jax.experimental.pallas import tpu as pltpu
from jax.sharding import PartitionSpec as P

NV = 32
NC = 64
N = 32768
NA = 128
NB = 256
NG = 6144
HALF = NG // 2
LANES = 128
PAIRS = 16
PARTS = (1024, 1024, 1152)
WIDE = HALF + LANES
AXES = ("z", "y", "x")
ORDERS = (("x", "y", "z"), ("y", "z", "x"), ("z", "x", "y"))
STRIDES = tuple({o[0]: 32, o[1]: 128, o[2]: 512} for o in ORDERS)
K = 2048
MIB = 1024 * 1024
VM = pl.BlockSpec(memory_space=pltpu.VMEM)
SM = pl.BlockSpec(memory_space=pltpu.SMEM)
HBM = pl.BlockSpec(memory_space=pltpu.HBM)


def split_bf16(a):
    hi = a.astype(np.float32).astype(jnp.bfloat16)
    lo = (a - hi.astype(np.float64)).astype(np.float32).astype(jnp.bfloat16)
    return hi, lo


def dft_constants():
    k1 = np.arange(NA)[:, None]
    ang = 2.0 * math.pi * ((k1 * np.arange(NA)[None, :]) % NA) / NA
    fh, fl = split_bf16(np.concatenate([np.cos(ang), np.sin(ang)], 0))
    first = np.concatenate([fh, fl], 1)
    tw = 2.0 * math.pi * ((k1 * np.arange(NB)[None, :]) % N) / N
    norm = math.sqrt(2.0 / N)
    tcos = (np.cos(tw) * norm).astype(np.float32)
    tsin = (np.sin(tw) * norm).astype(np.float32)
    b2 = 2.0 * math.pi * ((np.arange(NB)[:, None] * np.arange(NA)[None, :]) % NB) / NB
    sh, sl = split_bf16(np.concatenate([np.cos(b2), -np.sin(b2)], 0))
    second = np.concatenate([sh, sl, sh], 0)
    return first, tcos, tsin, second


def transform(psi, first, tcos, tsin, second, spec):
    bands = [psi[:, i].astype(jnp.float32).reshape(NA, NB) for i in range(8)]
    ca = tcos[...]
    sa = tsin[...]
    for p in range(PAIRS):
        d = (bands[p // 4] * bands[4 + p % 4]).astype(jnp.bfloat16)
        y = jnp.dot(first[...], jnp.concatenate([d, d], 0), preferred_element_type=jnp.float32)
        a, b = y[:NA], y[NA:]
        uv = jnp.concatenate([a * ca - b * sa, a * sa + b * ca], 1)
        hi = uv.astype(jnp.bfloat16)
        lo = (uv - hi.astype(jnp.float32)).astype(jnp.bfloat16)
        x = jnp.dot(
            jnp.concatenate([hi, hi, lo], 1), second[...], preferred_element_type=jnp.float32
        ).astype(jnp.bfloat16)
        spec[p * 64 : p * 64 + 64, 0:128] = x[:64]
        spec[p * 64 : p * 64 + 64, 128:256] = x[64:]


def pick(spec, gidx, meta, out):
    width = 256

    def step(i, carry):
        at = pl.ds(pl.multiple_of(i * width, width), width)
        g = gidx[:, at]
        k1 = lax.bitwise_and(g, 127)
        kk = lax.shift_right_logical(k1, 6) * 128 + lax.shift_right_logical(g, 7)
        hot = jnp.where(
            lax.broadcasted_iota(jnp.int32, (256, width), 0) == kk, 1.0, 0.0
        ).astype(jnp.bfloat16)
        o = jnp.dot(spec[...], hot, preferred_element_type=jnp.float32)
        m = lax.broadcasted_iota(jnp.int32, (64, width), 0) == lax.bitwise_and(k1, 63)
        picked = jnp.sum(jnp.where(m[None], o.reshape(PAIRS, 64, width), 0.0), axis=1)
        out[:, at] = picked.astype(jnp.bfloat16)
        return carry

    lax.fori_loop(0, HALF // width, step, 0)
    out[:, HALF:WIDE] = meta[...]


def transform_kernel(psi, gidx, meta, first, tcos, tsin, second, spec, out):
    transform(psi, first, tcos, tsin, second, spec)
    pick(spec, gidx, meta, out)


def rho_spectrum(psi, gidx, meta):
    return pl.pallas_call(
        transform_kernel,
        out_shape=[
            jax.ShapeDtypeStruct((PAIRS * 64, 256), jnp.bfloat16),
            jax.ShapeDtypeStruct((PAIRS, WIDE), jnp.bfloat16),
        ],
        in_specs=[VM] * 7,
        out_specs=[VM] * 2,
        compiler_params=pltpu.CompilerParams(vmem_limit_bytes=24 * MIB),
        name="rho_spectrum",
    )(psi, gidx, meta, *(jnp.asarray(c) for c in dft_constants()))


def rho_pick(spec, gidx, meta):
    return pl.pallas_call(
        pick,
        out_shape=jax.ShapeDtypeStruct((PAIRS, WIDE), jnp.bfloat16),
        in_specs=[VM] * 3,
        out_specs=VM,
        compiler_params=pltpu.CompilerParams(vmem_limit_bytes=24 * MIB),
        name="rho_pick",
    )(spec, gidx, meta)


def device_index(z, y, x, c):
    return (z * 4 + (y >> 1) * 2 + c) * 8 + (y & 1) * 4 + x


@functools.cache
def ring_pairs(axis, way):
    pairs = []
    for z in range(4):
        for y in range(4):
            for x in range(4):
                for c in range(2):
                    to = {"z": z, "y": y, "x": x}
                    to[axis] = (to[axis] + (way if c == 0 else -way)) % 4
                    pairs.append((device_index(z, y, x, c), device_index(to["z"], to["y"], to["x"], c)))
    return tuple(pairs)


@functools.cache
def core_pairs():
    return tuple(
        (device_index(z, y, x, c), device_index(z, y, x, 1 - c))
        for z in range(4) for y in range(4) for x in range(4) for c in range(2)
    )


def send(a, pairs):
    return lax.ppermute(a, ("ga", "ba"), pairs)


def ring_gather(a, axis):
    near = send(a, ring_pairs(axis, 1))
    other = send(a, ring_pairs(axis, -1))
    far = send(near, ring_pairs(axis, 1))
    return [a, near, other, far]


def in_vmem(a):
    return pltpu.with_memory_space_constraint(a, pltpu.VMEM)


def weighted_kernel(place, omega, *refs):
    pieces = [refs[4 * t : 4 * t + 4] for t in range(3)]
    left, weight = refs[12:]
    block0 = place[0] * 3
    w2 = omega[0] * omega[0]
    for d3 in range(4):
        m = pieces[2][d3][:, 1024:1152].astype(jnp.float32)
        delta = m[:, 0:1] + m[:, 1:2] + m[:, 2:3]
        w = -4.0 * m[:, 3:4] * delta / (delta * delta + w2) / math.sqrt(NV * NC)
        weight[d3 * 512 : d3 * 512 + 512, :] = jnp.broadcast_to(w, (512, LANES))
    for e in range(3):
        block = block0 + e
        for t in range(3):

            @pl.when(block // 8 == t)
            def _(e=e, t=t, block=block):
                lane = pl.ds(pl.multiple_of((block - 8 * t) * LANES, LANES), LANES)
                for n in range(64):
                    at = {"z": n // 16, "y": (n // 4) % 4, "x": n % 4}
                    src = sum(STRIDES[t][a] * at[a] for a in AXES)
                    wsrc = sum(STRIDES[2][a] * at[a] for a in AXES)
                    left[n * 32 : n * 32 + 32, e * LANES : (e + 1) * LANES] = (
                        pieces[t][src // 512][src % 512 : src % 512 + 32, lane].astype(jnp.float32)
                        * weight[wsrc : wsrc + 32, :]
                    ).astype(jnp.bfloat16)


def weighted(place, omega, pieces):
    return pl.pallas_call(
        weighted_kernel,
        out_shape=jax.ShapeDtypeStruct((K, 384), jnp.bfloat16),
        in_specs=[SM, SM] + [VM] * 12,
        out_specs=VM,
        scratch_shapes=[pltpu.VMEM((K, LANES), jnp.float32)],
        compiler_params=pltpu.CompilerParams(vmem_limit_bytes=24 * MIB),
        name="weighted",
    )(place, omega, *pieces)


SWAPPED = (0, 2, 1, 3)


def transposed(left, t, left_t, other):
    first, second, last = ORDERS[t]
    for d3 in range(4):
        rows = []
        for d2 in range(4):
            for d1 in range(4):
                at = {first: d1, second: d2, last: d3}
                if other:
                    src = sum(STRIDES[0][a] * SWAPPED[at[a]] for a in AXES)
                    rows += [left[src + 16 : src + 32, :], left[src : src + 16, :]]
                else:
                    src = sum(STRIDES[0][a] * at[a] for a in AXES)
                    rows.append(left[src : src + 32, :])
        left_t[:, d3 * 512 : d3 * 512 + 512] = jnp.concatenate(rows, 0).T


def product(left_t, pieces, cols):
    acc = jnp.dot(left_t[:, 0:512], pieces[0][:, cols], preferred_element_type=jnp.float32)
    for d3 in range(1, 4):
        acc += jnp.dot(
            left_t[:, d3 * 512 : d3 * 512 + 512], pieces[d3][:, cols], preferred_element_type=jnp.float32
        )
    return acc


def out_lane(block, half):
    return (block // 3) * 6 + half * 3 + lax.rem(block, 3)


def own_kernel(core, left, *refs):
    pieces = [refs[4 * t : 4 * t + 4] for t in range(3)]
    out, left_t, result, sem = refs[12:]
    half = core[0]

    def copies(n):
        slot = lax.rem(n, 2)
        return [
            pltpu.make_async_copy(
                result.at[slot, :, pl.ds(j * LANES, LANES)],
                out.at[:, pl.ds(pl.multiple_of(out_lane(n * 4 + j, half) * LANES, LANES), LANES)],
                sem.at[slot, j],
            )
            for j in range(4)
        ]

    for t in range(3):
        transposed(left, t, left_t, False)

        def step(i, carry, t=t):
            n = t * 2 + i

            @pl.when(n >= 2)
            def _():
                for copy in copies(n - 2):
                    copy.wait()

            for j in range(2):
                cols = pl.ds(pl.multiple_of(i * 512 + j * 256, 256), 256)
                result[lax.rem(n, 2), :, j * 256 : j * 256 + 256] = product(left_t, pieces[t], cols)
            for copy in copies(n):
                copy.start()
            return carry

        lax.fori_loop(0, 2, step, 0)
    for n in (4, 5):
        for copy in copies(n):
            copy.wait()


def own_half(core, left, pieces):
    return pl.pallas_call(
        own_kernel,
        out_shape=jax.ShapeDtypeStruct((384, NG), jnp.float32),
        in_specs=[SM, VM] + [VM] * 12,
        out_specs=HBM,
        scratch_shapes=[
            pltpu.VMEM((384, K), jnp.bfloat16),
            pltpu.VMEM((2, 384, 512), jnp.float32),
            pltpu.SemaphoreType.DMA((2, 4)),
        ],
        compiler_params=pltpu.CompilerParams(vmem_limit_bytes=24 * MIB),
        cost_estimate=pl.CostEstimate(flops=2 * 384 * HALF * K, bytes_accessed=20 * MIB, transcendentals=0),
        name="own_half",
    )(core, left, *pieces)


def other_kernel(t, left, p0, p1, p2, p3, out, left_t):
    transposed(left, t, left_t, True)

    def step(i, carry):
        cols = pl.ds(pl.multiple_of(i * 256, 256), 256)
        out[:, cols] = product(left_t, (p0, p1, p2, p3), cols).astype(jnp.bfloat16)
        return carry

    lax.fori_loop(0, 4, step, 0)


def other_rows(t, left, pieces):
    return pl.pallas_call(
        functools.partial(other_kernel, t),
        out_shape=jax.ShapeDtypeStruct((384, 1024), jnp.bfloat16),
        in_specs=[VM] * 5,
        out_specs=VM,
        scratch_shapes=[pltpu.VMEM((384, K), jnp.bfloat16)],
        compiler_params=pltpu.CompilerParams(vmem_limit_bytes=24 * MIB),
        cost_estimate=pl.CostEstimate(flops=2 * 384 * 1024 * K, bytes_accessed=6 * MIB, transcendentals=0),
        name="other_rows",
    )(left, *pieces)


def finish_kernel(core, r0, r1, r2, _, out, wide, sem):
    half = 1 - core[0]

    def copies(t):
        return [
            pltpu.make_async_copy(
                wide.at[t, :, pl.ds(j * LANES, LANES)],
                out.at[:, pl.ds(pl.multiple_of(out_lane(t * 8 + j, half) * LANES, LANES), LANES)],
                sem.at[t, j],
            )
            for j in range(8)
        ]

    for t, r in enumerate((r0, r1, r2)):
        for j, copy in enumerate(copies(t)):
            at = slice(j * LANES, j * LANES + LANES)
            wide[t, :, at] = r[:, at].astype(jnp.float32)
            copy.start()
    for t in range(3):
        for copy in copies(t):
            copy.wait()


def finish(core, rows, out):
    return pl.pallas_call(
        finish_kernel,
        out_shape=jax.ShapeDtypeStruct((384, NG), jnp.float32),
        in_specs=[SM, VM, VM, VM, HBM],
        out_specs=HBM,
        scratch_shapes=[pltpu.VMEM((3, 384, 1024), jnp.float32), pltpu.SemaphoreType.DMA((3, 8))],
        input_output_aliases={4: 0},
        compiler_params=pltpu.CompilerParams(vmem_limit_bytes=24 * MIB),
        name="finish",
    )(core, *rows, out)


def on_device(psi_val, psi_con, e_val, e_con, occ, omega, g_index):
    ga = lax.axis_index("ga")
    ba = lax.axis_index("ba")
    core = lax.rem(ga, 2).astype(jnp.int32)
    con = psi_con.reshape(16, 4, 8, NB)
    val = jnp.broadcast_to(psi_val.reshape(1, 4, 8, NB), (16, 4, 8, NB))
    psi = lax.all_to_all(jnp.concatenate([val, con], 1), "ga", 0, 0, tiled=True)

    delta = (lax.dynamic_slice(e_con, (ga * 4,), (4,))[None, :] - e_val[:, None]).reshape(PAIRS)
    taken = jnp.broadcast_to(occ.astype(jnp.float32)[:, None], (4, 4)).reshape(PAIRS)
    d1 = lax.reduce_precision(delta, 8, 7)
    d2 = lax.reduce_precision(delta - d1, 8, 7)
    d3 = delta - d1 - d2
    meta = jnp.stack([d1, d2, d3, taken], 1).astype(jnp.bfloat16)
    meta = jnp.pad(meta, ((0, 0), (0, LANES - 4)))

    halves = g_index.reshape(8, 2, 384).transpose(1, 0, 2).reshape(2, HALF)
    kept = lax.dynamic_slice(halves, (core, 0), (1, HALF))
    given = lax.dynamic_slice(halves, (1 - core, 0), (1, HALF))
    spec, give = rho_spectrum(psi, given, meta)
    got = send(give, core_pairs())
    keep = rho_pick(spec, kept, meta)

    pieces = []
    start = 0
    for t in range(3):
        first, second, last = ORDERS[t]
        cols = slice(start, start + PARTS[t])
        start += PARTS[t]
        a = jnp.concatenate([keep[:, cols], got[:, cols]], 0)
        a = jnp.concatenate(ring_gather(a, first), 0)
        a = jnp.concatenate(ring_gather(a, second), 0)
        pieces.append([in_vmem(b) for b in ring_gather(a, last)])
    everything = pieces[0] + pieces[1] + pieces[2]

    place = lax.div(ga, 2).astype(jnp.int32).reshape(1)
    mine_omega = lax.dynamic_slice(omega, (ba,), (1,))
    left = weighted(place, mine_omega, everything)
    left_other = send(left, core_pairs())
    out = own_half(core.reshape(1), left, everything)
    rows = [send(other_rows(t, left_other, pieces[t]), core_pairs()) for t in range(3)]
    return finish(core.reshape(1), rows, out)[None]


def solution(mesh):
    placed = (P("ba", "ga"), P(None, "ga"), P("ba"), P(), P("ba"), P(), P())
    return jax.shard_map(
        on_device, mesh=mesh, in_specs=placed, out_specs=P("ba", "ga", None), check_vma=False
    )
```

time: 502 us -> 171 us (0.34)
  matrix products: 208 us -> 0 us
  waiting for transfers between devices: 254 us -> 60.8 us
  starting transfers between devices: 0.04 us -> 48.3 us
  Pallas kernels: 0 us -> 45.1 us
  blocking collectives: 22.9 us -> 0 us
  between operations: 13.5 us -> 0.57 us
  local copies, waits for them, and re-layouts: 1.52 us -> 12.9 us
    dot_general x2 -> x0, matrix products: 208 us -> none  [the longest x1 190 us: on_device(): lax.dot_general(table, density, (((1,), (1,)), ((), ())), preferred_eleme...]
    all_gather x1 -> x0, waiting for transfers between devices: 162 us -> none  [on_device(): lax.all_gather(mine, 'ga', axis=1, tiled=True)]
    reduce_scatter x1 -> x0, waiting for transfers between devices: 91.6 us -> none  [on_device(): lax.psum_scatter(lax.dot_general(table, density, (((1,), (1,)), ((), ()))...]
    ppermute x0 -> x32, waiting for transfers between devices: none -> 50.2 us  [send(): return lax.ppermute(a, ('ga', 'ba'), pairs)]
    pallas_call x0 -> x8, Pallas kernels: none -> 45.1 us  [the longest x3 13.5 us: other_rows(): pl.pallas_call(functools.partial(other_kernel, t), out_shape=jax.ShapeDty...]
    ppermute x0 -> x32, starting transfers between devices: none -> 38.9 us  [send(): return lax.ppermute(a, ('ga', 'ba'), pairs)]
    all_to_all x1 -> x0, blocking collectives: 22.9 us -> none  [on_device(): mine = lax.all_to_all(scaled, 'ba', split_axis=0, concat_axis=2, tiled=True)]
    all_to_all x0 -> x1, waiting for transfers between devices: none -> 10.7 us  [on_device(): psi = lax.all_to_all(jnp.concatenate([val, con], 1), 'ga', 0, 0, tiled=True)]
  transfers between devices with their start and end apart: 2 -> 33, of which waited for: 2 -> 13; matrix products, arithmetic and copies ran while one was open for 0% -> 4% of each run, Pallas kernels for 0% -> 12%
where the time goes in v2:
time: 171 us; the launch traced here: 169 us
  waiting for transfers between devices  60.8 us (36%)
  starting transfers between devices  48.3 us (28%)
  Pallas kernels  45.1 us (26%)
  local copies, waits for them, and re-layouts  12.9 us (8%)
    ppermute x32, waiting for transfers between devices, send(): return lax.ppermute(a, ('ga', 'ba'), pairs)  50.2 us
    ppermute x32, starting transfers between devices, send(): return lax.ppermute(a, ('ga', 'ba'), pairs)  38.9 us
    pallas_call x3, Pallas kernels, other_rows(): pl.pallas_call(functools.partial(other_kernel, t), out_shape=jax.ShapeDty...  13.5 us
    pallas_call x1, Pallas kernels, own_half(): pl.pallas_call(own_kernel, out_shape=jax.ShapeDtypeStruct((384, NG), jnp....  11.5 us
    all_to_all x1, waiting for transfers between devices, on_device(): psi = lax.all_to_all(jnp.concatenate([val, con], 1), 'ga', 0, 0, tiled=True)  10.7 us
    unnamed x48, local copies, waits for them, and re-layouts  10.4 us
    all_to_all x1, starting transfers between devices, on_device(): psi = lax.all_to_all(jnp.concatenate([val, con], 1), 'ga', 0, 0, tiled=True)  9.46 us
    pallas_call x1, Pallas kernels, rho_spectrum(): pl.pallas_call(transform_kernel, out_shape=[jax.ShapeDtypeStruct((PAIRS *...  8.36 us
  transfers between devices with their start and end apart: 33, of which 13 were waited for; matrix products, arithmetic and copies ran while one was open for 4% of the time, Pallas kernels for 12%

profile of v2, /device:TPU:1, one launch (start us, length us, event | category | flops | bytes accessed | tf_op | source)
XLA Modules:
  0.0 168.7 jit_solution(15812030507050002293)
XLA Ops:
  2.7 9.5 %all-to-all-start = ((bf16[16,8,8,256]{3,2,1,0:T(8,128)(2,1)}), bf16[16,8,8,256]{3,2,1,0:T(8,128)(2,1)S(1)}, u32[]{:S(2)}, u32[]{:S(2)}) async-start(bf16[16,8,8,256]{3,2,1,0:T(8,128)(2,1)} %pad_maximum_fusion), calls=%async_computation | async-start | bytes 1048576 | tf_op jit(solution)/shard_map/all_to_all | solution.py:357
  12.8 10.7 %all-to-all-done.psi = bf16[16,8,8,256]{3,2,1,0:T(8,128)(2,1)S(1)} async-done(((bf16[16,8,8,256]{3,2,1,0:T(8,128)(2,1)}), bf16[16,8,8,256]{3,2,1,0:T(8,128)(2,1)S(1)}, u32[]{:S(2)}, u32[]{:S(2)}) %all-to-all-start) | async-done | bytes 524320 | tf_op jit(solution)/shard_map/all_to_all | solution.py:357
  23.5 8.4 %rho_spectrum.1 = (bf16[1024,256]{1,0:T(8,128)(2,1)S(1)}, bf16[16,3200]{1,0:T(8,128)(2,1)S(1)}) custom-call(bf16[16,8,8,256]{3,2,1,0:T(8,128)(2,1)S(1)} %all-to-all-done.psi, s32[1,3072]{1,0:T(1,128)S(1)} %get-tuple-element.46.gidx, bf16[16,128]{1,0:T(8,128)(2,1)S(1)} %pad.4.meta, bf16[256,256]{1,0:T(8,128)(2,1)S(1)} %copy-done.7, f32[128,256]{1,0:T(8,128)S(1)} %copy-done.8, ...), custom_call_target="tpu_custom_call" | custom-call | tf_op jit(solution)/shard_map/rho_spectrum/pallas_call | solution.py:99
  31.8 3.8 %rho_pick.1 = bf16[16,3200]{1,0:T(8,128)(2,1)S(1)} custom-call(bf16[1024,256]{1,0:T(8,128)(2,1)S(1)} %get-tuple-element.7.spec, s32[1,3072]{1,0:T(1,128)S(1)} %get-tuple-element.45.gidx, bf16[16,128]{1,0:T(8,128)(2,1)S(1)} %pad.4.meta), custom_call_target="tpu_custom_call" | custom-call | tf_op jit(solution)/shard_map/rho_pick/pallas_call | solution.py:113
  35.7 1.2 collective-permute-start
  41.6 2.4 %collective-permute-start.1 = (bf16[32,1024]{1,0:T(8,128)(2,1)S(1)}, bf16[32,1024]{1,0:T(8,128)(2,1)S(1)}, u32[]{:S(2)}, u32[]{:S(2)}) collective-permute-start(bf16[32,1024]{1,0:T(8,128)(2,1)S(1)} %pad_maximum_fusion.2), channel_id=1, source_target_pairs={{0,1},{8,11},{1,2},{9,8},{2,3},{10,9},{3,0},{11,10},{4,5},{12,15},... | collective-permute-start | bytes 196616 | tf_op jit(solution)/shard_map/ppermute | solution.py:149
  45.4 1.6 collective-permute-start.12
  47.6 3.0 %collective-permute-start.3 = (bf16[32,1024]{1,0:T(8,128)(2,1)S(1)}, bf16[32,1024]{1,0:T(8,128)(2,1)S(1)}, u32[]{:S(2)}, u32[]{:S(2)}) collective-permute-start(bf16[32,1024]{1,0:T(8,128)(2,1)S(1)} %collective-permute-done.1), channel_id=1, source_target_pairs={{0,1},{8,11},{1,2},{9,8},{2,3},{10,9},{3,0},{11,10},{4,5},{12,15},... | collective-permute-start | bytes 196616 | tf_op jit(solution)/shard_map/ppermute | solution.py:149
  51.2 1.8 %collective-permute-start.21 = (bf16[32,1152]{1,0:T(8,128)(2,1)S(1)}, bf16[32,1152]{1,0:T(8,128)(2,1)S(1)}, u32[]{:S(2)}, u32[]{:S(2)}) collective-permute-start(bf16[32,1152]{1,0:T(8,128)(2,1)S(1)} %collective-permute-done.19), channel_id=1, source_target_pairs={{0,32},{8,104},{1,33},{9,105},{2,34},{10,106},{3,35},{11,107},{4,3... | collective-permute-start | bytes 221192 | tf_op jit(solution)/shard_map/ppermute | solution.py:149
  53.2 1.5 collective-permute-start.14
  55.3 1.5 collective-permute-start.5
  58.7 2.1 %collective-permute-done.4 = bf16[128,1024]{1,0:T(8,128)(2,1)S(1)} collective-permute-done((bf16[128,1024]{1,0:T(8,128)(2,1)S(1)}, bf16[128,1024]{1,0:T(8,128)(2,1)S(1)}, u32[]{:S(2)}, u32[]{:S(2)}) %collective-permute-start.4) | collective-permute-done | bytes 262176 | tf_op jit(solution)/shard_map/ppermute | solution.py:149
  60.8 1.3 collective-permute-start.15
  64.1 2.9 %collective-permute-start.24 = (bf16[128,1152]{1,0:T(8,128)(2,1)S(1)}, bf16[128,1152]{1,0:T(8,128)(2,1)S(1)}, u32[]{:S(2)}, u32[]{:S(2)}) collective-permute-start(bf16[128,1152]{1,0:T(8,128)(2,1)S(1)} %collective-permute-done.22), channel_id=1, source_target_pairs={{0,1},{8,11},{1,2},{9,8},{2,3},{10,9},{3,0},{11,10},{4,5},{12,15},... | collective-permute-start | bytes 884744 | tf_op jit(solution)/shard_map/ppermute | solution.py:149
  67.1 6.6 %collective-permute-done.24 = bf16[128,1152]{1,0:T(8,128)(2,1)S(1)} collective-permute-done((bf16[128,1152]{1,0:T(8,128)(2,1)S(1)}, bf16[128,1152]{1,0:T(8,128)(2,1)S(1)}, u32[]{:S(2)}, u32[]{:S(2)}) %collective-permute-start.24) | collective-permute-done | bytes 294944 | tf_op jit(solution)/shard_map/ppermute | solution.py:149
  74.7 3.5 %collective-permute-start.16 = (bf16[512,1024]{1,0:T(8,128)(2,1)S(1)}, bf16[512,1024]{1,0:T(8,128)(2,1)}, u32[]{:S(2)}, u32[]{:S(2)}) collective-permute-start(bf16[512,1024]{1,0:T(8,128)(2,1)S(1)} %constant_dynamic-update-slice_fusion.18.refs_4_.p0), channel_id=1, source_target_pairs={{0,1},{8,11},{1,2},{9,8},{2,3},{10,9},{3,0},{11,10},{4,5},{12,15},... | collective-permute-start | bytes 3145736 | tf_op jit(solution)/shard_map/ppermute | solution.py:149
  81.3 8.5 %collective-permute-done.25.refs_9_.p1 = bf16[512,1152]{1,0:T(8,128)(2,1)S(1)} collective-permute-done((bf16[512,1152]{1,0:T(8,128)(2,1)S(1)}, bf16[512,1152]{1,0:T(8,128)(2,1)S(1)}, u32[]{:S(2)}, u32[]{:S(2)}) %collective-permute-start.25) | collective-permute-done | bytes 1179680 | tf_op jit(solution)/shard_map/ppermute | solution.py:149
  90.5 4.7 %collective-permute-done.16.refs_5_.p1 = bf16[512,1024]{1,0:T(8,128)(2,1)} collective-permute-done((bf16[512,1024]{1,0:T(8,128)(2,1)S(1)}, bf16[512,1024]{1,0:T(8,128)(2,1)}, u32[]{:S(2)}, u32[]{:S(2)}) %collective-permute-start.16) | collective-permute-done | bytes 1048608 | tf_op jit(solution)/shard_map/ppermute | solution.py:149
  95.2 6.5 %collective-permute-done.17.refs_6_.p2 = bf16[512,1024]{1,0:T(8,128)(2,1)S(1)} collective-permute-done((bf16[512,1024]{1,0:T(8,128)(2,1)S(1)}, bf16[512,1024]{1,0:T(8,128)(2,1)S(1)}, u32[]{:S(2)}, u32[]{:S(2)}) %collective-permute-start.17) | collective-permute-done | bytes 1048608 | tf_op jit(solution)/shard_map/ppermute | solution.py:149
  102.7 1.7 collective-permute-start.9
  104.9 7.4 %collective-permute-done.8.refs_2_.p2 = bf16[512,1024]{1,0:T(8,128)(2,1)} collective-permute-done((bf16[512,1024]{1,0:T(8,128)(2,1)}, bf16[512,1024]{1,0:T(8,128)(2,1)}, u32[]{:S(2)}, u32[]{:S(2)}) %collective-permute-start.8) | collective-permute-done | bytes 1048608 | tf_op jit(solution)/shard_map/ppermute | solution.py:149
  112.4 4.6 %collective-permute-done.18.refs_7_.p3 = bf16[512,1024]{1,0:T(8,128)(2,1)} collective-permute-done((bf16[512,1024]{1,0:T(8,128)(2,1)}, bf16[512,1024]{1,0:T(8,128)(2,1)}, u32[]{:S(2)}, u32[]{:S(2)}) %collective-permute-start.18) | collective-permute-done | bytes 1048608 | tf_op jit(solution)/shard_map/ppermute | solution.py:149
  116.9 5.0 %collective-permute-done.9.refs_3_.p3 = bf16[512,1024]{1,0:T(8,128)(2,1)} collective-permute-done((bf16[512,1024]{1,0:T(8,128)(2,1)}, bf16[512,1024]{1,0:T(8,128)(2,1)}, u32[]{:S(2)}, u32[]{:S(2)}) %collective-permute-start.9) | collective-permute-done | bytes 1048608 | tf_op jit(solution)/shard_map/ppermute | solution.py:149
  122.0 1.2 copy-done.1
  124.5 5.6 %weighted.1.left = bf16[2048,384]{1,0:T(8,128)(2,1)S(1)} custom-call(s32[1]{0:T(128)} %bitcast.1.place, f32[1]{0:T(128)} %dynamic_slice.12.omega, bf16[512,1024]{1,0:T(8,128)(2,1)} %constant_dynamic-update-slice_fusion.5.refs_0_.p0, bf16[512,1024]{1,0:T(8,128)(2,1)} %collective-permute-done.7.refs_1_.p1, ...), custom_call_target="tpu_custom_call" | custom-call | tf_op jit(solution)/shard_map/weighted/pallas_call | solution.py:191
  130.1 6.7 %collective-permute-start.28 = (bf16[2048,384]{1,0:T(8,128)(2,1)S(1)}, bf16[2048,384]{1,0:T(8,128)(2,1)S(1)}, u32[]{:S(2)}, u32[]{:S(2)}) collective-permute-start(bf16[2048,384]{1,0:T(8,128)(2,1)S(1)} %weighted.1.left), channel_id=1, source_target_pairs={{0,8},{8,0},{1,9},{9,1},{2,10},{10,2},{3,11},{11,3},{4,12},{12,4},... | collective-permute-start | bytes 4718600 | tf_op jit(solution)/shard_map/ppermute | solution.py:149
  136.8 3.0 %collective-permute-done.28.left = bf16[2048,384]{1,0:T(8,128)(2,1)S(1)} collective-permute-done((bf16[2048,384]{1,0:T(8,128)(2,1)S(1)}, bf16[2048,384]{1,0:T(8,128)(2,1)S(1)}, u32[]{:S(2)}, u32[]{:S(2)}) %collective-permute-start.28) | collective-permute-done | bytes 1572896 | tf_op jit(solution)/shard_map/ppermute | solution.py:149
  139.8 4.1 %other_rows.5 = bf16[384,1024]{1,0:T(8,128)(2,1)S(1)} custom-call(bf16[2048,384]{1,0:T(8,128)(2,1)S(1)} %collective-permute-done.28.left, bf16[512,1152]{1,0:T(8,128)(2,1)S(1)} %constant_dynamic-update-slice_fusion.31.refs_8_.p0, bf16[512,1152]{1,0:T(8,128)(2,1)S(1)} %collective-permute-done.25.refs_9_.p1, ...), custom_call_target="tpu_custom_call" | custom-call | flops 1610612736 | bytes 6291456 | tf_op jit(solution)/shard_map/other_rows/pallas_call | solution.py:303
  144.3 4.4 %other_rows.4 = bf16[384,1024]{1,0:T(8,128)(2,1)S(1)} custom-call(bf16[2048,384]{1,0:T(8,128)(2,1)S(1)} %collective-permute-done.28.left, bf16[512,1024]{1,0:T(8,128)(2,1)S(1)} %copy-done.2, bf16[512,1024]{1,0:T(8,128)(2,1)} %collective-permute-done.16.refs_5_.p1, bf16[512,1024]{1,0:T(8,128)(2,1)S(1)} %copy-done.5, ...), custom_call_target="tpu_custom_call" | custom-call | flops 1610612736 | bytes 6291456 | tf_op jit(solution)/shard_map/other_rows/pallas_call | solution.py:303
  149.0 5.0 %other_rows.3 = bf16[384,1024]{1,0:T(8,128)(2,1)S(1)} custom-call(bf16[2048,384]{1,0:T(8,128)(2,1)S(1)} %collective-permute-done.28.left, bf16[512,1024]{1,0:T(8,128)(2,1)} %constant_dynamic-update-slice_fusion.5.refs_0_.p0, bf16[512,1024]{1,0:T(8,128)(2,1)} %collective-permute-done.7.refs_1_.p1, bf16[512,1024]{1,0:T(8,128)(2,1)} %collective-permute-done.8.refs_2_.p2, ...), custom_call_target="tpu_custom_call" | custom-call | flops 1610612736 | bytes 6291456 | tf_op jit(solution)/shard_map/other_rows/pallas_call | solution.py:303
  154.6 11.5 %own_half.1._ = f32[384,6144]{1,0:T(8,128)} custom-call(s32[1]{0:T(128)} %bitcast.core, bf16[2048,384]{1,0:T(8,128)(2,1)S(1)} %weighted.1.left, bf16[512,1024]{1,0:T(8,128)(2,1)} %constant_dynamic-update-slice_fusion.5.refs_0_.p0, bf16[512,1024]{1,0:T(8,128)(2,1)} %collective-permute-done.7.refs_1_.p1, bf16[512,1024]{1,0:T(8,128)(2,1)} %collective-permute-done.8.refs_2_.p2, ...), custom_call_target="tpu_custom_call" | custom-call | flops 4831838208 | bytes 20971520 | tf_op jit(solution)/shard_map/own_half/pallas_call | solution.py:275
  166.1 2.4 %finish.1 = f32[384,6144]{1,0:T(8,128)} custom-call(s32[1]{0:T(128)} %bitcast.core, bf16[384,1024]{1,0:T(8,128)(2,1)S(1)} %collective-permute-done.29.r0, bf16[384,1024]{1,0:T(8,128)(2,1)S(1)} %collective-permute-done.30.r1, bf16[384,1024]{1,0:T(8,128)(2,1)S(1)} %collective-permute-done.31.r2, f32[384,6144]{1,0:T(8,128)} %own_half.1._), custom_call_target="tpu_custom_call", output_to_operand_aliasing={{}: (4, {})} | custom-call | tf_op jit(solution)/shard_map/finish/pallas_call | solution.py:339
  (114 shorter events, 24.2 us)
Async XLA Ops:
  2.7 20.8 %all-to-all-start = ((bf16[16,8,8,256]{3,2,1,0:T(8,128)(2,1)}), bf16[16,8,8,256]{3,2,1,0:T(8,128)(2,1)S(1)}, u32[]{:S(2)}, u32[]{:S(2)}) async-start(bf16[16,8,8,256]{3,2,1,0:T(8,128)(2,1)} %pad_maximum_fusion), calls=%async_computation | async-start | bytes 1048576 | tf_op jit(solution)/shard_map/all_to_all | solution.py:357
  37.9 13.3 %collective-permute-start.19 = (bf16[32,1152]{1,0:T(8,128)(2,1)S(1)}, bf16[32,1152]{1,0:T(8,128)(2,1)S(1)}, u32[]{:S(2)}, u32[]{:S(2)}) collective-permute-start(bf16[32,1152]{1,0:T(8,128)(2,1)S(1)} %pad_maximum_fusion.1), channel_id=1, source_target_pairs={{0,32},{8,104},{1,33},{9,105},{2,34},{10,106},{3,35},{11,107},{4,3... | collective-permute-start | bytes 221192 | tf_op jit(solution)/shard_map/ppermute | solution.py:149
  38.6 14.5 %collective-permute-start.20 = (bf16[32,1152]{1,0:T(8,128)(2,1)S(1)}, bf16[32,1152]{1,0:T(8,128)(2,1)S(1)}, u32[]{:S(2)}, u32[]{:S(2)}) collective-permute-start(bf16[32,1152]{1,0:T(8,128)(2,1)S(1)} %pad_maximum_fusion.1), channel_id=1, source_target_pairs={{0,96},{8,40},{1,97},{9,41},{2,98},{10,42},{3,99},{11,43},{4,100},... | collective-permute-start | bytes 221192 | tf_op jit(solution)/shard_map/ppermute | solution.py:149
  40.1 3.9 %collective-permute-start.10 = (bf16[32,1024]{1,0:T(8,128)(2,1)S(1)}, bf16[32,1024]{1,0:T(8,128)(2,1)S(1)}, u32[]{:S(2)}, u32[]{:S(2)}) collective-permute-start(bf16[32,1024]{1,0:T(8,128)(2,1)S(1)} %pad_maximum_fusion.3), channel_id=1, source_target_pairs={{0,4},{8,28},{1,5},{9,29},{2,6},{10,30},{3,7},{11,31},{4,16},{12,8... | collective-permute-start | bytes 196616 | tf_op jit(solution)/shard_map/ppermute | solution.py:149
  40.4 7.1 %collective-permute-start.11 = (bf16[32,1024]{1,0:T(8,128)(2,1)S(1)}, bf16[32,1024]{1,0:T(8,128)(2,1)S(1)}, u32[]{:S(2)}, u32[]{:S(2)}) collective-permute-start(bf16[32,1024]{1,0:T(8,128)(2,1)S(1)} %pad_maximum_fusion.3), channel_id=1, source_target_pairs={{0,20},{8,12},{1,21},{9,13},{2,22},{10,14},{3,23},{11,15},{4,0},{1... | collective-permute-start | bytes 196616 | tf_op jit(solution)/shard_map/ppermute | solution.py:149
  41.6 3.8 %collective-permute-start.1 = (bf16[32,1024]{1,0:T(8,128)(2,1)S(1)}, bf16[32,1024]{1,0:T(8,128)(2,1)S(1)}, u32[]{:S(2)}, u32[]{:S(2)}) collective-permute-start(bf16[32,1024]{1,0:T(8,128)(2,1)S(1)} %pad_maximum_fusion.2), channel_id=1, source_target_pairs={{0,1},{8,11},{1,2},{9,8},{2,3},{10,9},{3,0},{11,10},{4,5},{12,15},... | collective-permute-start | bytes 196616 | tf_op jit(solution)/shard_map/ppermute | solution.py:149
  44.0 6.5 %collective-permute-start.2 = (bf16[32,1024]{1,0:T(8,128)(2,1)S(1)}, bf16[32,1024]{1,0:T(8,128)(2,1)S(1)}, u32[]{:S(2)}, u32[]{:S(2)}) collective-permute-start(bf16[32,1024]{1,0:T(8,128)(2,1)S(1)} %pad_maximum_fusion.2), channel_id=1, source_target_pairs={{0,3},{8,9},{1,0},{9,10},{2,1},{10,11},{3,2},{11,8},{4,7},{12,13},... | collective-permute-start | bytes 196616 | tf_op jit(solution)/shard_map/ppermute | solution.py:149
  45.4 7.8 %collective-permute-start.12 = (bf16[32,1024]{1,0:T(8,128)(2,1)S(1)}, bf16[32,1024]{1,0:T(8,128)(2,1)S(1)}, u32[]{:S(2)}, u32[]{:S(2)}) collective-permute-start(bf16[32,1024]{1,0:T(8,128)(2,1)S(1)} %collective-permute-done.10), channel_id=1, source_target_pairs={{0,4},{8,28},{1,5},{9,29},{2,6},{10,30},{3,7},{11,31},{4,16},{12,8... | collective-permute-start | bytes 196616 | tf_op jit(solution)/shard_map/ppermute | solution.py:149
  47.6 7.1 %collective-permute-start.3 = (bf16[32,1024]{1,0:T(8,128)(2,1)S(1)}, bf16[32,1024]{1,0:T(8,128)(2,1)S(1)}, u32[]{:S(2)}, u32[]{:S(2)}) collective-permute-start(bf16[32,1024]{1,0:T(8,128)(2,1)S(1)} %collective-permute-done.1), channel_id=1, source_target_pairs={{0,1},{8,11},{1,2},{9,8},{2,3},{10,9},{3,0},{11,10},{4,5},{12,15},... | collective-permute-start | bytes 196616 | tf_op jit(solution)/shard_map/ppermute | solution.py:149
  51.2 5.6 %collective-permute-start.21 = (bf16[32,1152]{1,0:T(8,128)(2,1)S(1)}, bf16[32,1152]{1,0:T(8,128)(2,1)S(1)}, u32[]{:S(2)}, u32[]{:S(2)}) collective-permute-start(bf16[32,1152]{1,0:T(8,128)(2,1)S(1)} %collective-permute-done.19), channel_id=1, source_target_pairs={{0,32},{8,104},{1,33},{9,105},{2,34},{10,106},{3,35},{11,107},{4,3... | collective-permute-start | bytes 221192 | tf_op jit(solution)/shard_map/ppermute | solution.py:149
  53.1 5.6 %collective-permute-start.13 = (bf16[128,1024]{1,0:T(8,128)(2,1)S(1)}, bf16[128,1024]{1,0:T(8,128)(2,1)S(1)}, u32[]{:S(2)}, u32[]{:S(2)}) collective-permute-start(bf16[128,1024]{1,0:T(8,128)(2,1)S(1)} %get-tuple-element.33), channel_id=1, source_target_pairs={{0,32},{8,104},{1,33},{9,105},{2,34},{10,106},{3,35},{11,107},{4,3... | collective-permute-start | bytes 786440 | tf_op jit(solution)/shard_map/ppermute | solution.py:149
  53.2 9.6 %collective-permute-start.14 = (bf16[128,1024]{1,0:T(8,128)(2,1)S(1)}, bf16[128,1024]{1,0:T(8,128)(2,1)S(1)}, u32[]{:S(2)}, u32[]{:S(2)}) collective-permute-start(bf16[128,1024]{1,0:T(8,128)(2,1)S(1)} %get-tuple-element.33), channel_id=1, source_target_pairs={{0,96},{8,40},{1,97},{9,41},{2,98},{10,42},{3,99},{11,43},{4,100},... | collective-permute-start | bytes 786440 | tf_op jit(solution)/shard_map/ppermute | solution.py:149
  55.3 5.5 %collective-permute-start.4 = (bf16[128,1024]{1,0:T(8,128)(2,1)S(1)}, bf16[128,1024]{1,0:T(8,128)(2,1)S(1)}, u32[]{:S(2)}, u32[]{:S(2)}) collective-permute-start(bf16[128,1024]{1,0:T(8,128)(2,1)S(1)} %get-tuple-element.39), channel_id=1, source_target_pairs={{0,4},{8,28},{1,5},{9,29},{2,6},{10,30},{3,7},{11,31},{4,16},{12,8... | collective-permute-start | bytes 786440 | tf_op jit(solution)/shard_map/ppermute | solution.py:149
  55.3 18.6 %collective-permute-start.5 = (bf16[128,1024]{1,0:T(8,128)(2,1)S(1)}, bf16[128,1024]{1,0:T(8,128)(2,1)S(1)}, u32[]{:S(2)}, u32[]{:S(2)}) collective-permute-start(bf16[128,1024]{1,0:T(8,128)(2,1)S(1)} %get-tuple-element.39), channel_id=1, source_target_pairs={{0,20},{8,12},{1,21},{9,13},{2,22},{10,14},{3,23},{11,15},{4,0},{1... | collective-permute-start | bytes 786440 | tf_op jit(solution)/shard_map/ppermute | solution.py:149
  56.8 7.3 %collective-permute-start.22 = (bf16[128,1152]{1,0:T(8,128)(2,1)S(1)}, bf16[128,1152]{1,0:T(8,128)(2,1)S(1)}, u32[]{:S(2)}, u32[]{:S(2)}) collective-permute-start(bf16[128,1152]{1,0:T(8,128)(2,1)S(1)} %get-tuple-element.27), channel_id=1, source_target_pairs={{0,1},{8,11},{1,2},{9,8},{2,3},{10,9},{3,0},{11,10},{4,5},{12,15},... | collective-permute-start | bytes 884744 | tf_op jit(solution)/shard_map/ppermute | solution.py:149
  58.7 8.3 %collective-permute-start.23 = (bf16[128,1152]{1,0:T(8,128)(2,1)S(1)}, bf16[128,1152]{1,0:T(8,128)(2,1)S(1)}, u32[]{:S(2)}, u32[]{:S(2)}) collective-permute-start(bf16[128,1152]{1,0:T(8,128)(2,1)S(1)} %get-tuple-element.27), channel_id=1, source_target_pairs={{0,3},{8,9},{1,0},{9,10},{2,1},{10,11},{3,2},{11,8},{4,7},{12,13},... | collective-permute-start | bytes 884744 | tf_op jit(solution)/shard_map/ppermute | solution.py:149
  60.8 13.8 %collective-permute-start.15 = (bf16[128,1024]{1,0:T(8,128)(2,1)S(1)}, bf16[128,1024]{1,0:T(8,128)(2,1)S(1)}, u32[]{:S(2)}, u32[]{:S(2)}) collective-permute-start(bf16[128,1024]{1,0:T(8,128)(2,1)S(1)} %collective-permute-done.13), channel_id=1, source_target_pairs={{0,32},{8,104},{1,33},{9,105},{2,34},{10,106},{3,35},{11,107},{4,3... | collective-permute-start | bytes 786440 | tf_op jit(solution)/shard_map/ppermute | solution.py:149
  62.8 16.3 %collective-permute-start.6 = (bf16[128,1024]{1,0:T(8,128)(2,1)S(1)}, bf16[128,1024]{1,0:T(8,128)(2,1)S(1)}, u32[]{:S(2)}, u32[]{:S(2)}) collective-permute-start(bf16[128,1024]{1,0:T(8,128)(2,1)S(1)} %collective-permute-done.4), channel_id=1, source_target_pairs={{0,4},{8,28},{1,5},{9,29},{2,6},{10,30},{3,7},{11,31},{4,16},{12,8... | collective-permute-start | bytes 786440 | tf_op jit(solution)/shard_map/ppermute | solution.py:149
  64.1 9.7 %collective-permute-start.24 = (bf16[128,1152]{1,0:T(8,128)(2,1)S(1)}, bf16[128,1152]{1,0:T(8,128)(2,1)S(1)}, u32[]{:S(2)}, u32[]{:S(2)}) collective-permute-start(bf16[128,1152]{1,0:T(8,128)(2,1)S(1)} %collective-permute-done.22), channel_id=1, source_target_pairs={{0,1},{8,11},{1,2},{9,8},{2,3},{10,9},{3,0},{11,10},{4,5},{12,15},... | collective-permute-start | bytes 884744 | tf_op jit(solution)/shard_map/ppermute | solution.py:149
  73.8 16.0 %collective-permute-start.25 = (bf16[512,1152]{1,0:T(8,128)(2,1)S(1)}, bf16[512,1152]{1,0:T(8,128)(2,1)S(1)}, u32[]{:S(2)}, u32[]{:S(2)}) collective-permute-start(bf16[512,1152]{1,0:T(8,128)(2,1)S(1)} %constant_dynamic-update-slice_fusion.31.refs_8_.p0), channel_id=1, source_target_pairs={{0,4},{8,28},{1,5},{9,29},{2,6},{10,30},{3,7},{11,31},{4,16},{12,8... | collective-permute-start | bytes 3538952 | tf_op jit(solution)/shard_map/ppermute | solution.py:149
  74.7 20.6 %collective-permute-start.16 = (bf16[512,1024]{1,0:T(8,128)(2,1)S(1)}, bf16[512,1024]{1,0:T(8,128)(2,1)}, u32[]{:S(2)}, u32[]{:S(2)}) collective-permute-start(bf16[512,1024]{1,0:T(8,128)(2,1)S(1)} %constant_dynamic-update-slice_fusion.18.refs_4_.p0), channel_id=1, source_target_pairs={{0,1},{8,11},{1,2},{9,8},{2,3},{10,9},{3,0},{11,10},{4,5},{12,15},... | collective-permute-start | bytes 3145736 | tf_op jit(solution)/shard_map/ppermute | solution.py:149
  78.1 23.5 %collective-permute-start.17 = (bf16[512,1024]{1,0:T(8,128)(2,1)S(1)}, bf16[512,1024]{1,0:T(8,128)(2,1)S(1)}, u32[]{:S(2)}, u32[]{:S(2)}) collective-permute-start(bf16[512,1024]{1,0:T(8,128)(2,1)S(1)} %constant_dynamic-update-slice_fusion.18.refs_4_.p0), channel_id=1, source_target_pairs={{0,3},{8,9},{1,0},{9,10},{2,1},{10,11},{3,2},{11,8},{4,7},{12,13},... | collective-permute-start | bytes 3145736 | tf_op jit(solution)/shard_map/ppermute | solution.py:149
  79.8 22.9 %collective-permute-start.7 = (bf16[512,1024]{1,0:T(8,128)(2,1)}, bf16[512,1024]{1,0:T(8,128)(2,1)}, u32[]{:S(2)}, u32[]{:S(2)}) collective-permute-start(bf16[512,1024]{1,0:T(8,128)(2,1)} %constant_dynamic-update-slice_fusion.5.refs_0_.p0), channel_id=1, source_target_pairs={{0,32},{8,104},{1,33},{9,105},{2,34},{10,106},{3,35},{11,107},{4,3... | collective-permute-start | bytes 3145736 | tf_op jit(solution)/shard_map/ppermute | solution.py:149
  80.7 31.6 %collective-permute-start.26 = (bf16[512,1152]{1,0:T(8,128)(2,1)S(1)}, bf16[512,1152]{1,0:T(8,128)(2,1)S(1)}, u32[]{:S(2)}, u32[]{:S(2)}) collective-permute-start(bf16[512,1152]{1,0:T(8,128)(2,1)S(1)} %constant_dynamic-update-slice_fusion.31.refs_8_.p0), channel_id=1, source_target_pairs={{0,20},{8,12},{1,21},{9,13},{2,22},{10,14},{3,23},{11,15},{4,0},{1... | collective-permute-start | bytes 3538952 | tf_op jit(solution)/shard_map/ppermute | solution.py:149
  89.8 32.2 %collective-permute-start.27 = (bf16[512,1152]{1,0:T(8,128)(2,1)S(1)}, bf16[512,1152]{1,0:T(8,128)(2,1)}, u32[]{:S(2)}, u32[]{:S(2)}) collective-permute-start(bf16[512,1152]{1,0:T(8,128)(2,1)S(1)} %collective-permute-done.25.refs_9_.p1), channel_id=1, source_target_pairs={{0,4},{8,28},{1,5},{9,29},{2,6},{10,30},{3,7},{11,31},{4,16},{12,8... | collective-permute-start | bytes 3538952 | tf_op jit(solution)/shard_map/ppermute | solution.py:149
  95.2 17.2 %collective-permute-start.8 = (bf16[512,1024]{1,0:T(8,128)(2,1)}, bf16[512,1024]{1,0:T(8,128)(2,1)}, u32[]{:S(2)}, u32[]{:S(2)}) collective-permute-start(bf16[512,1024]{1,0:T(8,128)(2,1)} %constant_dynamic-update-slice_fusion.5.refs_0_.p0), channel_id=1, source_target_pairs={{0,96},{8,40},{1,97},{9,41},{2,98},{10,42},{3,99},{11,43},{4,100},... | collective-permute-start | bytes 3145736 | tf_op jit(solution)/shard_map/ppermute | solution.py:149
  102.7 14.3 %collective-permute-start.18 = (bf16[512,1024]{1,0:T(8,128)(2,1)}, bf16[512,1024]{1,0:T(8,128)(2,1)}, u32[]{:S(2)}, u32[]{:S(2)}) collective-permute-start(bf16[512,1024]{1,0:T(8,128)(2,1)} %collective-permute-done.16.refs_5_.p1), channel_id=1, source_target_pairs={{0,1},{8,11},{1,2},{9,8},{2,3},{10,9},{3,0},{11,10},{4,5},{12,15},... | collective-permute-start | bytes 3145736 | tf_op jit(solution)/shard_map/ppermute | solution.py:149
  102.7 19.3 %collective-permute-start.9 = (bf16[512,1024]{1,0:T(8,128)(2,1)}, bf16[512,1024]{1,0:T(8,128)(2,1)}, u32[]{:S(2)}, u32[]{:S(2)}) collective-permute-start(bf16[512,1024]{1,0:T(8,128)(2,1)} %collective-permute-done.7.refs_1_.p1), channel_id=1, source_target_pairs={{0,32},{8,104},{1,33},{9,105},{2,34},{10,106},{3,35},{11,107},{4,3... | collective-permute-start | bytes 3145736 | tf_op jit(solution)/shard_map/ppermute | solution.py:149
  130.1 9.7 %collective-permute-start.28 = (bf16[2048,384]{1,0:T(8,128)(2,1)S(1)}, bf16[2048,384]{1,0:T(8,128)(2,1)S(1)}, u32[]{:S(2)}, u32[]{:S(2)}) collective-permute-start(bf16[2048,384]{1,0:T(8,128)(2,1)S(1)} %weighted.1.left), channel_id=1, source_target_pairs={{0,8},{8,0},{1,9},{9,1},{2,10},{10,2},{3,11},{11,3},{4,12},{12,4},... | collective-permute-start | bytes 4718600 | tf_op jit(solution)/shard_map/ppermute | solution.py:149
  143.9 22.2 %collective-permute-start.31 = (bf16[384,1024]{1,0:T(8,128)(2,1)S(1)}, bf16[384,1024]{1,0:T(8,128)(2,1)S(1)}, u32[]{:S(2)}, u32[]{:S(2)}) collective-permute-start(bf16[384,1024]{1,0:T(8,128)(2,1)S(1)} %other_rows.5), channel_id=1, source_target_pairs={{0,8},{8,0},{1,9},{9,1},{2,10},{10,2},{3,11},{11,3},{4,12},{12,4},... | collective-permute-start | bytes 2359304 | tf_op jit(solution)/shard_map/ppermute | solution.py:149
  148.7 17.4 %collective-permute-start.30 = (bf16[384,1024]{1,0:T(8,128)(2,1)S(1)}, bf16[384,1024]{1,0:T(8,128)(2,1)S(1)}, u32[]{:S(2)}, u32[]{:S(2)}) collective-permute-start(bf16[384,1024]{1,0:T(8,128)(2,1)S(1)} %other_rows.4), channel_id=1, source_target_pairs={{0,8},{8,0},{1,9},{9,1},{2,10},{10,2},{3,11},{11,3},{4,12},{12,4},... | collective-permute-start | bytes 2359304 | tf_op jit(solution)/shard_map/ppermute | solution.py:149
  154.0 12.2 %collective-permute-start.29 = (bf16[384,1024]{1,0:T(8,128)(2,1)S(1)}, bf16[384,1024]{1,0:T(8,128)(2,1)S(1)}, u32[]{:S(2)}, u32[]{:S(2)}) collective-permute-start(bf16[384,1024]{1,0:T(8,128)(2,1)S(1)} %other_rows.3), channel_id=1, source_target_pairs={{0,8},{8,0},{1,9},{9,1},{2,10},{10,2},{3,11},{11,3},{4,12},{12,4},... | collective-permute-start | bytes 2359304 | tf_op jit(solution)/shard_map/ppermute | solution.py:149
  (16 other events, 201.3 us)

commit v3 on v2

--- a/solution.py
+++ b/solution.py
@@ -149,6 +149,23 @@
     return lax.ppermute(a, ("ga", "ba"), pairs)
 
 
+def far_pairs(axis):
+    pairs = []
+    for z in range(4):
+        for y in range(4):
+            for x in range(4):
+                for c in range(2):
+                    to = {"z": z, "y": y, "x": x}
+                    to[axis] = (to[axis] + 2) % 4
+                    pairs.append((device_index(z, y, x, c), device_index(to["z"], to["y"], to["x"], c)))
+    return tuple(pairs)
+
+
+def direct_gather(a, axis):
+    pairs = (ring_pairs(axis, 1), ring_pairs(axis, -1), far_pairs(axis))
+    return jnp.concatenate([a] + [send(a, p) for p in pairs], 0)
+
+
 def ring_gather(a, axis):
     near = send(a, ring_pairs(axis, 1))
     other = send(a, ring_pairs(axis, -1))
@@ -163,28 +180,26 @@
 def weighted_kernel(place, omega, *refs):
     pieces = [refs[4 * t : 4 * t + 4] for t in range(3)]
     left, weight = refs[12:]
-    block0 = place[0] * 3
+    cols = pl.ds(pl.multiple_of(place[0] * LANES, LANES), LANES)
     w2 = omega[0] * omega[0]
+    row = lax.broadcasted_iota(jnp.int32, (LANES, 2 * LANES), 0)
+    lane = lax.broadcasted_iota(jnp.int32, (LANES, 2 * LANES), 1)
+    spread = jnp.where((row < 3) & (lane < LANES) | (row == 3) & (lane >= LANES), 1.0, 0.0)
+    spread = spread.astype(jnp.bfloat16)
     for d3 in range(4):
-        m = pieces[2][d3][:, 1024:1152].astype(jnp.float32)
-        delta = m[:, 0:1] + m[:, 1:2] + m[:, 2:3]
-        w = -4.0 * m[:, 3:4] * delta / (delta * delta + w2) / math.sqrt(NV * NC)
-        weight[d3 * 512 : d3 * 512 + 512, :] = jnp.broadcast_to(w, (512, LANES))
-    for e in range(3):
-        block = block0 + e
-        for t in range(3):
-
-            @pl.when(block // 8 == t)
-            def _(e=e, t=t, block=block):
-                lane = pl.ds(pl.multiple_of((block - 8 * t) * LANES, LANES), LANES)
-                for n in range(64):
-                    at = {"z": n // 16, "y": (n // 4) % 4, "x": n % 4}
-                    src = sum(STRIDES[t][a] * at[a] for a in AXES)
-                    wsrc = sum(STRIDES[2][a] * at[a] for a in AXES)
-                    left[n * 32 : n * 32 + 32, e * LANES : (e + 1) * LANES] = (
-                        pieces[t][src // 512][src % 512 : src % 512 + 32, lane].astype(jnp.float32)
-                        * weight[wsrc : wsrc + 32, :]
-                    ).astype(jnp.bfloat16)
+        m = jnp.dot(pieces[2][d3][:, 1024:1152], spread, preferred_element_type=jnp.float32)
+        delta, taken = m[:, :LANES], m[:, LANES:]
+        weight[d3 * 512 : d3 * 512 + 512, :] = (
+            (-4.0 / math.sqrt(NV * NC)) * taken * delta / (delta * delta + w2)
+        )
+    for t in range(3):
+        for n in range(64):
+            at = {"z": n // 16, "y": (n // 4) % 4, "x": n % 4}
+            src, dst, wsrc = (sum(STRIDES[o][a] * at[a] for a in AXES) for o in (t, 0, 2))
+            block = pieces[t][src // 512][src % 512 : src % 512 + 32, cols].astype(jnp.float32)
+            left[dst : dst + 32, t * LANES : (t + 1) * LANES] = (
+                block * weight[wsrc : wsrc + 32, :]
+            ).astype(jnp.bfloat16)
 
 
 def weighted(place, omega, pieces):
@@ -202,8 +217,9 @@
 SWAPPED = (0, 2, 1, 3)
 
 
-def transposed(left, t, left_t, other):
+def product(left, pieces, t, other):
     first, second, last = ORDERS[t]
+    acc = None
     for d3 in range(4):
         rows = []
         for d2 in range(4):
@@ -215,123 +231,82 @@
                 else:
                     src = sum(STRIDES[0][a] * at[a] for a in AXES)
                     rows.append(left[src : src + 32, :])
-        left_t[:, d3 * 512 : d3 * 512 + 512] = jnp.concatenate(rows, 0).T
-
-
-def product(left_t, pieces, cols):
-    acc = jnp.dot(left_t[:, 0:512], pieces[0][:, cols], preferred_element_type=jnp.float32)
-    for d3 in range(1, 4):
-        acc += jnp.dot(
-            left_t[:, d3 * 512 : d3 * 512 + 512], pieces[d3][:, cols], preferred_element_type=jnp.float32
+        term = lax.dot_general(
+            jnp.concatenate(rows, 0),
+            pieces[d3][:, :1024],
+            (((0,), (0,)), ((), ())),
+            preferred_element_type=jnp.float32,
         )
+        acc = term if acc is None else acc + term
     return acc
 
 
-def out_lane(block, half):
-    return (block // 3) * 6 + half * 3 + lax.rem(block, 3)
-
-
-def own_kernel(core, left, *refs):
-    pieces = [refs[4 * t : 4 * t + 4] for t in range(3)]
-    out, left_t, result, sem = refs[12:]
-    half = core[0]
-
-    def copies(n):
-        slot = lax.rem(n, 2)
-        return [
-            pltpu.make_async_copy(
-                result.at[slot, :, pl.ds(j * LANES, LANES)],
-                out.at[:, pl.ds(pl.multiple_of(out_lane(n * 4 + j, half) * LANES, LANES), LANES)],
-                sem.at[slot, j],
-            )
-            for j in range(4)
-        ]
-
-    for t in range(3):
-        transposed(left, t, left_t, False)
-
-        def step(i, carry, t=t):
-            n = t * 2 + i
-
-            @pl.when(n >= 2)
-            def _():
-                for copy in copies(n - 2):
-                    copy.wait()
-
-            for j in range(2):
-                cols = pl.ds(pl.multiple_of(i * 512 + j * 256, 256), 256)
-                result[lax.rem(n, 2), :, j * 256 : j * 256 + 256] = product(left_t, pieces[t], cols)
-            for copy in copies(n):
-                copy.start()
-            return carry
-
-        lax.fori_loop(0, 2, step, 0)
-    for n in (4, 5):
-        for copy in copies(n):
+def part_copies(t, half, wide, out, sem):
+    return [
+        pltpu.make_async_copy(
+            wide.at[:, pl.ds(j * LANES, LANES)],
+            out.at[:, pl.ds(pl.multiple_of(((j * 2 + half) * 3 + t) * LANES, LANES), LANES)],
+            sem.at[j],
+        )
+        for j in range(8)
+    ]
+
+
+def own_kernel(parts, core, left, *refs):
+    n = len(parts)
+    out, wide, sem = refs[-3:]
+    for i, t in enumerate(parts):
+        wide[i] = product(left, refs[4 * i : 4 * i + 4], t, False)
+        for copy in part_copies(t, core[0], wide.at[i], out, sem.at[i]):
+            copy.start()
+    for i, t in enumerate(parts):
+        for copy in part_copies(t, core[0], wide.at[i], out, sem.at[i]):
             copy.wait()
 
 
-def own_half(core, left, pieces):
-    return pl.pallas_call(
-        own_kernel,
+def own_rows(parts, core, left, pieces, out):
+    n = len(parts)
+    before = [] if out is None else [out]
+    return pl.pallas_call(
+        functools.partial(own_kernel, parts),
         out_shape=jax.ShapeDtypeStruct((384, NG), jnp.float32),
-        in_specs=[SM, VM] + [VM] * 12,
+        in_specs=[SM, VM] + [VM] * (4 * n) + [HBM] * len(before),
         out_specs=HBM,
-        scratch_shapes=[
-            pltpu.VMEM((384, K), jnp.bfloat16),
-            pltpu.VMEM((2, 384, 512), jnp.float32),
-            pltpu.SemaphoreType.DMA((2, 4)),
-        ],
-        compiler_params=pltpu.CompilerParams(vmem_limit_bytes=24 * MIB),
-        cost_estimate=pl.CostEstimate(flops=2 * 384 * HALF * K, bytes_accessed=20 * MIB, transcendentals=0),
-        name="own_half",
-    )(core, left, *pieces)
-
-
-def other_kernel(t, left, p0, p1, p2, p3, out, left_t):
-    transposed(left, t, left_t, True)
-
-    def step(i, carry):
-        cols = pl.ds(pl.multiple_of(i * 256, 256), 256)
-        out[:, cols] = product(left_t, (p0, p1, p2, p3), cols).astype(jnp.bfloat16)
-        return carry
-
-    lax.fori_loop(0, 4, step, 0)
-
-
-def other_rows(t, left, pieces):
+        scratch_shapes=[pltpu.VMEM((n, 384, 1024), jnp.float32), pltpu.SemaphoreType.DMA((n, 8))],
+        input_output_aliases={2 + 4 * n: 0} if before else {},
+        compiler_params=pltpu.CompilerParams(vmem_limit_bytes=24 * MIB),
+        cost_estimate=pl.CostEstimate(
+            flops=n * 2 * 384 * 1024 * K, bytes_accessed=n * 6 * MIB, transcendentals=0
+        ),
+        name="own_rows",
+    )(core, left, *[p for t in parts for p in pieces[t]], *before)
+
+
+def other_kernel(t, left, p0, p1, p2, p3, _, out):
+    out[...] = product(left, (p0, p1, p2, p3), t, True).astype(jnp.bfloat16)
+
+
+def other_rows(t, left, pieces, after):
     return pl.pallas_call(
         functools.partial(other_kernel, t),
         out_shape=jax.ShapeDtypeStruct((384, 1024), jnp.bfloat16),
-        in_specs=[VM] * 5,
+        in_specs=[VM] * 5 + [HBM],
         out_specs=VM,
-        scratch_shapes=[pltpu.VMEM((384, K), jnp.bfloat16)],
         compiler_params=pltpu.CompilerParams(vmem_limit_bytes=24 * MIB),
         cost_estimate=pl.CostEstimate(flops=2 * 384 * 1024 * K, bytes_accessed=6 * MIB, transcendentals=0),
         name="other_rows",
-    )(left, *pieces)
+    )(left, *pieces, after)
 
 
 def finish_kernel(core, r0, r1, r2, _, out, wide, sem):
-    half = 1 - core[0]
-
-    def copies(t):
-        return [
-            pltpu.make_async_copy(
-                wide.at[t, :, pl.ds(j * LANES, LANES)],
-                out.at[:, pl.ds(pl.multiple_of(out_lane(t * 8 + j, half) * LANES, LANES), LANES)],
-                sem.at[t, j],
-            )
-            for j in range(8)
-        ]
-
     for t, r in enumerate((r0, r1, r2)):
-        for j, copy in enumerate(copies(t)):
+        copies = part_copies(t, 1 - core[0], wide.at[t], out, sem.at[t])
+        for j, copy in enumerate(copies):
             at = slice(j * LANES, j * LANES + LANES)
             wide[t, :, at] = r[:, at].astype(jnp.float32)
             copy.start()
     for t in range(3):
-        for copy in copies(t):
+        for copy in part_copies(t, 1 - core[0], wide.at[t], out, sem.at[t]):
             copy.wait()
 
 
@@ -364,7 +339,7 @@
     meta = jnp.stack([d1, d2, d3, taken], 1).astype(jnp.bfloat16)
     meta = jnp.pad(meta, ((0, 0), (0, LANES - 4)))
 
-    halves = g_index.reshape(8, 2, 384).transpose(1, 0, 2).reshape(2, HALF)
+    halves = g_index.reshape(8, 2, 3, LANES).transpose(1, 2, 0, 3).reshape(2, HALF)
     kept = lax.dynamic_slice(halves, (core, 0), (1, HALF))
     given = lax.dynamic_slice(halves, (1 - core, 0), (1, HALF))
     spec, give = rho_spectrum(psi, given, meta)
@@ -378,18 +353,19 @@
         cols = slice(start, start + PARTS[t])
         start += PARTS[t]
         a = jnp.concatenate([keep[:, cols], got[:, cols]], 0)
-        a = jnp.concatenate(ring_gather(a, first), 0)
-        a = jnp.concatenate(ring_gather(a, second), 0)
+        a = direct_gather(direct_gather(a, first), second)
         pieces.append([in_vmem(b) for b in ring_gather(a, last)])
     everything = pieces[0] + pieces[1] + pieces[2]
 
     place = lax.div(ga, 2).astype(jnp.int32).reshape(1)
     mine_omega = lax.dynamic_slice(omega, (ba,), (1,))
+    core = core.reshape(1)
     left = weighted(place, mine_omega, everything)
     left_other = send(left, core_pairs())
-    out = own_half(core.reshape(1), left, everything)
-    rows = [send(other_rows(t, left_other, pieces[t]), core_pairs()) for t in range(3)]
-    return finish(core.reshape(1), rows, out)[None]
+    out = own_rows((0,), core, left, pieces, None)
+    rows = [send(other_rows(t, left_other, pieces[t], out), core_pairs()) for t in range(3)]
+    out = own_rows((1, 2), core, left, pieces, out)
+    return finish(core, rows, out)[None]
 
 
 def solution(mesh):

time: 171 us -> 187 us (1.094)
  waiting for transfers between devices: 60.8 us -> 77.7 us
  Pallas kernels: 45.1 us -> 41.5 us
  local copies, waits for them, and re-layouts: 12.9 us -> 16.3 us
    ppermute x32, waiting for transfers between devices: 50.2 us -> 67.1 us  [send(): return lax.ppermute(a, ('ga', 'ba'), pairs)]
    unnamed x48 -> x53, local copies, waits for them, and re-layouts: 10.4 us -> 13.8 us
    pallas_call x3, Pallas kernels: 13.5 us -> 10.6 us  [other_rows(): pl.pallas_call(functools.partial(other_kernel, t), out_shape=jax.ShapeDty...]
    pallas_call x1 -> x2, Pallas kernels: 11.5 us -> 11.8 us  [own_rows(): pl.pallas_call(functools.partial(own_kernel, parts), out_shape=jax.ShapeD...]
  transfers between devices with their start and end apart: 33 -> 33, of which waited for: 13 -> 15; matrix products, arithmetic and copies ran while one was open for 4% -> 4% of each run, Pallas kernels for 12% -> 12%
where the time goes in v3:
time: 187 us
  waiting for transfers between devices  77.7 us (42%)
  starting transfers between devices  49.3 us (26%)
  Pallas kernels  41.5 us (22%)
  local copies, waits for them, and re-layouts  16.3 us (9%)
    ppermute x32, waiting for transfers between devices, send(): return lax.ppermute(a, ('ga', 'ba'), pairs)  67.1 us
    ppermute x32, starting transfers between devices, send(): return lax.ppermute(a, ('ga', 'ba'), pairs)  39.9 us
    unnamed x53, local copies, waits for them, and re-layouts  13.8 us
    pallas_call x2, Pallas kernels, own_rows(): pl.pallas_call(functools.partial(own_kernel, parts), out_shape=jax.ShapeD...  11.8 us
    all_to_all x1, waiting for transfers between devices, on_device(): psi = lax.all_to_all(jnp.concatenate([val, con], 1), 'ga', 0, 0, tiled=True)  10.6 us
    pallas_call x3, Pallas kernels, other_rows(): pl.pallas_call(functools.partial(other_kernel, t), out_shape=jax.ShapeDty...  10.6 us
    all_to_all x1, starting transfers between devices, on_device(): psi = lax.all_to_all(jnp.concatenate([val, con], 1), 'ga', 0, 0, tiled=True)  9.46 us
    pallas_call x1, Pallas kernels, rho_spectrum(): pl.pallas_call(transform_kernel, out_shape=[jax.ShapeDtypeStruct((PAIRS *...  8.36 us
  transfers between devices with their start and end apart: 33, of which 15 were waited for; matrix products, arithmetic and copies ran while one was open for 4% of the time, Pallas kernels for 12%

profile of v3, /device:TPU:1, one launch (start us, length us, event | category | flops | bytes accessed | tf_op | source)
XLA Modules:
  0.0 186.5 jit_solution(14923079221097786533)
XLA Ops:
  2.7 9.5 %all-to-all-start = ((bf16[16,8,8,256]{3,2,1,0:T(8,128)(2,1)}), bf16[16,8,8,256]{3,2,1,0:T(8,128)(2,1)S(1)}, u32[]{:S(2)}, u32[]{:S(2)}) async-start(bf16[16,8,8,256]{3,2,1,0:T(8,128)(2,1)} %pad_maximum_fusion), calls=%async_computation | async-start | bytes 1048576 | tf_op jit(solution)/shard_map/all_to_all | solution.py:332
  12.8 10.6 %all-to-all-done.psi = bf16[16,8,8,256]{3,2,1,0:T(8,128)(2,1)S(1)} async-done(((bf16[16,8,8,256]{3,2,1,0:T(8,128)(2,1)}), bf16[16,8,8,256]{3,2,1,0:T(8,128)(2,1)S(1)}, u32[]{:S(2)}, u32[]{:S(2)}) %all-to-all-start) | async-done | bytes 524320 | tf_op jit(solution)/shard_map/all_to_all | solution.py:332
  23.5 8.4 %rho_spectrum.1 = (bf16[1024,256]{1,0:T(8,128)(2,1)S(1)}, bf16[16,3200]{1,0:T(8,128)(2,1)S(1)}) custom-call(bf16[16,8,8,256]{3,2,1,0:T(8,128)(2,1)S(1)} %all-to-all-done.psi, s32[1,3072]{1,0:T(1,128)S(1)} %get-tuple-element.46.gidx, bf16[16,128]{1,0:T(8,128)(2,1)S(1)} %pad.4.meta, bf16[256,256]{1,0:T(8,128)(2,1)S(1)} %copy-done.11, ...), custom_call_target="tpu_custom_call" | custom-call | tf_op jit(solution)/shard_map/rho_spectrum/pallas_call | solution.py:99
  33.1 3.8 %rho_pick.1 = bf16[16,3200]{1,0:T(8,128)(2,1)S(1)} custom-call(bf16[1024,256]{1,0:T(8,128)(2,1)S(1)} %get-tuple-element.7.spec, s32[1,3072]{1,0:T(1,128)S(1)} %get-tuple-element.45.gidx, bf16[16,128]{1,0:T(8,128)(2,1)S(1)} %pad.4.meta), custom_call_target="tpu_custom_call" | custom-call | tf_op jit(solution)/shard_map/rho_pick/pallas_call | solution.py:113
  38.8 2.1 %collective-permute-start.19 = (bf16[32,1152]{1,0:T(8,128)(2,1)S(1)}, bf16[32,1152]{1,0:T(8,128)(2,1)S(1)}, u32[]{:S(2)}, u32[]{:S(2)}) collective-permute-start(bf16[32,1152]{1,0:T(8,128)(2,1)S(1)} %pad_maximum_fusion.1), channel_id=1, source_target_pairs={{0,32},{8,104},{1,33},{9,105},{2,34},{10,106},{3,35},{11,107},{4,3... | collective-permute-start | bytes 221192 | tf_op jit(solution)/shard_map/ppermute | solution.py:149
  41.6 2.7 %collective-permute-start.3 = (bf16[32,1024]{1,0:T(8,128)(2,1)S(1)}, bf16[32,1024]{1,0:T(8,128)(2,1)S(1)}, u32[]{:S(2)}, u32[]{:S(2)}) collective-permute-start(bf16[32,1024]{1,0:T(8,128)(2,1)S(1)} %pad_maximum_fusion.2), channel_id=1, source_target_pairs={{0,2},{8,10},{1,3},{9,11},{2,0},{10,8},{3,1},{11,9},{4,6},{12,14},... | collective-permute-start | bytes 196616 | tf_op jit(solution)/shard_map/ppermute | solution.py:149
  45.2 2.5 %collective-permute-done.1 = bf16[32,1024]{1,0:T(8,128)(2,1)S(1)} collective-permute-done((bf16[32,1024]{1,0:T(8,128)(2,1)S(1)}, bf16[32,1024]{1,0:T(8,128)(2,1)S(1)}, u32[]{:S(2)}, u32[]{:S(2)}) %collective-permute-start.1) | collective-permute-done | bytes 65568 | tf_op jit(solution)/shard_map/ppermute | solution.py:149
  47.9 2.9 %collective-permute-done.10 = bf16[32,1024]{1,0:T(8,128)(2,1)S(1)} collective-permute-done((bf16[32,1024]{1,0:T(8,128)(2,1)S(1)}, bf16[32,1024]{1,0:T(8,128)(2,1)S(1)}, u32[]{:S(2)}, u32[]{:S(2)}) %collective-permute-start.10) | collective-permute-done | bytes 65568 | tf_op jit(solution)/shard_map/ppermute | solution.py:149
  51.8 3.4 %collective-permute-done.11 = bf16[32,1024]{1,0:T(8,128)(2,1)S(1)} collective-permute-done((bf16[32,1024]{1,0:T(8,128)(2,1)S(1)}, bf16[32,1024]{1,0:T(8,128)(2,1)S(1)}, u32[]{:S(2)}, u32[]{:S(2)}) %collective-permute-start.11) | collective-permute-done | bytes 65568 | tf_op jit(solution)/shard_map/ppermute | solution.py:149
  55.8 4.0 %collective-permute-done.12 = bf16[32,1024]{1,0:T(8,128)(2,1)S(1)} collective-permute-done((bf16[32,1024]{1,0:T(8,128)(2,1)S(1)}, bf16[32,1024]{1,0:T(8,128)(2,1)S(1)}, u32[]{:S(2)}, u32[]{:S(2)}) %collective-permute-start.12) | collective-permute-done | bytes 65568 | tf_op jit(solution)/shard_map/ppermute | solution.py:149
  61.8 2.6 %collective-permute-done.2 = bf16[32,1024]{1,0:T(8,128)(2,1)S(1)} collective-permute-done((bf16[32,1024]{1,0:T(8,128)(2,1)S(1)}, bf16[32,1024]{1,0:T(8,128)(2,1)S(1)}, u32[]{:S(2)}, u32[]{:S(2)}) %collective-permute-start.2) | collective-permute-done | bytes 65568 | tf_op jit(solution)/shard_map/ppermute | solution.py:149
  64.5 1.9 %collective-permute-start.15 = (bf16[128,1024]{1,0:T(8,128)(2,1)S(1)}, bf16[128,1024]{1,0:T(8,128)(2,1)S(1)}, u32[]{:S(2)}, u32[]{:S(2)}) collective-permute-start(bf16[128,1024]{1,0:T(8,128)(2,1)S(1)} %get-tuple-element.33), channel_id=1, source_target_pairs={{0,64},{8,72},{1,65},{9,73},{2,66},{10,74},{3,67},{11,75},{4,68},{... | collective-permute-start | bytes 786440 | tf_op jit(solution)/shard_map/ppermute | solution.py:149
  66.6 1.7 collective-permute-start.4
  68.5 4.7 %collective-permute-done.4 = bf16[128,1024]{1,0:T(8,128)(2,1)S(1)} collective-permute-done((bf16[128,1024]{1,0:T(8,128)(2,1)S(1)}, bf16[128,1024]{1,0:T(8,128)(2,1)S(1)}, u32[]{:S(2)}, u32[]{:S(2)}) %collective-permute-start.4) | collective-permute-done | bytes 262176 | tf_op jit(solution)/shard_map/ppermute | solution.py:149
  74.7 1.6 collective-permute-done.5
  76.4 6.3 %collective-permute-start.13 = (bf16[128,1024]{1,0:T(8,128)(2,1)S(1)}, bf16[128,1024]{1,0:T(8,128)(2,1)S(1)}, u32[]{:S(2)}, u32[]{:S(2)}) collective-permute-start(bf16[128,1024]{1,0:T(8,128)(2,1)S(1)} %get-tuple-element.33), channel_id=1, source_target_pairs={{0,32},{8,104},{1,33},{9,105},{2,34},{10,106},{3,35},{11,107},{4,3... | collective-permute-start | bytes 786440 | tf_op jit(solution)/shard_map/ppermute | solution.py:149
  83.9 10.2 %collective-permute-done.23 = bf16[128,1152]{1,0:T(8,128)(2,1)S(1)} collective-permute-done((bf16[128,1152]{1,0:T(8,128)(2,1)S(1)}, bf16[128,1152]{1,0:T(8,128)(2,1)S(1)}, u32[]{:S(2)}, u32[]{:S(2)}) %collective-permute-start.23) | collective-permute-done | bytes 294944 | tf_op jit(solution)/shard_map/ppermute | solution.py:149
  94.3 2.6 %collective-permute-start.7 = (bf16[512,1024]{1,0:T(8,128)(2,1)S(1)}, bf16[512,1024]{1,0:T(8,128)(2,1)}, u32[]{:S(2)}, u32[]{:S(2)}) collective-permute-start(bf16[512,1024]{1,0:T(8,128)(2,1)S(1)} %constant_dynamic-update-slice_fusion.5.refs_0_.p0), channel_id=1, source_target_pairs={{0,32},{8,104},{1,33},{9,105},{2,34},{10,106},{3,35},{11,107},{4,3... | collective-permute-start | bytes 3145736 | tf_op jit(solution)/shard_map/ppermute | solution.py:149
  100.7 13.8 %collective-permute-done.25.refs_9_.p1.refs_5_ = bf16[512,1152]{1,0:T(8,128)(2,1)S(1)} collective-permute-done((bf16[512,1152]{1,0:T(8,128)(2,1)S(1)}, bf16[512,1152]{1,0:T(8,128)(2,1)S(1)}, u32[]{:S(2)}, u32[]{:S(2)}) %collective-permute-start.25) | collective-permute-done | bytes 1179680 | tf_op jit(solution)/shard_map/ppermute | solution.py:149
  115.5 4.1 %collective-permute-done.7.refs_1_.p1 = bf16[512,1024]{1,0:T(8,128)(2,1)} collective-permute-done((bf16[512,1024]{1,0:T(8,128)(2,1)S(1)}, bf16[512,1024]{1,0:T(8,128)(2,1)}, u32[]{:S(2)}, u32[]{:S(2)}) %collective-permute-start.7) | collective-permute-done | bytes 1048608 | tf_op jit(solution)/shard_map/ppermute | solution.py:149
  119.6 3.5 %collective-permute-start.9 = (bf16[512,1024]{1,0:T(8,128)(2,1)}, bf16[512,1024]{1,0:T(8,128)(2,1)}, u32[]{:S(2)}, u32[]{:S(2)}) collective-permute-start(bf16[512,1024]{1,0:T(8,128)(2,1)} %collective-permute-done.7.refs_1_.p1), channel_id=1, source_target_pairs={{0,32},{8,104},{1,33},{9,105},{2,34},{10,106},{3,35},{11,107},{4,3... | collective-permute-start | bytes 3145736 | tf_op jit(solution)/shard_map/ppermute | solution.py:149
  123.7 10.6 %collective-permute-done.17.refs_6_.p2.refs_2_ = bf16[512,1024]{1,0:T(8,128)(2,1)} collective-permute-done((bf16[512,1024]{1,0:T(8,128)(2,1)}, bf16[512,1024]{1,0:T(8,128)(2,1)}, u32[]{:S(2)}, u32[]{:S(2)}) %collective-permute-start.17) | collective-permute-done | bytes 1048608 | tf_op jit(solution)/shard_map/ppermute | solution.py:149
  135.1 5.6 %collective-permute-done.18.refs_7_.p3.refs_3_ = bf16[512,1024]{1,0:T(8,128)(2,1)} collective-permute-done((bf16[512,1024]{1,0:T(8,128)(2,1)}, bf16[512,1024]{1,0:T(8,128)(2,1)}, u32[]{:S(2)}, u32[]{:S(2)}) %collective-permute-start.18) | collective-permute-done | bytes 1048608 | tf_op jit(solution)/shard_map/ppermute | solution.py:149
  143.2 4.6 %weighted.1.left = bf16[2048,384]{1,0:T(8,128)(2,1)S(1)} custom-call(s32[1]{0:T(128)} %bitcast.1.place, f32[1]{0:T(128)} %dynamic_slice.12.omega, bf16[512,1024]{1,0:T(8,128)(2,1)S(1)} %copy-done.3, bf16[512,1024]{1,0:T(8,128)(2,1)} %collective-permute-done.7.refs_1_.p1, bf16[512,1024]{1,0:T(8,128)(2,1)S(1)} %copy-done.6, ...), custom_call_target="tpu_custom_call" | custom-call | tf_op jit(solution)/shard_map/weighted/pallas_call | solution.py:206
  147.8 8.3 %collective-permute-start.28 = (bf16[2048,384]{1,0:T(8,128)(2,1)S(1)}, bf16[2048,384]{1,0:T(8,128)(2,1)S(1)}, u32[]{:S(2)}, u32[]{:S(2)}) collective-permute-start(bf16[2048,384]{1,0:T(8,128)(2,1)S(1)} %weighted.1.left), channel_id=1, source_target_pairs={{0,8},{8,0},{1,9},{9,1},{2,10},{10,2},{3,11},{11,3},{4,12},{12,4},... | collective-permute-start | bytes 4718600 | tf_op jit(solution)/shard_map/ppermute | solution.py:149
  156.1 4.6 %own_rows.2._.refs_8_ = f32[384,6144]{1,0:T(8,128)} custom-call(s32[1]{0:T(128)} %bitcast.core, bf16[2048,384]{1,0:T(8,128)(2,1)S(1)} %weighted.1.left, bf16[512,1024]{1,0:T(8,128)(2,1)S(1)} %copy-done.4, bf16[512,1024]{1,0:T(8,128)(2,1)} %collective-permute-done.7.refs_1_.p1, bf16[512,1024]{1,0:T(8,128)(2,1)S(1)} %copy-done.7, ...), custom_call_target="tpu_custom_call" | custom-call | flops 1610612736 | bytes 6291456 | tf_op jit(solution)/shard_map/own_rows/pallas_call | solution.py:270
  160.7 3.7 %copy-done = f32[384,6144]{1,0:T(8,128)S(1)} copy-done((f32[384,6144]{1,0:T(8,128)S(1)}, f32[384,6144]{1,0:T(8,128)}, u32[]{:S(2)}) %copy-start) | copy-done | bytes 9437208
  164.4 4.1 %other_rows.4 = bf16[384,1024]{1,0:T(8,128)(2,1)S(1)} custom-call(bf16[2048,384]{1,0:T(8,128)(2,1)S(1)} %collective-permute-done.28.left, bf16[512,1024]{1,0:T(8,128)(2,1)} %constant_dynamic-update-slice_fusion.18.refs_4_.p0.refs_0_, bf16[512,1024]{1,0:T(8,128)(2,1)} %collective-permute-done.16.refs_5_.p1.refs_1_, ...), custom_call_target="tpu_custom_call" | custom-call | flops 1610612736 | bytes 6291456 | tf_op jit(solution)/shard_map/other_rows/pallas_call | solution.py:290
  169.3 3.1 %other_rows.5 = bf16[384,1024]{1,0:T(8,128)(2,1)S(1)} custom-call(bf16[2048,384]{1,0:T(8,128)(2,1)S(1)} %collective-permute-done.28.left, bf16[512,1152]{1,0:T(8,128)(2,1)S(1)} %constant_dynamic-update-slice_fusion.31.refs_8_.p0.refs_4_, bf16[512,1152]{1,0:T(8,128)(2,1)S(1)} %collective-permute-done.25.refs_9_.p1.refs_5_, ...), custom_call_target="tpu_custom_call" | custom-call | flops 1610612736 | bytes 6291456 | tf_op jit(solution)/shard_map/other_rows/pallas_call | solution.py:290
  172.5 3.3 %other_rows.3 = bf16[384,1024]{1,0:T(8,128)(2,1)S(1)} custom-call(bf16[2048,384]{1,0:T(8,128)(2,1)S(1)} %collective-permute-done.28.left, bf16[512,1024]{1,0:T(8,128)(2,1)S(1)} %copy-done.4, bf16[512,1024]{1,0:T(8,128)(2,1)} %collective-permute-done.7.refs_1_.p1, bf16[512,1024]{1,0:T(8,128)(2,1)S(1)} %copy-done.7, ...), custom_call_target="tpu_custom_call" | custom-call | flops 1610612736 | bytes 6291456 | tf_op jit(solution)/shard_map/other_rows/pallas_call | solution.py:290
  176.6 7.2 %own_rows.3._ = f32[384,6144]{1,0:T(8,128)} custom-call(s32[1]{0:T(128)} %bitcast.core, bf16[2048,384]{1,0:T(8,128)(2,1)S(1)} %weighted.1.left, bf16[512,1024]{1,0:T(8,128)(2,1)} %constant_dynamic-update-slice_fusion.18.refs_4_.p0.refs_0_, bf16[512,1024]{1,0:T(8,128)(2,1)} %collective-permute-done.16.refs_5_.p1.refs_1_, ...), custom_call_target="tpu_custom_call", output_to_operand_aliasing={{}: (10, {})} | custom-call | flops 3221225472 | bytes 12582912 | tf_op jit(solution)/shard_map/own_rows/pallas_call | solution.py:270
  183.9 2.4 %finish.1 = f32[384,6144]{1,0:T(8,128)} custom-call(s32[1]{0:T(128)} %bitcast.core, bf16[384,1024]{1,0:T(8,128)(2,1)S(1)} %collective-permute-done.29.r0, bf16[384,1024]{1,0:T(8,128)(2,1)S(1)} %collective-permute-done.30.r1, bf16[384,1024]{1,0:T(8,128)(2,1)S(1)} %collective-permute-done.31.r2, f32[384,6144]{1,0:T(8,128)} %own_rows.3._), custom_call_target="tpu_custom_call", output_to_operand_aliasing={{}: (4, {})} | custom-call | tf_op jit(solution)/shard_map/finish/pallas_call | solution.py:314
  (121 shorter events, 25.4 us)
Async XLA Ops:
  2.7 20.8 %all-to-all-start = ((bf16[16,8,8,256]{3,2,1,0:T(8,128)(2,1)}), bf16[16,8,8,256]{3,2,1,0:T(8,128)(2,1)S(1)}, u32[]{:S(2)}, u32[]{:S(2)}) async-start(bf16[16,8,8,256]{3,2,1,0:T(8,128)(2,1)} %pad_maximum_fusion), calls=%async_computation | async-start | bytes 1048576 | tf_op jit(solution)/shard_map/all_to_all | solution.py:332
  31.8 5.7 %collective-permute-start = (bf16[16,3200]{1,0:T(8,128)(2,1)S(1)}, bf16[16,3200]{1,0:T(8,128)(2,1)S(1)}, u32[]{:S(2)}, u32[]{:S(2)}) collective-permute-start(bf16[16,3200]{1,0:T(8,128)(2,1)S(1)} %get-tuple-element.8), channel_id=1, source_target_pairs={{0,8},{8,0},{1,9},{9,1},{2,10},{10,2},{3,11},{11,3},{4,12},{12,4},... | collective-permute-start | bytes 307208 | tf_op jit(solution)/shard_map/ppermute | solution.py:149
  37.6 30.7 %collective-permute-start.21 = (bf16[32,1152]{1,0:T(8,128)(2,1)S(1)}, bf16[32,1152]{1,0:T(8,128)(2,1)S(1)}, u32[]{:S(2)}, u32[]{:S(2)}) collective-permute-start(bf16[32,1152]{1,0:T(8,128)(2,1)S(1)} %pad_maximum_fusion.1), channel_id=1, source_target_pairs={{0,64},{8,72},{1,65},{9,73},{2,66},{10,74},{3,67},{11,75},{4,68},{... | collective-permute-start | bytes 221192 | tf_op jit(solution)/shard_map/ppermute | solution.py:149
  38.3 28.3 %collective-permute-start.20 = (bf16[32,1152]{1,0:T(8,128)(2,1)S(1)}, bf16[32,1152]{1,0:T(8,128)(2,1)S(1)}, u32[]{:S(2)}, u32[]{:S(2)}) collective-permute-start(bf16[32,1152]{1,0:T(8,128)(2,1)S(1)} %pad_maximum_fusion.1), channel_id=1, source_target_pairs={{0,96},{8,40},{1,97},{9,41},{2,98},{10,42},{3,99},{11,43},{4,100},... | collective-permute-start | bytes 221192 | tf_op jit(solution)/shard_map/ppermute | solution.py:149
  38.8 27.6 %collective-permute-start.19 = (bf16[32,1152]{1,0:T(8,128)(2,1)S(1)}, bf16[32,1152]{1,0:T(8,128)(2,1)S(1)}, u32[]{:S(2)}, u32[]{:S(2)}) collective-permute-start(bf16[32,1152]{1,0:T(8,128)(2,1)S(1)} %pad_maximum_fusion.1), channel_id=1, source_target_pairs={{0,32},{8,104},{1,33},{9,105},{2,34},{10,106},{3,35},{11,107},{4,3... | collective-permute-start | bytes 221192 | tf_op jit(solution)/shard_map/ppermute | solution.py:149
  41.6 24.8 %collective-permute-start.3 = (bf16[32,1024]{1,0:T(8,128)(2,1)S(1)}, bf16[32,1024]{1,0:T(8,128)(2,1)S(1)}, u32[]{:S(2)}, u32[]{:S(2)}) collective-permute-start(bf16[32,1024]{1,0:T(8,128)(2,1)S(1)} %pad_maximum_fusion.2), channel_id=1, source_target_pairs={{0,2},{8,10},{1,3},{9,11},{2,0},{10,8},{3,1},{11,9},{4,6},{12,14},... | collective-permute-start | bytes 196616 | tf_op jit(solution)/shard_map/ppermute | solution.py:149
  44.3 3.4 %collective-permute-start.1 = (bf16[32,1024]{1,0:T(8,128)(2,1)S(1)}, bf16[32,1024]{1,0:T(8,128)(2,1)S(1)}, u32[]{:S(2)}, u32[]{:S(2)}) collective-permute-start(bf16[32,1024]{1,0:T(8,128)(2,1)S(1)} %pad_maximum_fusion.2), channel_id=1, source_target_pairs={{0,1},{8,11},{1,2},{9,8},{2,3},{10,9},{3,0},{11,10},{4,5},{12,15},... | collective-permute-start | bytes 196616 | tf_op jit(solution)/shard_map/ppermute | solution.py:149
  50.8 4.4 %collective-permute-start.11 = (bf16[32,1024]{1,0:T(8,128)(2,1)S(1)}, bf16[32,1024]{1,0:T(8,128)(2,1)S(1)}, u32[]{:S(2)}, u32[]{:S(2)}) collective-permute-start(bf16[32,1024]{1,0:T(8,128)(2,1)S(1)} %pad_maximum_fusion.3), channel_id=1, source_target_pairs={{0,20},{8,12},{1,21},{9,13},{2,22},{10,14},{3,23},{11,15},{4,0},{1... | collective-permute-start | bytes 196616 | tf_op jit(solution)/shard_map/ppermute | solution.py:149
  55.2 4.6 %collective-permute-start.12 = (bf16[32,1024]{1,0:T(8,128)(2,1)S(1)}, bf16[32,1024]{1,0:T(8,128)(2,1)S(1)}, u32[]{:S(2)}, u32[]{:S(2)}) collective-permute-start(bf16[32,1024]{1,0:T(8,128)(2,1)S(1)} %pad_maximum_fusion.3), channel_id=1, source_target_pairs={{0,16},{8,24},{1,17},{9,25},{2,18},{10,26},{3,19},{11,27},{4,20},{... | collective-permute-start | bytes 196616 | tf_op jit(solution)/shard_map/ppermute | solution.py:149
  59.8 4.6 %collective-permute-start.2 = (bf16[32,1024]{1,0:T(8,128)(2,1)S(1)}, bf16[32,1024]{1,0:T(8,128)(2,1)S(1)}, u32[]{:S(2)}, u32[]{:S(2)}) collective-permute-start(bf16[32,1024]{1,0:T(8,128)(2,1)S(1)} %pad_maximum_fusion.2), channel_id=1, source_target_pairs={{0,3},{8,9},{1,0},{9,10},{2,1},{10,11},{3,2},{11,8},{4,7},{12,13},... | collective-permute-start | bytes 196616 | tf_op jit(solution)/shard_map/ppermute | solution.py:149
  64.5 34.4 %collective-permute-start.15 = (bf16[128,1024]{1,0:T(8,128)(2,1)S(1)}, bf16[128,1024]{1,0:T(8,128)(2,1)S(1)}, u32[]{:S(2)}, u32[]{:S(2)}) collective-permute-start(bf16[128,1024]{1,0:T(8,128)(2,1)S(1)} %get-tuple-element.33), channel_id=1, source_target_pairs={{0,64},{8,72},{1,65},{9,73},{2,66},{10,74},{3,67},{11,75},{4,68},{... | collective-permute-start | bytes 786440 | tf_op jit(solution)/shard_map/ppermute | solution.py:149
  66.4 31.8 %collective-permute-start.14 = (bf16[128,1024]{1,0:T(8,128)(2,1)S(1)}, bf16[128,1024]{1,0:T(8,128)(2,1)S(1)}, u32[]{:S(2)}, u32[]{:S(2)}) collective-permute-start(bf16[128,1024]{1,0:T(8,128)(2,1)S(1)} %get-tuple-element.33), channel_id=1, source_target_pairs={{0,96},{8,40},{1,97},{9,41},{2,98},{10,42},{3,99},{11,43},{4,100},... | collective-permute-start | bytes 786440 | tf_op jit(solution)/shard_map/ppermute | solution.py:149
  66.5 16.2 %collective-permute-start.6 = (bf16[128,1024]{1,0:T(8,128)(2,1)S(1)}, bf16[128,1024]{1,0:T(8,128)(2,1)S(1)}, u32[]{:S(2)}, u32[]{:S(2)}) collective-permute-start(bf16[128,1024]{1,0:T(8,128)(2,1)S(1)} %get-tuple-element.39), channel_id=1, source_target_pairs={{0,16},{8,24},{1,17},{9,25},{2,18},{10,26},{3,19},{11,27},{4,20},{... | collective-permute-start | bytes 786440 | tf_op jit(solution)/shard_map/ppermute | solution.py:149
  66.6 6.6 %collective-permute-start.4 = (bf16[128,1024]{1,0:T(8,128)(2,1)S(1)}, bf16[128,1024]{1,0:T(8,128)(2,1)S(1)}, u32[]{:S(2)}, u32[]{:S(2)}) collective-permute-start(bf16[128,1024]{1,0:T(8,128)(2,1)S(1)} %get-tuple-element.39), channel_id=1, source_target_pairs={{0,4},{8,28},{1,5},{9,29},{2,6},{10,30},{3,7},{11,31},{4,16},{12,8... | collective-permute-start | bytes 786440 | tf_op jit(solution)/shard_map/ppermute | solution.py:149
  68.3 8.0 %collective-permute-start.5 = (bf16[128,1024]{1,0:T(8,128)(2,1)S(1)}, bf16[128,1024]{1,0:T(8,128)(2,1)S(1)}, u32[]{:S(2)}, u32[]{:S(2)}) collective-permute-start(bf16[128,1024]{1,0:T(8,128)(2,1)S(1)} %get-tuple-element.39), channel_id=1, source_target_pairs={{0,20},{8,12},{1,21},{9,13},{2,22},{10,14},{3,23},{11,15},{4,0},{1... | collective-permute-start | bytes 786440 | tf_op jit(solution)/shard_map/ppermute | solution.py:149
  73.2 9.6 %collective-permute-start.22 = (bf16[128,1152]{1,0:T(8,128)(2,1)S(1)}, bf16[128,1152]{1,0:T(8,128)(2,1)S(1)}, u32[]{:S(2)}, u32[]{:S(2)}) collective-permute-start(bf16[128,1152]{1,0:T(8,128)(2,1)S(1)} %get-tuple-element.27), channel_id=1, source_target_pairs={{0,1},{8,11},{1,2},{9,8},{2,3},{10,9},{3,0},{11,10},{4,5},{12,15},... | collective-permute-start | bytes 884744 | tf_op jit(solution)/shard_map/ppermute | solution.py:149
  76.4 20.6 %collective-permute-start.13 = (bf16[128,1024]{1,0:T(8,128)(2,1)S(1)}, bf16[128,1024]{1,0:T(8,128)(2,1)S(1)}, u32[]{:S(2)}, u32[]{:S(2)}) collective-permute-start(bf16[128,1024]{1,0:T(8,128)(2,1)S(1)} %get-tuple-element.33), channel_id=1, source_target_pairs={{0,32},{8,104},{1,33},{9,105},{2,34},{10,106},{3,35},{11,107},{4,3... | collective-permute-start | bytes 786440 | tf_op jit(solution)/shard_map/ppermute | solution.py:149
  82.7 11.4 %collective-permute-start.23 = (bf16[128,1152]{1,0:T(8,128)(2,1)S(1)}, bf16[128,1152]{1,0:T(8,128)(2,1)S(1)}, u32[]{:S(2)}, u32[]{:S(2)}) collective-permute-start(bf16[128,1152]{1,0:T(8,128)(2,1)S(1)} %get-tuple-element.27), channel_id=1, source_target_pairs={{0,3},{8,9},{1,0},{9,10},{2,1},{10,11},{3,2},{11,8},{4,7},{12,13},... | collective-permute-start | bytes 884744 | tf_op jit(solution)/shard_map/ppermute | solution.py:149
  82.8 11.5 %collective-permute-start.24 = (bf16[128,1152]{1,0:T(8,128)(2,1)S(1)}, bf16[128,1152]{1,0:T(8,128)(2,1)S(1)}, u32[]{:S(2)}, u32[]{:S(2)}) collective-permute-start(bf16[128,1152]{1,0:T(8,128)(2,1)S(1)} %get-tuple-element.27), channel_id=1, source_target_pairs={{0,2},{8,10},{1,3},{9,11},{2,0},{10,8},{3,1},{11,9},{4,6},{12,14},... | collective-permute-start | bytes 884744 | tf_op jit(solution)/shard_map/ppermute | solution.py:149
  94.1 20.4 %collective-permute-start.8 = (bf16[512,1024]{1,0:T(8,128)(2,1)S(1)}, bf16[512,1024]{1,0:T(8,128)(2,1)S(1)}, u32[]{:S(2)}, u32[]{:S(2)}) collective-permute-start(bf16[512,1024]{1,0:T(8,128)(2,1)S(1)} %constant_dynamic-update-slice_fusion.5.refs_0_.p0), channel_id=1, source_target_pairs={{0,96},{8,40},{1,97},{9,41},{2,98},{10,42},{3,99},{11,43},{4,100},... | collective-permute-start | bytes 3145736 | tf_op jit(solution)/shard_map/ppermute | solution.py:149
  94.3 25.2 %collective-permute-start.7 = (bf16[512,1024]{1,0:T(8,128)(2,1)S(1)}, bf16[512,1024]{1,0:T(8,128)(2,1)}, u32[]{:S(2)}, u32[]{:S(2)}) collective-permute-start(bf16[512,1024]{1,0:T(8,128)(2,1)S(1)} %constant_dynamic-update-slice_fusion.5.refs_0_.p0), channel_id=1, source_target_pairs={{0,32},{8,104},{1,33},{9,105},{2,34},{10,106},{3,35},{11,107},{4,3... | collective-permute-start | bytes 3145736 | tf_op jit(solution)/shard_map/ppermute | solution.py:149
  97.0 17.5 %collective-permute-start.25 = (bf16[512,1152]{1,0:T(8,128)(2,1)S(1)}, bf16[512,1152]{1,0:T(8,128)(2,1)S(1)}, u32[]{:S(2)}, u32[]{:S(2)}) collective-permute-start(bf16[512,1152]{1,0:T(8,128)(2,1)S(1)} %constant_dynamic-update-slice_fusion.31.refs_8_.p0.refs_4_), channel_id=1, source_target_pairs={{0,4},{8,28},{1,5},{9,29},{2,6},{10,30},{3,7},{11,31},{4,16},{12,8... | collective-permute-start | bytes 3538952 | tf_op jit(solution)/shard_map/ppermute | solution.py:149
  99.6 23.5 %collective-permute-start.16 = (bf16[512,1024]{1,0:T(8,128)(2,1)}, bf16[512,1024]{1,0:T(8,128)(2,1)}, u32[]{:S(2)}, u32[]{:S(2)}) collective-permute-start(bf16[512,1024]{1,0:T(8,128)(2,1)} %constant_dynamic-update-slice_fusion.18.refs_4_.p0.refs_0_), channel_id=1, source_target_pairs={{0,1},{8,11},{1,2},{9,8},{2,3},{10,9},{3,0},{11,10},{4,5},{12,15},... | collective-permute-start | bytes 3145736 | tf_op jit(solution)/shard_map/ppermute | solution.py:149
  99.6 34.7 %collective-permute-start.26 = (bf16[512,1152]{1,0:T(8,128)(2,1)S(1)}, bf16[512,1152]{1,0:T(8,128)(2,1)S(1)}, u32[]{:S(2)}, u32[]{:S(2)}) collective-permute-start(bf16[512,1152]{1,0:T(8,128)(2,1)S(1)} %constant_dynamic-update-slice_fusion.31.refs_8_.p0.refs_4_), channel_id=1, source_target_pairs={{0,20},{8,12},{1,21},{9,13},{2,22},{10,14},{3,23},{11,15},{4,0},{1... | collective-permute-start | bytes 3538952 | tf_op jit(solution)/shard_map/ppermute | solution.py:149
  114.5 26.3 %collective-permute-start.27 = (bf16[512,1152]{1,0:T(8,128)(2,1)S(1)}, bf16[512,1152]{1,0:T(8,128)(2,1)}, u32[]{:S(2)}, u32[]{:S(2)}) collective-permute-start(bf16[512,1152]{1,0:T(8,128)(2,1)S(1)} %collective-permute-done.25.refs_9_.p1.refs_5_), channel_id=1, source_target_pairs={{0,4},{8,28},{1,5},{9,29},{2,6},{10,30},{3,7},{11,31},{4,16},{12,8... | collective-permute-start | bytes 3538952 | tf_op jit(solution)/shard_map/ppermute | solution.py:149
  115.5 18.8 %collective-permute-start.17 = (bf16[512,1024]{1,0:T(8,128)(2,1)}, bf16[512,1024]{1,0:T(8,128)(2,1)}, u32[]{:S(2)}, u32[]{:S(2)}) collective-permute-start(bf16[512,1024]{1,0:T(8,128)(2,1)} %constant_dynamic-update-slice_fusion.18.refs_4_.p0.refs_0_), channel_id=1, source_target_pairs={{0,3},{8,9},{1,0},{9,10},{2,1},{10,11},{3,2},{11,8},{4,7},{12,13},... | collective-permute-start | bytes 3145736 | tf_op jit(solution)/shard_map/ppermute | solution.py:149
  119.6 15.6 %collective-permute-start.9 = (bf16[512,1024]{1,0:T(8,128)(2,1)}, bf16[512,1024]{1,0:T(8,128)(2,1)}, u32[]{:S(2)}, u32[]{:S(2)}) collective-permute-start(bf16[512,1024]{1,0:T(8,128)(2,1)} %collective-permute-done.7.refs_1_.p1), channel_id=1, source_target_pairs={{0,32},{8,104},{1,33},{9,105},{2,34},{10,106},{3,35},{11,107},{4,3... | collective-permute-start | bytes 3145736 | tf_op jit(solution)/shard_map/ppermute | solution.py:149
  123.1 17.7 %collective-permute-start.18 = (bf16[512,1024]{1,0:T(8,128)(2,1)}, bf16[512,1024]{1,0:T(8,128)(2,1)}, u32[]{:S(2)}, u32[]{:S(2)}) collective-permute-start(bf16[512,1024]{1,0:T(8,128)(2,1)} %collective-permute-done.16.refs_5_.p1.refs_1_), channel_id=1, source_target_pairs={{0,1},{8,11},{1,2},{9,8},{2,3},{10,9},{3,0},{11,10},{4,5},{12,15},... | collective-permute-start | bytes 3145736 | tf_op jit(solution)/shard_map/ppermute | solution.py:149
  147.8 12.9 %collective-permute-start.28 = (bf16[2048,384]{1,0:T(8,128)(2,1)S(1)}, bf16[2048,384]{1,0:T(8,128)(2,1)S(1)}, u32[]{:S(2)}, u32[]{:S(2)}) collective-permute-start(bf16[2048,384]{1,0:T(8,128)(2,1)S(1)} %weighted.1.left), channel_id=1, source_target_pairs={{0,8},{8,0},{1,9},{9,1},{2,10},{10,2},{3,11},{11,3},{4,12},{12,4},... | collective-permute-start | bytes 4718600 | tf_op jit(solution)/shard_map/ppermute | solution.py:149
  168.5 15.4 %collective-permute-start.30 = (bf16[384,1024]{1,0:T(8,128)(2,1)S(1)}, bf16[384,1024]{1,0:T(8,128)(2,1)S(1)}, u32[]{:S(2)}, u32[]{:S(2)}) collective-permute-start(bf16[384,1024]{1,0:T(8,128)(2,1)S(1)} %other_rows.4), channel_id=1, source_target_pairs={{0,8},{8,0},{1,9},{9,1},{2,10},{10,2},{3,11},{11,3},{4,12},{12,4},... | collective-permute-start | bytes 2359304 | tf_op jit(solution)/shard_map/ppermute | solution.py:149
  172.4 11.5 %collective-permute-start.31 = (bf16[384,1024]{1,0:T(8,128)(2,1)S(1)}, bf16[384,1024]{1,0:T(8,128)(2,1)S(1)}, u32[]{:S(2)}, u32[]{:S(2)}) collective-permute-start(bf16[384,1024]{1,0:T(8,128)(2,1)S(1)} %other_rows.5), channel_id=1, source_target_pairs={{0,8},{8,0},{1,9},{9,1},{2,10},{10,2},{3,11},{11,3},{4,12},{12,4},... | collective-permute-start | bytes 2359304 | tf_op jit(solution)/shard_map/ppermute | solution.py:149
  175.9 8.0 %collective-permute-start.29 = (bf16[384,1024]{1,0:T(8,128)(2,1)S(1)}, bf16[384,1024]{1,0:T(8,128)(2,1)S(1)}, u32[]{:S(2)}, u32[]{:S(2)}) collective-permute-start(bf16[384,1024]{1,0:T(8,128)(2,1)S(1)} %other_rows.3), channel_id=1, source_target_pairs={{0,8},{8,0},{1,9},{9,1},{2,10},{10,2},{3,11},{11,3},{4,12},{12,4},... | collective-permute-start | bytes 2359304 | tf_op jit(solution)/shard_map/ppermute | solution.py:149
  (18 other events, 215.1 us)

commit v4 on v3

v4 whole, which is shorter than its diff:
```python
import functools
import itertools
import math

import jax
import jax.numpy as jnp
import numpy as np
from jax import lax
from jax.experimental import pallas as pl
from jax.experimental.pallas import tpu as pltpu
from jax.sharding import PartitionSpec as P

NV = 32
NC = 64
N = 32768
NA = 128
NB = 256
NG = 6144
HALF = NG // 2
ROWS = 384
LANES = 128
PAIRS = 16
WIDE = HALF + LANES
BLOCK = 2 * PAIRS
CHUNK = 768
MIB = 1024 * 1024
VM = pl.BlockSpec(memory_space=pltpu.VMEM)
SM = pl.BlockSpec(memory_space=pltpu.SMEM)
HBM = pl.BlockSpec(memory_space=pltpu.HBM)
PARAMS = pltpu.CompilerParams(vmem_limit_bytes=14 * MIB)

NEAR = ((0, 0, 0), (2, 2, 2), (1, 1, 1), (3, 3, 3))
EVEN = ((0, 0, 0), (2, 0, 0), (0, 2, 0), (0, 0, 2))
STEP = ((0, 0, 0), (1, 0, 0), (0, 1, 0), (0, 0, 1))


def split_bf16(a):
    hi = a.astype(np.float32).astype(jnp.bfloat16)
    lo = (a - hi.astype(np.float64)).astype(np.float32).astype(jnp.bfloat16)
    return hi, lo


def dft_constants():
    k1 = np.arange(NA)[:, None]
    ang = 2.0 * math.pi * ((k1 * np.arange(NA)[None, :]) % NA) / NA
    fh, fl = split_bf16(np.concatenate([np.cos(ang), np.sin(ang)], 0))
    first = np.concatenate([fh, fl], 1)
    tw = 2.0 * math.pi * ((k1 * np.arange(NB)[None, :]) % N) / N
    norm = math.sqrt(2.0 / N)
    tcos = (np.cos(tw) * norm).astype(np.float32)
    tsin = (np.sin(tw) * norm).astype(np.float32)
    b2 = 2.0 * math.pi * ((np.arange(NB)[:, None] * np.arange(NA)[None, :]) % NB) / NB
    sh, sl = split_bf16(np.concatenate([np.cos(b2), -np.sin(b2)], 0))
    second = np.concatenate([sh, sl, sh], 0)
    return first, tcos, tsin, second


def transform(psi, first, tcos, tsin, second, spec):
    bands = [psi[:, i].astype(jnp.float32).reshape(NA, NB) for i in range(8)]
    ca = tcos[...]
    sa = tsin[...]
    for p in range(PAIRS):
        d = (bands[p // 4] * bands[4 + p % 4]).astype(jnp.bfloat16)
        y = jnp.dot(first[...], jnp.concatenate([d, d], 0), preferred_element_type=jnp.float32)
        a, b = y[:NA], y[NA:]
        uv = jnp.concatenate([a * ca - b * sa, a * sa + b * ca], 1)
        hi = uv.astype(jnp.bfloat16)
        lo = (uv - hi.astype(jnp.float32)).astype(jnp.bfloat16)
        x = jnp.dot(
            jnp.concatenate([hi, hi, lo], 1), second[...], preferred_element_type=jnp.float32
        ).astype(jnp.bfloat16)
        spec[p * 64 : p * 64 + 64, 0:128] = x[:64]
        spec[p * 64 : p * 64 + 64, 128:256] = x[64:]


def pick(spec, gidx, meta, out):
    width = 256

    def step(i, carry):
        at = pl.ds(pl.multiple_of(i * width, width), width)
        g = gidx[:, at]
        k1 = lax.bitwise_and(g, 127)
        kk = lax.shift_right_logical(k1, 6) * 128 + lax.shift_right_logical(g, 7)
        hot = jnp.where(
            lax.broadcasted_iota(jnp.int32, (256, width), 0) == kk, 1.0, 0.0
        ).astype(jnp.bfloat16)
        o = jnp.dot(spec[...], hot, preferred_element_type=jnp.float32)
        m = lax.broadcasted_iota(jnp.int32, (64, width), 0) == lax.bitwise_and(k1, 63)
        picked = jnp.sum(jnp.where(m[None], o.reshape(PAIRS, 64, width), 0.0), axis=1)
        out[:, at] = picked.astype(jnp.bfloat16)
        return carry

    lax.fori_loop(0, HALF // width, step, 0)
    out[:, HALF:WIDE] = meta[...]


def transform_kernel(psi, gidx, meta, first, tcos, tsin, second, spec, out):
    transform(psi, first, tcos, tsin, second, spec)
    pick(spec, gidx, meta, out)


def rho_spectrum(psi, gidx, meta):
    return pl.pallas_call(
        transform_kernel,
        out_shape=[
            jax.ShapeDtypeStruct((PAIRS * 64, 256), jnp.bfloat16),
            jax.ShapeDtypeStruct((PAIRS, WIDE), jnp.bfloat16),
        ],
        in_specs=[VM] * 7,
        out_specs=[VM] * 2,
        compiler_params=PARAMS,
        name="rho_spectrum",
    )(psi, gidx, meta, *(jnp.asarray(c) for c in dft_constants()))


def rho_pick(spec, gidx, meta):
    return pl.pallas_call(
        pick,
        out_shape=jax.ShapeDtypeStruct((PAIRS, WIDE), jnp.bfloat16),
        in_specs=[VM] * 3,
        out_specs=VM,
        compiler_params=PARAMS,
        name="rho_pick",
    )(spec, gidx, meta)


def device_index(x, y, z, c):
    return (z * 4 + (y >> 1) * 2 + c) * 8 + (y & 1) * 4 + x


CHIPS = tuple(itertools.product(range(4), repeat=3))


@functools.cache
def offset_pairs(offset):
    return tuple(
        (device_index(*chip, c), device_index(*((a + (1 - 2 * c) * b) % 4 for a, b in zip(chip, offset)), c))
        for chip in CHIPS for c in range(2)
    )


@functools.cache
def core_pairs():
    return tuple((device_index(*chip, c), device_index(*chip, 1 - c)) for chip in CHIPS for c in range(2))


def send(a, pairs):
    return lax.ppermute(a, ("ga", "ba"), pairs)


def level(a, offsets):
    return [a] + [send(a, offset_pairs(offset)) for offset in offsets[1:]]


def join_kernel(n, *refs):
    out = refs[n]
    row = 0
    for ref in refs[:n]:
        out[row : row + ref.shape[0], :] = ref[...]
        row += ref.shape[0]


def join(blocks):
    rows = sum(b.shape[0] for b in blocks)
    return pl.pallas_call(
        functools.partial(join_kernel, len(blocks)),
        out_shape=jax.ShapeDtypeStruct((rows, WIDE), jnp.bfloat16),
        in_specs=[VM] * len(blocks),
        out_specs=VM,
        compiler_params=PARAMS,
        name="join",
    )(*blocks)


def deal_kernel(b0, b1, b2, b3, out0, out1):
    for i, ref in enumerate((b0, b1, b2, b3)):
        out0[i * 64 : i * 64 + 64, :] = ref[0:64, :]
        out1[i * 64 : i * 64 + 64, :] = ref[64:128, :]


def deal(blocks):
    return pl.pallas_call(
        deal_kernel,
        out_shape=[jax.ShapeDtypeStruct((256, WIDE), jnp.bfloat16)] * 2,
        in_specs=[VM] * 4,
        out_specs=[VM] * 2,
        compiler_params=PARAMS,
        name="deal",
    )(*blocks)


def place_of(half, step):
    return [
        tuple(sum(v) % 4 for v in zip(NEAR[2 * half + i], EVEN[j], STEP[step]))
        for j in range(4) for i in range(2)
    ]


def mirrored(half, step):
    places = place_of(half, step)
    return [places.index(tuple(-v % 4 for v in p)) for p in places]


def weighted_kernel(place, omega, *refs):
    pieces, left = refs[:-2], refs[-1]
    w2 = omega[0] * omega[0]
    row = lax.broadcasted_iota(jnp.int32, (LANES, 2 * LANES), 0)
    lane = lax.broadcasted_iota(jnp.int32, (LANES, 2 * LANES), 1)
    spread = jnp.where((row < 3) & (lane < LANES) | (row == 3) & (lane >= LANES), 1.0, 0.0)
    spread = spread.astype(jnp.bfloat16)
    for i, piece in enumerate(pieces):
        m = jnp.dot(piece[:, HALF:WIDE], spread, preferred_element_type=jnp.float32)
        delta, taken = m[:, :LANES], m[:, LANES:]
        weight = (-4.0 / math.sqrt(NV * NC)) * taken * delta / (delta * delta + w2)
        for e in range(3):
            cols = pl.ds(pl.multiple_of(place[0] * ROWS + e * LANES, LANES), LANES)
            left[i * 256 : i * 256 + 256, e * LANES : (e + 1) * LANES] = (
                piece[:, cols].astype(jnp.float32) * weight
            ).astype(jnp.bfloat16)


def weighted(place, omega, pieces, tie):
    return pl.pallas_call(
        weighted_kernel,
        out_shape=jax.ShapeDtypeStruct((256 * len(pieces), ROWS), jnp.bfloat16),
        in_specs=[SM, SM] + [VM] * (len(pieces) + 1),
        out_specs=VM,
        compiler_params=PARAMS,
        name="weighted",
    )(place, omega, *pieces, tie)


def product(names, other, left, pieces, cols):
    total = None
    for i, (half, step) in enumerate(names):
        if other:
            rows = []
            for j in mirrored(half, step):
                at = i * 256 + j * BLOCK
                rows += [left[at + PAIRS : at + BLOCK, :], left[at : at + PAIRS, :]]
            mine = jnp.concatenate(rows, 0)
        else:
            mine = left[i * 256 : i * 256 + 256, :]
        term = lax.dot_general(
            mine, pieces[i][:, cols], (((0,), (0,)), ((), ())), preferred_element_type=jnp.float32
        )
        total = term if total is None else total + term
    return total


def chunk(i, width=CHUNK, start=0):
    return pl.ds(pl.multiple_of(start + i * width, LANES), width)


def cost(names, columns):
    return pl.CostEstimate(
        flops=2 * ROWS * columns * 256 * len(names),
        bytes_accessed=(2 * 256 * len(names) + 8 * ROWS) * columns,
        transcendentals=0,
    )


def partial_kernel(names, other, left, *refs):
    pieces, before = refs[: len(names)], refs[len(names) : -3]
    out, after = refs[-2:]
    after[...] = jnp.zeros_like(after)

    def step(i, carry):
        total = product(names, other, left, pieces, chunk(i))
        out[:, chunk(i)] = total + before[0][:, chunk(i)] if before else total
        return carry

    lax.fori_loop(0, HALF // CHUNK, step, 0)


TIE = jax.ShapeDtypeStruct((8, LANES), jnp.float32)


def partial_rows(names, other, left, pieces, before, tie):
    before = [] if before is None else [before]
    return pl.pallas_call(
        functools.partial(partial_kernel, names, other),
        out_shape=[jax.ShapeDtypeStruct((ROWS, HALF), jnp.float32), TIE],
        in_specs=[VM] * (2 + len(names) + len(before)),
        out_specs=[VM] * 2,
        input_output_aliases={1 + len(names): 0} if before else {},
        compiler_params=PARAMS,
        cost_estimate=cost(names, HALF),
        name="partial_other" if other else "partial_own",
    )(left, *pieces, *before, tie)


def own_kernel(names, core, left, *refs):
    pieces = refs[: len(names)]
    before, out, tie, wide, sem = refs[len(names) :]
    tie[...] = jnp.zeros_like(tie)

    def copies(i):
        slot = lax.rem(i, 2)
        return [
            pltpu.make_async_copy(
                wide.at[slot, :, pl.ds(j * ROWS, ROWS)],
                out.at[:, pl.ds(pl.multiple_of(((i * 2 + j) * 2 + core[0]) * ROWS, LANES), ROWS)],
                sem.at[slot, j],
            )
            for j in range(2)
        ]

    def step(i, carry):
        @pl.when(i >= 2)
        def _():
            for copy in copies(i - 2):
                copy.wait()

        wide[lax.rem(i, 2)] = product(names, False, left, pieces, chunk(i)) + before[:, chunk(i)]
        for copy in copies(i):
            copy.start()
        return carry

    lax.fori_loop(0, 4, step, 0)
    for i in (2, 3):
        for copy in copies(i):
            copy.wait()


def own_rows(names, core, left, pieces, before):
    return pl.pallas_call(
        functools.partial(own_kernel, names),
        out_shape=[jax.ShapeDtypeStruct((ROWS, NG), jnp.float32), TIE],
        in_specs=[SM, VM] + [VM] * (len(names) + 1),
        out_specs=[HBM, VM],
        scratch_shapes=[pltpu.VMEM((2, ROWS, CHUNK), jnp.float32), pltpu.SemaphoreType.DMA((2, 2))],
        compiler_params=PARAMS,
        cost_estimate=cost(names, HALF),
        name="own_rows",
    )(core, left, *pieces, before)


def other_kernel(names, start, left, *refs):
    pieces = refs[: len(names)]
    before, _, out = refs[len(names) :]

    def step(i, carry):
        total = product(names, True, left, pieces, chunk(i, start=start)) + before[:, chunk(i, start=start)]
        out[:, chunk(i)] = total.astype(jnp.bfloat16)
        return carry

    lax.fori_loop(0, 2, step, 0)


def other_rows(names, start, left, pieces, before, tie):
    return pl.pallas_call(
        functools.partial(other_kernel, names, start),
        out_shape=jax.ShapeDtypeStruct((ROWS, HALF // 2), jnp.bfloat16),
        in_specs=[VM] * (len(names) + 3),
        out_specs=VM,
        compiler_params=PARAMS,
        cost_estimate=cost(names, HALF // 2),
        name="other_rows",
    )(left, *pieces, before, tie)


def finish_kernel(core, r0, r1, _, out, wide, sem):
    def copy(i):
        return pltpu.make_async_copy(
            wide.at[:, pl.ds(i * ROWS, ROWS)],
            out.at[:, pl.ds(pl.multiple_of((i * 2 + 1 - core[0]) * ROWS, LANES), ROWS)],
            sem.at[i],
        )

    for i in range(8):
        src = (r0, r1)[i // 4]
        wide[:, i * ROWS : (i + 1) * ROWS] = src[:, (i % 4) * ROWS : (i % 4 + 1) * ROWS].astype(jnp.float32)
        copy(i).start()
    for i in range(8):
        copy(i).wait()


def finish(core, rows, out):
    return pl.pallas_call(
        finish_kernel,
        out_shape=jax.ShapeDtypeStruct((ROWS, NG), jnp.float32),
        in_specs=[SM, VM, VM, HBM],
        out_specs=HBM,
        scratch_shapes=[pltpu.VMEM((ROWS, HALF), jnp.float32), pltpu.SemaphoreType.DMA((8,))],
        input_output_aliases={3: 0},
        compiler_params=PARAMS,
        name="finish",
    )(core, *rows, out)


def in_vmem(a):
    return pltpu.with_memory_space_constraint(a, pltpu.VMEM)


def on_device(psi_val, psi_con, e_val, e_con, occ, omega, g_index):
    ga = lax.axis_index("ga")
    ba = lax.axis_index("ba")
    core = lax.rem(ga, 2).astype(jnp.int32)
    con = psi_con.reshape(16, 4, 8, NB)
    val = jnp.broadcast_to(psi_val.reshape(1, 4, 8, NB), (16, 4, 8, NB))
    psi = lax.all_to_all(jnp.concatenate([val, con], 1), "ga", 0, 0, tiled=True)

    delta = (lax.dynamic_slice(e_con, (ga * 4,), (4,))[None, :] - e_val[:, None]).reshape(PAIRS)
    taken = jnp.broadcast_to(occ.astype(jnp.float32)[:, None], (4, 4)).reshape(PAIRS)
    d1 = lax.reduce_precision(delta, 8, 7)
    d2 = lax.reduce_precision(delta - d1, 8, 7)
    d3 = delta - d1 - d2
    meta = jnp.stack([d1, d2, d3, taken], 1).astype(jnp.bfloat16)
    meta = jnp.pad(meta, ((0, 0), (0, LANES - 4)))

    halves = g_index.reshape(8, 2, ROWS).transpose(1, 0, 2).reshape(2, HALF)
    kept = lax.dynamic_slice(halves, (core, 0), (1, HALF))
    given = lax.dynamic_slice(halves, (1 - core, 0), (1, HALF))
    spec, give = rho_spectrum(psi, given, meta)
    got = send(give, core_pairs())
    keep = rho_pick(spec, kept, meta)

    a = join(level(join([keep, got]), NEAR))
    halved = [[in_vmem(b) for b in level(m, STEP)] for m in deal(level(a, EVEN))]

    place = lax.div(ga, 2).astype(jnp.int32).reshape(1)
    mine_omega = lax.dynamic_slice(omega, (ba,), (1,))
    core = core.reshape(1)
    own = other = None
    tie = jnp.zeros(TIE.shape, TIE.dtype)
    groups = (((0, 0), (1, 0)), ((0, 1), (0, 2), (0, 3)), ((1, 1), (1, 2), (1, 3)))
    for names in groups:
        pieces = [halved[h][s] for h, s in names]
        left = weighted(place, mine_omega, pieces, tie)
        mirror = send(left, core_pairs())
        if names is not groups[-1]:
            own, tie = partial_rows(names, False, left, pieces, own, tie)
            other, tie = partial_rows(names, True, mirror, pieces, other, tie)
    out, tie = own_rows(names, core, left, pieces, own)
    rows = [send(other_rows(names, s, mirror, pieces, other, tie), core_pairs()) for s in (0, HALF // 2)]
    return finish(core, rows, out)[None]


def solution(mesh):
    placed = (P("ba", "ga"), P(None, "ga"), P("ba"), P(), P("ba"), P(), P())
    return jax.shard_map(
        on_device, mesh=mesh, in_specs=placed, out_specs=P("ba", "ga", None), check_vma=False
    )
```

time: 187 us -> 142 us (0.76)
  waiting for transfers between devices: 77.7 us -> 51.8 us
  local copies, waits for them, and re-layouts: 16.3 us -> 5.62 us
  starting transfers between devices: 49.3 us -> 39.1 us
  Pallas kernels: 41.5 us -> 43.5 us
    ppermute x32 -> x18, waiting for transfers between devices: 67.1 us -> 41.2 us  [send(): return lax.ppermute(a, ('ga', 'ba'), pairs)]
    ppermute x32 -> x18, starting transfers between devices: 39.9 us -> 29.7 us  [send(): return lax.ppermute(a, ('ga', 'ba'), pairs)]
    unnamed x53 -> x24, local copies, waits for them, and re-layouts: 13.8 us -> 4.52 us
    pallas_call x7 -> x14, Pallas kernels: 29.3 us -> 31.3 us  [the longest x4 15.1 us: partial_rows(): pl.pallas_call(functools.partial(partial_kernel, names, other), out_shape...]
  transfers between devices with their start and end apart: 33 -> 19, of which waited for: 15 -> 9; matrix products, arithmetic and copies ran while one was open for 4% -> 1% of each run, Pallas kernels for 12% -> 21%
where the time goes in v4:
time: 142 us; the launch traced here: 141 us
  waiting for transfers between devices  51.8 us (36%)
  Pallas kernels  43.5 us (31%)
  starting transfers between devices  39.1 us (28%)
  local copies, waits for them, and re-layouts  5.62 us (4%)
    ppermute x18, waiting for transfers between devices, send(): return lax.ppermute(a, ('ga', 'ba'), pairs)  41.2 us
    ppermute x18, starting transfers between devices, send(): return lax.ppermute(a, ('ga', 'ba'), pairs)  29.7 us
    pallas_call x4, Pallas kernels, partial_rows(): pl.pallas_call(functools.partial(partial_kernel, names, other), out_shape...  15.1 us
    all_to_all x1, waiting for transfers between devices, on_device(): psi = lax.all_to_all(jnp.concatenate([val, con], 1), 'ga', 0, 0, tiled=True)  10.7 us
    all_to_all x1, starting transfers between devices, on_device(): psi = lax.all_to_all(jnp.concatenate([val, con], 1), 'ga', 0, 0, tiled=True)  9.46 us
    pallas_call x1, Pallas kernels, rho_spectrum(): pl.pallas_call(transform_kernel, out_shape=[jax.ShapeDtypeStruct((PAIRS *...  8.36 us
    pallas_call x3, Pallas kernels, weighted(): pl.pallas_call(weighted_kernel, out_shape=jax.ShapeDtypeStruct((256 * len...  5.67 us
    unnamed x24, local copies, waits for them, and re-layouts  4.52 us
  transfers between devices with their start and end apart: 19, of which 9 were waited for; matrix products, arithmetic and copies ran while one was open for 1% of the time, Pallas kernels for 21%

profile of v4, /device:TPU:1, one launch (start us, length us, event | category | flops | bytes accessed | tf_op | source)
XLA Modules:
  0.0 141.5 jit_solution(725206304747419796)
XLA Ops:
  2.8 9.5 %all-to-all-start = ((bf16[16,8,8,256]{3,2,1,0:T(8,128)(2,1)}), bf16[16,8,8,256]{3,2,1,0:T(8,128)(2,1)S(1)}, u32[]{:S(2)}, u32[]{:S(2)}) async-start(bf16[16,8,8,256]{3,2,1,0:T(8,128)(2,1)} %pad_maximum_fusion), calls=%async_computation | async-start | bytes 1048576 | tf_op jit(solution)/shard_map/all_to_all | solution.py:402
  12.9 10.7 %all-to-all-done.psi = bf16[16,8,8,256]{3,2,1,0:T(8,128)(2,1)S(1)} async-done(((bf16[16,8,8,256]{3,2,1,0:T(8,128)(2,1)}), bf16[16,8,8,256]{3,2,1,0:T(8,128)(2,1)S(1)}, u32[]{:S(2)}, u32[]{:S(2)}) %all-to-all-start) | async-done | bytes 524320 | tf_op jit(solution)/shard_map/all_to_all | solution.py:402
  23.6 8.4 %rho_spectrum.1 = (bf16[1024,256]{1,0:T(8,128)(2,1)S(1)}, bf16[16,3200]{1,0:T(8,128)(2,1)S(1)}) custom-call(bf16[16,8,8,256]{3,2,1,0:T(8,128)(2,1)S(1)} %all-to-all-done.psi, s32[1,3072]{1,0:T(1,128)S(1)} %get-tuple-element.34.gidx, bf16[16,128]{1,0:T(8,128)(2,1)S(1)} %pad.4.meta, bf16[256,256]{1,0:T(8,128)(2,1)S(1)} %copy-done.3, f32[128,256]{1,0:T(8,128)S(1)} %copy-done.4, ...), custom_call_target="tpu_custom_call" | custom-call | tf_op jit(solution)/shard_map/rho_spectrum/pallas_call | solution.py:103
  33.2 3.8 %rho_pick.1.refs_0_ = bf16[16,3200]{1,0:T(8,128)(2,1)S(1)} custom-call(bf16[1024,256]{1,0:T(8,128)(2,1)S(1)} %get-tuple-element.19.spec, s32[1,3072]{1,0:T(1,128)S(1)} %get-tuple-element.33.gidx, bf16[16,128]{1,0:T(8,128)(2,1)S(1)} %pad.4.meta), custom_call_target="tpu_custom_call" | custom-call | tf_op jit(solution)/shard_map/rho_pick/pallas_call | solution.py:117
  37.1 3.2 %collective-permute-start.1 = (bf16[32,3200]{1,0:T(8,128)(2,1)S(1)}, bf16[32,3200]{1,0:T(8,128)(2,1)S(1)}, u32[]{:S(2)}, u32[]{:S(2)}) collective-permute-start(bf16[32,3200]{1,0:T(8,128)(2,1)S(1)} %join.2.refs_0_), channel_id=1, source_target_pairs={{0,82},{8,90},{32,114},{40,122},{64,18},{72,26},{96,50},{104,58},{... | collective-permute-start | bytes 614408 | tf_op jit(solution)/shard_map/ppermute | solution.py:148
  40.2 3.6 %collective-permute-start.2 = (bf16[32,3200]{1,0:T(8,128)(2,1)S(1)}, bf16[32,3200]{1,0:T(8,128)(2,1)S(1)}, u32[]{:S(2)}, u32[]{:S(2)}) collective-permute-start(bf16[32,3200]{1,0:T(8,128)(2,1)S(1)} %join.2.refs_0_), channel_id=1, source_target_pairs={{0,37},{8,127},{32,69},{40,31},{64,101},{72,63},{96,5},{104,95},{4... | collective-permute-start | bytes 614408 | tf_op jit(solution)/shard_map/ppermute | solution.py:148
  43.9 6.8 %collective-permute-done.1.refs_1_ = bf16[32,3200]{1,0:T(8,128)(2,1)S(1)} collective-permute-done((bf16[32,3200]{1,0:T(8,128)(2,1)S(1)}, bf16[32,3200]{1,0:T(8,128)(2,1)S(1)}, u32[]{:S(2)}, u32[]{:S(2)}) %collective-permute-start.1) | collective-permute-done | bytes 204832 | tf_op jit(solution)/shard_map/ppermute | solution.py:148
  50.6 1.5 %collective-permute-done.2.refs_2_ = bf16[32,3200]{1,0:T(8,128)(2,1)S(1)} collective-permute-done((bf16[32,3200]{1,0:T(8,128)(2,1)S(1)}, bf16[32,3200]{1,0:T(8,128)(2,1)S(1)}, u32[]{:S(2)}, u32[]{:S(2)}) %collective-permute-start.2) | collective-permute-done | bytes 204832 | tf_op jit(solution)/shard_map/ppermute | solution.py:148
  52.2 2.5 %collective-permute-done.3.refs_3_ = bf16[32,3200]{1,0:T(8,128)(2,1)S(1)} collective-permute-done((bf16[32,3200]{1,0:T(8,128)(2,1)S(1)}, bf16[32,3200]{1,0:T(8,128)(2,1)S(1)}, u32[]{:S(2)}, u32[]{:S(2)}) %collective-permute-start.3) | collective-permute-done | bytes 204832 | tf_op jit(solution)/shard_map/ppermute | solution.py:148
  54.7 2.9 %collective-permute-start.4 = (bf16[128,3200]{1,0:T(8,128)(2,1)S(1)}, bf16[128,3200]{1,0:T(8,128)(2,1)S(1)}, u32[]{:S(2)}, u32[]{:S(2)}) collective-permute-start(bf16[128,3200]{1,0:T(8,128)(2,1)S(1)} %join.3.b0), channel_id=1, source_target_pairs={{0,2},{8,10},{32,34},{40,42},{64,66},{72,74},{96,98},{104,106},{4,... | collective-permute-start | bytes 2457608 | tf_op jit(solution)/shard_map/ppermute | solution.py:148
  58.7 17.6 %collective-permute-done.4.b1 = bf16[128,3200]{1,0:T(8,128)(2,1)S(1)} collective-permute-done((bf16[128,3200]{1,0:T(8,128)(2,1)S(1)}, bf16[128,3200]{1,0:T(8,128)(2,1)S(1)}, u32[]{:S(2)}, u32[]{:S(2)}) %collective-permute-start.4) | collective-permute-done | bytes 819232 | tf_op jit(solution)/shard_map/ppermute | solution.py:148
  76.4 2.1 %collective-permute-done.5.b2 = bf16[128,3200]{1,0:T(8,128)(2,1)S(1)} collective-permute-done((bf16[128,3200]{1,0:T(8,128)(2,1)S(1)}, bf16[128,3200]{1,0:T(8,128)(2,1)S(1)}, u32[]{:S(2)}, u32[]{:S(2)}) %collective-permute-start.5) | collective-permute-done | bytes 819232 | tf_op jit(solution)/shard_map/ppermute | solution.py:148
  78.5 1.4 deal.1
  81.0 1.6 %collective-permute-start.10 = (bf16[256,3200]{1,0:T(8,128)(2,1)}, bf16[256,3200]{1,0:T(8,128)(2,1)S(1)}, u32[]{:S(2)}, u32[]{:S(2)}) collective-permute-start(bf16[256,3200]{1,0:T(8,128)(2,1)} %get-tuple-element.22.refs_0_), channel_id=1, source_target_pairs={{0,1},{8,11},{32,33},{40,43},{64,65},{72,75},{96,97},{104,107},{4,... | collective-permute-start | bytes 4915208 | tf_op jit(solution)/shard_map/ppermute | solution.py:148
  82.7 1.3 collective-permute-start.11
  85.1 1.4 %copy-done.1 = bf16[256,3200]{1,0:T(8,128)(2,1)S(1)} copy-done((bf16[256,3200]{1,0:T(8,128)(2,1)S(1)}, bf16[256,3200]{1,0:T(8,128)(2,1)}, u32[]{:S(2)}) %copy-start.1) | copy-done | bytes 1638424
  86.6 2.3 %weighted.3.left = bf16[512,384]{1,0:T(8,128)(2,1)S(1)} custom-call(s32[1]{0:T(128)} %bitcast.1.place, f32[1]{0:T(128)} %dynamic_slice.12.omega, bf16[256,3200]{1,0:T(8,128)(2,1)} %get-tuple-element.22.refs_0_, bf16[256,3200]{1,0:T(8,128)(2,1)S(1)} %copy-done.1, f32[8,128]{1,0:T(8,128)S(1)} %broadcast_in_dim.24.refs_2_), custom_call_target="tpu_custom_call" | custom-call | tf_op jit(solution)/shard_map/weighted/pallas_call | solution.py:223
  89.0 2.1 %collective-permute-start.7 = (bf16[256,3200]{1,0:T(8,128)(2,1)S(1)}, bf16[256,3200]{1,0:T(8,128)(2,1)S(1)}, u32[]{:S(2)}, u32[]{:S(2)}) collective-permute-start(bf16[256,3200]{1,0:T(8,128)(2,1)S(1)} %copy-done.1), channel_id=1, source_target_pairs={{0,1},{8,11},{32,33},{40,43},{64,65},{72,75},{96,97},{104,107},{4,... | collective-permute-start | bytes 4915208 | tf_op jit(solution)/shard_map/ppermute | solution.py:148
  91.0 2.6 %collective-permute-start.8 = (bf16[256,3200]{1,0:T(8,128)(2,1)S(1)}, bf16[256,3200]{1,0:T(8,128)(2,1)S(1)}, u32[]{:S(2)}, u32[]{:S(2)}) collective-permute-start(bf16[256,3200]{1,0:T(8,128)(2,1)S(1)} %copy-done.1), channel_id=1, source_target_pairs={{0,4},{8,28},{32,36},{40,60},{64,68},{72,92},{96,100},{104,124},{4... | collective-permute-start | bytes 4915208 | tf_op jit(solution)/shard_map/ppermute | solution.py:148
  93.6 8.0 %collective-permute-done.10.refs_0_ = bf16[256,3200]{1,0:T(8,128)(2,1)S(1)} collective-permute-done((bf16[256,3200]{1,0:T(8,128)(2,1)}, bf16[256,3200]{1,0:T(8,128)(2,1)S(1)}, u32[]{:S(2)}, u32[]{:S(2)}) %collective-permute-start.10) | collective-permute-done | bytes 1638432 | tf_op jit(solution)/shard_map/ppermute | solution.py:148
  101.8 3.4 %partial_own.2 = (f32[384,3072]{1,0:T(8,128)S(1)}, f32[8,128]{1,0:T(8,128)S(1)}) custom-call(bf16[512,384]{1,0:T(8,128)(2,1)S(1)} %weighted.3.left, bf16[256,3200]{1,0:T(8,128)(2,1)} %get-tuple-element.22.refs_0_, bf16[256,3200]{1,0:T(8,128)(2,1)S(1)} %copy-done.1, f32[8,128]{1,0:T(8,128)S(1)} %broadcast_in_dim.24.refs_2_), custom_call_target="tpu_custom_call" | custom-call | flops 1207959552 | bytes 12582912 | tf_op jit(solution)/shard_map/partial_own/pallas_call | solution.py:281
  105.2 3.4 %partial_other.2 = (f32[384,3072]{1,0:T(8,128)S(1)}, f32[8,128]{1,0:T(8,128)S(1)}) custom-call(bf16[512,384]{1,0:T(8,128)(2,1)S(1)} %collective-permute-done.13.left, bf16[256,3200]{1,0:T(8,128)(2,1)} %get-tuple-element.22.refs_0_, bf16[256,3200]{1,0:T(8,128)(2,1)S(1)} %copy-done.1, f32[8,128]{1,0:T(8,128)S(1)} %get-tuple-element.23.refs_2_), custom_call_target="tpu_custom_call" | custom-call | flops 1207959552 | bytes 12582912 | tf_op jit(solution)/shard_map/partial_other/pallas_call | solution.py:281
  108.7 2.4 %weighted.4.left = bf16[768,384]{1,0:T(8,128)(2,1)S(1)} custom-call(s32[1]{0:T(128)} %bitcast.1.place, f32[1]{0:T(128)} %dynamic_slice.12.omega, bf16[256,3200]{1,0:T(8,128)(2,1)S(1)} %collective-permute-done.10.refs_0_, bf16[256,3200]{1,0:T(8,128)(2,1)S(1)} %collective-permute-done.11.refs_1_, bf16[256,3200]{1,0:T(8,128)(2,1)} %collective-permute-done.12.refs_2_, ...), custom_call_target="tpu_custom_call" | custom-call | tf_op jit(solution)/shard_map/weighted/pallas_call | solution.py:223
  111.1 4.3 %collective-permute-start.14 = (bf16[768,384]{1,0:T(8,128)(2,1)S(1)}, bf16[768,384]{1,0:T(8,128)(2,1)S(1)}, u32[]{:S(2)}, u32[]{:S(2)}) collective-permute-start(bf16[768,384]{1,0:T(8,128)(2,1)S(1)} %weighted.4.left), channel_id=1, source_target_pairs={{0,8},{8,0},{32,40},{40,32},{64,72},{72,64},{96,104},{104,96},{4,1... | collective-permute-start | bytes 1769480 | tf_op jit(solution)/shard_map/ppermute | solution.py:148
  115.3 4.1 %partial_own.3 = (f32[384,3072]{1,0:T(8,128)S(1)}, f32[8,128]{1,0:T(8,128)S(1)}) custom-call(bf16[768,384]{1,0:T(8,128)(2,1)S(1)} %weighted.4.left, bf16[256,3200]{1,0:T(8,128)(2,1)S(1)} %collective-permute-done.10.refs_0_, bf16[256,3200]{1,0:T(8,128)(2,1)S(1)} %collective-permute-done.11.refs_1_, ...), custom_call_target="tpu_custom_call", output_to_operand_aliasing={{0}: (4, {})} | custom-call | flops 1811939328 | bytes 14155776 | tf_op jit(solution)/shard_map/partial_own/pallas_call | solution.py:281
  119.5 4.1 %partial_other.3 = (f32[384,3072]{1,0:T(8,128)S(1)}, f32[8,128]{1,0:T(8,128)S(1)}) custom-call(bf16[768,384]{1,0:T(8,128)(2,1)S(1)} %collective-permute-done.14.left, bf16[256,3200]{1,0:T(8,128)(2,1)S(1)} %collective-permute-done.10.refs_0_, bf16[256,3200]{1,0:T(8,128)(2,1)S(1)} %collective-permute-done.11.refs_1_, ...), custom_call_target="tpu_custom_call", output_to_operand_aliasing={{0}: (4, {})} | custom-call | flops 1811939328 | bytes 14155776 | tf_op jit(solution)/shard_map/partial_other/pallas_call | solution.py:281
  124.6 4.4 %collective-permute-start.15 = (bf16[768,384]{1,0:T(8,128)(2,1)S(1)}, bf16[768,384]{1,0:T(8,128)(2,1)S(1)}, u32[]{:S(2)}, u32[]{:S(2)}) collective-permute-start(bf16[768,384]{1,0:T(8,128)(2,1)S(1)} %weighted.5.left), channel_id=1, source_target_pairs={{0,8},{8,0},{32,40},{40,32},{64,72},{72,64},{96,104},{104,96},{4,1... | collective-permute-start | bytes 1769480 | tf_op jit(solution)/shard_map/ppermute | solution.py:148
  128.9 4.1 %own_rows.1 = (f32[384,6144]{1,0:T(8,128)}, f32[8,128]{1,0:T(8,128)S(1)}) custom-call(s32[1]{0:T(128)} %bitcast.core, bf16[768,384]{1,0:T(8,128)(2,1)S(1)} %weighted.5.left, bf16[256,3200]{1,0:T(8,128)(2,1)S(1)} %collective-permute-done.7.refs_0_, bf16[256,3200]{1,0:T(8,128)(2,1)S(1)} %collective-permute-done.8.refs_1_, ...), custom_call_target="tpu_custom_call" | custom-call | flops 1811939328 | bytes 14155776 | tf_op jit(solution)/shard_map/own_rows/pallas_call | solution.py:327
  133.1 1.4 other_rows.3
  134.5 1.3 other_rows.2
  137.4 1.7 %collective-permute-done.16.r0 = bf16[384,1536]{1,0:T(8,128)(2,1)S(1)} collective-permute-done((bf16[384,1536]{1,0:T(8,128)(2,1)S(1)}, bf16[384,1536]{1,0:T(8,128)(2,1)S(1)}, u32[]{:S(2)}, u32[]{:S(2)}) %collective-permute-start.16) | collective-permute-done | bytes 1179680 | tf_op jit(solution)/shard_map/ppermute | solution.py:148
  139.1 2.3 %finish.1 = f32[384,6144]{1,0:T(8,128)} custom-call(s32[1]{0:T(128)} %bitcast.core, bf16[384,1536]{1,0:T(8,128)(2,1)S(1)} %collective-permute-done.16.r0, bf16[384,1536]{1,0:T(8,128)(2,1)S(1)} %collective-permute-done.17.r1, f32[384,6144]{1,0:T(8,128)} %get-tuple-element.32._), custom_call_target="tpu_custom_call", output_to_operand_aliasing={{}: (3, {})} | custom-call | tf_op jit(solution)/shard_map/finish/pallas_call | solution.py:380
  (62 shorter events, 10.9 us)
Async XLA Ops:
  0.0 23.6 %copy-start.3 = (bf16[256,256]{1,0:T(8,128)(2,1)S(1)}, bf16[256,256]{1,0:T(8,128)(2,1)}, u32[]{:S(2)}) copy-start(bf16[256,256]{1,0:T(8,128)(2,1)} %constant.39.clone.first) | copy-start | bytes 393220
  0.0 23.6 %copy-start.4 = (f32[128,256]{1,0:T(8,128)S(1)}, f32[128,256]{1,0:T(8,128)}, u32[]{:S(2)}) copy-start(f32[128,256]{1,0:T(8,128)} %constant.40.clone.tcos) | copy-start | bytes 393220
  0.0 23.6 %copy-start.5 = (f32[128,256]{1,0:T(8,128)S(1)}, f32[128,256]{1,0:T(8,128)}, u32[]{:S(2)}) copy-start(f32[128,256]{1,0:T(8,128)} %constant.41.clone.tsin) | copy-start | bytes 393220
  0.0 23.6 %copy-start.2 = (bf16[1536,128]{1,0:T(8,128)(2,1)S(1)}, bf16[1536,128]{1,0:T(8,128)(2,1)}, u32[]{:S(2)}) copy-start(bf16[1536,128]{1,0:T(8,128)(2,1)} %constant.42.clone.second) | copy-start | bytes 1179652
  0.0 12.2 %copy-start.8 = (f32[64]{0:T(128)S(1)}, f32[64]{0:T(128)}, u32[]{:S(2)}) copy-start(f32[64]{0:T(128)} %param.14) | copy-start | bytes 772
  0.0 12.3 %copy-start.7 = (f32[4]{0:T(128)S(1)}, f32[4]{0:T(128)}, u32[]{:S(2)}) copy-start(f32[4]{0:T(128)} %param.13) | copy-start | bytes 52
  0.0 12.5 %copy-start.9 = (s32[4]{0:T(128)S(1)}, s32[4]{0:T(128)}, u32[]{:S(2)}) copy-start(s32[4]{0:T(128)} %param.15) | copy-start | bytes 52
  0.1 12.5 %copy-start.6 = (s32[6144]{0:T(1024)S(1)}, s32[6144]{0:T(1024)}, u32[]{:S(2)}) copy-start(s32[6144]{0:T(1024)} %param.17) | copy-start | bytes 73732
  2.8 20.8 %all-to-all-start = ((bf16[16,8,8,256]{3,2,1,0:T(8,128)(2,1)}), bf16[16,8,8,256]{3,2,1,0:T(8,128)(2,1)S(1)}, u32[]{:S(2)}, u32[]{:S(2)}) async-start(bf16[16,8,8,256]{3,2,1,0:T(8,128)(2,1)} %pad_maximum_fusion), calls=%async_computation | async-start | bytes 1048576 | tf_op jit(solution)/shard_map/all_to_all | solution.py:402
  31.9 5.1 %collective-permute-start = (bf16[16,3200]{1,0:T(8,128)(2,1)S(1)}, bf16[16,3200]{1,0:T(8,128)(2,1)S(1)}, u32[]{:S(2)}, u32[]{:S(2)}) collective-permute-start(bf16[16,3200]{1,0:T(8,128)(2,1)S(1)} %get-tuple-element.20), channel_id=1, source_target_pairs={{0,8},{8,0},{32,40},{40,32},{64,72},{72,64},{96,104},{104,96},{4,1... | collective-permute-start | bytes 307208 | tf_op jit(solution)/shard_map/ppermute | solution.py:148
  37.1 13.6 %collective-permute-start.1 = (bf16[32,3200]{1,0:T(8,128)(2,1)S(1)}, bf16[32,3200]{1,0:T(8,128)(2,1)S(1)}, u32[]{:S(2)}, u32[]{:S(2)}) collective-permute-start(bf16[32,3200]{1,0:T(8,128)(2,1)S(1)} %join.2.refs_0_), channel_id=1, source_target_pairs={{0,82},{8,90},{32,114},{40,122},{64,18},{72,26},{96,50},{104,58},{... | collective-permute-start | bytes 614408 | tf_op jit(solution)/shard_map/ppermute | solution.py:148
  40.2 11.9 %collective-permute-start.2 = (bf16[32,3200]{1,0:T(8,128)(2,1)S(1)}, bf16[32,3200]{1,0:T(8,128)(2,1)S(1)}, u32[]{:S(2)}, u32[]{:S(2)}) collective-permute-start(bf16[32,3200]{1,0:T(8,128)(2,1)S(1)} %join.2.refs_0_), channel_id=1, source_target_pairs={{0,37},{8,127},{32,69},{40,31},{64,101},{72,63},{96,5},{104,95},{4... | collective-permute-start | bytes 614408 | tf_op jit(solution)/shard_map/ppermute | solution.py:148
  43.9 10.8 %collective-permute-start.3 = (bf16[32,3200]{1,0:T(8,128)(2,1)S(1)}, bf16[32,3200]{1,0:T(8,128)(2,1)S(1)}, u32[]{:S(2)}, u32[]{:S(2)}) collective-permute-start(bf16[32,3200]{1,0:T(8,128)(2,1)S(1)} %join.2.refs_0_), channel_id=1, source_target_pairs={{0,119},{8,45},{32,23},{40,77},{64,55},{72,109},{96,87},{104,13},{... | collective-permute-start | bytes 614408 | tf_op jit(solution)/shard_map/ppermute | solution.py:148
  54.7 29.8 %copy-start.10 = (f32[8]{0:T(128)S(1)}, f32[8]{0:T(128)}, u32[]{:S(2)}) copy-start(f32[8]{0:T(128)} %param.16) | copy-start | bytes 100
  54.7 21.6 %collective-permute-start.4 = (bf16[128,3200]{1,0:T(8,128)(2,1)S(1)}, bf16[128,3200]{1,0:T(8,128)(2,1)S(1)}, u32[]{:S(2)}, u32[]{:S(2)}) collective-permute-start(bf16[128,3200]{1,0:T(8,128)(2,1)S(1)} %join.3.b0), channel_id=1, source_target_pairs={{0,2},{8,10},{32,34},{40,42},{64,66},{72,74},{96,98},{104,106},{4,... | collective-permute-start | bytes 2457608 | tf_op jit(solution)/shard_map/ppermute | solution.py:148
  57.6 20.8 %collective-permute-start.5 = (bf16[128,3200]{1,0:T(8,128)(2,1)S(1)}, bf16[128,3200]{1,0:T(8,128)(2,1)S(1)}, u32[]{:S(2)}, u32[]{:S(2)}) collective-permute-start(bf16[128,3200]{1,0:T(8,128)(2,1)S(1)} %join.3.b0), channel_id=1, source_target_pairs={{0,16},{8,24},{32,48},{40,56},{64,80},{72,88},{96,112},{104,120},{... | collective-permute-start | bytes 2457608 | tf_op jit(solution)/shard_map/ppermute | solution.py:148
  58.3 20.2 %collective-permute-start.6 = (bf16[128,3200]{1,0:T(8,128)(2,1)S(1)}, bf16[128,3200]{1,0:T(8,128)(2,1)S(1)}, u32[]{:S(2)}, u32[]{:S(2)}) collective-permute-start(bf16[128,3200]{1,0:T(8,128)(2,1)S(1)} %join.3.b0), channel_id=1, source_target_pairs={{0,64},{8,72},{32,96},{40,104},{64,0},{72,8},{96,32},{104,40},{4,6... | collective-permute-start | bytes 2457608 | tf_op jit(solution)/shard_map/ppermute | solution.py:148
  79.8 1.2 copy-start
  81.0 20.6 %collective-permute-start.10 = (bf16[256,3200]{1,0:T(8,128)(2,1)}, bf16[256,3200]{1,0:T(8,128)(2,1)S(1)}, u32[]{:S(2)}, u32[]{:S(2)}) collective-permute-start(bf16[256,3200]{1,0:T(8,128)(2,1)} %get-tuple-element.22.refs_0_), channel_id=1, source_target_pairs={{0,1},{8,11},{32,33},{40,43},{64,65},{72,75},{96,97},{104,107},{4,... | collective-permute-start | bytes 4915208 | tf_op jit(solution)/shard_map/ppermute | solution.py:148
  82.7 26.0 %collective-permute-start.11 = (bf16[256,3200]{1,0:T(8,128)(2,1)}, bf16[256,3200]{1,0:T(8,128)(2,1)S(1)}, u32[]{:S(2)}, u32[]{:S(2)}) collective-permute-start(bf16[256,3200]{1,0:T(8,128)(2,1)} %get-tuple-element.22.refs_0_), channel_id=1, source_target_pairs={{0,4},{8,28},{32,36},{40,60},{64,68},{72,92},{96,100},{104,124},{4... | collective-permute-start | bytes 4915208 | tf_op jit(solution)/shard_map/ppermute | solution.py:148
  84.0 24.7 %collective-permute-start.12 = (bf16[256,3200]{1,0:T(8,128)(2,1)}, bf16[256,3200]{1,0:T(8,128)(2,1)}, u32[]{:S(2)}, u32[]{:S(2)}) collective-permute-start(bf16[256,3200]{1,0:T(8,128)(2,1)} %get-tuple-element.22.refs_0_), channel_id=1, source_target_pairs={{0,32},{8,104},{32,64},{40,8},{64,96},{72,40},{96,0},{104,72},{4,3... | collective-permute-start | bytes 4915208 | tf_op jit(solution)/shard_map/ppermute | solution.py:148
  85.1 1.4 %copy-start.1 = (bf16[256,3200]{1,0:T(8,128)(2,1)S(1)}, bf16[256,3200]{1,0:T(8,128)(2,1)}, u32[]{:S(2)}) copy-start(bf16[256,3200]{1,0:T(8,128)(2,1)} %copy-done) | copy-start | bytes 4915204
  88.9 2.1 %collective-permute-start.13 = (bf16[512,384]{1,0:T(8,128)(2,1)S(1)}, bf16[512,384]{1,0:T(8,128)(2,1)S(1)}, u32[]{:S(2)}, u32[]{:S(2)}) collective-permute-start(bf16[512,384]{1,0:T(8,128)(2,1)S(1)} %weighted.3.left), channel_id=1, source_target_pairs={{0,8},{8,0},{32,40},{40,32},{64,72},{72,64},{96,104},{104,96},{4,1... | collective-permute-start | bytes 1179656 | tf_op jit(solution)/shard_map/ppermute | solution.py:148
  89.0 34.6 %collective-permute-start.7 = (bf16[256,3200]{1,0:T(8,128)(2,1)S(1)}, bf16[256,3200]{1,0:T(8,128)(2,1)S(1)}, u32[]{:S(2)}, u32[]{:S(2)}) collective-permute-start(bf16[256,3200]{1,0:T(8,128)(2,1)S(1)} %copy-done.1), channel_id=1, source_target_pairs={{0,1},{8,11},{32,33},{40,43},{64,65},{72,75},{96,97},{104,107},{4,... | collective-permute-start | bytes 4915208 | tf_op jit(solution)/shard_map/ppermute | solution.py:148
  91.0 32.6 %collective-permute-start.8 = (bf16[256,3200]{1,0:T(8,128)(2,1)S(1)}, bf16[256,3200]{1,0:T(8,128)(2,1)S(1)}, u32[]{:S(2)}, u32[]{:S(2)}) collective-permute-start(bf16[256,3200]{1,0:T(8,128)(2,1)S(1)} %copy-done.1), channel_id=1, source_target_pairs={{0,4},{8,28},{32,36},{40,60},{64,68},{72,92},{96,100},{104,124},{4... | collective-permute-start | bytes 4915208 | tf_op jit(solution)/shard_map/ppermute | solution.py:148
  101.6 22.0 %collective-permute-start.9 = (bf16[256,3200]{1,0:T(8,128)(2,1)S(1)}, bf16[256,3200]{1,0:T(8,128)(2,1)S(1)}, u32[]{:S(2)}, u32[]{:S(2)}) collective-permute-start(bf16[256,3200]{1,0:T(8,128)(2,1)S(1)} %copy-done.1), channel_id=1, source_target_pairs={{0,32},{8,104},{32,64},{40,8},{64,96},{72,40},{96,0},{104,72},{4,3... | collective-permute-start | bytes 4915208 | tf_op jit(solution)/shard_map/ppermute | solution.py:148
  111.1 8.4 %collective-permute-start.14 = (bf16[768,384]{1,0:T(8,128)(2,1)S(1)}, bf16[768,384]{1,0:T(8,128)(2,1)S(1)}, u32[]{:S(2)}, u32[]{:S(2)}) collective-permute-start(bf16[768,384]{1,0:T(8,128)(2,1)S(1)} %weighted.4.left), channel_id=1, source_target_pairs={{0,8},{8,0},{32,40},{40,32},{64,72},{72,64},{96,104},{104,96},{4,1... | collective-permute-start | bytes 1769480 | tf_op jit(solution)/shard_map/ppermute | solution.py:148
  124.6 8.5 %collective-permute-start.15 = (bf16[768,384]{1,0:T(8,128)(2,1)S(1)}, bf16[768,384]{1,0:T(8,128)(2,1)S(1)}, u32[]{:S(2)}, u32[]{:S(2)}) collective-permute-start(bf16[768,384]{1,0:T(8,128)(2,1)S(1)} %weighted.5.left), channel_id=1, source_target_pairs={{0,8},{8,0},{32,40},{40,32},{64,72},{72,64},{96,104},{104,96},{4,1... | collective-permute-start | bytes 1769480 | tf_op jit(solution)/shard_map/ppermute | solution.py:148
  134.4 2.9 %collective-permute-start.17 = (bf16[384,1536]{1,0:T(8,128)(2,1)S(1)}, bf16[384,1536]{1,0:T(8,128)(2,1)S(1)}, u32[]{:S(2)}, u32[]{:S(2)}) collective-permute-start(bf16[384,1536]{1,0:T(8,128)(2,1)S(1)} %other_rows.3), channel_id=1, source_target_pairs={{0,8},{8,0},{32,40},{40,32},{64,72},{72,64},{96,104},{104,96},{4,1... | collective-permute-start | bytes 3538952 | tf_op jit(solution)/shard_map/ppermute | solution.py:148
  135.9 3.2 %collective-permute-start.16 = (bf16[384,1536]{1,0:T(8,128)(2,1)S(1)}, bf16[384,1536]{1,0:T(8,128)(2,1)S(1)}, u32[]{:S(2)}, u32[]{:S(2)}) collective-permute-start(bf16[384,1536]{1,0:T(8,128)(2,1)S(1)} %other_rows.2), channel_id=1, source_target_pairs={{0,8},{8,0},{32,40},{40,32},{64,72},{72,64},{96,104},{104,96},{4,1... | collective-permute-start | bytes 3538952 | tf_op jit(solution)/shard_map/ppermute | solution.py:148

commit v5 on v4

--- a/solution.py
+++ b/solution.py
@@ -153,40 +153,23 @@
 
 
 def join_kernel(n, *refs):
-    out = refs[n]
+    out = refs[-1]
     row = 0
     for ref in refs[:n]:
         out[row : row + ref.shape[0], :] = ref[...]
         row += ref.shape[0]
 
 
-def join(blocks):
+def join(blocks, after=()):
     rows = sum(b.shape[0] for b in blocks)
     return pl.pallas_call(
         functools.partial(join_kernel, len(blocks)),
         out_shape=jax.ShapeDtypeStruct((rows, WIDE), jnp.bfloat16),
-        in_specs=[VM] * len(blocks),
+        in_specs=[VM] * (len(blocks) + len(after)),
         out_specs=VM,
         compiler_params=PARAMS,
         name="join",
-    )(*blocks)
-
-
-def deal_kernel(b0, b1, b2, b3, out0, out1):
-    for i, ref in enumerate((b0, b1, b2, b3)):
-        out0[i * 64 : i * 64 + 64, :] = ref[0:64, :]
-        out1[i * 64 : i * 64 + 64, :] = ref[64:128, :]
-
-
-def deal(blocks):
-    return pl.pallas_call(
-        deal_kernel,
-        out_shape=[jax.ShapeDtypeStruct((256, WIDE), jnp.bfloat16)] * 2,
-        in_specs=[VM] * 4,
-        out_specs=[VM] * 2,
-        compiler_params=PARAMS,
-        name="deal",
-    )(*blocks)
+    )(*blocks, *after)
 
 
 def place_of(half, step):
@@ -290,55 +273,60 @@
     )(left, *pieces, *before, tie)
 
 
-def own_kernel(names, core, left, *refs):
+def own_kernel(names, start, n_swapped, core, left, *refs):
     pieces = refs[: len(names)]
-    before, out, tie, wide, sem = refs[len(names) :]
-    tie[...] = jnp.zeros_like(tie)
-
-    def copies(i):
-        slot = lax.rem(i, 2)
-        return [
-            pltpu.make_async_copy(
-                wide.at[slot, :, pl.ds(j * ROWS, ROWS)],
-                out.at[:, pl.ds(pl.multiple_of(((i * 2 + j) * 2 + core[0]) * ROWS, LANES), ROWS)],
-                sem.at[slot, j],
-            )
-            for j in range(2)
-        ]
-
-    def step(i, carry):
-        @pl.when(i >= 2)
-        def _():
-            for copy in copies(i - 2):
-                copy.wait()
-
-        wide[lax.rem(i, 2)] = product(names, False, left, pieces, chunk(i)) + before[:, chunk(i)]
-        for copy in copies(i):
-            copy.start()
-        return carry
-
-    lax.fori_loop(0, 4, step, 0)
-    for i in (2, 3):
-        for copy in copies(i):
-            copy.wait()
-
-
-def own_rows(names, core, left, pieces, before):
-    return pl.pallas_call(
-        functools.partial(own_kernel, names),
-        out_shape=[jax.ShapeDtypeStruct((ROWS, NG), jnp.float32), TIE],
-        in_specs=[SM, VM] + [VM] * (len(names) + 1),
-        out_specs=[HBM, VM],
-        scratch_shapes=[pltpu.VMEM((2, ROWS, CHUNK), jnp.float32), pltpu.SemaphoreType.DMA((2, 2))],
-        compiler_params=PARAMS,
-        cost_estimate=cost(names, HALF),
+    before = refs[len(names)]
+    swapped = refs[len(names) + 1 : len(names) + 1 + n_swapped]
+    out, wide, sem, wide_swapped, sem_swapped = refs[-5:]
+
+    def copy(src, block, half, s):
+        return pltpu.make_async_copy(
+            src, out.at[:, pl.ds(pl.multiple_of((block * 2 + half) * ROWS, LANES), ROWS)], s
+        )
+
+    copies = []
+    for i in range(4 * n_swapped):
+        at = slice(i * ROWS, (i + 1) * ROWS)
+        src = slice((i % 4) * ROWS, (i % 4 + 1) * ROWS)
+        wide_swapped[:, at] = swapped[i // 4][:, src].astype(jnp.float32)
+        copies.append(copy(wide_swapped.at[:, pl.ds(i * ROWS, ROWS)], i, 1 - core[0], sem_swapped.at[i]))
+        copies[-1].start()
+    for i in range(2):
+        cols = slice(start + i * CHUNK, start + (i + 1) * CHUNK)
+        wide[:, i * CHUNK : (i + 1) * CHUNK] = product(names, False, left, pieces, cols) + before[:, cols]
+        for j in (2 * i, 2 * i + 1):
+            block = start // ROWS + j
+            copies.append(copy(wide.at[:, pl.ds(j * ROWS, ROWS)], block, core[0], sem.at[j]))
+            copies[-1].start()
+    for c in copies:
+        c.wait()
+
+
+def own_rows(names, start, core, left, pieces, before, swapped, after):
+    grows = after.shape == (ROWS, NG)
+    n = len(swapped)
+    return pl.pallas_call(
+        functools.partial(own_kernel, names, start, n),
+        out_shape=jax.ShapeDtypeStruct((ROWS, NG), jnp.float32),
+        in_specs=[SM, VM] + [VM] * (len(names) + 1 + n) + [HBM if grows else VM],
+        out_specs=HBM,
+        scratch_shapes=[
+            pltpu.VMEM((ROWS, HALF // 2), jnp.float32),
+            pltpu.SemaphoreType.DMA((4,)),
+            pltpu.VMEM((ROWS, HALF) if n else (8, LANES), jnp.float32),
+            pltpu.SemaphoreType.DMA((8,)),
+        ],
+        input_output_aliases={3 + len(names) + n: 0} if grows else {},
+        compiler_params=PARAMS,
+        cost_estimate=cost(names, HALF // 2),
         name="own_rows",
-    )(core, left, *pieces, before)
+    )(core, left, *pieces, before, *swapped, after)
 
 
 def other_kernel(names, start, left, *refs):
     pieces = refs[: len(names)]
-    before, _, out = refs[len(names) :]
+    before, _, out, after = refs[len(names) :]
+    after[...] = jnp.zeros_like(after)
 
     def step(i, carry):
         total = product(names, True, left, pieces, chunk(i, start=start)) + before[:, chunk(i, start=start)]
@@ -351,42 +339,13 @@
 def other_rows(names, start, left, pieces, before, tie):
     return pl.pallas_call(
         functools.partial(other_kernel, names, start),
-        out_shape=jax.ShapeDtypeStruct((ROWS, HALF // 2), jnp.bfloat16),
+        out_shape=[jax.ShapeDtypeStruct((ROWS, HALF // 2), jnp.bfloat16), TIE],
         in_specs=[VM] * (len(names) + 3),
-        out_specs=VM,
+        out_specs=[VM] * 2,
         compiler_params=PARAMS,
         cost_estimate=cost(names, HALF // 2),
         name="other_rows",
     )(left, *pieces, before, tie)
-
-
-def finish_kernel(core, r0, r1, _, out, wide, sem):
-    def copy(i):
-        return pltpu.make_async_copy(
-            wide.at[:, pl.ds(i * ROWS, ROWS)],
-            out.at[:, pl.ds(pl.multiple_of((i * 2 + 1 - core[0]) * ROWS, LANES), ROWS)],
-            sem.at[i],
-        )
-
-    for i in range(8):
-        src = (r0, r1)[i // 4]
-        wide[:, i * ROWS : (i + 1) * ROWS] = src[:, (i % 4) * ROWS : (i % 4 + 1) * ROWS].astype(jnp.float32)
-        copy(i).start()
-    for i in range(8):
-        copy(i).wait()
-
-
-def finish(core, rows, out):
-    return pl.pallas_call(
-        finish_kernel,
-        out_shape=jax.ShapeDtypeStruct((ROWS, NG), jnp.float32),
-        in_specs=[SM, VM, VM, HBM],
-        out_specs=HBM,
-        scratch_shapes=[pltpu.VMEM((ROWS, HALF), jnp.float32), pltpu.SemaphoreType.DMA((8,))],
-        input_output_aliases={3: 0},
-        compiler_params=PARAMS,
-        name="finish",
-    )(core, *rows, out)
 
 
 def in_vmem(a):
@@ -416,15 +375,19 @@
     got = send(give, core_pairs())
     keep = rho_pick(spec, kept, meta)
 
-    a = join(level(join([keep, got]), NEAR))
-    halved = [[in_vmem(b) for b in level(m, STEP)] for m in deal(level(a, EVEN))]
+    mine = join([keep, got])
+    near = {o: send(mine, offset_pairs(o)) for o in (NEAR[2], NEAR[3], NEAR[1])}
+    halved = [None, None]
+    for half, blocks in ((1, [near[NEAR[2]], near[NEAR[3]]]), (0, [mine, near[NEAR[1]]])):
+        a = join(level(join(blocks), EVEN), [near[NEAR[1]]] if half else [])
+        halved[half] = [in_vmem(b) for b in level(a, STEP)]
 
     place = lax.div(ga, 2).astype(jnp.int32).reshape(1)
     mine_omega = lax.dynamic_slice(omega, (ba,), (1,))
     core = core.reshape(1)
     own = other = None
     tie = jnp.zeros(TIE.shape, TIE.dtype)
-    groups = (((0, 0), (1, 0)), ((0, 1), (0, 2), (0, 3)), ((1, 1), (1, 2), (1, 3)))
+    groups = (((1, 0), (0, 0)), ((1, 1), (1, 2), (1, 3)), ((0, 1), (0, 2), (0, 3)))
     for names in groups:
         pieces = [halved[h][s] for h, s in names]
         left = weighted(place, mine_omega, pieces, tie)
@@ -432,9 +395,12 @@
         if names is not groups[-1]:
             own, tie = partial_rows(names, False, left, pieces, own, tie)
             other, tie = partial_rows(names, True, mirror, pieces, other, tie)
-    out, tie = own_rows(names, core, left, pieces, own)
-    rows = [send(other_rows(names, s, mirror, pieces, other, tie), core_pairs()) for s in (0, HALF // 2)]
-    return finish(core, rows, out)[None]
+    rows = []
+    for start in (0, HALF // 2):
+        row, tie = other_rows(names, start, mirror, pieces, other, tie)
+        rows.append(send(row, core_pairs()))
+    out = own_rows(names, 0, core, left, pieces, own, [], tie)
+    return own_rows(names, HALF // 2, core, left, pieces, own, rows, out)[None]
 
 
 def solution(mesh):

time: 142 us -> 159 us (1.12)
  starting transfers between devices: 39.1 us -> 75 us
  waiting for transfers between devices: 51.8 us -> 31.1 us
  Pallas kernels: 43.5 us -> 46 us
    ppermute x18 -> x21, starting transfers between devices: 29.7 us -> 65.6 us  [send(): return lax.ppermute(a, ('ga', 'ba'), pairs)]
    ppermute x18 -> x21, waiting for transfers between devices: 41.2 us -> 20.4 us  [send(): return lax.ppermute(a, ('ga', 'ba'), pairs)]
    pallas_call x2 -> x5, Pallas kernels: 0.07 us -> 3.46 us  [join(): pl.pallas_call(functools.partial(join_kernel, len(blocks)), out_shape=jax...]
    pallas_call x5 -> x4, Pallas kernels: 10.5 us -> 9.63 us  [the longest x2 6.93 us: own_rows(): pl.pallas_call(functools.partial(own_kernel, names, start, n), out_shape=...]
  transfers between devices with their start and end apart: 19 -> 22, of which waited for: 9 -> 7; matrix products, arithmetic and copies ran while one was open for 1% -> 1% of each run, Pallas kernels for 21% -> 18%
where the time goes in v5:
time: 159 us; the launch traced here: 158 us
  starting transfers between devices  75 us (47%)
  Pallas kernels  46 us (29%)
  waiting for transfers between devices  31.1 us (20%)
  local copies, waits for them, and re-layouts  4.72 us (3%)
    ppermute x21, starting transfers between devices, send(): return lax.ppermute(a, ('ga', 'ba'), pairs)  65.6 us
    ppermute x21, waiting for transfers between devices, send(): return lax.ppermute(a, ('ga', 'ba'), pairs)  20.4 us
    pallas_call x4, Pallas kernels, partial_rows(): pl.pallas_call(functools.partial(partial_kernel, names, other), out_shape...  15.1 us
    all_to_all x1, waiting for transfers between devices, on_device(): psi = lax.all_to_all(jnp.concatenate([val, con], 1), 'ga', 0, 0, tiled=True)  10.7 us
    all_to_all x1, starting transfers between devices, on_device(): psi = lax.all_to_all(jnp.concatenate([val, con], 1), 'ga', 0, 0, tiled=True)  9.46 us
    pallas_call x1, Pallas kernels, rho_spectrum(): pl.pallas_call(transform_kernel, out_shape=[jax.ShapeDtypeStruct((PAIRS *...  8.36 us
    pallas_call x2, Pallas kernels, own_rows(): pl.pallas_call(functools.partial(own_kernel, names, start, n), out_shape=...  6.93 us
    pallas_call x3, Pallas kernels, weighted(): pl.pallas_call(weighted_kernel, out_shape=jax.ShapeDtypeStruct((256 * len...  5.63 us
  transfers between devices with their start and end apart: 22, of which 7 were waited for; matrix products, arithmetic and copies ran while one was open for 1% of the time, Pallas kernels for 18%

profile of v5, /device:TPU:1, one launch (start us, length us, event | category | flops | bytes accessed | tf_op | source)
XLA Modules:
  0.0 158.2 jit_solution(9911715855068801527)
XLA Ops:
  2.7 9.5 %all-to-all-start = ((bf16[16,8,8,256]{3,2,1,0:T(8,128)(2,1)}), bf16[16,8,8,256]{3,2,1,0:T(8,128)(2,1)S(1)}, u32[]{:S(2)}, u32[]{:S(2)}) async-start(bf16[16,8,8,256]{3,2,1,0:T(8,128)(2,1)} %pad_maximum_fusion), calls=%async_computation | async-start | bytes 1048576 | tf_op jit(solution)/shard_map/all_to_all | solution.py:361
  12.8 10.7 %all-to-all-done.psi = bf16[16,8,8,256]{3,2,1,0:T(8,128)(2,1)S(1)} async-done(((bf16[16,8,8,256]{3,2,1,0:T(8,128)(2,1)}), bf16[16,8,8,256]{3,2,1,0:T(8,128)(2,1)S(1)}, u32[]{:S(2)}, u32[]{:S(2)}) %all-to-all-start) | async-done | bytes 524320 | tf_op jit(solution)/shard_map/all_to_all | solution.py:361
  23.5 8.4 %rho_spectrum.1 = (bf16[1024,256]{1,0:T(8,128)(2,1)S(1)}, bf16[16,3200]{1,0:T(8,128)(2,1)S(1)}) custom-call(bf16[16,8,8,256]{3,2,1,0:T(8,128)(2,1)S(1)} %all-to-all-done.psi, s32[1,3072]{1,0:T(1,128)S(1)} %get-tuple-element.34.gidx, bf16[16,128]{1,0:T(8,128)(2,1)S(1)} %pad.4.meta, bf16[256,256]{1,0:T(8,128)(2,1)S(1)} %copy-done.5, f32[128,256]{1,0:T(8,128)S(1)} %copy-done.4, ...), custom_call_target="tpu_custom_call" | custom-call | tf_op jit(solution)/shard_map/rho_spectrum/pallas_call | solution.py:103
  33.1 3.8 %rho_pick.1.refs_0_ = bf16[16,3200]{1,0:T(8,128)(2,1)S(1)} custom-call(bf16[1024,256]{1,0:T(8,128)(2,1)S(1)} %get-tuple-element.19.spec, s32[1,3072]{1,0:T(1,128)S(1)} %get-tuple-element.33.gidx, bf16[16,128]{1,0:T(8,128)(2,1)S(1)} %pad.4.meta), custom_call_target="tpu_custom_call" | custom-call | tf_op jit(solution)/shard_map/rho_pick/pallas_call | solution.py:117
  37.2 6.8 %collective-permute-start.8 = (bf16[32,3200]{1,0:T(8,128)(2,1)S(1)}, bf16[32,3200]{1,0:T(8,128)(2,1)S(1)}, u32[]{:S(2)}, u32[]{:S(2)}) collective-permute-start(bf16[32,3200]{1,0:T(8,128)(2,1)S(1)} %join.5.refs_0_), channel_id=1, source_target_pairs={{0,37},{8,127},{32,69},{40,31},{64,101},{72,63},{96,5},{104,95},{4... | collective-permute-start | bytes 614408 | tf_op jit(solution)/shard_map/ppermute | solution.py:148
  44.0 3.1 %collective-permute-done.9.refs_1_ = bf16[32,3200]{1,0:T(8,128)(2,1)S(1)} collective-permute-done((bf16[32,3200]{1,0:T(8,128)(2,1)S(1)}, bf16[32,3200]{1,0:T(8,128)(2,1)S(1)}, u32[]{:S(2)}, u32[]{:S(2)}) %collective-permute-start.9) | collective-permute-done | bytes 204832 | tf_op jit(solution)/shard_map/ppermute | solution.py:148
  47.3 2.4 %collective-permute-start.11 = (bf16[64,3200]{1,0:T(8,128)(2,1)S(1)}, bf16[64,3200]{1,0:T(8,128)(2,1)S(1)}, u32[]{:S(2)}, u32[]{:S(2)}) collective-permute-start(bf16[64,3200]{1,0:T(8,128)(2,1)S(1)} %join.8.refs_0_), channel_id=1, source_target_pairs={{0,16},{8,24},{32,48},{40,56},{64,80},{72,88},{96,112},{104,120},{... | collective-permute-start | bytes 1228808 | tf_op jit(solution)/shard_map/ppermute | solution.py:148
  50.8 4.8 %collective-permute-start.1 = (bf16[32,3200]{1,0:T(8,128)(2,1)S(1)}, bf16[32,3200]{1,0:T(8,128)(2,1)S(1)}, u32[]{:S(2)}, u32[]{:S(2)}) collective-permute-start(bf16[32,3200]{1,0:T(8,128)(2,1)S(1)} %join.5.refs_0_), channel_id=1, source_target_pairs={{0,82},{8,90},{32,114},{40,122},{64,18},{72,26},{96,50},{104,58},{... | collective-permute-start | bytes 614408 | tf_op jit(solution)/shard_map/ppermute | solution.py:148
  55.6 9.1 %collective-permute-done.1.refs_1_.refs_4_ = bf16[32,3200]{1,0:T(8,128)(2,1)S(1)} collective-permute-done((bf16[32,3200]{1,0:T(8,128)(2,1)S(1)}, bf16[32,3200]{1,0:T(8,128)(2,1)S(1)}, u32[]{:S(2)}, u32[]{:S(2)}) %collective-permute-start.1) | collective-permute-done | bytes 204832 | tf_op jit(solution)/shard_map/ppermute | solution.py:148
  66.0 3.6 %collective-permute-start.15 = (bf16[256,3200]{1,0:T(8,128)(2,1)}, bf16[256,3200]{1,0:T(8,128)(2,1)S(1)}, u32[]{:S(2)}, u32[]{:S(2)}) collective-permute-start(bf16[256,3200]{1,0:T(8,128)(2,1)} %join.9.refs_0_), channel_id=1, source_target_pairs={{0,32},{8,104},{32,64},{40,8},{64,96},{72,40},{96,0},{104,72},{4,3... | collective-permute-start | bytes 4915208 | tf_op jit(solution)/shard_map/ppermute | solution.py:148
  70.4 1.8 %collective-permute-start.3 = (bf16[64,3200]{1,0:T(8,128)(2,1)}, bf16[64,3200]{1,0:T(8,128)(2,1)}, u32[]{:S(2)}, u32[]{:S(2)}) collective-permute-start(bf16[64,3200]{1,0:T(8,128)(2,1)} %join.6.refs_0_), channel_id=1, source_target_pairs={{0,16},{8,24},{32,48},{40,56},{64,80},{72,88},{96,112},{104,120},{... | collective-permute-start | bytes 1228808 | tf_op jit(solution)/shard_map/ppermute | solution.py:148
  72.2 4.5 %collective-permute-start.2 = (bf16[64,3200]{1,0:T(8,128)(2,1)}, bf16[64,3200]{1,0:T(8,128)(2,1)}, u32[]{:S(2)}, u32[]{:S(2)}) collective-permute-start(bf16[64,3200]{1,0:T(8,128)(2,1)} %join.6.refs_0_), channel_id=1, source_target_pairs={{0,2},{8,10},{32,34},{40,42},{64,66},{72,74},{96,98},{104,106},{4,... | collective-permute-start | bytes 1228808 | tf_op jit(solution)/shard_map/ppermute | solution.py:148
  76.6 1.5 collective-permute-start.14
  78.2 3.9 %collective-permute-done.4.refs_3_ = bf16[64,3200]{1,0:T(8,128)(2,1)S(1)} collective-permute-done((bf16[64,3200]{1,0:T(8,128)(2,1)}, bf16[64,3200]{1,0:T(8,128)(2,1)S(1)}, u32[]{:S(2)}, u32[]{:S(2)}) %collective-permute-start.4) | collective-permute-done | bytes 409632 | tf_op jit(solution)/shard_map/ppermute | solution.py:148
  82.8 7.8 %collective-permute-start.13 = (bf16[256,3200]{1,0:T(8,128)(2,1)}, bf16[256,3200]{1,0:T(8,128)(2,1)}, u32[]{:S(2)}, u32[]{:S(2)}) collective-permute-start(bf16[256,3200]{1,0:T(8,128)(2,1)} %join.9.refs_0_), channel_id=1, source_target_pairs={{0,1},{8,11},{32,33},{40,43},{64,65},{72,75},{96,97},{104,107},{4,... | collective-permute-start | bytes 4915208 | tf_op jit(solution)/shard_map/ppermute | solution.py:148
  92.3 1.4 join.7.refs_1_
  93.6 2.3 %weighted.3.left = bf16[512,384]{1,0:T(8,128)(2,1)S(1)} custom-call(s32[1]{0:T(128)} %bitcast.1.place, f32[1]{0:T(128)} %dynamic_slice.12.omega, bf16[256,3200]{1,0:T(8,128)(2,1)} %join.9.refs_0_, bf16[256,3200]{1,0:T(8,128)(2,1)S(1)} %join.7.refs_1_, f32[8,128]{1,0:T(8,128)S(1)} %broadcast_in_dim.24.refs_2_), custom_call_target="tpu_custom_call" | custom-call | tf_op jit(solution)/shard_map/weighted/pallas_call | solution.py:206
  96.0 14.6 %collective-permute-start.16 = (bf16[512,384]{1,0:T(8,128)(2,1)S(1)}, bf16[512,384]{1,0:T(8,128)(2,1)S(1)}, u32[]{:S(2)}, u32[]{:S(2)}) collective-permute-start(bf16[512,384]{1,0:T(8,128)(2,1)S(1)} %weighted.3.left), channel_id=1, source_target_pairs={{0,8},{8,0},{32,40},{40,32},{64,72},{72,64},{96,104},{104,96},{4,1... | collective-permute-start | bytes 1179656 | tf_op jit(solution)/shard_map/ppermute | solution.py:148
  110.6 1.3 collective-permute-done.16.left
  112.0 2.7 %collective-permute-start.5 = (bf16[256,3200]{1,0:T(8,128)(2,1)S(1)}, bf16[256,3200]{1,0:T(8,128)(2,1)S(1)}, u32[]{:S(2)}, u32[]{:S(2)}) collective-permute-start(bf16[256,3200]{1,0:T(8,128)(2,1)S(1)} %join.7.refs_1_), channel_id=1, source_target_pairs={{0,1},{8,11},{32,33},{40,43},{64,65},{72,75},{96,97},{104,107},{4,... | collective-permute-start | bytes 4915208 | tf_op jit(solution)/shard_map/ppermute | solution.py:148
  114.7 3.4 %partial_own.2 = (f32[384,3072]{1,0:T(8,128)S(1)}, f32[8,128]{1,0:T(8,128)S(1)}) custom-call(bf16[512,384]{1,0:T(8,128)(2,1)S(1)} %weighted.3.left, bf16[256,3200]{1,0:T(8,128)(2,1)} %join.9.refs_0_, bf16[256,3200]{1,0:T(8,128)(2,1)S(1)} %join.7.refs_1_, f32[8,128]{1,0:T(8,128)S(1)} %broadcast_in_dim.24.refs_2_), custom_call_target="tpu_custom_call" | custom-call | flops 1207959552 | bytes 12582912 | tf_op jit(solution)/shard_map/partial_own/pallas_call | solution.py:264
  118.2 3.4 %partial_other.2 = (f32[384,3072]{1,0:T(8,128)S(1)}, f32[8,128]{1,0:T(8,128)S(1)}) custom-call(bf16[512,384]{1,0:T(8,128)(2,1)S(1)} %collective-permute-done.16.left, bf16[256,3200]{1,0:T(8,128)(2,1)} %join.9.refs_0_, bf16[256,3200]{1,0:T(8,128)(2,1)S(1)} %join.7.refs_1_, f32[8,128]{1,0:T(8,128)S(1)} %get-tuple-element.21.refs_2_), custom_call_target="tpu_custom_call" | custom-call | flops 1207959552 | bytes 12582912 | tf_op jit(solution)/shard_map/partial_other/pallas_call | solution.py:264
  121.6 2.4 %weighted.4.left = bf16[768,384]{1,0:T(8,128)(2,1)S(1)} custom-call(s32[1]{0:T(128)} %bitcast.1.place, f32[1]{0:T(128)} %dynamic_slice.12.omega, bf16[256,3200]{1,0:T(8,128)(2,1)} %collective-permute-done.13.refs_0_, bf16[256,3200]{1,0:T(8,128)(2,1)S(1)} %collective-permute-done.14.refs_1_, bf16[256,3200]{1,0:T(8,128)(2,1)S(1)} %collective-permute-done.15.refs_2_, ...), custom_call_target="tpu_custom_call" | custom-call | tf_op jit(solution)/shard_map/weighted/pallas_call | solution.py:206
  124.0 4.9 %collective-permute-start.17 = (bf16[768,384]{1,0:T(8,128)(2,1)S(1)}, bf16[768,384]{1,0:T(8,128)(2,1)S(1)}, u32[]{:S(2)}, u32[]{:S(2)}) collective-permute-start(bf16[768,384]{1,0:T(8,128)(2,1)S(1)} %weighted.4.left), channel_id=1, source_target_pairs={{0,8},{8,0},{32,40},{40,32},{64,72},{72,64},{96,104},{104,96},{4,1... | collective-permute-start | bytes 1769480 | tf_op jit(solution)/shard_map/ppermute | solution.py:148
  128.9 4.1 %partial_own.3 = (f32[384,3072]{1,0:T(8,128)S(1)}, f32[8,128]{1,0:T(8,128)S(1)}) custom-call(bf16[768,384]{1,0:T(8,128)(2,1)S(1)} %weighted.4.left, bf16[256,3200]{1,0:T(8,128)(2,1)} %collective-permute-done.13.refs_0_, bf16[256,3200]{1,0:T(8,128)(2,1)S(1)} %collective-permute-done.14.refs_1_, ...), custom_call_target="tpu_custom_call", output_to_operand_aliasing={{0}: (4, {})} | custom-call | flops 1811939328 | bytes 14155776 | tf_op jit(solution)/shard_map/partial_own/pallas_call | solution.py:264
  133.0 4.1 %partial_other.3 = (f32[384,3072]{1,0:T(8,128)S(1)}, f32[8,128]{1,0:T(8,128)S(1)}) custom-call(bf16[768,384]{1,0:T(8,128)(2,1)S(1)} %collective-permute-done.17.left, bf16[256,3200]{1,0:T(8,128)(2,1)} %collective-permute-done.13.refs_0_, bf16[256,3200]{1,0:T(8,128)(2,1)S(1)} %collective-permute-done.14.refs_1_, ...), custom_call_target="tpu_custom_call", output_to_operand_aliasing={{0}: (4, {})} | custom-call | flops 1811939328 | bytes 14155776 | tf_op jit(solution)/shard_map/partial_other/pallas_call | solution.py:264
  138.1 6.8 %collective-permute-start.18 = (bf16[768,384]{1,0:T(8,128)(2,1)S(1)}, bf16[768,384]{1,0:T(8,128)(2,1)S(1)}, u32[]{:S(2)}, u32[]{:S(2)}) collective-permute-start(bf16[768,384]{1,0:T(8,128)(2,1)S(1)} %weighted.5.left), channel_id=1, source_target_pairs={{0,8},{8,0},{32,40},{40,32},{64,72},{72,64},{96,104},{104,96},{4,1... | collective-permute-start | bytes 1769480 | tf_op jit(solution)/shard_map/ppermute | solution.py:148
  144.9 1.6 %collective-permute-done.18.left = bf16[768,384]{1,0:T(8,128)(2,1)S(1)} collective-permute-done((bf16[768,384]{1,0:T(8,128)(2,1)S(1)}, bf16[768,384]{1,0:T(8,128)(2,1)S(1)}, u32[]{:S(2)}, u32[]{:S(2)}) %collective-permute-start.18) | collective-permute-done | bytes 589856 | tf_op jit(solution)/shard_map/ppermute | solution.py:148
  146.6 1.4 other_rows.2
  147.9 1.3 other_rows.3
  149.9 2.7 %own_rows.2.refs_6_ = f32[384,6144]{1,0:T(8,128)} custom-call(s32[1]{0:T(128)} %bitcast.core, bf16[768,384]{1,0:T(8,128)(2,1)S(1)} %weighted.5.left, bf16[256,3200]{1,0:T(8,128)(2,1)S(1)} %collective-permute-done.5.refs_0_, bf16[256,3200]{1,0:T(8,128)(2,1)S(1)} %collective-permute-done.6.refs_1_, bf16[256,3200]{1,0:T(8,128)(2,1)S(1)} %collective-permute-done.7.refs_2_, ...), custom_call_target="tpu_custom_call" | custom-call | flops 905969664 | bytes 7077888 | tf_op jit(solution)/shard_map/own_rows/pallas_call | solution.py:308
  153.9 4.2 %own_rows.3 = f32[384,6144]{1,0:T(8,128)} custom-call(s32[1]{0:T(128)} %bitcast.core, bf16[768,384]{1,0:T(8,128)(2,1)S(1)} %weighted.5.left, bf16[256,3200]{1,0:T(8,128)(2,1)S(1)} %collective-permute-done.5.refs_0_, bf16[256,3200]{1,0:T(8,128)(2,1)S(1)} %collective-permute-done.6.refs_1_, ...), custom_call_target="tpu_custom_call", output_to_operand_aliasing={{}: (8, {})} | custom-call | flops 905969664 | bytes 7077888 | tf_op jit(solution)/shard_map/own_rows/pallas_call | solution.py:308
  (70 shorter events, 13.3 us)
Async XLA Ops:
  0.0 23.5 %copy-start.2 = (bf16[1536,128]{1,0:T(8,128)(2,1)S(1)}, bf16[1536,128]{1,0:T(8,128)(2,1)}, u32[]{:S(2)}) copy-start(bf16[1536,128]{1,0:T(8,128)(2,1)} %constant.42.clone.second) | copy-start | bytes 1179652
  0.0 23.5 %copy-start.3 = (f32[128,256]{1,0:T(8,128)S(1)}, f32[128,256]{1,0:T(8,128)}, u32[]{:S(2)}) copy-start(f32[128,256]{1,0:T(8,128)} %constant.41.clone.tsin) | copy-start | bytes 393220
  0.0 23.5 %copy-start.4 = (f32[128,256]{1,0:T(8,128)S(1)}, f32[128,256]{1,0:T(8,128)}, u32[]{:S(2)}) copy-start(f32[128,256]{1,0:T(8,128)} %constant.40.clone.tcos) | copy-start | bytes 393220
  0.0 23.5 %copy-start.5 = (bf16[256,256]{1,0:T(8,128)(2,1)S(1)}, bf16[256,256]{1,0:T(8,128)(2,1)}, u32[]{:S(2)}) copy-start(bf16[256,256]{1,0:T(8,128)(2,1)} %constant.39.clone.first) | copy-start | bytes 393220
  0.0 12.2 %copy-start.8 = (f32[64]{0:T(128)S(1)}, f32[64]{0:T(128)}, u32[]{:S(2)}) copy-start(f32[64]{0:T(128)} %param.14) | copy-start | bytes 772
  0.0 12.2 %copy-start.7 = (f32[4]{0:T(128)S(1)}, f32[4]{0:T(128)}, u32[]{:S(2)}) copy-start(f32[4]{0:T(128)} %param.13) | copy-start | bytes 52
  0.0 12.4 %copy-start.9 = (s32[4]{0:T(128)S(1)}, s32[4]{0:T(128)}, u32[]{:S(2)}) copy-start(s32[4]{0:T(128)} %param.15) | copy-start | bytes 52
  0.1 12.7 %copy-start.6 = (s32[6144]{0:T(1024)S(1)}, s32[6144]{0:T(1024)}, u32[]{:S(2)}) copy-start(s32[6144]{0:T(1024)} %param.17) | copy-start | bytes 73732
  2.7 20.8 %all-to-all-start = ((bf16[16,8,8,256]{3,2,1,0:T(8,128)(2,1)}), bf16[16,8,8,256]{3,2,1,0:T(8,128)(2,1)S(1)}, u32[]{:S(2)}, u32[]{:S(2)}) async-start(bf16[16,8,8,256]{3,2,1,0:T(8,128)(2,1)} %pad_maximum_fusion), calls=%async_computation | async-start | bytes 1048576 | tf_op jit(solution)/shard_map/all_to_all | solution.py:361
  31.9 5.1 %collective-permute-start = (bf16[16,3200]{1,0:T(8,128)(2,1)S(1)}, bf16[16,3200]{1,0:T(8,128)(2,1)S(1)}, u32[]{:S(2)}, u32[]{:S(2)}) collective-permute-start(bf16[16,3200]{1,0:T(8,128)(2,1)S(1)} %get-tuple-element.20), channel_id=1, source_target_pairs={{0,8},{8,0},{32,40},{40,32},{64,72},{72,64},{96,104},{104,96},{4,1... | collective-permute-start | bytes 307208 | tf_op jit(solution)/shard_map/ppermute | solution.py:148
  37.0 10.1 %collective-permute-start.9 = (bf16[32,3200]{1,0:T(8,128)(2,1)S(1)}, bf16[32,3200]{1,0:T(8,128)(2,1)S(1)}, u32[]{:S(2)}, u32[]{:S(2)}) collective-permute-start(bf16[32,3200]{1,0:T(8,128)(2,1)S(1)} %join.5.refs_0_), channel_id=1, source_target_pairs={{0,119},{8,45},{32,23},{40,77},{64,55},{72,109},{96,87},{104,13},{... | collective-permute-start | bytes 614408 | tf_op jit(solution)/shard_map/ppermute | solution.py:148
  37.2 9.9 %collective-permute-start.8 = (bf16[32,3200]{1,0:T(8,128)(2,1)S(1)}, bf16[32,3200]{1,0:T(8,128)(2,1)S(1)}, u32[]{:S(2)}, u32[]{:S(2)}) collective-permute-start(bf16[32,3200]{1,0:T(8,128)(2,1)S(1)} %join.5.refs_0_), channel_id=1, source_target_pairs={{0,37},{8,127},{32,69},{40,31},{64,101},{72,63},{96,5},{104,95},{4... | collective-permute-start | bytes 614408 | tf_op jit(solution)/shard_map/ppermute | solution.py:148
  47.2 43.5 %copy-start.10 = (f32[8]{0:T(128)S(1)}, f32[8]{0:T(128)}, u32[]{:S(2)}) copy-start(f32[8]{0:T(128)} %param.16) | copy-start | bytes 100
  47.2 17.5 %collective-permute-start.12 = (bf16[64,3200]{1,0:T(8,128)(2,1)S(1)}, bf16[64,3200]{1,0:T(8,128)(2,1)S(1)}, u32[]{:S(2)}, u32[]{:S(2)}) collective-permute-start(bf16[64,3200]{1,0:T(8,128)(2,1)S(1)} %join.8.refs_0_), channel_id=1, source_target_pairs={{0,64},{8,72},{32,96},{40,104},{64,0},{72,8},{96,32},{104,40},{4,6... | collective-permute-start | bytes 1228808 | tf_op jit(solution)/shard_map/ppermute | solution.py:148
  47.3 17.4 %collective-permute-start.11 = (bf16[64,3200]{1,0:T(8,128)(2,1)S(1)}, bf16[64,3200]{1,0:T(8,128)(2,1)S(1)}, u32[]{:S(2)}, u32[]{:S(2)}) collective-permute-start(bf16[64,3200]{1,0:T(8,128)(2,1)S(1)} %join.8.refs_0_), channel_id=1, source_target_pairs={{0,16},{8,24},{32,48},{40,56},{64,80},{72,88},{96,112},{104,120},{... | collective-permute-start | bytes 1228808 | tf_op jit(solution)/shard_map/ppermute | solution.py:148
  49.6 15.1 %collective-permute-start.10 = (bf16[64,3200]{1,0:T(8,128)(2,1)S(1)}, bf16[64,3200]{1,0:T(8,128)(2,1)S(1)}, u32[]{:S(2)}, u32[]{:S(2)}) collective-permute-start(bf16[64,3200]{1,0:T(8,128)(2,1)S(1)} %join.8.refs_0_), channel_id=1, source_target_pairs={{0,2},{8,10},{32,34},{40,42},{64,66},{72,74},{96,98},{104,106},{4,... | collective-permute-start | bytes 1228808 | tf_op jit(solution)/shard_map/ppermute | solution.py:148
  50.8 13.9 %collective-permute-start.1 = (bf16[32,3200]{1,0:T(8,128)(2,1)S(1)}, bf16[32,3200]{1,0:T(8,128)(2,1)S(1)}, u32[]{:S(2)}, u32[]{:S(2)}) collective-permute-start(bf16[32,3200]{1,0:T(8,128)(2,1)S(1)} %join.5.refs_0_), channel_id=1, source_target_pairs={{0,82},{8,90},{32,114},{40,122},{64,18},{72,26},{96,50},{104,58},{... | collective-permute-start | bytes 614408 | tf_op jit(solution)/shard_map/ppermute | solution.py:148
  66.0 46.0 %collective-permute-start.15 = (bf16[256,3200]{1,0:T(8,128)(2,1)}, bf16[256,3200]{1,0:T(8,128)(2,1)S(1)}, u32[]{:S(2)}, u32[]{:S(2)}) collective-permute-start(bf16[256,3200]{1,0:T(8,128)(2,1)} %join.9.refs_0_), channel_id=1, source_target_pairs={{0,32},{8,104},{32,64},{40,8},{64,96},{72,40},{96,0},{104,72},{4,3... | collective-permute-start | bytes 4915208 | tf_op jit(solution)/shard_map/ppermute | solution.py:148
  70.4 11.6 %collective-permute-start.4 = (bf16[64,3200]{1,0:T(8,128)(2,1)}, bf16[64,3200]{1,0:T(8,128)(2,1)S(1)}, u32[]{:S(2)}, u32[]{:S(2)}) collective-permute-start(bf16[64,3200]{1,0:T(8,128)(2,1)} %join.6.refs_0_), channel_id=1, source_target_pairs={{0,64},{8,72},{32,96},{40,104},{64,0},{72,8},{96,32},{104,40},{4,6... | collective-permute-start | bytes 1228808 | tf_op jit(solution)/shard_map/ppermute | solution.py:148
  70.4 20.9 %collective-permute-start.3 = (bf16[64,3200]{1,0:T(8,128)(2,1)}, bf16[64,3200]{1,0:T(8,128)(2,1)}, u32[]{:S(2)}, u32[]{:S(2)}) collective-permute-start(bf16[64,3200]{1,0:T(8,128)(2,1)} %join.6.refs_0_), channel_id=1, source_target_pairs={{0,16},{8,24},{32,48},{40,56},{64,80},{72,88},{96,112},{104,120},{... | collective-permute-start | bytes 1228808 | tf_op jit(solution)/shard_map/ppermute | solution.py:148
  72.2 19.1 %collective-permute-start.2 = (bf16[64,3200]{1,0:T(8,128)(2,1)}, bf16[64,3200]{1,0:T(8,128)(2,1)}, u32[]{:S(2)}, u32[]{:S(2)}) collective-permute-start(bf16[64,3200]{1,0:T(8,128)(2,1)} %join.6.refs_0_), channel_id=1, source_target_pairs={{0,2},{8,10},{32,34},{40,42},{64,66},{72,74},{96,98},{104,106},{4,... | collective-permute-start | bytes 1228808 | tf_op jit(solution)/shard_map/ppermute | solution.py:148
  76.6 45.0 %collective-permute-start.14 = (bf16[256,3200]{1,0:T(8,128)(2,1)}, bf16[256,3200]{1,0:T(8,128)(2,1)S(1)}, u32[]{:S(2)}, u32[]{:S(2)}) collective-permute-start(bf16[256,3200]{1,0:T(8,128)(2,1)} %join.9.refs_0_), channel_id=1, source_target_pairs={{0,4},{8,28},{32,36},{40,60},{64,68},{72,92},{96,100},{104,124},{4... | collective-permute-start | bytes 4915208 | tf_op jit(solution)/shard_map/ppermute | solution.py:148
  82.8 38.9 %collective-permute-start.13 = (bf16[256,3200]{1,0:T(8,128)(2,1)}, bf16[256,3200]{1,0:T(8,128)(2,1)}, u32[]{:S(2)}, u32[]{:S(2)}) collective-permute-start(bf16[256,3200]{1,0:T(8,128)(2,1)} %join.9.refs_0_), channel_id=1, source_target_pairs={{0,1},{8,11},{32,33},{40,43},{64,65},{72,75},{96,97},{104,107},{4,... | collective-permute-start | bytes 4915208 | tf_op jit(solution)/shard_map/ppermute | solution.py:148
  91.3 1.0 copy-start.1
  96.0 16.0 %collective-permute-start.16 = (bf16[512,384]{1,0:T(8,128)(2,1)S(1)}, bf16[512,384]{1,0:T(8,128)(2,1)S(1)}, u32[]{:S(2)}, u32[]{:S(2)}) collective-permute-start(bf16[512,384]{1,0:T(8,128)(2,1)S(1)} %weighted.3.left), channel_id=1, source_target_pairs={{0,8},{8,0},{32,40},{40,32},{64,72},{72,64},{96,104},{104,96},{4,1... | collective-permute-start | bytes 1179656 | tf_op jit(solution)/shard_map/ppermute | solution.py:148
  110.6 26.6 %collective-permute-start.7 = (bf16[256,3200]{1,0:T(8,128)(2,1)S(1)}, bf16[256,3200]{1,0:T(8,128)(2,1)S(1)}, u32[]{:S(2)}, u32[]{:S(2)}) collective-permute-start(bf16[256,3200]{1,0:T(8,128)(2,1)S(1)} %join.7.refs_1_), channel_id=1, source_target_pairs={{0,32},{8,104},{32,64},{40,8},{64,96},{72,40},{96,0},{104,72},{4,3... | collective-permute-start | bytes 4915208 | tf_op jit(solution)/shard_map/ppermute | solution.py:148
  111.9 25.2 %collective-permute-start.6 = (bf16[256,3200]{1,0:T(8,128)(2,1)S(1)}, bf16[256,3200]{1,0:T(8,128)(2,1)S(1)}, u32[]{:S(2)}, u32[]{:S(2)}) collective-permute-start(bf16[256,3200]{1,0:T(8,128)(2,1)S(1)} %join.7.refs_1_), channel_id=1, source_target_pairs={{0,4},{8,28},{32,36},{40,60},{64,68},{72,92},{96,100},{104,124},{4... | collective-permute-start | bytes 4915208 | tf_op jit(solution)/shard_map/ppermute | solution.py:148
  112.0 25.2 %collective-permute-start.5 = (bf16[256,3200]{1,0:T(8,128)(2,1)S(1)}, bf16[256,3200]{1,0:T(8,128)(2,1)S(1)}, u32[]{:S(2)}, u32[]{:S(2)}) collective-permute-start(bf16[256,3200]{1,0:T(8,128)(2,1)S(1)} %join.7.refs_1_), channel_id=1, source_target_pairs={{0,1},{8,11},{32,33},{40,43},{64,65},{72,75},{96,97},{104,107},{4,... | collective-permute-start | bytes 4915208 | tf_op jit(solution)/shard_map/ppermute | solution.py:148
  124.0 9.0 %collective-permute-start.17 = (bf16[768,384]{1,0:T(8,128)(2,1)S(1)}, bf16[768,384]{1,0:T(8,128)(2,1)S(1)}, u32[]{:S(2)}, u32[]{:S(2)}) collective-permute-start(bf16[768,384]{1,0:T(8,128)(2,1)S(1)} %weighted.4.left), channel_id=1, source_target_pairs={{0,8},{8,0},{32,40},{40,32},{64,72},{72,64},{96,104},{104,96},{4,1... | collective-permute-start | bytes 1769480 | tf_op jit(solution)/shard_map/ppermute | solution.py:148
  138.1 8.4 %collective-permute-start.18 = (bf16[768,384]{1,0:T(8,128)(2,1)S(1)}, bf16[768,384]{1,0:T(8,128)(2,1)S(1)}, u32[]{:S(2)}, u32[]{:S(2)}) collective-permute-start(bf16[768,384]{1,0:T(8,128)(2,1)S(1)} %weighted.5.left), channel_id=1, source_target_pairs={{0,8},{8,0},{32,40},{40,32},{64,72},{72,64},{96,104},{104,96},{4,1... | collective-permute-start | bytes 1769480 | tf_op jit(solution)/shard_map/ppermute | solution.py:148
  149.3 3.3 %collective-permute-start.20 = (bf16[384,1536]{1,0:T(8,128)(2,1)S(1)}, bf16[384,1536]{1,0:T(8,128)(2,1)S(1)}, u32[]{:S(2)}, u32[]{:S(2)}) collective-permute-start(bf16[384,1536]{1,0:T(8,128)(2,1)S(1)} %get-tuple-element.31), channel_id=1, source_target_pairs={{0,8},{8,0},{32,40},{40,32},{64,72},{72,64},{96,104},{104,96},{4,1... | collective-permute-start | bytes 3538952 | tf_op jit(solution)/shard_map/ppermute | solution.py:148
  149.7 4.2 %collective-permute-start.19 = (bf16[384,1536]{1,0:T(8,128)(2,1)S(1)}, bf16[384,1536]{1,0:T(8,128)(2,1)S(1)}, u32[]{:S(2)}, u32[]{:S(2)}) collective-permute-start(bf16[384,1536]{1,0:T(8,128)(2,1)S(1)} %get-tuple-element.29), channel_id=1, source_target_pairs={{0,8},{8,0},{32,40},{40,32},{64,72},{72,64},{96,104},{104,96},{4,1... | collective-permute-start | bytes 3538952 | tf_op jit(solution)/shard_map/ppermute | solution.py:148
  (1 other events, 0.8 us)

commit v6 on v4

--- a/solution.py
+++ b/solution.py
@@ -42,39 +42,56 @@
 
 def dft_constants():
     k1 = np.arange(NA)[:, None]
-    ang = 2.0 * math.pi * ((k1 * np.arange(NA)[None, :]) % NA) / NA
-    fh, fl = split_bf16(np.concatenate([np.cos(ang), np.sin(ang)], 0))
-    first = np.concatenate([fh, fl], 1)
+    chip, a = np.arange(8)[:, None], np.arange(8)[None, :]
+    kinds = [((chip * 2 + kind) * 8 + a).reshape(64) for kind in range(2)]
+    first = []
+    for core in range(2):
+        order = np.concatenate([kinds[core], kinds[1 - core]])
+        ang = 2.0 * math.pi * ((k1 * order[None, :]) % NA) / NA
+        fh, fl = split_bf16(np.concatenate([np.cos(ang), np.sin(ang)], 0))
+        first.append(np.concatenate([fh, fl], 1))
     tw = 2.0 * math.pi * ((k1 * np.arange(NB)[None, :]) % N) / N
     norm = math.sqrt(2.0 / N)
     tcos = (np.cos(tw) * norm).astype(np.float32)
     tsin = (np.sin(tw) * norm).astype(np.float32)
     b2 = 2.0 * math.pi * ((np.arange(NB)[:, None] * np.arange(NA)[None, :]) % NB) / NB
     sh, sl = split_bf16(np.concatenate([np.cos(b2), -np.sin(b2)], 0))
-    second = np.concatenate([sh, sl, sh], 0)
-    return first, tcos, tsin, second
-
-
-def transform(psi, first, tcos, tsin, second, spec):
-    bands = [psi[:, i].astype(jnp.float32).reshape(NA, NB) for i in range(8)]
+    return np.stack(first), tcos, tsin, np.concatenate([sh, sl], 1)
+
+
+def transform(core, mine, others, first, tcos, tsin, second, spec, high, low):
+    def band(row):
+        both = jnp.concatenate([mine[:, row], others[:, row]], 0)
+        return both.astype(jnp.float32).reshape(NA, NB)
+
+    con = [band(core[0] * 4 + i) for i in range(4)]
     ca = tcos[...]
     sa = tsin[...]
-    for p in range(PAIRS):
-        d = (bands[p // 4] * bands[4 + p % 4]).astype(jnp.bfloat16)
-        y = jnp.dot(first[...], jnp.concatenate([d, d], 0), preferred_element_type=jnp.float32)
-        a, b = y[:NA], y[NA:]
-        uv = jnp.concatenate([a * ca - b * sa, a * sa + b * ca], 1)
-        hi = uv.astype(jnp.bfloat16)
-        lo = (uv - hi.astype(jnp.float32)).astype(jnp.bfloat16)
-        x = jnp.dot(
-            jnp.concatenate([hi, hi, lo], 1), second[...], preferred_element_type=jnp.float32
-        ).astype(jnp.bfloat16)
-        spec[p * 64 : p * 64 + 64, 0:128] = x[:64]
-        spec[p * 64 : p * 64 + 64, 128:256] = x[64:]
+    f = first[core[0]]
+    for v in range(4):
+        val = band(8 + v)
+        for c in range(4):
+            d = (val * con[c]).astype(jnp.bfloat16)
+            y = jnp.dot(f, jnp.concatenate([d, d], 0), preferred_element_type=jnp.float32)
+            a, b = y[:NA], y[NA:]
+            uv = jnp.concatenate([a * ca - b * sa, a * sa + b * ca], 1)
+            hi = uv.astype(jnp.bfloat16)
+            at = slice((v * 4 + c) * NA, (v * 4 + c + 1) * NA)
+            high[at, :] = hi
+            low[at, :] = (uv - hi.astype(jnp.float32)).astype(jnp.bfloat16)
+    for n in range(4):
+        at = slice(n * 512, n * 512 + 512)
+        y = jnp.dot(high[at, :], second[...], preferred_element_type=jnp.float32)
+        z = jnp.dot(low[at, :], second[:, :NA], preferred_element_type=jnp.float32)
+        x = (y[:, :NA] + (y[:, NA:] + z)).astype(jnp.bfloat16)
+        for i in range(4):
+            p = n * 4 + i
+            spec[p * 64 : p * 64 + 64, 0:128] = x[i * NA : i * NA + 64]
+            spec[p * 64 : p * 64 + 64, 128:256] = x[i * NA + 64 : i * NA + NA]
 
 
 def pick(spec, gidx, meta, out):
-    width = 256
+    width = 1024
 
     def step(i, carry):
         at = pl.ds(pl.multiple_of(i * width, width), width)
@@ -94,23 +111,24 @@
     out[:, HALF:WIDE] = meta[...]
 
 
-def transform_kernel(psi, gidx, meta, first, tcos, tsin, second, spec, out):
-    transform(psi, first, tcos, tsin, second, spec)
+def transform_kernel(core, mine, others, gidx, meta, first, tcos, tsin, second, spec, out, high, low):
+    transform(core, mine, others, first, tcos, tsin, second, spec, high, low)
     pick(spec, gidx, meta, out)
 
 
-def rho_spectrum(psi, gidx, meta):
+def rho_spectrum(core, mine, others, gidx, meta):
     return pl.pallas_call(
         transform_kernel,
         out_shape=[
             jax.ShapeDtypeStruct((PAIRS * 64, 256), jnp.bfloat16),
             jax.ShapeDtypeStruct((PAIRS, WIDE), jnp.bfloat16),
         ],
-        in_specs=[VM] * 7,
+        in_specs=[SM] + [VM] * 8,
         out_specs=[VM] * 2,
+        scratch_shapes=[pltpu.VMEM((PAIRS * NA, 2 * NB), jnp.bfloat16)] * 2,
         compiler_params=PARAMS,
         name="rho_spectrum",
-    )(psi, gidx, meta, *(jnp.asarray(c) for c in dft_constants()))
+    )(core, mine, others, gidx, meta, *(jnp.asarray(c) for c in dft_constants()))
 
 
 def rho_pick(spec, gidx, meta):
@@ -290,50 +308,41 @@
     )(left, *pieces, *before, tie)
 
 
-def own_kernel(names, core, left, *refs):
+def own_kernel(names, start, core, left, *refs):
     pieces = refs[: len(names)]
-    before, out, tie, wide, sem = refs[len(names) :]
+    before, _, out, tie, wide, sem = refs[len(names) :]
     tie[...] = jnp.zeros_like(tie)
-
-    def copies(i):
-        slot = lax.rem(i, 2)
-        return [
-            pltpu.make_async_copy(
-                wide.at[slot, :, pl.ds(j * ROWS, ROWS)],
-                out.at[:, pl.ds(pl.multiple_of(((i * 2 + j) * 2 + core[0]) * ROWS, LANES), ROWS)],
-                sem.at[slot, j],
+    copies = []
+    for i in range(2):
+        cols = slice(start + i * CHUNK, start + (i + 1) * CHUNK)
+        wide[:, i * CHUNK : (i + 1) * CHUNK] = product(names, False, left, pieces, cols) + before[:, cols]
+        for j in (2 * i, 2 * i + 1):
+            block = (start // ROWS + j) * 2 + core[0]
+            copies.append(
+                pltpu.make_async_copy(
+                    wide.at[:, pl.ds(j * ROWS, ROWS)],
+                    out.at[:, pl.ds(pl.multiple_of(block * ROWS, LANES), ROWS)],
+                    sem.at[j],
+                )
             )
-            for j in range(2)
-        ]
-
-    def step(i, carry):
-        @pl.when(i >= 2)
-        def _():
-            for copy in copies(i - 2):
-                copy.wait()
-
-        wide[lax.rem(i, 2)] = product(names, False, left, pieces, chunk(i)) + before[:, chunk(i)]
-        for copy in copies(i):
-            copy.start()
-        return carry
-
-    lax.fori_loop(0, 4, step, 0)
-    for i in (2, 3):
-        for copy in copies(i):
-            copy.wait()
-
-
-def own_rows(names, core, left, pieces, before):
-    return pl.pallas_call(
-        functools.partial(own_kernel, names),
+            copies[-1].start()
+    for copy in copies:
+        copy.wait()
+
+
+def own_rows(names, start, core, left, pieces, before, after):
+    grows = after.shape == (ROWS, NG)
+    return pl.pallas_call(
+        functools.partial(own_kernel, names, start),
         out_shape=[jax.ShapeDtypeStruct((ROWS, NG), jnp.float32), TIE],
-        in_specs=[SM, VM] + [VM] * (len(names) + 1),
+        in_specs=[SM, VM] + [VM] * (len(names) + 1) + [HBM if grows else VM],
         out_specs=[HBM, VM],
-        scratch_shapes=[pltpu.VMEM((2, ROWS, CHUNK), jnp.float32), pltpu.SemaphoreType.DMA((2, 2))],
-        compiler_params=PARAMS,
-        cost_estimate=cost(names, HALF),
+        scratch_shapes=[pltpu.VMEM((ROWS, HALF // 2), jnp.float32), pltpu.SemaphoreType.DMA((4,))],
+        input_output_aliases={3 + len(names): 0} if grows else {},
+        compiler_params=PARAMS,
+        cost_estimate=cost(names, HALF // 2),
         name="own_rows",
-    )(core, left, *pieces, before)
+    )(core, left, *pieces, before, after)
 
 
 def other_kernel(names, start, left, *refs):
@@ -397,9 +406,13 @@
     ga = lax.axis_index("ga")
     ba = lax.axis_index("ba")
     core = lax.rem(ga, 2).astype(jnp.int32)
-    con = psi_con.reshape(16, 4, 8, NB)
-    val = jnp.broadcast_to(psi_val.reshape(1, 4, 8, NB), (16, 4, 8, NB))
-    psi = lax.all_to_all(jnp.concatenate([val, con], 1), "ga", 0, 0, tiled=True)
+    con = psi_con.reshape(8, 8, 8, NB)
+    val = jnp.broadcast_to(psi_val.reshape(1, 4, 8, NB), (8, 4, 8, NB))
+    kinds = [[2 * i + c for i in range(8)] for c in range(2)]
+    psi = lax.all_to_all(
+        jnp.concatenate([con, val], 1), "ga", 0, 0, tiled=True, axis_index_groups=kinds
+    )
+    psi_other = send(psi, core_pairs())
 
     delta = (lax.dynamic_slice(e_con, (ga * 4,), (4,))[None, :] - e_val[:, None]).reshape(PAIRS)
     taken = jnp.broadcast_to(occ.astype(jnp.float32)[:, None], (4, 4)).reshape(PAIRS)
@@ -412,7 +425,7 @@
     halves = g_index.reshape(8, 2, ROWS).transpose(1, 0, 2).reshape(2, HALF)
     kept = lax.dynamic_slice(halves, (core, 0), (1, HALF))
     given = lax.dynamic_slice(halves, (1 - core, 0), (1, HALF))
-    spec, give = rho_spectrum(psi, given, meta)
+    spec, give = rho_spectrum(core.reshape(1), psi, psi_other, given, meta)
     got = send(give, core_pairs())
     keep = rho_pick(spec, kept, meta)
 
@@ -432,8 +445,9 @@
         if names is not groups[-1]:
             own, tie = partial_rows(names, False, left, pieces, own, tie)
             other, tie = partial_rows(names, True, mirror, pieces, other, tie)
-    out, tie = own_rows(names, core, left, pieces, own)
+    out, tie = own_rows(names, 0, core, left, pieces, own, tie)
     rows = [send(other_rows(names, s, mirror, pieces, other, tie), core_pairs()) for s in (0, HALF // 2)]
+    out, _ = own_rows(names, HALF // 2, core, left, pieces, own, out)
     return finish(core, rows, out)[None]
 
 

time: 142 us -> 135 us (0.951)
  waiting for transfers between devices: 51.8 us -> 47.3 us
  Pallas kernels: 43.5 us -> 39.5 us
  starting transfers between devices: 39.1 us -> 40.7 us
    pallas_call x1, Pallas kernels: 8.36 us -> 4.37 us  [rho_spectrum(): pl.pallas_call(transform_kernel, out_shape=[jax.ShapeDtypeStruct((PAIRS *...]
    ppermute x18 -> x19, starting transfers between devices: 29.7 us -> 32.2 us  [send(): return lax.ppermute(a, ('ga', 'ba'), pairs)]
    ppermute x18 -> x19, waiting for transfers between devices: 41.2 us -> 38.8 us  [send(): return lax.ppermute(a, ('ga', 'ba'), pairs)]
    all_to_all x1, waiting for transfers between devices: 10.7 us -> 8.52 us  [on_device(): lax.all_to_all(jnp.concatenate([con, val], 1), 'ga', 0, 0, tiled=True, ax...]
    pallas_call x1 -> x2, Pallas kernels: 4.11 us -> 5.91 us  [own_rows(): pl.pallas_call(functools.partial(own_kernel, names, start), out_shape=[ja...]
    pallas_call x1, Pallas kernels: 3.84 us -> 2.28 us  [rho_pick(): pl.pallas_call(pick, out_shape=jax.ShapeDtypeStruct((PAIRS, WIDE), jnp.bf...]
  transfers between devices with their start and end apart: 19 -> 20, of which waited for: 9 -> 8; matrix products, arithmetic and copies ran while one was open for 1% -> 1% of each run, Pallas kernels for 21% -> 22%
where the time goes in v6:
time: 135 us; the launch traced here: 134 us
  waiting for transfers between devices  47.3 us (35%)
  starting transfers between devices  40.7 us (30%)
  Pallas kernels  39.5 us (29%)
  local copies, waits for them, and re-layouts  5.5 us (4%)
    ppermute x19, waiting for transfers between devices, send(): return lax.ppermute(a, ('ga', 'ba'), pairs)  38.8 us
    ppermute x19, starting transfers between devices, send(): return lax.ppermute(a, ('ga', 'ba'), pairs)  32.2 us
    pallas_call x4, Pallas kernels, partial_rows(): pl.pallas_call(functools.partial(partial_kernel, names, other), out_shape...  15.1 us
    all_to_all x1, waiting for transfers between devices, on_device(): lax.all_to_all(jnp.concatenate([con, val], 1), 'ga', 0, 0, tiled=True, ax...  8.52 us
    all_to_all x1, starting transfers between devices, on_device(): lax.all_to_all(jnp.concatenate([con, val], 1), 'ga', 0, 0, tiled=True, ax...  8.49 us
    pallas_call x2, Pallas kernels, own_rows(): pl.pallas_call(functools.partial(own_kernel, names, start), out_shape=[ja...  5.91 us
    pallas_call x3, Pallas kernels, weighted(): pl.pallas_call(weighted_kernel, out_shape=jax.ShapeDtypeStruct((256 * len...  5.44 us
    unnamed x24, local copies, waits for them, and re-layouts  4.44 us
  transfers between devices with their start and end apart: 20, of which 8 were waited for; matrix products, arithmetic and copies ran while one was open for 1% of the time, Pallas kernels for 22%

profile of v6, /device:TPU:1, one launch (start us, length us, event | category | flops | bytes accessed | tf_op | source)
XLA Modules:
  0.0 134.4 jit_solution(11272049861738990959)
XLA Ops:
  2.7 8.5 %all-to-all-start = ((bf16[8,12,8,256]{3,2,1,0:T(8,128)(2,1)}), bf16[8,12,8,256]{3,2,1,0:T(8,128)(2,1)S(1)}, u32[]{:S(2)}, u32[]{:S(2)}) async-start(bf16[8,12,8,256]{3,2,1,0:T(8,128)(2,1)} %pad_maximum_fusion), calls=%async_computation | async-start | bytes 786432 | tf_op jit(solution)/shard_map/all_to_all | solution.py:412
  11.6 8.5 %all-to-all-done.mine = bf16[8,12,8,256]{3,2,1,0:T(8,128)(2,1)S(1)} async-done(((bf16[8,12,8,256]{3,2,1,0:T(8,128)(2,1)}), bf16[8,12,8,256]{3,2,1,0:T(8,128)(2,1)S(1)}, u32[]{:S(2)}, u32[]{:S(2)}) %all-to-all-start) | async-done | bytes 393248 | tf_op jit(solution)/shard_map/all_to_all | solution.py:412
  20.1 2.2 %collective-permute-start = (bf16[8,12,8,256]{3,2,1,0:T(8,128)(2,1)S(1)}, bf16[8,12,8,256]{3,2,1,0:T(8,128)(2,1)S(1)}, u32[]{:S(2)}, u32[]{:S(2)}) collective-permute-start(bf16[8,12,8,256]{3,2,1,0:T(8,128)(2,1)S(1)} %all-to-all-done.mine), channel_id=1, source_target_pairs={{0,8},{8,0},{32,40},{40,32},{64,72},{72,64},{96,104},{104,96},{4,1... | collective-permute-start | bytes 1179656 | tf_op jit(solution)/shard_map/ppermute | solution.py:166
  23.6 4.4 %rho_spectrum.1 = (bf16[1024,256]{1,0:T(8,128)(2,1)S(1)}, bf16[16,3200]{1,0:T(8,128)(2,1)S(1)}) custom-call(s32[1]{0:T(128)} %bitcast.core, bf16[8,12,8,256]{3,2,1,0:T(8,128)(2,1)S(1)} %all-to-all-done.mine, bf16[8,12,8,256]{3,2,1,0:T(8,128)(2,1)S(1)} %collective-permute-done.others, s32[1,3072]{1,0:T(1,128)S(1)} %get-tuple-element.36.gidx, ...), custom_call_target="tpu_custom_call" | custom-call | tf_op jit(solution)/shard_map/rho_spectrum/pallas_call | solution.py:120
  28.5 2.3 %rho_pick.1.refs_0_ = bf16[16,3200]{1,0:T(8,128)(2,1)S(1)} custom-call(bf16[1024,256]{1,0:T(8,128)(2,1)S(1)} %get-tuple-element.20.spec, s32[1,3072]{1,0:T(1,128)S(1)} %get-tuple-element.35.gidx, bf16[16,128]{1,0:T(8,128)(2,1)S(1)} %pad.4.meta), custom_call_target="tpu_custom_call" | custom-call | tf_op jit(solution)/shard_map/rho_pick/pallas_call | solution.py:135
  30.8 3.3 %collective-permute-start.2 = (bf16[32,3200]{1,0:T(8,128)(2,1)S(1)}, bf16[32,3200]{1,0:T(8,128)(2,1)S(1)}, u32[]{:S(2)}, u32[]{:S(2)}) collective-permute-start(bf16[32,3200]{1,0:T(8,128)(2,1)S(1)} %join.2.refs_0_), channel_id=1, source_target_pairs={{0,82},{8,90},{32,114},{40,122},{64,18},{72,26},{96,50},{104,58},{... | collective-permute-start | bytes 614408 | tf_op jit(solution)/shard_map/ppermute | solution.py:166
  34.0 4.5 %collective-permute-start.3 = (bf16[32,3200]{1,0:T(8,128)(2,1)S(1)}, bf16[32,3200]{1,0:T(8,128)(2,1)S(1)}, u32[]{:S(2)}, u32[]{:S(2)}) collective-permute-start(bf16[32,3200]{1,0:T(8,128)(2,1)S(1)} %join.2.refs_0_), channel_id=1, source_target_pairs={{0,37},{8,127},{32,69},{40,31},{64,101},{72,63},{96,5},{104,95},{4... | collective-permute-start | bytes 614408 | tf_op jit(solution)/shard_map/ppermute | solution.py:166
  38.5 5.2 %collective-permute-done.2.refs_1_ = bf16[32,3200]{1,0:T(8,128)(2,1)S(1)} collective-permute-done((bf16[32,3200]{1,0:T(8,128)(2,1)S(1)}, bf16[32,3200]{1,0:T(8,128)(2,1)S(1)}, u32[]{:S(2)}, u32[]{:S(2)}) %collective-permute-start.2) | collective-permute-done | bytes 204832 | tf_op jit(solution)/shard_map/ppermute | solution.py:166
  43.7 2.6 %collective-permute-done.3.refs_2_ = bf16[32,3200]{1,0:T(8,128)(2,1)S(1)} collective-permute-done((bf16[32,3200]{1,0:T(8,128)(2,1)S(1)}, bf16[32,3200]{1,0:T(8,128)(2,1)S(1)}, u32[]{:S(2)}, u32[]{:S(2)}) %collective-permute-start.3) | collective-permute-done | bytes 204832 | tf_op jit(solution)/shard_map/ppermute | solution.py:166
  46.3 2.2 %collective-permute-done.4.refs_3_ = bf16[32,3200]{1,0:T(8,128)(2,1)S(1)} collective-permute-done((bf16[32,3200]{1,0:T(8,128)(2,1)S(1)}, bf16[32,3200]{1,0:T(8,128)(2,1)S(1)}, u32[]{:S(2)}, u32[]{:S(2)}) %collective-permute-start.4) | collective-permute-done | bytes 204832 | tf_op jit(solution)/shard_map/ppermute | solution.py:166
  48.6 2.7 %collective-permute-start.5 = (bf16[128,3200]{1,0:T(8,128)(2,1)S(1)}, bf16[128,3200]{1,0:T(8,128)(2,1)S(1)}, u32[]{:S(2)}, u32[]{:S(2)}) collective-permute-start(bf16[128,3200]{1,0:T(8,128)(2,1)S(1)} %join.3.b0), channel_id=1, source_target_pairs={{0,2},{8,10},{32,34},{40,42},{64,66},{72,74},{96,98},{104,106},{4,... | collective-permute-start | bytes 2457608 | tf_op jit(solution)/shard_map/ppermute | solution.py:166
  52.6 17.8 %collective-permute-done.5.b1 = bf16[128,3200]{1,0:T(8,128)(2,1)S(1)} collective-permute-done((bf16[128,3200]{1,0:T(8,128)(2,1)S(1)}, bf16[128,3200]{1,0:T(8,128)(2,1)S(1)}, u32[]{:S(2)}, u32[]{:S(2)}) %collective-permute-start.5) | collective-permute-done | bytes 819232 | tf_op jit(solution)/shard_map/ppermute | solution.py:166
  70.5 1.7 %collective-permute-done.6.b2 = bf16[128,3200]{1,0:T(8,128)(2,1)S(1)} collective-permute-done((bf16[128,3200]{1,0:T(8,128)(2,1)S(1)}, bf16[128,3200]{1,0:T(8,128)(2,1)S(1)}, u32[]{:S(2)}, u32[]{:S(2)}) %collective-permute-start.6) | collective-permute-done | bytes 819232 | tf_op jit(solution)/shard_map/ppermute | solution.py:166
  72.2 1.4 %deal.1 = (bf16[256,3200]{1,0:T(8,128)(2,1)}, bf16[256,3200]{1,0:T(8,128)(2,1)S(1)}) custom-call(bf16[128,3200]{1,0:T(8,128)(2,1)S(1)} %join.3.b0, bf16[128,3200]{1,0:T(8,128)(2,1)S(1)} %collective-permute-done.5.b1, bf16[128,3200]{1,0:T(8,128)(2,1)S(1)} %collective-permute-done.6.b2, bf16[128,3200]{1,0:T(8,128)(2,1)S(1)} %collective-permute-done.7.b3), custom_call_target="tpu_custom_call" | custom-call | tf_op jit(solution)/shard_map/deal/pallas_call | solution.py:200
  74.7 1.7 %collective-permute-start.11 = (bf16[256,3200]{1,0:T(8,128)(2,1)}, bf16[256,3200]{1,0:T(8,128)(2,1)S(1)}, u32[]{:S(2)}, u32[]{:S(2)}) collective-permute-start(bf16[256,3200]{1,0:T(8,128)(2,1)} %get-tuple-element.23.refs_0_), channel_id=1, source_target_pairs={{0,1},{8,11},{32,33},{40,43},{64,65},{72,75},{96,97},{104,107},{4,... | collective-permute-start | bytes 4915208 | tf_op jit(solution)/shard_map/ppermute | solution.py:166
  76.4 1.5 %collective-permute-start.12 = (bf16[256,3200]{1,0:T(8,128)(2,1)}, bf16[256,3200]{1,0:T(8,128)(2,1)S(1)}, u32[]{:S(2)}, u32[]{:S(2)}) collective-permute-start(bf16[256,3200]{1,0:T(8,128)(2,1)} %get-tuple-element.23.refs_0_), channel_id=1, source_target_pairs={{0,4},{8,28},{32,36},{40,60},{64,68},{72,92},{96,100},{104,124},{4... | collective-permute-start | bytes 4915208 | tf_op jit(solution)/shard_map/ppermute | solution.py:166
  78.8 1.4 %copy-done.1 = bf16[256,3200]{1,0:T(8,128)(2,1)S(1)} copy-done((bf16[256,3200]{1,0:T(8,128)(2,1)S(1)}, bf16[256,3200]{1,0:T(8,128)(2,1)}, u32[]{:S(2)}) %copy-start.1) | copy-done | bytes 1638424
  80.2 2.2 %weighted.3.left = bf16[512,384]{1,0:T(8,128)(2,1)S(1)} custom-call(s32[1]{0:T(128)} %bitcast.1.place, f32[1]{0:T(128)} %dynamic_slice.12.omega, bf16[256,3200]{1,0:T(8,128)(2,1)} %get-tuple-element.23.refs_0_, bf16[256,3200]{1,0:T(8,128)(2,1)S(1)} %copy-done.1, f32[8,128]{1,0:T(8,128)S(1)} %broadcast_in_dim.24.refs_2_), custom_call_target="tpu_custom_call" | custom-call | tf_op jit(solution)/shard_map/weighted/pallas_call | solution.py:241
  82.5 2.5 %collective-permute-start.8 = (bf16[256,3200]{1,0:T(8,128)(2,1)S(1)}, bf16[256,3200]{1,0:T(8,128)(2,1)S(1)}, u32[]{:S(2)}, u32[]{:S(2)}) collective-permute-start(bf16[256,3200]{1,0:T(8,128)(2,1)S(1)} %copy-done.1), channel_id=1, source_target_pairs={{0,1},{8,11},{32,33},{40,43},{64,65},{72,75},{96,97},{104,107},{4,... | collective-permute-start | bytes 4915208 | tf_op jit(solution)/shard_map/ppermute | solution.py:166
  85.0 2.4 %collective-permute-start.9 = (bf16[256,3200]{1,0:T(8,128)(2,1)S(1)}, bf16[256,3200]{1,0:T(8,128)(2,1)S(1)}, u32[]{:S(2)}, u32[]{:S(2)}) collective-permute-start(bf16[256,3200]{1,0:T(8,128)(2,1)S(1)} %copy-done.1), channel_id=1, source_target_pairs={{0,4},{8,28},{32,36},{40,60},{64,68},{72,92},{96,100},{104,124},{4... | collective-permute-start | bytes 4915208 | tf_op jit(solution)/shard_map/ppermute | solution.py:166
  87.4 7.9 %collective-permute-done.11.refs_0_ = bf16[256,3200]{1,0:T(8,128)(2,1)S(1)} collective-permute-done((bf16[256,3200]{1,0:T(8,128)(2,1)}, bf16[256,3200]{1,0:T(8,128)(2,1)S(1)}, u32[]{:S(2)}, u32[]{:S(2)}) %collective-permute-start.11) | collective-permute-done | bytes 1638432 | tf_op jit(solution)/shard_map/ppermute | solution.py:166
  95.3 3.4 %partial_own.2 = (f32[384,3072]{1,0:T(8,128)S(1)}, f32[8,128]{1,0:T(8,128)S(1)}) custom-call(bf16[512,384]{1,0:T(8,128)(2,1)S(1)} %weighted.3.left, bf16[256,3200]{1,0:T(8,128)(2,1)} %get-tuple-element.23.refs_0_, bf16[256,3200]{1,0:T(8,128)(2,1)S(1)} %copy-done.1, f32[8,128]{1,0:T(8,128)S(1)} %broadcast_in_dim.24.refs_2_), custom_call_target="tpu_custom_call" | custom-call | flops 1207959552 | bytes 12582912 | tf_op jit(solution)/shard_map/partial_own/pallas_call | solution.py:299
  98.8 3.4 %partial_other.2 = (f32[384,3072]{1,0:T(8,128)S(1)}, f32[8,128]{1,0:T(8,128)S(1)}) custom-call(bf16[512,384]{1,0:T(8,128)(2,1)S(1)} %collective-permute-done.14.left, bf16[256,3200]{1,0:T(8,128)(2,1)} %get-tuple-element.23.refs_0_, bf16[256,3200]{1,0:T(8,128)(2,1)S(1)} %copy-done.1, f32[8,128]{1,0:T(8,128)S(1)} %get-tuple-element.24.refs_2_), custom_call_target="tpu_custom_call" | custom-call | flops 1207959552 | bytes 12582912 | tf_op jit(solution)/shard_map/partial_other/pallas_call | solution.py:299
  102.2 2.3 %weighted.4.left = bf16[768,384]{1,0:T(8,128)(2,1)S(1)} custom-call(s32[1]{0:T(128)} %bitcast.1.place, f32[1]{0:T(128)} %dynamic_slice.12.omega, bf16[256,3200]{1,0:T(8,128)(2,1)S(1)} %collective-permute-done.11.refs_0_, bf16[256,3200]{1,0:T(8,128)(2,1)S(1)} %collective-permute-done.12.refs_1_, bf16[256,3200]{1,0:T(8,128)(2,1)} %collective-permute-done.13.refs_2_, ...), custom_call_target="tpu_custom_call" | custom-call | tf_op jit(solution)/shard_map/weighted/pallas_call | solution.py:241
  104.6 4.6 %collective-permute-start.15 = (bf16[768,384]{1,0:T(8,128)(2,1)S(1)}, bf16[768,384]{1,0:T(8,128)(2,1)S(1)}, u32[]{:S(2)}, u32[]{:S(2)}) collective-permute-start(bf16[768,384]{1,0:T(8,128)(2,1)S(1)} %weighted.4.left), channel_id=1, source_target_pairs={{0,8},{8,0},{32,40},{40,32},{64,72},{72,64},{96,104},{104,96},{4,1... | collective-permute-start | bytes 1769480 | tf_op jit(solution)/shard_map/ppermute | solution.py:166
  109.1 4.1 %partial_own.3 = (f32[384,3072]{1,0:T(8,128)S(1)}, f32[8,128]{1,0:T(8,128)S(1)}) custom-call(bf16[768,384]{1,0:T(8,128)(2,1)S(1)} %weighted.4.left, bf16[256,3200]{1,0:T(8,128)(2,1)S(1)} %collective-permute-done.11.refs_0_, bf16[256,3200]{1,0:T(8,128)(2,1)S(1)} %collective-permute-done.12.refs_1_, ...), custom_call_target="tpu_custom_call", output_to_operand_aliasing={{0}: (4, {})} | custom-call | flops 1811939328 | bytes 14155776 | tf_op jit(solution)/shard_map/partial_own/pallas_call | solution.py:299
  113.3 4.1 %partial_other.3 = (f32[384,3072]{1,0:T(8,128)S(1)}, f32[8,128]{1,0:T(8,128)S(1)}) custom-call(bf16[768,384]{1,0:T(8,128)(2,1)S(1)} %collective-permute-done.15.left, bf16[256,3200]{1,0:T(8,128)(2,1)S(1)} %collective-permute-done.11.refs_0_, bf16[256,3200]{1,0:T(8,128)(2,1)S(1)} %collective-permute-done.12.refs_1_, ...), custom_call_target="tpu_custom_call", output_to_operand_aliasing={{0}: (4, {})} | custom-call | flops 1811939328 | bytes 14155776 | tf_op jit(solution)/shard_map/partial_other/pallas_call | solution.py:299
  118.3 4.3 %collective-permute-start.16 = (bf16[768,384]{1,0:T(8,128)(2,1)S(1)}, bf16[768,384]{1,0:T(8,128)(2,1)S(1)}, u32[]{:S(2)}, u32[]{:S(2)}) collective-permute-start(bf16[768,384]{1,0:T(8,128)(2,1)S(1)} %weighted.5.left), channel_id=1, source_target_pairs={{0,8},{8,0},{32,40},{40,32},{64,72},{72,64},{96,104},{104,96},{4,1... | collective-permute-start | bytes 1769480 | tf_op jit(solution)/shard_map/ppermute | solution.py:166
  122.6 2.7 %own_rows.2 = (f32[384,6144]{1,0:T(8,128)}, f32[8,128]{1,0:T(8,128)S(1)}) custom-call(s32[1]{0:T(128)} %bitcast.core, bf16[768,384]{1,0:T(8,128)(2,1)S(1)} %weighted.5.left, bf16[256,3200]{1,0:T(8,128)(2,1)S(1)} %collective-permute-done.8.refs_0_, bf16[256,3200]{1,0:T(8,128)(2,1)S(1)} %collective-permute-done.9.refs_1_, ...), custom_call_target="tpu_custom_call" | custom-call | flops 905969664 | bytes 7077888 | tf_op jit(solution)/shard_map/own_rows/pallas_call | solution.py:335
  125.3 1.4 %other_rows.2 = bf16[384,1536]{1,0:T(8,128)(2,1)S(1)} custom-call(bf16[768,384]{1,0:T(8,128)(2,1)S(1)} %collective-permute-done.16.left, bf16[256,3200]{1,0:T(8,128)(2,1)S(1)} %collective-permute-done.8.refs_0_, bf16[256,3200]{1,0:T(8,128)(2,1)S(1)} %collective-permute-done.9.refs_1_, bf16[256,3200]{1,0:T(8,128)(2,1)S(1)} %collective-permute-done.10.refs_2_, ...), custom_call_target="tpu_custom_call" | custom-call | flops 905969664 | bytes 7077888 | tf_op jit(solution)/shard_map/other_rows/pallas_call | solution.py:361
  128.6 3.2 %own_rows.3 = (f32[384,6144]{1,0:T(8,128)}, f32[8,128]{1,0:T(8,128)}) custom-call(s32[1]{0:T(128)} %bitcast.core, bf16[768,384]{1,0:T(8,128)(2,1)S(1)} %weighted.5.left, bf16[256,3200]{1,0:T(8,128)(2,1)S(1)} %collective-permute-done.8.refs_0_, bf16[256,3200]{1,0:T(8,128)(2,1)S(1)} %collective-permute-done.9.refs_1_, ...), custom_call_target="tpu_custom_call", output_to_operand_aliasing={{0}: (6, {})} | custom-call | flops 905969664 | bytes 7077888 | tf_op jit(solution)/shard_map/own_rows/pallas_call | solution.py:335
  131.9 2.3 %finish.1 = f32[384,6144]{1,0:T(8,128)} custom-call(s32[1]{0:T(128)} %bitcast.core, bf16[384,1536]{1,0:T(8,128)(2,1)S(1)} %collective-permute-done.17.r0, bf16[384,1536]{1,0:T(8,128)(2,1)S(1)} %collective-permute-done.18.r1, f32[384,6144]{1,0:T(8,128)} %get-tuple-element.34._), custom_call_target="tpu_custom_call", output_to_operand_aliasing={{}: (3, {})} | custom-call | tf_op jit(solution)/shard_map/finish/pallas_call | solution.py:389
  (65 shorter events, 11.2 us)
Async XLA Ops:
  0.0 23.6 %copy-start.2 = (bf16[2,256,256]{2,1,0:T(8,128)(2,1)S(1)}, bf16[2,256,256]{2,1,0:T(8,128)(2,1)}, u32[]{:S(2)}) copy-start(bf16[2,256,256]{2,1,0:T(8,128)(2,1)} %constant.39.clone.first) | copy-start | bytes 786436
  0.0 23.6 %copy-start.4 = (f32[128,256]{1,0:T(8,128)S(1)}, f32[128,256]{1,0:T(8,128)}, u32[]{:S(2)}) copy-start(f32[128,256]{1,0:T(8,128)} %constant.40.clone.tcos) | copy-start | bytes 393220
  0.0 23.6 %copy-start.5 = (f32[128,256]{1,0:T(8,128)S(1)}, f32[128,256]{1,0:T(8,128)}, u32[]{:S(2)}) copy-start(f32[128,256]{1,0:T(8,128)} %constant.41.clone.tsin) | copy-start | bytes 393220
  0.0 23.6 %copy-start.3 = (bf16[512,256]{1,0:T(8,128)(2,1)S(1)}, bf16[512,256]{1,0:T(8,128)(2,1)}, u32[]{:S(2)}) copy-start(bf16[512,256]{1,0:T(8,128)(2,1)} %constant.42.clone.second) | copy-start | bytes 786436
  0.0 11.1 %copy-start.6 = (s32[6144]{0:T(1024)S(1)}, s32[6144]{0:T(1024)}, u32[]{:S(2)}) copy-start(s32[6144]{0:T(1024)} %param.17) | copy-start | bytes 73732
  0.0 11.1 %copy-start.8 = (s32[4]{0:T(128)S(1)}, s32[4]{0:T(128)}, u32[]{:S(2)}) copy-start(s32[4]{0:T(128)} %param.15) | copy-start | bytes 52
  0.0 11.3 %copy-start.9 = (f32[64]{0:T(128)S(1)}, f32[64]{0:T(128)}, u32[]{:S(2)}) copy-start(f32[64]{0:T(128)} %param.14) | copy-start | bytes 772
  0.1 11.4 %copy-start.7 = (f32[4]{0:T(128)S(1)}, f32[4]{0:T(128)}, u32[]{:S(2)}) copy-start(f32[4]{0:T(128)} %param.13) | copy-start | bytes 52
  2.7 17.5 %all-to-all-start = ((bf16[8,12,8,256]{3,2,1,0:T(8,128)(2,1)}), bf16[8,12,8,256]{3,2,1,0:T(8,128)(2,1)S(1)}, u32[]{:S(2)}, u32[]{:S(2)}) async-start(bf16[8,12,8,256]{3,2,1,0:T(8,128)(2,1)} %pad_maximum_fusion), calls=%async_computation | async-start | bytes 786432 | tf_op jit(solution)/shard_map/all_to_all | solution.py:412
  20.1 3.5 %collective-permute-start = (bf16[8,12,8,256]{3,2,1,0:T(8,128)(2,1)S(1)}, bf16[8,12,8,256]{3,2,1,0:T(8,128)(2,1)S(1)}, u32[]{:S(2)}, u32[]{:S(2)}) collective-permute-start(bf16[8,12,8,256]{3,2,1,0:T(8,128)(2,1)S(1)} %all-to-all-done.mine), channel_id=1, source_target_pairs={{0,8},{8,0},{32,40},{40,32},{64,72},{72,64},{96,104},{104,96},{4,1... | collective-permute-start | bytes 1179656 | tf_op jit(solution)/shard_map/ppermute | solution.py:166
  28.0 2.7 %collective-permute-start.1 = (bf16[16,3200]{1,0:T(8,128)(2,1)S(1)}, bf16[16,3200]{1,0:T(8,128)(2,1)S(1)}, u32[]{:S(2)}, u32[]{:S(2)}) collective-permute-start(bf16[16,3200]{1,0:T(8,128)(2,1)S(1)} %get-tuple-element.21), channel_id=1, source_target_pairs={{0,8},{8,0},{32,40},{40,32},{64,72},{72,64},{96,104},{104,96},{4,1... | collective-permute-start | bytes 307208 | tf_op jit(solution)/shard_map/ppermute | solution.py:166
  30.8 12.9 %collective-permute-start.2 = (bf16[32,3200]{1,0:T(8,128)(2,1)S(1)}, bf16[32,3200]{1,0:T(8,128)(2,1)S(1)}, u32[]{:S(2)}, u32[]{:S(2)}) collective-permute-start(bf16[32,3200]{1,0:T(8,128)(2,1)S(1)} %join.2.refs_0_), channel_id=1, source_target_pairs={{0,82},{8,90},{32,114},{40,122},{64,18},{72,26},{96,50},{104,58},{... | collective-permute-start | bytes 614408 | tf_op jit(solution)/shard_map/ppermute | solution.py:166
  34.0 12.2 %collective-permute-start.3 = (bf16[32,3200]{1,0:T(8,128)(2,1)S(1)}, bf16[32,3200]{1,0:T(8,128)(2,1)S(1)}, u32[]{:S(2)}, u32[]{:S(2)}) collective-permute-start(bf16[32,3200]{1,0:T(8,128)(2,1)S(1)} %join.2.refs_0_), channel_id=1, source_target_pairs={{0,37},{8,127},{32,69},{40,31},{64,101},{72,63},{96,5},{104,95},{4... | collective-permute-start | bytes 614408 | tf_op jit(solution)/shard_map/ppermute | solution.py:166
  38.5 10.0 %collective-permute-start.4 = (bf16[32,3200]{1,0:T(8,128)(2,1)S(1)}, bf16[32,3200]{1,0:T(8,128)(2,1)S(1)}, u32[]{:S(2)}, u32[]{:S(2)}) collective-permute-start(bf16[32,3200]{1,0:T(8,128)(2,1)S(1)} %join.2.refs_0_), channel_id=1, source_target_pairs={{0,119},{8,45},{32,23},{40,77},{64,55},{72,109},{96,87},{104,13},{... | collective-permute-start | bytes 614408 | tf_op jit(solution)/shard_map/ppermute | solution.py:166
  48.6 29.6 %copy-start.10 = (f32[8]{0:T(128)S(1)}, f32[8]{0:T(128)}, u32[]{:S(2)}) copy-start(f32[8]{0:T(128)} %param.16) | copy-start | bytes 100
  48.6 21.8 %collective-permute-start.5 = (bf16[128,3200]{1,0:T(8,128)(2,1)S(1)}, bf16[128,3200]{1,0:T(8,128)(2,1)S(1)}, u32[]{:S(2)}, u32[]{:S(2)}) collective-permute-start(bf16[128,3200]{1,0:T(8,128)(2,1)S(1)} %join.3.b0), channel_id=1, source_target_pairs={{0,2},{8,10},{32,34},{40,42},{64,66},{72,74},{96,98},{104,106},{4,... | collective-permute-start | bytes 2457608 | tf_op jit(solution)/shard_map/ppermute | solution.py:166
  51.3 20.9 %collective-permute-start.6 = (bf16[128,3200]{1,0:T(8,128)(2,1)S(1)}, bf16[128,3200]{1,0:T(8,128)(2,1)S(1)}, u32[]{:S(2)}, u32[]{:S(2)}) collective-permute-start(bf16[128,3200]{1,0:T(8,128)(2,1)S(1)} %join.3.b0), channel_id=1, source_target_pairs={{0,16},{8,24},{32,48},{40,56},{64,80},{72,88},{96,112},{104,120},{... | collective-permute-start | bytes 2457608 | tf_op jit(solution)/shard_map/ppermute | solution.py:166
  52.0 20.2 %collective-permute-start.7 = (bf16[128,3200]{1,0:T(8,128)(2,1)S(1)}, bf16[128,3200]{1,0:T(8,128)(2,1)S(1)}, u32[]{:S(2)}, u32[]{:S(2)}) collective-permute-start(bf16[128,3200]{1,0:T(8,128)(2,1)S(1)} %join.3.b0), channel_id=1, source_target_pairs={{0,64},{8,72},{32,96},{40,104},{64,0},{72,8},{96,32},{104,40},{4,6... | collective-permute-start | bytes 2457608 | tf_op jit(solution)/shard_map/ppermute | solution.py:166
  73.6 1.2 copy-start
  74.7 20.6 %collective-permute-start.11 = (bf16[256,3200]{1,0:T(8,128)(2,1)}, bf16[256,3200]{1,0:T(8,128)(2,1)S(1)}, u32[]{:S(2)}, u32[]{:S(2)}) collective-permute-start(bf16[256,3200]{1,0:T(8,128)(2,1)} %get-tuple-element.23.refs_0_), channel_id=1, source_target_pairs={{0,1},{8,11},{32,33},{40,43},{64,65},{72,75},{96,97},{104,107},{4,... | collective-permute-start | bytes 4915208 | tf_op jit(solution)/shard_map/ppermute | solution.py:166
  76.4 25.8 %collective-permute-start.12 = (bf16[256,3200]{1,0:T(8,128)(2,1)}, bf16[256,3200]{1,0:T(8,128)(2,1)S(1)}, u32[]{:S(2)}, u32[]{:S(2)}) collective-permute-start(bf16[256,3200]{1,0:T(8,128)(2,1)} %get-tuple-element.23.refs_0_), channel_id=1, source_target_pairs={{0,4},{8,28},{32,36},{40,60},{64,68},{72,92},{96,100},{104,124},{4... | collective-permute-start | bytes 4915208 | tf_op jit(solution)/shard_map/ppermute | solution.py:166
  78.0 24.3 %collective-permute-start.13 = (bf16[256,3200]{1,0:T(8,128)(2,1)}, bf16[256,3200]{1,0:T(8,128)(2,1)}, u32[]{:S(2)}, u32[]{:S(2)}) collective-permute-start(bf16[256,3200]{1,0:T(8,128)(2,1)} %get-tuple-element.23.refs_0_), channel_id=1, source_target_pairs={{0,32},{8,104},{32,64},{40,8},{64,96},{72,40},{96,0},{104,72},{4,3... | collective-permute-start | bytes 4915208 | tf_op jit(solution)/shard_map/ppermute | solution.py:166
  78.8 1.4 %copy-start.1 = (bf16[256,3200]{1,0:T(8,128)(2,1)S(1)}, bf16[256,3200]{1,0:T(8,128)(2,1)}, u32[]{:S(2)}) copy-start(bf16[256,3200]{1,0:T(8,128)(2,1)} %copy-done) | copy-start | bytes 4915204
  82.4 2.6 %collective-permute-start.14 = (bf16[512,384]{1,0:T(8,128)(2,1)S(1)}, bf16[512,384]{1,0:T(8,128)(2,1)S(1)}, u32[]{:S(2)}, u32[]{:S(2)}) collective-permute-start(bf16[512,384]{1,0:T(8,128)(2,1)S(1)} %weighted.3.left), channel_id=1, source_target_pairs={{0,8},{8,0},{32,40},{40,32},{64,72},{72,64},{96,104},{104,96},{4,1... | collective-permute-start | bytes 1179656 | tf_op jit(solution)/shard_map/ppermute | solution.py:166
  82.5 34.8 %collective-permute-start.8 = (bf16[256,3200]{1,0:T(8,128)(2,1)S(1)}, bf16[256,3200]{1,0:T(8,128)(2,1)S(1)}, u32[]{:S(2)}, u32[]{:S(2)}) collective-permute-start(bf16[256,3200]{1,0:T(8,128)(2,1)S(1)} %copy-done.1), channel_id=1, source_target_pairs={{0,1},{8,11},{32,33},{40,43},{64,65},{72,75},{96,97},{104,107},{4,... | collective-permute-start | bytes 4915208 | tf_op jit(solution)/shard_map/ppermute | solution.py:166
  85.0 32.4 %collective-permute-start.9 = (bf16[256,3200]{1,0:T(8,128)(2,1)S(1)}, bf16[256,3200]{1,0:T(8,128)(2,1)S(1)}, u32[]{:S(2)}, u32[]{:S(2)}) collective-permute-start(bf16[256,3200]{1,0:T(8,128)(2,1)S(1)} %copy-done.1), channel_id=1, source_target_pairs={{0,4},{8,28},{32,36},{40,60},{64,68},{72,92},{96,100},{104,124},{4... | collective-permute-start | bytes 4915208 | tf_op jit(solution)/shard_map/ppermute | solution.py:166
  95.3 22.1 %collective-permute-start.10 = (bf16[256,3200]{1,0:T(8,128)(2,1)S(1)}, bf16[256,3200]{1,0:T(8,128)(2,1)S(1)}, u32[]{:S(2)}, u32[]{:S(2)}) collective-permute-start(bf16[256,3200]{1,0:T(8,128)(2,1)S(1)} %copy-done.1), channel_id=1, source_target_pairs={{0,32},{8,104},{32,64},{40,8},{64,96},{72,40},{96,0},{104,72},{4,3... | collective-permute-start | bytes 4915208 | tf_op jit(solution)/shard_map/ppermute | solution.py:166
  104.6 8.7 %collective-permute-start.15 = (bf16[768,384]{1,0:T(8,128)(2,1)S(1)}, bf16[768,384]{1,0:T(8,128)(2,1)S(1)}, u32[]{:S(2)}, u32[]{:S(2)}) collective-permute-start(bf16[768,384]{1,0:T(8,128)(2,1)S(1)} %weighted.4.left), channel_id=1, source_target_pairs={{0,8},{8,0},{32,40},{40,32},{64,72},{72,64},{96,104},{104,96},{4,1... | collective-permute-start | bytes 1769480 | tf_op jit(solution)/shard_map/ppermute | solution.py:166
  118.3 7.0 %collective-permute-start.16 = (bf16[768,384]{1,0:T(8,128)(2,1)S(1)}, bf16[768,384]{1,0:T(8,128)(2,1)S(1)}, u32[]{:S(2)}, u32[]{:S(2)}) collective-permute-start(bf16[768,384]{1,0:T(8,128)(2,1)S(1)} %weighted.5.left), channel_id=1, source_target_pairs={{0,8},{8,0},{32,40},{40,32},{64,72},{72,64},{96,104},{104,96},{4,1... | collective-permute-start | bytes 1769480 | tf_op jit(solution)/shard_map/ppermute | solution.py:166
  126.6 5.3 %collective-permute-start.17 = (bf16[384,1536]{1,0:T(8,128)(2,1)S(1)}, bf16[384,1536]{1,0:T(8,128)(2,1)S(1)}, u32[]{:S(2)}, u32[]{:S(2)}) collective-permute-start(bf16[384,1536]{1,0:T(8,128)(2,1)S(1)} %other_rows.2), channel_id=1, source_target_pairs={{0,8},{8,0},{32,40},{40,32},{64,72},{72,64},{96,104},{104,96},{4,1... | collective-permute-start | bytes 3538952 | tf_op jit(solution)/shard_map/ppermute | solution.py:166
  128.1 3.8 %collective-permute-start.18 = (bf16[384,1536]{1,0:T(8,128)(2,1)S(1)}, bf16[384,1536]{1,0:T(8,128)(2,1)S(1)}, u32[]{:S(2)}, u32[]{:S(2)}) collective-permute-start(bf16[384,1536]{1,0:T(8,128)(2,1)S(1)} %other_rows.3), channel_id=1, source_target_pairs={{0,8},{8,0},{32,40},{40,32},{64,72},{72,64},{96,104},{104,96},{4,1... | collective-permute-start | bytes 3538952 | tf_op jit(solution)/shard_map/ppermute | solution.py:166

commit v7 on v6

--- a/solution.py
+++ b/solution.py
@@ -42,11 +42,10 @@
 
 def dft_constants():
     k1 = np.arange(NA)[:, None]
-    chip, a = np.arange(8)[:, None], np.arange(8)[None, :]
-    kinds = [((chip * 2 + kind) * 8 + a).reshape(64) for kind in range(2)]
+    a, kind, chip = np.arange(8)[:, None, None], np.arange(2)[:, None], np.arange(8)
     first = []
     for core in range(2):
-        order = np.concatenate([kinds[core], kinds[1 - core]])
+        order = ((chip * 2 + (kind + core) % 2) * 8 + a).reshape(NA)
         ang = 2.0 * math.pi * ((k1 * order[None, :]) % NA) / NA
         fh, fl = split_bf16(np.concatenate([np.cos(ang), np.sin(ang)], 0))
         first.append(np.concatenate([fh, fl], 1))
@@ -59,17 +58,49 @@
     return np.stack(first), tcos, tsin, np.concatenate([sh, sl], 1)
 
 
-def transform(core, mine, others, first, tcos, tsin, second, spec, high, low):
-    def band(row):
-        both = jnp.concatenate([mine[:, row], others[:, row]], 0)
-        return both.astype(jnp.float32).reshape(NA, NB)
-
-    con = [band(core[0] * 4 + i) for i in range(4)]
+def payload_kernel(val, con, out):
+    v = val[...].astype(jnp.float32)
+    values = jnp.concatenate([v[:, :1024], v[:, 1024:]], 0)
+    for chip in range(8):
+        c = con[chip * 8 : chip * 8 + 8, :].astype(jnp.float32)
+        rows = jnp.concatenate([c[:, :1024], c[:, 1024:], values], 0)
+        out[chip] = rows.astype(jnp.bfloat16)
+
+
+def payload(val, con):
+    return pl.pallas_call(
+        payload_kernel,
+        out_shape=jax.ShapeDtypeStruct((8, 24, 1024), jnp.bfloat16),
+        in_specs=[VM] * 2,
+        out_specs=VM,
+        compiler_params=PARAMS,
+        name="payload",
+    )(val, con)
+
+
+def transform(core, mine, others, first, tcos, tsin, second, spec, high, low, grid):
+    for kind, ref in enumerate((mine, others)):
+        for chip in range(8):
+            for j in range(8):
+                grid[kind, j, chip * 24 : chip * 24 + 24, :] = ref[
+                    chip, :, j * LANES : (j + 1) * LANES
+                ].astype(jnp.float32)
+
+    def band(row, apart):
+        parts = []
+        for half in range(2):
+            at = pl.ds(row + half * apart, 8, stride=24)
+            for a in range(4):
+                for kind in range(2):
+                    parts.append(jnp.concatenate([grid[kind, 2 * a + j, at, :] for j in range(2)], 1))
+        return jnp.concatenate(parts, 0)
+
+    con = [band(core[0] * 4 + i, 8) for i in range(4)]
     ca = tcos[...]
     sa = tsin[...]
     f = first[core[0]]
     for v in range(4):
-        val = band(8 + v)
+        val = band(16 + v, 4)
         for c in range(4):
             d = (val * con[c]).astype(jnp.bfloat16)
             y = jnp.dot(f, jnp.concatenate([d, d], 0), preferred_element_type=jnp.float32)
@@ -111,8 +142,8 @@
     out[:, HALF:WIDE] = meta[...]
 
 
-def transform_kernel(core, mine, others, gidx, meta, first, tcos, tsin, second, spec, out, high, low):
-    transform(core, mine, others, first, tcos, tsin, second, spec, high, low)
+def transform_kernel(core, mine, others, gidx, meta, first, tcos, tsin, second, spec, out, high, low, grid):
+    transform(core, mine, others, first, tcos, tsin, second, spec, high, low, grid)
     pick(spec, gidx, meta, out)
 
 
@@ -125,7 +156,8 @@
         ],
         in_specs=[SM] + [VM] * 8,
         out_specs=[VM] * 2,
-        scratch_shapes=[pltpu.VMEM((PAIRS * NA, 2 * NB), jnp.bfloat16)] * 2,
+        scratch_shapes=[pltpu.VMEM((PAIRS * NA, 2 * NB), jnp.bfloat16)] * 2
+        + [pltpu.VMEM((2, 8, 8 * 24, LANES), jnp.float32)],
         compiler_params=PARAMS,
         name="rho_spectrum",
     )(core, mine, others, gidx, meta, *(jnp.asarray(c) for c in dft_constants()))
@@ -398,6 +430,22 @@
     )(core, *rows, out)
 
 
+def held_kernel(a, _, out):
+    pass
+
+
+def held(a, tie):
+    return pl.pallas_call(
+        held_kernel,
+        out_shape=jax.ShapeDtypeStruct(a.shape, a.dtype),
+        in_specs=[VM] * 2,
+        out_specs=VM,
+        input_output_aliases={0: 0},
+        compiler_params=PARAMS,
+        name="held",
+    )(a, tie)
+
+
 def in_vmem(a):
     return pltpu.with_memory_space_constraint(a, pltpu.VMEM)
 
@@ -406,12 +454,8 @@
     ga = lax.axis_index("ga")
     ba = lax.axis_index("ba")
     core = lax.rem(ga, 2).astype(jnp.int32)
-    con = psi_con.reshape(8, 8, 8, NB)
-    val = jnp.broadcast_to(psi_val.reshape(1, 4, 8, NB), (8, 4, 8, NB))
     kinds = [[2 * i + c for i in range(8)] for c in range(2)]
-    psi = lax.all_to_all(
-        jnp.concatenate([con, val], 1), "ga", 0, 0, tiled=True, axis_index_groups=kinds
-    )
+    psi = lax.all_to_all(payload(psi_val, psi_con), "ga", 0, 0, tiled=True, axis_index_groups=kinds)
     psi_other = send(psi, core_pairs())
 
     delta = (lax.dynamic_slice(e_con, (ga * 4,), (4,))[None, :] - e_val[:, None]).reshape(PAIRS)
@@ -426,25 +470,31 @@
     kept = lax.dynamic_slice(halves, (core, 0), (1, HALF))
     given = lax.dynamic_slice(halves, (1 - core, 0), (1, HALF))
     spec, give = rho_spectrum(core.reshape(1), psi, psi_other, given, meta)
-    got = send(give, core_pairs())
+    swapped = send(give, core_pairs())
     keep = rho_pick(spec, kept, meta)
 
-    a = join(level(join([keep, got]), NEAR))
-    halved = [[in_vmem(b) for b in level(m, STEP)] for m in deal(level(a, EVEN))]
+    a = join(level(join([keep, swapped]), NEAR))
+    sources = deal(level(a, EVEN))
+    got = {(h, 0): m for h, m in enumerate(sources)}
+    for h in range(2):
+        for s in range(1, 3 + (h == 0)):
+            got[h, s] = send(sources[h], offset_pairs(STEP[s]))
 
     place = lax.div(ga, 2).astype(jnp.int32).reshape(1)
     mine_omega = lax.dynamic_slice(omega, (ba,), (1,))
     core = core.reshape(1)
     own = other = None
     tie = jnp.zeros(TIE.shape, TIE.dtype)
-    groups = (((0, 0), (1, 0)), ((0, 1), (0, 2), (0, 3)), ((1, 1), (1, 2), (1, 3)))
+    groups = (((0, 0), (1, 0)), ((1, 1), (1, 2)), ((0, 1), (0, 2), (0, 3)), ((1, 3),))
     for names in groups:
-        pieces = [halved[h][s] for h, s in names]
+        pieces = [in_vmem(got[name]) for name in names]
         left = weighted(place, mine_omega, pieces, tie)
         mirror = send(left, core_pairs())
         if names is not groups[-1]:
             own, tie = partial_rows(names, False, left, pieces, own, tie)
             other, tie = partial_rows(names, True, mirror, pieces, other, tie)
+        if names is groups[0]:
+            got[1, 3] = send(held(sources[1], tie), offset_pairs(STEP[3]))
     out, tie = own_rows(names, 0, core, left, pieces, own, tie)
     rows = [send(other_rows(names, s, mirror, pieces, other, tie), core_pairs()) for s in (0, HALF // 2)]
     out, _ = own_rows(names, HALF // 2, core, left, pieces, own, out)

time: 135 us -> 136 us (level)
  Pallas kernels: 39.5 us -> 43.3 us
  starting transfers between devices: 40.7 us -> 39.1 us
    pallas_call x0 -> x2, Pallas kernels: none -> 3.4 us  [the longest x1 2.62 us: held(): pl.pallas_call(held_kernel, out_shape=jax.ShapeDtypeStruct(a.shape, a.dty...]
    unnamed x24 -> x14, local copies, waits for them, and re-layouts: 4.44 us -> 1.69 us
    all_to_all x1, waiting for transfers between devices: 8.52 us -> 5.85 us  [on_device(): lax.all_to_all(payload(psi_val, psi_con), 'ga', 0, 0, tiled=True, axis_in...]
    pallas_call x4 -> x6, Pallas kernels: 15.1 us -> 17.6 us  [partial_rows(): pl.pallas_call(functools.partial(partial_kernel, names, other), out_shape...]
    ppermute x19 -> x20, waiting for transfers between devices: 38.8 us -> 41.2 us  [send(): return lax.ppermute(a, ('ga', 'ba'), pairs)]
    pallas_call x2, Pallas kernels: 5.91 us -> 4.29 us  [own_rows(): pl.pallas_call(functools.partial(own_kernel, names, start), out_shape=[ja...]
    ppermute x19 -> x20, starting transfers between devices: 32.2 us -> 30.6 us  [send(): return lax.ppermute(a, ('ga', 'ba'), pairs)]
    pallas_call x3 -> x4, Pallas kernels: 5.44 us -> 5.38 us  [weighted(): pl.pallas_call(weighted_kernel, out_shape=jax.ShapeDtypeStruct((256 * len...]
  transfers between devices with their start and end apart: 20 -> 21, of which waited for: 8 -> 11; matrix products, arithmetic and copies ran while one was open for 1% -> 3% of each run, Pallas kernels for 22% -> 24%
where the time goes in v7:
time: 136 us; the launch traced here: 135 us
  waiting for transfers between devices  47 us (35%)
  Pallas kernels  43.3 us (32%)
  starting transfers between devices  39.1 us (29%)
  local copies, waits for them, and re-layouts  4.16 us (3%)
  other arithmetic  1.41 us (1%)
    ppermute x20, waiting for transfers between devices, send(): return lax.ppermute(a, ('ga', 'ba'), pairs)  41.2 us
    ppermute x20, starting transfers between devices, send(): return lax.ppermute(a, ('ga', 'ba'), pairs)  30.6 us
    pallas_call x6, Pallas kernels, partial_rows(): pl.pallas_call(functools.partial(partial_kernel, names, other), out_shape...  17.6 us
    all_to_all x1, starting transfers between devices, on_device(): lax.all_to_all(payload(psi_val, psi_con), 'ga', 0, 0, tiled=True, axis_in...  8.49 us
    all_to_all x1, waiting for transfers between devices, on_device(): lax.all_to_all(payload(psi_val, psi_con), 'ga', 0, 0, tiled=True, axis_in...  5.85 us
    pallas_call x4, Pallas kernels, weighted(): pl.pallas_call(weighted_kernel, out_shape=jax.ShapeDtypeStruct((256 * len...  5.38 us
    pallas_call x1, Pallas kernels, rho_spectrum(): pl.pallas_call(transform_kernel, out_shape=[jax.ShapeDtypeStruct((PAIRS *...  4.58 us
    pallas_call x2, Pallas kernels, own_rows(): pl.pallas_call(functools.partial(own_kernel, names, start), out_shape=[ja...  4.29 us
  transfers between devices with their start and end apart: 21, of which 11 were waited for; matrix products, arithmetic and copies ran while one was open for 3% of the time, Pallas kernels for 24%

profile of v7, /device:TPU:1, one launch (start us, length us, event | category | flops | bytes accessed | tf_op | source)
XLA Modules:
  0.0 135.3 jit_solution(7889484063587079879)
XLA Ops:
  2.5 8.5 %all-to-all-start = ((bf16[8,24,1024]{2,1,0:T(8,128)(2,1)}), bf16[8,24,1024]{2,1,0:T(8,128)(2,1)S(1)}, u32[]{:S(2)}, u32[]{:S(2)}) async-start(bf16[8,24,1024]{2,1,0:T(8,128)(2,1)} %payload.1), calls=%async_computation | async-start | bytes 786432 | tf_op jit(solution)/shard_map/all_to_all | solution.py:458
  14.1 5.8 %all-to-all-done.mine = bf16[8,24,1024]{2,1,0:T(8,128)(2,1)S(1)} async-done(((bf16[8,24,1024]{2,1,0:T(8,128)(2,1)}), bf16[8,24,1024]{2,1,0:T(8,128)(2,1)S(1)}, u32[]{:S(2)}, u32[]{:S(2)}) %all-to-all-start) | async-done | bytes 393248 | tf_op jit(solution)/shard_map/all_to_all | solution.py:458
  19.9 2.2 %collective-permute-start = (bf16[8,24,1024]{2,1,0:T(8,128)(2,1)S(1)}, bf16[8,24,1024]{2,1,0:T(8,128)(2,1)S(1)}, u32[]{:S(2)}, u32[]{:S(2)}) collective-permute-start(bf16[8,24,1024]{2,1,0:T(8,128)(2,1)S(1)} %all-to-all-done.mine), channel_id=1, source_target_pairs={{0,8},{8,0},{32,40},{40,32},{64,72},{72,64},{96,104},{104,96},{4,1... | collective-permute-start | bytes 1179656 | tf_op jit(solution)/shard_map/ppermute | solution.py:198
  23.5 4.6 %rho_spectrum.1 = (bf16[1024,256]{1,0:T(8,128)(2,1)S(1)}, bf16[16,3200]{1,0:T(8,128)(2,1)S(1)}) custom-call(s32[1]{0:T(128)} %bitcast.core, bf16[8,24,1024]{2,1,0:T(8,128)(2,1)S(1)} %all-to-all-done.mine, bf16[8,24,1024]{2,1,0:T(8,128)(2,1)S(1)} %collective-permute-done.others, s32[1,3072]{1,0:T(1,128)S(1)} %get-tuple-element.44.gidx, ...), custom_call_target="tpu_custom_call" | custom-call | tf_op jit(solution)/shard_map/rho_spectrum/pallas_call | solution.py:151
  28.5 2.3 %rho_pick.1.refs_0_ = bf16[16,3200]{1,0:T(8,128)(2,1)S(1)} custom-call(bf16[1024,256]{1,0:T(8,128)(2,1)S(1)} %get-tuple-element.24.spec, s32[1,3072]{1,0:T(1,128)S(1)} %get-tuple-element.43.gidx, bf16[16,128]{1,0:T(8,128)(2,1)S(1)} %pad.4.meta), custom_call_target="tpu_custom_call" | custom-call | tf_op jit(solution)/shard_map/rho_pick/pallas_call | solution.py:167
  30.8 3.2 %collective-permute-start.2 = (bf16[32,3200]{1,0:T(8,128)(2,1)S(1)}, bf16[32,3200]{1,0:T(8,128)(2,1)S(1)}, u32[]{:S(2)}, u32[]{:S(2)}) collective-permute-start(bf16[32,3200]{1,0:T(8,128)(2,1)S(1)} %join.2.refs_0_), channel_id=1, source_target_pairs={{0,82},{8,90},{32,114},{40,122},{64,18},{72,26},{96,50},{104,58},{... | collective-permute-start | bytes 614408 | tf_op jit(solution)/shard_map/ppermute | solution.py:198
  34.0 4.5 %collective-permute-start.3 = (bf16[32,3200]{1,0:T(8,128)(2,1)S(1)}, bf16[32,3200]{1,0:T(8,128)(2,1)S(1)}, u32[]{:S(2)}, u32[]{:S(2)}) collective-permute-start(bf16[32,3200]{1,0:T(8,128)(2,1)S(1)} %join.2.refs_0_), channel_id=1, source_target_pairs={{0,37},{8,127},{32,69},{40,31},{64,101},{72,63},{96,5},{104,95},{4... | collective-permute-start | bytes 614408 | tf_op jit(solution)/shard_map/ppermute | solution.py:198
  38.5 5.2 %collective-permute-done.2.refs_1_ = bf16[32,3200]{1,0:T(8,128)(2,1)S(1)} collective-permute-done((bf16[32,3200]{1,0:T(8,128)(2,1)S(1)}, bf16[32,3200]{1,0:T(8,128)(2,1)S(1)}, u32[]{:S(2)}, u32[]{:S(2)}) %collective-permute-start.2) | collective-permute-done | bytes 204832 | tf_op jit(solution)/shard_map/ppermute | solution.py:198
  43.8 2.4 %collective-permute-done.3.refs_2_ = bf16[32,3200]{1,0:T(8,128)(2,1)S(1)} collective-permute-done((bf16[32,3200]{1,0:T(8,128)(2,1)S(1)}, bf16[32,3200]{1,0:T(8,128)(2,1)S(1)}, u32[]{:S(2)}, u32[]{:S(2)}) %collective-permute-start.3) | collective-permute-done | bytes 204832 | tf_op jit(solution)/shard_map/ppermute | solution.py:198
  46.2 2.4 %collective-permute-done.4.refs_3_ = bf16[32,3200]{1,0:T(8,128)(2,1)S(1)} collective-permute-done((bf16[32,3200]{1,0:T(8,128)(2,1)S(1)}, bf16[32,3200]{1,0:T(8,128)(2,1)S(1)}, u32[]{:S(2)}, u32[]{:S(2)}) %collective-permute-start.4) | collective-permute-done | bytes 204832 | tf_op jit(solution)/shard_map/ppermute | solution.py:198
  48.6 2.7 %collective-permute-start.5 = (bf16[128,3200]{1,0:T(8,128)(2,1)S(1)}, bf16[128,3200]{1,0:T(8,128)(2,1)S(1)}, u32[]{:S(2)}, u32[]{:S(2)}) collective-permute-start(bf16[128,3200]{1,0:T(8,128)(2,1)S(1)} %join.3.b0), channel_id=1, source_target_pairs={{0,2},{8,10},{32,34},{40,42},{64,66},{72,74},{96,98},{104,106},{4,... | collective-permute-start | bytes 2457608 | tf_op jit(solution)/shard_map/ppermute | solution.py:198
  52.6 17.8 %collective-permute-done.5.b1 = bf16[128,3200]{1,0:T(8,128)(2,1)S(1)} collective-permute-done((bf16[128,3200]{1,0:T(8,128)(2,1)S(1)}, bf16[128,3200]{1,0:T(8,128)(2,1)S(1)}, u32[]{:S(2)}, u32[]{:S(2)}) %collective-permute-start.5) | collective-permute-done | bytes 819232 | tf_op jit(solution)/shard_map/ppermute | solution.py:198
  70.4 1.7 %collective-permute-done.6.b2 = bf16[128,3200]{1,0:T(8,128)(2,1)S(1)} collective-permute-done((bf16[128,3200]{1,0:T(8,128)(2,1)S(1)}, bf16[128,3200]{1,0:T(8,128)(2,1)S(1)}, u32[]{:S(2)}, u32[]{:S(2)}) %collective-permute-start.6) | collective-permute-done | bytes 819232 | tf_op jit(solution)/shard_map/ppermute | solution.py:198
  72.2 2.0 %deal.1 = (bf16[256,3200]{1,0:T(8,128)(2,1)}, bf16[256,3200]{1,0:T(8,128)(2,1)}) custom-call(bf16[128,3200]{1,0:T(8,128)(2,1)S(1)} %join.3.b0, bf16[128,3200]{1,0:T(8,128)(2,1)S(1)} %collective-permute-done.5.b1, bf16[128,3200]{1,0:T(8,128)(2,1)S(1)} %collective-permute-done.6.b2, bf16[128,3200]{1,0:T(8,128)(2,1)S(1)} %collective-permute-done.7.b3), custom_call_target="tpu_custom_call" | custom-call | tf_op jit(solution)/shard_map/deal/pallas_call | solution.py:232
  74.1 2.2 %collective-permute-start.14 = (bf16[256,3200]{1,0:T(8,128)(2,1)}, bf16[256,3200]{1,0:T(8,128)(2,1)S(1)}, u32[]{:S(2)}, u32[]{:S(2)}) collective-permute-start(bf16[256,3200]{1,0:T(8,128)(2,1)} %get-tuple-element.26.refs_1_.a), channel_id=1, source_target_pairs={{0,4},{8,28},{32,36},{40,60},{64,68},{72,92},{96,100},{104,124},{4... | collective-permute-start | bytes 4915208 | tf_op jit(solution)/shard_map/ppermute | solution.py:198
  78.0 2.8 %weighted.4.left = bf16[512,384]{1,0:T(8,128)(2,1)S(1)} custom-call(s32[1]{0:T(128)} %bitcast.1.place, f32[1]{0:T(128)} %dynamic_slice.12.omega, bf16[256,3200]{1,0:T(8,128)(2,1)} %get-tuple-element.27.refs_0_, bf16[256,3200]{1,0:T(8,128)(2,1)} %get-tuple-element.26.refs_1_.a, f32[8,128]{1,0:T(8,128)S(1)} %broadcast_in_dim.7.refs_2_), custom_call_target="tpu_custom_call" | custom-call | tf_op jit(solution)/shard_map/weighted/pallas_call | solution.py:273
  80.8 2.7 %collective-permute-start.10 = (bf16[256,3200]{1,0:T(8,128)(2,1)}, bf16[256,3200]{1,0:T(8,128)(2,1)S(1)}, u32[]{:S(2)}, u32[]{:S(2)}) collective-permute-start(bf16[256,3200]{1,0:T(8,128)(2,1)} %get-tuple-element.27.refs_0_), channel_id=1, source_target_pairs={{0,1},{8,11},{32,33},{40,43},{64,65},{72,75},{96,97},{104,107},{4,... | collective-permute-start | bytes 4915208 | tf_op jit(solution)/shard_map/ppermute | solution.py:198
  83.5 2.0 %collective-permute-start.11 = (bf16[256,3200]{1,0:T(8,128)(2,1)}, bf16[256,3200]{1,0:T(8,128)(2,1)S(1)}, u32[]{:S(2)}, u32[]{:S(2)}) collective-permute-start(bf16[256,3200]{1,0:T(8,128)(2,1)} %get-tuple-element.27.refs_0_), channel_id=1, source_target_pairs={{0,4},{8,28},{32,36},{40,60},{64,68},{72,92},{96,100},{104,124},{4... | collective-permute-start | bytes 4915208 | tf_op jit(solution)/shard_map/ppermute | solution.py:198
  85.9 3.9 %partial_own.3 = (f32[384,3072]{1,0:T(8,128)S(1)}, f32[8,128]{1,0:T(8,128)S(1)}) custom-call(bf16[512,384]{1,0:T(8,128)(2,1)S(1)} %weighted.4.left, bf16[256,3200]{1,0:T(8,128)(2,1)} %get-tuple-element.27.refs_0_, bf16[256,3200]{1,0:T(8,128)(2,1)} %get-tuple-element.26.refs_1_.a, f32[8,128]{1,0:T(8,128)S(1)} %broadcast_in_dim.7.refs_2_), custom_call_target="tpu_custom_call" | custom-call | flops 1207959552 | bytes 12582912 | tf_op jit(solution)/shard_map/partial_own/pallas_call | solution.py:331
  89.9 3.9 %partial_other.3 = (f32[384,3072]{1,0:T(8,128)S(1)}, f32[8,128]{1,0:T(8,128)S(1)}) custom-call(bf16[512,384]{1,0:T(8,128)(2,1)S(1)} %collective-permute-done.8.left, bf16[256,3200]{1,0:T(8,128)(2,1)} %get-tuple-element.27.refs_0_, bf16[256,3200]{1,0:T(8,128)(2,1)} %get-tuple-element.26.refs_1_.a, f32[8,128]{1,0:T(8,128)S(1)} %get-tuple-element.28.refs_2_), custom_call_target="tpu_custom_call" | custom-call | flops 1207959552 | bytes 12582912 | tf_op jit(solution)/shard_map/partial_other/pallas_call | solution.py:331
  94.7 2.1 %collective-permute-done.13.refs_0_ = bf16[256,3200]{1,0:T(8,128)(2,1)S(1)} collective-permute-done((bf16[256,3200]{1,0:T(8,128)(2,1)}, bf16[256,3200]{1,0:T(8,128)(2,1)S(1)}, u32[]{:S(2)}, u32[]{:S(2)}) %collective-permute-start.13) | collective-permute-done | bytes 1638432 | tf_op jit(solution)/shard_map/ppermute | solution.py:198
  96.8 2.6 %held.1 = bf16[256,3200]{1,0:T(8,128)(2,1)} custom-call(bf16[256,3200]{1,0:T(8,128)(2,1)} %get-tuple-element.26.refs_1_.a, f32[8,128]{1,0:T(8,128)S(1)} %get-tuple-element.29._.refs_2_.refs_3_), custom_call_target="tpu_custom_call", output_to_operand_aliasing={{}: (0, {})} | custom-call | tf_op jit(solution)/shard_map/held/pallas_call | solution.py:438
  100.5 2.9 %collective-permute-start.15 = (bf16[512,384]{1,0:T(8,128)(2,1)S(1)}, bf16[512,384]{1,0:T(8,128)(2,1)S(1)}, u32[]{:S(2)}, u32[]{:S(2)}) collective-permute-start(bf16[512,384]{1,0:T(8,128)(2,1)S(1)} %weighted.5.left), channel_id=1, source_target_pairs={{0,8},{8,0},{32,40},{40,32},{64,72},{72,64},{96,104},{104,96},{4,1... | collective-permute-start | bytes 1179656 | tf_op jit(solution)/shard_map/ppermute | solution.py:198
  103.4 2.2 %partial_own.4 = (f32[384,3072]{1,0:T(8,128)S(1)}, f32[8,128]{1,0:T(8,128)S(1)}) custom-call(bf16[512,384]{1,0:T(8,128)(2,1)S(1)} %weighted.5.left, bf16[256,3200]{1,0:T(8,128)(2,1)S(1)} %collective-permute-done.13.refs_0_, bf16[256,3200]{1,0:T(8,128)(2,1)S(1)} %collective-permute-done.14.refs_1_, ...), custom_call_target="tpu_custom_call", output_to_operand_aliasing={{0}: (3, {})} | custom-call | flops 1207959552 | bytes 12582912 | tf_op jit(solution)/shard_map/partial_own/pallas_call | solution.py:331
  105.6 2.2 %partial_other.4 = (f32[384,3072]{1,0:T(8,128)S(1)}, f32[8,128]{1,0:T(8,128)S(1)}) custom-call(bf16[512,384]{1,0:T(8,128)(2,1)S(1)} %collective-permute-done.15.left, bf16[256,3200]{1,0:T(8,128)(2,1)S(1)} %collective-permute-done.13.refs_0_, bf16[256,3200]{1,0:T(8,128)(2,1)S(1)} %collective-permute-done.14.refs_1_, ...), custom_call_target="tpu_custom_call", output_to_operand_aliasing={{0}: (3, {})} | custom-call | flops 1207959552 | bytes 12582912 | tf_op jit(solution)/shard_map/partial_other/pallas_call | solution.py:331
  107.7 6.6 %collective-permute-done.10.refs_0_ = bf16[256,3200]{1,0:T(8,128)(2,1)S(1)} collective-permute-done((bf16[256,3200]{1,0:T(8,128)(2,1)}, bf16[256,3200]{1,0:T(8,128)(2,1)S(1)}, u32[]{:S(2)}, u32[]{:S(2)}) %collective-permute-start.10) | collective-permute-done | bytes 1638432 | tf_op jit(solution)/shard_map/ppermute | solution.py:198
  115.3 2.9 %collective-permute-start.16 = (bf16[768,384]{1,0:T(8,128)(2,1)S(1)}, bf16[768,384]{1,0:T(8,128)(2,1)S(1)}, u32[]{:S(2)}, u32[]{:S(2)}) collective-permute-start(bf16[768,384]{1,0:T(8,128)(2,1)S(1)} %weighted.6.left), channel_id=1, source_target_pairs={{0,8},{8,0},{32,40},{40,32},{64,72},{72,64},{96,104},{104,96},{4,1... | collective-permute-start | bytes 1769480 | tf_op jit(solution)/shard_map/ppermute | solution.py:198
  118.2 2.7 %partial_own.5 = (f32[384,3072]{1,0:T(8,128)S(1)}, f32[8,128]{1,0:T(8,128)S(1)}) custom-call(bf16[768,384]{1,0:T(8,128)(2,1)S(1)} %weighted.6.left, bf16[256,3200]{1,0:T(8,128)(2,1)S(1)} %collective-permute-done.10.refs_0_, bf16[256,3200]{1,0:T(8,128)(2,1)S(1)} %collective-permute-done.11.refs_1_, ...), custom_call_target="tpu_custom_call", output_to_operand_aliasing={{0}: (4, {})} | custom-call | flops 1811939328 | bytes 14155776 | tf_op jit(solution)/shard_map/partial_own/pallas_call | solution.py:331
  120.9 2.7 %partial_other.5 = (f32[384,3072]{1,0:T(8,128)S(1)}, f32[8,128]{1,0:T(8,128)S(1)}) custom-call(bf16[768,384]{1,0:T(8,128)(2,1)S(1)} %collective-permute-done.16.left, bf16[256,3200]{1,0:T(8,128)(2,1)S(1)} %collective-permute-done.10.refs_0_, bf16[256,3200]{1,0:T(8,128)(2,1)S(1)} %collective-permute-done.11.refs_1_, ...), custom_call_target="tpu_custom_call", output_to_operand_aliasing={{0}: (4, {})} | custom-call | flops 1811939328 | bytes 14155776 | tf_op jit(solution)/shard_map/partial_other/pallas_call | solution.py:331
  125.7 1.8 %own_rows.2 = (f32[384,6144]{1,0:T(8,128)}, f32[8,128]{1,0:T(8,128)S(1)}) custom-call(s32[1]{0:T(128)} %bitcast.core, bf16[256,384]{1,0:T(8,128)(2,1)S(1)} %weighted.7.left, bf16[256,3200]{1,0:T(8,128)(2,1)S(1)} %collective-permute-done.9.refs_0_, f32[384,3072]{1,0:T(8,128)S(1)} %get-tuple-element.39.refs_1_, f32[8,128]{1,0:T(8,128)S(1)} %get-tuple-element.37.refs_1_.refs_2_), custom_call_target="tpu_custom_call" | custom-call | flops 301989888 | bytes 5505024 | tf_op jit(solution)/shard_map/own_rows/pallas_call | solution.py:367
  129.7 2.4 %own_rows.3 = (f32[384,6144]{1,0:T(8,128)}, f32[8,128]{1,0:T(8,128)}) custom-call(s32[1]{0:T(128)} %bitcast.core, bf16[256,384]{1,0:T(8,128)(2,1)S(1)} %weighted.7.left, bf16[256,3200]{1,0:T(8,128)(2,1)S(1)} %collective-permute-done.9.refs_0_, f32[384,3072]{1,0:T(8,128)S(1)} %get-tuple-element.39.refs_1_, ...), custom_call_target="tpu_custom_call", output_to_operand_aliasing={{0}: (4, {})} | custom-call | flops 301989888 | bytes 5505024 | tf_op jit(solution)/shard_map/own_rows/pallas_call | solution.py:367
  132.9 2.3 %finish.1 = f32[384,6144]{1,0:T(8,128)} custom-call(s32[1]{0:T(128)} %bitcast.core, bf16[384,1536]{1,0:T(8,128)(2,1)S(1)} %collective-permute-done.18.r0, bf16[384,1536]{1,0:T(8,128)(2,1)S(1)} %collective-permute-done.19.r1, f32[384,6144]{1,0:T(8,128)} %get-tuple-element.42._), custom_call_target="tpu_custom_call", output_to_operand_aliasing={{}: (3, {})} | custom-call | tf_op jit(solution)/shard_map/finish/pallas_call | solution.py:421
  (60 shorter events, 18.8 us)
Async XLA Ops:
  0.0 0.9 copy-start
  1.0 0.7 copy-start.5
  1.7 21.8 %copy-start.1 = (bf16[2,256,256]{2,1,0:T(8,128)(2,1)S(1)}, bf16[2,256,256]{2,1,0:T(8,128)(2,1)}, u32[]{:S(2)}) copy-start(bf16[2,256,256]{2,1,0:T(8,128)(2,1)} %constant.39.clone.first) | copy-start | bytes 786436
  1.7 21.8 %copy-start.2 = (bf16[512,256]{1,0:T(8,128)(2,1)S(1)}, bf16[512,256]{1,0:T(8,128)(2,1)}, u32[]{:S(2)}) copy-start(bf16[512,256]{1,0:T(8,128)(2,1)} %constant.42.clone.second) | copy-start | bytes 786436
  1.7 21.8 %copy-start.3 = (f32[128,256]{1,0:T(8,128)S(1)}, f32[128,256]{1,0:T(8,128)}, u32[]{:S(2)}) copy-start(f32[128,256]{1,0:T(8,128)} %constant.40.clone.tcos) | copy-start | bytes 393220
  1.7 21.8 %copy-start.4 = (f32[128,256]{1,0:T(8,128)S(1)}, f32[128,256]{1,0:T(8,128)}, u32[]{:S(2)}) copy-start(f32[128,256]{1,0:T(8,128)} %constant.41.clone.tsin) | copy-start | bytes 393220
  2.5 17.5 %all-to-all-start = ((bf16[8,24,1024]{2,1,0:T(8,128)(2,1)}), bf16[8,24,1024]{2,1,0:T(8,128)(2,1)S(1)}, u32[]{:S(2)}, u32[]{:S(2)}) async-start(bf16[8,24,1024]{2,1,0:T(8,128)(2,1)} %payload.1), calls=%async_computation | async-start | bytes 786432 | tf_op jit(solution)/shard_map/all_to_all | solution.py:458
  19.9 3.5 %collective-permute-start = (bf16[8,24,1024]{2,1,0:T(8,128)(2,1)S(1)}, bf16[8,24,1024]{2,1,0:T(8,128)(2,1)S(1)}, u32[]{:S(2)}, u32[]{:S(2)}) collective-permute-start(bf16[8,24,1024]{2,1,0:T(8,128)(2,1)S(1)} %all-to-all-done.mine), channel_id=1, source_target_pairs={{0,8},{8,0},{32,40},{40,32},{64,72},{72,64},{96,104},{104,96},{4,1... | collective-permute-start | bytes 1179656 | tf_op jit(solution)/shard_map/ppermute | solution.py:198
  28.0 2.8 %collective-permute-start.1 = (bf16[16,3200]{1,0:T(8,128)(2,1)S(1)}, bf16[16,3200]{1,0:T(8,128)(2,1)S(1)}, u32[]{:S(2)}, u32[]{:S(2)}) collective-permute-start(bf16[16,3200]{1,0:T(8,128)(2,1)S(1)} %get-tuple-element.25), channel_id=1, source_target_pairs={{0,8},{8,0},{32,40},{40,32},{64,72},{72,64},{96,104},{104,96},{4,1... | collective-permute-start | bytes 307208 | tf_op jit(solution)/shard_map/ppermute | solution.py:198
  30.8 12.9 %collective-permute-start.2 = (bf16[32,3200]{1,0:T(8,128)(2,1)S(1)}, bf16[32,3200]{1,0:T(8,128)(2,1)S(1)}, u32[]{:S(2)}, u32[]{:S(2)}) collective-permute-start(bf16[32,3200]{1,0:T(8,128)(2,1)S(1)} %join.2.refs_0_), channel_id=1, source_target_pairs={{0,82},{8,90},{32,114},{40,122},{64,18},{72,26},{96,50},{104,58},{... | collective-permute-start | bytes 614408 | tf_op jit(solution)/shard_map/ppermute | solution.py:198
  34.0 12.1 %collective-permute-start.3 = (bf16[32,3200]{1,0:T(8,128)(2,1)S(1)}, bf16[32,3200]{1,0:T(8,128)(2,1)S(1)}, u32[]{:S(2)}, u32[]{:S(2)}) collective-permute-start(bf16[32,3200]{1,0:T(8,128)(2,1)S(1)} %join.2.refs_0_), channel_id=1, source_target_pairs={{0,37},{8,127},{32,69},{40,31},{64,101},{72,63},{96,5},{104,95},{4... | collective-permute-start | bytes 614408 | tf_op jit(solution)/shard_map/ppermute | solution.py:198
  38.5 10.0 %collective-permute-start.4 = (bf16[32,3200]{1,0:T(8,128)(2,1)S(1)}, bf16[32,3200]{1,0:T(8,128)(2,1)S(1)}, u32[]{:S(2)}, u32[]{:S(2)}) collective-permute-start(bf16[32,3200]{1,0:T(8,128)(2,1)S(1)} %join.2.refs_0_), channel_id=1, source_target_pairs={{0,119},{8,45},{32,23},{40,77},{64,55},{72,109},{96,87},{104,13},{... | collective-permute-start | bytes 614408 | tf_op jit(solution)/shard_map/ppermute | solution.py:198
  48.6 28.7 %copy-start.6 = (f32[8]{0:T(128)S(1)}, f32[8]{0:T(128)}, u32[]{:S(2)}) copy-start(f32[8]{0:T(128)} %param.16) | copy-start | bytes 100
  48.6 21.8 %collective-permute-start.5 = (bf16[128,3200]{1,0:T(8,128)(2,1)S(1)}, bf16[128,3200]{1,0:T(8,128)(2,1)S(1)}, u32[]{:S(2)}, u32[]{:S(2)}) collective-permute-start(bf16[128,3200]{1,0:T(8,128)(2,1)S(1)} %join.3.b0), channel_id=1, source_target_pairs={{0,2},{8,10},{32,34},{40,42},{64,66},{72,74},{96,98},{104,106},{4,... | collective-permute-start | bytes 2457608 | tf_op jit(solution)/shard_map/ppermute | solution.py:198
  51.3 20.8 %collective-permute-start.6 = (bf16[128,3200]{1,0:T(8,128)(2,1)S(1)}, bf16[128,3200]{1,0:T(8,128)(2,1)S(1)}, u32[]{:S(2)}, u32[]{:S(2)}) collective-permute-start(bf16[128,3200]{1,0:T(8,128)(2,1)S(1)} %join.3.b0), channel_id=1, source_target_pairs={{0,16},{8,24},{32,48},{40,56},{64,80},{72,88},{96,112},{104,120},{... | collective-permute-start | bytes 2457608 | tf_op jit(solution)/shard_map/ppermute | solution.py:198
  52.0 20.2 %collective-permute-start.7 = (bf16[128,3200]{1,0:T(8,128)(2,1)S(1)}, bf16[128,3200]{1,0:T(8,128)(2,1)S(1)}, u32[]{:S(2)}, u32[]{:S(2)}) collective-permute-start(bf16[128,3200]{1,0:T(8,128)(2,1)S(1)} %join.3.b0), channel_id=1, source_target_pairs={{0,64},{8,72},{32,96},{40,104},{64,0},{72,8},{96,32},{104,40},{4,6... | collective-permute-start | bytes 2457608 | tf_op jit(solution)/shard_map/ppermute | solution.py:198
  74.1 20.6 %collective-permute-start.14 = (bf16[256,3200]{1,0:T(8,128)(2,1)}, bf16[256,3200]{1,0:T(8,128)(2,1)S(1)}, u32[]{:S(2)}, u32[]{:S(2)}) collective-permute-start(bf16[256,3200]{1,0:T(8,128)(2,1)} %get-tuple-element.26.refs_1_.a), channel_id=1, source_target_pairs={{0,4},{8,28},{32,36},{40,60},{64,68},{72,92},{96,100},{104,124},{4... | collective-permute-start | bytes 4915208 | tf_op jit(solution)/shard_map/ppermute | solution.py:198
  76.3 20.5 %collective-permute-start.13 = (bf16[256,3200]{1,0:T(8,128)(2,1)}, bf16[256,3200]{1,0:T(8,128)(2,1)S(1)}, u32[]{:S(2)}, u32[]{:S(2)}) collective-permute-start(bf16[256,3200]{1,0:T(8,128)(2,1)} %get-tuple-element.26.refs_1_.a), channel_id=1, source_target_pairs={{0,1},{8,11},{32,33},{40,43},{64,65},{72,75},{96,97},{104,107},{4,... | collective-permute-start | bytes 4915208 | tf_op jit(solution)/shard_map/ppermute | solution.py:198
  80.7 4.8 %collective-permute-start.8 = (bf16[512,384]{1,0:T(8,128)(2,1)S(1)}, bf16[512,384]{1,0:T(8,128)(2,1)S(1)}, u32[]{:S(2)}, u32[]{:S(2)}) collective-permute-start(bf16[512,384]{1,0:T(8,128)(2,1)S(1)} %weighted.4.left), channel_id=1, source_target_pairs={{0,8},{8,0},{32,40},{40,32},{64,72},{72,64},{96,104},{104,96},{4,1... | collective-permute-start | bytes 1179656 | tf_op jit(solution)/shard_map/ppermute | solution.py:198
  80.8 33.5 %collective-permute-start.10 = (bf16[256,3200]{1,0:T(8,128)(2,1)}, bf16[256,3200]{1,0:T(8,128)(2,1)S(1)}, u32[]{:S(2)}, u32[]{:S(2)}) collective-permute-start(bf16[256,3200]{1,0:T(8,128)(2,1)} %get-tuple-element.27.refs_0_), channel_id=1, source_target_pairs={{0,1},{8,11},{32,33},{40,43},{64,65},{72,75},{96,97},{104,107},{4,... | collective-permute-start | bytes 4915208 | tf_op jit(solution)/shard_map/ppermute | solution.py:198
  83.5 30.8 %collective-permute-start.11 = (bf16[256,3200]{1,0:T(8,128)(2,1)}, bf16[256,3200]{1,0:T(8,128)(2,1)S(1)}, u32[]{:S(2)}, u32[]{:S(2)}) collective-permute-start(bf16[256,3200]{1,0:T(8,128)(2,1)} %get-tuple-element.27.refs_0_), channel_id=1, source_target_pairs={{0,4},{8,28},{32,36},{40,60},{64,68},{72,92},{96,100},{104,124},{4... | collective-permute-start | bytes 4915208 | tf_op jit(solution)/shard_map/ppermute | solution.py:198
  85.5 28.8 %collective-permute-start.12 = (bf16[256,3200]{1,0:T(8,128)(2,1)}, bf16[256,3200]{1,0:T(8,128)(2,1)S(1)}, u32[]{:S(2)}, u32[]{:S(2)}) collective-permute-start(bf16[256,3200]{1,0:T(8,128)(2,1)} %get-tuple-element.27.refs_0_), channel_id=1, source_target_pairs={{0,32},{8,104},{32,64},{40,8},{64,96},{72,40},{96,0},{104,72},{4,3... | collective-permute-start | bytes 4915208 | tf_op jit(solution)/shard_map/ppermute | solution.py:198
  99.4 24.2 %collective-permute-start.9 = (bf16[256,3200]{1,0:T(8,128)(2,1)}, bf16[256,3200]{1,0:T(8,128)(2,1)S(1)}, u32[]{:S(2)}, u32[]{:S(2)}) collective-permute-start(bf16[256,3200]{1,0:T(8,128)(2,1)} %held.1), channel_id=1, source_target_pairs={{0,32},{8,104},{32,64},{40,8},{64,96},{72,40},{96,0},{104,72},{4,3... | collective-permute-start | bytes 4915208 | tf_op jit(solution)/shard_map/ppermute | solution.py:198
  100.5 5.1 %collective-permute-start.15 = (bf16[512,384]{1,0:T(8,128)(2,1)S(1)}, bf16[512,384]{1,0:T(8,128)(2,1)S(1)}, u32[]{:S(2)}, u32[]{:S(2)}) collective-permute-start(bf16[512,384]{1,0:T(8,128)(2,1)S(1)} %weighted.5.left), channel_id=1, source_target_pairs={{0,8},{8,0},{32,40},{40,32},{64,72},{72,64},{96,104},{104,96},{4,1... | collective-permute-start | bytes 1179656 | tf_op jit(solution)/shard_map/ppermute | solution.py:198
  115.3 5.6 %collective-permute-start.16 = (bf16[768,384]{1,0:T(8,128)(2,1)S(1)}, bf16[768,384]{1,0:T(8,128)(2,1)S(1)}, u32[]{:S(2)}, u32[]{:S(2)}) collective-permute-start(bf16[768,384]{1,0:T(8,128)(2,1)S(1)} %weighted.6.left), channel_id=1, source_target_pairs={{0,8},{8,0},{32,40},{40,32},{64,72},{72,64},{96,104},{104,96},{4,1... | collective-permute-start | bytes 1769480 | tf_op jit(solution)/shard_map/ppermute | solution.py:198
  124.4 3.1 %collective-permute-start.17 = (bf16[256,384]{1,0:T(8,128)(2,1)S(1)}, bf16[256,384]{1,0:T(8,128)(2,1)S(1)}, u32[]{:S(2)}, u32[]{:S(2)}) collective-permute-start(bf16[256,384]{1,0:T(8,128)(2,1)S(1)} %weighted.7.left), channel_id=1, source_target_pairs={{0,8},{8,0},{32,40},{40,32},{64,72},{72,64},{96,104},{104,96},{4,1... | collective-permute-start | bytes 589832 | tf_op jit(solution)/shard_map/ppermute | solution.py:198
  128.3 3.9 %collective-permute-start.18 = (bf16[384,1536]{1,0:T(8,128)(2,1)S(1)}, bf16[384,1536]{1,0:T(8,128)(2,1)S(1)}, u32[]{:S(2)}, u32[]{:S(2)}) collective-permute-start(bf16[384,1536]{1,0:T(8,128)(2,1)S(1)} %other_rows.2), channel_id=1, source_target_pairs={{0,8},{8,0},{32,40},{40,32},{64,72},{72,64},{96,104},{104,96},{4,1... | collective-permute-start | bytes 3538952 | tf_op jit(solution)/shard_map/ppermute | solution.py:198
  129.1 3.8 %collective-permute-start.19 = (bf16[384,1536]{1,0:T(8,128)(2,1)S(1)}, bf16[384,1536]{1,0:T(8,128)(2,1)S(1)}, u32[]{:S(2)}, u32[]{:S(2)}) collective-permute-start(bf16[384,1536]{1,0:T(8,128)(2,1)S(1)} %other_rows.3), channel_id=1, source_target_pairs={{0,8},{8,0},{32,40},{40,32},{64,72},{72,64},{96,104},{104,96},{4,1... | collective-permute-start | bytes 3538952 | tf_op jit(solution)/shard_map/ppermute | solution.py:198

commit v8 on v7

--- a/solution.py
+++ b/solution.py
@@ -58,11 +58,19 @@
     return np.stack(first), tcos, tsin, np.concatenate([sh, sl], 1)
 
 
-def payload_kernel(val, con, out):
-    v = val[...].astype(jnp.float32)
+def payload_kernel(val, con, out, val_here, con_here, sem):
+    copies = [
+        pltpu.make_async_copy(val, val_here, sem.at[0]),
+        pltpu.make_async_copy(con, con_here, sem.at[1]),
+    ]
+    for copy in copies:
+        copy.start()
+    for copy in copies:
+        copy.wait()
+    v = val_here[...].astype(jnp.float32)
     values = jnp.concatenate([v[:, :1024], v[:, 1024:]], 0)
     for chip in range(8):
-        c = con[chip * 8 : chip * 8 + 8, :].astype(jnp.float32)
+        c = con_here[chip * 8 : chip * 8 + 8, :].astype(jnp.float32)
         rows = jnp.concatenate([c[:, :1024], c[:, 1024:], values], 0)
         out[chip] = rows.astype(jnp.bfloat16)
 
@@ -71,8 +79,13 @@
     return pl.pallas_call(
         payload_kernel,
         out_shape=jax.ShapeDtypeStruct((8, 24, 1024), jnp.bfloat16),
-        in_specs=[VM] * 2,
+        in_specs=[HBM] * 2,
         out_specs=VM,
+        scratch_shapes=[
+            pltpu.VMEM(val.shape, val.dtype),
+            pltpu.VMEM(con.shape, con.dtype),
+            pltpu.SemaphoreType.DMA((2,)),
+        ],
         compiler_params=PARAMS,
         name="payload",
     )(val, con)
@@ -222,21 +235,27 @@
     )(*blocks)
 
 
-def deal_kernel(b0, b1, b2, b3, out0, out1):
+def deal_kernel(b0, b1, b2, b3, out0, out1, both):
     for i, ref in enumerate((b0, b1, b2, b3)):
-        out0[i * 64 : i * 64 + 64, :] = ref[0:64, :]
-        out1[i * 64 : i * 64 + 64, :] = ref[64:128, :]
+        for half, out in enumerate((out0, out1)):
+            rows = ref[half * 64 : half * 64 + 64, :]
+            out[i * 64 : i * 64 + 64, :] = rows
+            both[half * 256 + i * 64 : half * 256 + i * 64 + 64, :] = rows
 
 
 def deal(blocks):
     return pl.pallas_call(
         deal_kernel,
-        out_shape=[jax.ShapeDtypeStruct((256, WIDE), jnp.bfloat16)] * 2,
+        out_shape=[jax.ShapeDtypeStruct((rows, WIDE), jnp.bfloat16) for rows in (256, 256, 512)],
         in_specs=[VM] * 4,
-        out_specs=[VM] * 2,
+        out_specs=[VM] * 3,
         compiler_params=PARAMS,
         name="deal",
     )(*blocks)
+
+
+def halves(refs):
+    return [ref.at[pl.ds(at, 256)] for ref in refs for at in range(0, ref.shape[0], 256)]
 
 
 def place_of(half, step):
@@ -252,7 +271,7 @@
 
 
 def weighted_kernel(place, omega, *refs):
-    pieces, left = refs[:-2], refs[-1]
+    pieces, left = halves(refs[:-2]), refs[-1]
     w2 = omega[0] * omega[0]
     row = lax.broadcasted_iota(jnp.int32, (LANES, 2 * LANES), 0)
     lane = lax.broadcasted_iota(jnp.int32, (LANES, 2 * LANES), 1)
@@ -272,7 +291,7 @@
 def weighted(place, omega, pieces, tie):
     return pl.pallas_call(
         weighted_kernel,
-        out_shape=jax.ShapeDtypeStruct((256 * len(pieces), ROWS), jnp.bfloat16),
+        out_shape=jax.ShapeDtypeStruct((sum(p.shape[0] for p in pieces), ROWS), jnp.bfloat16),
         in_specs=[SM, SM] + [VM] * (len(pieces) + 1),
         out_specs=VM,
         compiler_params=PARAMS,
@@ -310,8 +329,8 @@
     )
 
 
-def partial_kernel(names, other, left, *refs):
-    pieces, before = refs[: len(names)], refs[len(names) : -3]
+def partial_kernel(names, n, other, left, *refs):
+    pieces, before = halves(refs[:n]), refs[n:-3]
     out, after = refs[-2:]
     after[...] = jnp.zeros_like(after)
 
@@ -329,20 +348,20 @@
 def partial_rows(names, other, left, pieces, before, tie):
     before = [] if before is None else [before]
     return pl.pallas_call(
-        functools.partial(partial_kernel, names, other),
+        functools.partial(partial_kernel, names, len(pieces), other),
         out_shape=[jax.ShapeDtypeStruct((ROWS, HALF), jnp.float32), TIE],
-        in_specs=[VM] * (2 + len(names) + len(before)),
+        in_specs=[VM] * (2 + len(pieces) + len(before)),
         out_specs=[VM] * 2,
-        input_output_aliases={1 + len(names): 0} if before else {},
+        input_output_aliases={1 + len(pieces): 0} if before else {},
         compiler_params=PARAMS,
         cost_estimate=cost(names, HALF),
         name="partial_other" if other else "partial_own",
     )(left, *pieces, *before, tie)
 
 
-def own_kernel(names, start, core, left, *refs):
-    pieces = refs[: len(names)]
-    before, _, out, tie, wide, sem = refs[len(names) :]
+def own_kernel(names, n, start, core, left, *refs):
+    pieces = halves(refs[:n])
+    before, _, out, tie, wide, sem = refs[n:]
     tie[...] = jnp.zeros_like(tie)
     copies = []
     for i in range(2):
@@ -365,21 +384,21 @@
 def own_rows(names, start, core, left, pieces, before, after):
     grows = after.shape == (ROWS, NG)
     return pl.pallas_call(
-        functools.partial(own_kernel, names, start),
+        functools.partial(own_kernel, names, len(pieces), start),
         out_shape=[jax.ShapeDtypeStruct((ROWS, NG), jnp.float32), TIE],
-        in_specs=[SM, VM] + [VM] * (len(names) + 1) + [HBM if grows else VM],
+        in_specs=[SM, VM] + [VM] * (len(pieces) + 1) + [HBM if grows else VM],
         out_specs=[HBM, VM],
         scratch_shapes=[pltpu.VMEM((ROWS, HALF // 2), jnp.float32), pltpu.SemaphoreType.DMA((4,))],
-        input_output_aliases={3 + len(names): 0} if grows else {},
+        input_output_aliases={3 + len(pieces): 0} if grows else {},
         compiler_params=PARAMS,
         cost_estimate=cost(names, HALF // 2),
         name="own_rows",
     )(core, left, *pieces, before, after)
 
 
-def other_kernel(names, start, left, *refs):
-    pieces = refs[: len(names)]
-    before, _, out = refs[len(names) :]
+def other_kernel(names, n, start, left, *refs):
+    pieces = halves(refs[:n])
+    before, _, out = refs[n:]
 
     def step(i, carry):
         total = product(names, True, left, pieces, chunk(i, start=start)) + before[:, chunk(i, start=start)]
@@ -391,9 +410,9 @@
 
 def other_rows(names, start, left, pieces, before, tie):
     return pl.pallas_call(
-        functools.partial(other_kernel, names, start),
+        functools.partial(other_kernel, names, len(pieces), start),
         out_shape=jax.ShapeDtypeStruct((ROWS, HALF // 2), jnp.bfloat16),
-        in_specs=[VM] * (len(names) + 3),
+        in_specs=[VM] * (len(pieces) + 3),
         out_specs=VM,
         compiler_params=PARAMS,
         cost_estimate=cost(names, HALF // 2),
@@ -430,22 +449,6 @@
     )(core, *rows, out)
 
 
-def held_kernel(a, _, out):
-    pass
-
-
-def held(a, tie):
-    return pl.pallas_call(
-        held_kernel,
-        out_shape=jax.ShapeDtypeStruct(a.shape, a.dtype),
-        in_specs=[VM] * 2,
-        out_specs=VM,
-        input_output_aliases={0: 0},
-        compiler_params=PARAMS,
-        name="held",
-    )(a, tie)
-
-
 def in_vmem(a):
     return pltpu.with_memory_space_constraint(a, pltpu.VMEM)
 
@@ -466,35 +469,34 @@
     meta = jnp.stack([d1, d2, d3, taken], 1).astype(jnp.bfloat16)
     meta = jnp.pad(meta, ((0, 0), (0, LANES - 4)))
 
-    halves = g_index.reshape(8, 2, ROWS).transpose(1, 0, 2).reshape(2, HALF)
-    kept = lax.dynamic_slice(halves, (core, 0), (1, HALF))
-    given = lax.dynamic_slice(halves, (1 - core, 0), (1, HALF))
+    kinds_of_rows = g_index.reshape(8, 2, ROWS).transpose(1, 0, 2).reshape(2, HALF)
+    kept = lax.dynamic_slice(kinds_of_rows, (core, 0), (1, HALF))
+    given = lax.dynamic_slice(kinds_of_rows, (1 - core, 0), (1, HALF))
     spec, give = rho_spectrum(core.reshape(1), psi, psi_other, given, meta)
     swapped = send(give, core_pairs())
     keep = rho_pick(spec, kept, meta)
 
     a = join(level(join([keep, swapped]), NEAR))
-    sources = deal(level(a, EVEN))
+    *sources, both = deal(level(a, EVEN))
     got = {(h, 0): m for h, m in enumerate(sources)}
     for h in range(2):
-        for s in range(1, 3 + (h == 0)):
+        for s in (1, 2):
             got[h, s] = send(sources[h], offset_pairs(STEP[s]))
+    got["z"] = send(both, offset_pairs(STEP[3]))
 
     place = lax.div(ga, 2).astype(jnp.int32).reshape(1)
     mine_omega = lax.dynamic_slice(omega, (ba,), (1,))
     core = core.reshape(1)
     own = other = None
     tie = jnp.zeros(TIE.shape, TIE.dtype)
-    groups = (((0, 0), (1, 0)), ((1, 1), (1, 2)), ((0, 1), (0, 2), (0, 3)), ((1, 3),))
+    groups = (((0, 0), (1, 0)), ((0, 1), (0, 2)), ((1, 1), (1, 2)), ((0, 3), (1, 3)))
     for names in groups:
-        pieces = [in_vmem(got[name]) for name in names]
+        pieces = [in_vmem(got[name]) for name in (("z",) if names is groups[-1] else names)]
         left = weighted(place, mine_omega, pieces, tie)
         mirror = send(left, core_pairs())
         if names is not groups[-1]:
             own, tie = partial_rows(names, False, left, pieces, own, tie)
             other, tie = partial_rows(names, True, mirror, pieces, other, tie)
-        if names is groups[0]:
-            got[1, 3] = send(held(sources[1], tie), offset_pairs(STEP[3]))
     out, tie = own_rows(names, 0, core, left, pieces, own, tie)
     rows = [send(other_rows(names, s, mirror, pieces, other, tie), core_pairs()) for s in (0, HALF // 2)]
     out, _ = own_rows(names, HALF // 2, core, left, pieces, own, out)

time: 136 us -> 140 us (1.029)
  Pallas kernels: 43.3 us -> 47.9 us
  waiting for transfers between devices: 47 us -> 42.5 us
  local copies, waits for them, and re-layouts: 4.16 us -> 7.85 us
    ppermute x20 -> x19, waiting for transfers between devices: 41.2 us -> 36.6 us  [send(): return lax.ppermute(a, ('ga', 'ba'), pairs)]
    pallas_call x16 -> x15, Pallas kernels: 33.3 us -> 37.7 us  [the longest x6 20.4 us: partial_rows(): pl.pallas_call(functools.partial(partial_kernel, names, len(pieces), othe...]
    unnamed x14, local copies, waits for them, and re-layouts: 1.69 us -> 5.38 us
    ppermute x20 -> x19, starting transfers between devices: 30.6 us -> 30.9 us  [send(): return lax.ppermute(a, ('ga', 'ba'), pairs)]
  transfers between devices with their start and end apart: 21 -> 20, of which waited for: 11 -> 12; matrix products, arithmetic and copies ran while one was open for 3% -> 3% of each run, Pallas kernels for 24% -> 25%
where the time goes in v8:
time: 140 us; the launch traced here: 139 us
  Pallas kernels  47.9 us (34%)
  waiting for transfers between devices  42.5 us (30%)
  starting transfers between devices  39.4 us (28%)
  local copies, waits for them, and re-layouts  7.85 us (6%)
  other arithmetic  1.41 us (1%)
    ppermute x19, waiting for transfers between devices, send(): return lax.ppermute(a, ('ga', 'ba'), pairs)  36.6 us
    ppermute x19, starting transfers between devices, send(): return lax.ppermute(a, ('ga', 'ba'), pairs)  30.9 us
    pallas_call x6, Pallas kernels, partial_rows(): pl.pallas_call(functools.partial(partial_kernel, names, len(pieces), othe...  20.4 us
    all_to_all x1, starting transfers between devices, on_device(): lax.all_to_all(payload(psi_val, psi_con), 'ga', 0, 0, tiled=True, axis_in...  8.51 us
    pallas_call x4, Pallas kernels, weighted(): pl.pallas_call(weighted_kernel, out_shape=jax.ShapeDtypeStruct((sum((p.sh...  7.33 us
    all_to_all x1, waiting for transfers between devices, on_device(): lax.all_to_all(payload(psi_val, psi_con), 'ga', 0, 0, tiled=True, axis_in...  5.85 us
    unnamed x14, local copies, waits for them, and re-layouts  5.38 us
    pallas_call x1, Pallas kernels, rho_spectrum(): pl.pallas_call(transform_kernel, out_shape=[jax.ShapeDtypeStruct((PAIRS *...  4.7 us
  transfers between devices with their start and end apart: 20, of which 12 were waited for; matrix products, arithmetic and copies ran while one was open for 3% of the time, Pallas kernels for 25%

profile of v8, /device:TPU:1, one launch (start us, length us, event | category | flops | bytes accessed | tf_op | source)
XLA Modules:
  0.0 139.4 jit_solution(7149303519395292948)
XLA Ops:
  2.5 8.5 %all-to-all-start = ((bf16[8,24,1024]{2,1,0:T(8,128)(2,1)}), bf16[8,24,1024]{2,1,0:T(8,128)(2,1)S(1)}, u32[]{:S(2)}, u32[]{:S(2)}) async-start(bf16[8,24,1024]{2,1,0:T(8,128)(2,1)} %payload.1), calls=%async_computation | async-start | bytes 786432 | tf_op jit(solution)/shard_map/all_to_all | solution.py:461
  14.1 5.8 %all-to-all-done.mine = bf16[8,24,1024]{2,1,0:T(8,128)(2,1)S(1)} async-done(((bf16[8,24,1024]{2,1,0:T(8,128)(2,1)}), bf16[8,24,1024]{2,1,0:T(8,128)(2,1)S(1)}, u32[]{:S(2)}, u32[]{:S(2)}) %all-to-all-start) | async-done | bytes 393248 | tf_op jit(solution)/shard_map/all_to_all | solution.py:461
  20.0 2.2 %collective-permute-start = (bf16[8,24,1024]{2,1,0:T(8,128)(2,1)S(1)}, bf16[8,24,1024]{2,1,0:T(8,128)(2,1)S(1)}, u32[]{:S(2)}, u32[]{:S(2)}) collective-permute-start(bf16[8,24,1024]{2,1,0:T(8,128)(2,1)S(1)} %all-to-all-done.mine), channel_id=1, source_target_pairs={{0,8},{8,0},{32,40},{40,32},{64,72},{72,64},{96,104},{104,96},{4,1... | collective-permute-start | bytes 1179656 | tf_op jit(solution)/shard_map/ppermute | solution.py:211
  27.2 4.7 %rho_spectrum.1 = (bf16[1024,256]{1,0:T(8,128)(2,1)S(1)}, bf16[16,3200]{1,0:T(8,128)(2,1)S(1)}) custom-call(s32[1]{0:T(128)} %bitcast.core, bf16[8,24,1024]{2,1,0:T(8,128)(2,1)S(1)} %all-to-all-done.mine, bf16[8,24,1024]{2,1,0:T(8,128)(2,1)S(1)} %collective-permute-done.others, s32[1,3072]{1,0:T(1,128)S(1)} %get-tuple-element.46.gidx, ...), custom_call_target="tpu_custom_call" | custom-call | tf_op jit(solution)/shard_map/rho_spectrum/pallas_call | solution.py:164
  32.3 2.3 %rho_pick.1.refs_0_ = bf16[16,3200]{1,0:T(8,128)(2,1)S(1)} custom-call(bf16[1024,256]{1,0:T(8,128)(2,1)S(1)} %get-tuple-element.25.spec, s32[1,3072]{1,0:T(1,128)S(1)} %get-tuple-element.45.gidx, bf16[16,128]{1,0:T(8,128)(2,1)S(1)} %pad.4.meta), custom_call_target="tpu_custom_call" | custom-call | tf_op jit(solution)/shard_map/rho_pick/pallas_call | solution.py:180
  34.7 3.2 %collective-permute-start.2 = (bf16[32,3200]{1,0:T(8,128)(2,1)S(1)}, bf16[32,3200]{1,0:T(8,128)(2,1)S(1)}, u32[]{:S(2)}, u32[]{:S(2)}) collective-permute-start(bf16[32,3200]{1,0:T(8,128)(2,1)S(1)} %join.2.refs_0_), channel_id=1, source_target_pairs={{0,82},{8,90},{32,114},{40,122},{64,18},{72,26},{96,50},{104,58},{... | collective-permute-start | bytes 614408 | tf_op jit(solution)/shard_map/ppermute | solution.py:211
  37.9 4.5 %collective-permute-start.3 = (bf16[32,3200]{1,0:T(8,128)(2,1)S(1)}, bf16[32,3200]{1,0:T(8,128)(2,1)S(1)}, u32[]{:S(2)}, u32[]{:S(2)}) collective-permute-start(bf16[32,3200]{1,0:T(8,128)(2,1)S(1)} %join.2.refs_0_), channel_id=1, source_target_pairs={{0,37},{8,127},{32,69},{40,31},{64,101},{72,63},{96,5},{104,95},{4... | collective-permute-start | bytes 614408 | tf_op jit(solution)/shard_map/ppermute | solution.py:211
  42.4 5.2 %collective-permute-done.2.refs_1_ = bf16[32,3200]{1,0:T(8,128)(2,1)S(1)} collective-permute-done((bf16[32,3200]{1,0:T(8,128)(2,1)S(1)}, bf16[32,3200]{1,0:T(8,128)(2,1)S(1)}, u32[]{:S(2)}, u32[]{:S(2)}) %collective-permute-start.2) | collective-permute-done | bytes 204832 | tf_op jit(solution)/shard_map/ppermute | solution.py:211
  47.6 2.5 %collective-permute-done.3.refs_2_ = bf16[32,3200]{1,0:T(8,128)(2,1)S(1)} collective-permute-done((bf16[32,3200]{1,0:T(8,128)(2,1)S(1)}, bf16[32,3200]{1,0:T(8,128)(2,1)S(1)}, u32[]{:S(2)}, u32[]{:S(2)}) %collective-permute-start.3) | collective-permute-done | bytes 204832 | tf_op jit(solution)/shard_map/ppermute | solution.py:211
  50.0 2.4 %collective-permute-done.4.refs_3_ = bf16[32,3200]{1,0:T(8,128)(2,1)S(1)} collective-permute-done((bf16[32,3200]{1,0:T(8,128)(2,1)S(1)}, bf16[32,3200]{1,0:T(8,128)(2,1)S(1)}, u32[]{:S(2)}, u32[]{:S(2)}) %collective-permute-start.4) | collective-permute-done | bytes 204832 | tf_op jit(solution)/shard_map/ppermute | solution.py:211
  52.5 2.7 %collective-permute-start.5 = (bf16[128,3200]{1,0:T(8,128)(2,1)S(1)}, bf16[128,3200]{1,0:T(8,128)(2,1)S(1)}, u32[]{:S(2)}, u32[]{:S(2)}) collective-permute-start(bf16[128,3200]{1,0:T(8,128)(2,1)S(1)} %join.3.b0), channel_id=1, source_target_pairs={{0,2},{8,10},{32,34},{40,42},{64,66},{72,74},{96,98},{104,106},{4,... | collective-permute-start | bytes 2457608 | tf_op jit(solution)/shard_map/ppermute | solution.py:211
  56.5 17.8 %collective-permute-done.5.b1 = bf16[128,3200]{1,0:T(8,128)(2,1)S(1)} collective-permute-done((bf16[128,3200]{1,0:T(8,128)(2,1)S(1)}, bf16[128,3200]{1,0:T(8,128)(2,1)S(1)}, u32[]{:S(2)}, u32[]{:S(2)}) %collective-permute-start.5) | collective-permute-done | bytes 819232 | tf_op jit(solution)/shard_map/ppermute | solution.py:211
  74.3 1.7 %collective-permute-done.6.b2 = bf16[128,3200]{1,0:T(8,128)(2,1)S(1)} collective-permute-done((bf16[128,3200]{1,0:T(8,128)(2,1)S(1)}, bf16[128,3200]{1,0:T(8,128)(2,1)S(1)}, u32[]{:S(2)}, u32[]{:S(2)}) %collective-permute-start.6) | collective-permute-done | bytes 819232 | tf_op jit(solution)/shard_map/ppermute | solution.py:211
  76.0 3.2 %deal.1 = (bf16[256,3200]{1,0:T(8,128)(2,1)}, bf16[256,3200]{1,0:T(8,128)(2,1)}, bf16[512,3200]{1,0:T(8,128)(2,1)}) custom-call(bf16[128,3200]{1,0:T(8,128)(2,1)S(1)} %join.3.b0, bf16[128,3200]{1,0:T(8,128)(2,1)S(1)} %collective-permute-done.5.b1, bf16[128,3200]{1,0:T(8,128)(2,1)S(1)} %collective-permute-done.6.b2, ...), custom_call_target="tpu_custom_call" | custom-call | tf_op jit(solution)/shard_map/deal/pallas_call | solution.py:247
  80.9 1.7 %collective-permute-start.12 = (bf16[256,3200]{1,0:T(8,128)(2,1)}, bf16[256,3200]{1,0:T(8,128)(2,1)}, u32[]{:S(2)}, u32[]{:S(2)}) collective-permute-start(bf16[256,3200]{1,0:T(8,128)(2,1)} %get-tuple-element.29.refs_0_), channel_id=1, source_target_pairs={{0,4},{8,28},{32,36},{40,60},{64,68},{72,92},{96,100},{104,124},{4... | collective-permute-start | bytes 4915208 | tf_op jit(solution)/shard_map/ppermute | solution.py:211
  83.2 2.8 %weighted.4.left = bf16[512,384]{1,0:T(8,128)(2,1)S(1)} custom-call(s32[1]{0:T(128)} %bitcast.1.place, f32[1]{0:T(128)} %dynamic_slice.12.omega, bf16[256,3200]{1,0:T(8,128)(2,1)} %get-tuple-element.29.refs_0_, bf16[256,3200]{1,0:T(8,128)(2,1)} %get-tuple-element.28.refs_1_, f32[8,128]{1,0:T(8,128)S(1)} %broadcast_in_dim.7.refs_2_), custom_call_target="tpu_custom_call" | custom-call | tf_op jit(solution)/shard_map/weighted/pallas_call | solution.py:292
  86.1 2.5 %collective-permute-start.9 = (bf16[256,3200]{1,0:T(8,128)(2,1)}, bf16[256,3200]{1,0:T(8,128)(2,1)S(1)}, u32[]{:S(2)}, u32[]{:S(2)}) collective-permute-start(bf16[256,3200]{1,0:T(8,128)(2,1)} %get-tuple-element.28.refs_1_), channel_id=1, source_target_pairs={{0,1},{8,11},{32,33},{40,43},{64,65},{72,75},{96,97},{104,107},{4,... | collective-permute-start | bytes 4915208 | tf_op jit(solution)/shard_map/ppermute | solution.py:211
  88.7 2.2 %collective-permute-start.10 = (bf16[256,3200]{1,0:T(8,128)(2,1)}, bf16[256,3200]{1,0:T(8,128)(2,1)S(1)}, u32[]{:S(2)}, u32[]{:S(2)}) collective-permute-start(bf16[256,3200]{1,0:T(8,128)(2,1)} %get-tuple-element.28.refs_1_), channel_id=1, source_target_pairs={{0,4},{8,28},{32,36},{40,60},{64,68},{72,92},{96,100},{104,124},{4... | collective-permute-start | bytes 4915208 | tf_op jit(solution)/shard_map/ppermute | solution.py:211
  90.9 3.9 %partial_own.3 = (f32[384,3072]{1,0:T(8,128)S(1)}, f32[8,128]{1,0:T(8,128)S(1)}) custom-call(bf16[512,384]{1,0:T(8,128)(2,1)S(1)} %weighted.4.left, bf16[256,3200]{1,0:T(8,128)(2,1)} %get-tuple-element.29.refs_0_, bf16[256,3200]{1,0:T(8,128)(2,1)} %get-tuple-element.28.refs_1_, f32[8,128]{1,0:T(8,128)S(1)} %broadcast_in_dim.7.refs_2_), custom_call_target="tpu_custom_call" | custom-call | flops 1207959552 | bytes 12582912 | tf_op jit(solution)/shard_map/partial_own/pallas_call | solution.py:350
  94.8 3.9 %partial_other.3 = (f32[384,3072]{1,0:T(8,128)S(1)}, f32[8,128]{1,0:T(8,128)S(1)}) custom-call(bf16[512,384]{1,0:T(8,128)(2,1)S(1)} %collective-permute-done.13.left, bf16[256,3200]{1,0:T(8,128)(2,1)} %get-tuple-element.29.refs_0_, bf16[256,3200]{1,0:T(8,128)(2,1)} %get-tuple-element.28.refs_1_, f32[8,128]{1,0:T(8,128)S(1)} %get-tuple-element.30.refs_2_), custom_call_target="tpu_custom_call" | custom-call | flops 1207959552 | bytes 12582912 | tf_op jit(solution)/shard_map/partial_other/pallas_call | solution.py:350
  99.8 1.7 %collective-permute-done.12.refs_1_ = bf16[256,3200]{1,0:T(8,128)(2,1)} collective-permute-done((bf16[256,3200]{1,0:T(8,128)(2,1)}, bf16[256,3200]{1,0:T(8,128)(2,1)}, u32[]{:S(2)}, u32[]{:S(2)}) %collective-permute-start.12) | collective-permute-done | bytes 1638432 | tf_op jit(solution)/shard_map/ppermute | solution.py:211
  101.5 2.8 %weighted.5.left = bf16[512,384]{1,0:T(8,128)(2,1)S(1)} custom-call(s32[1]{0:T(128)} %bitcast.1.place, f32[1]{0:T(128)} %dynamic_slice.12.omega, bf16[256,3200]{1,0:T(8,128)(2,1)} %collective-permute-done.11.refs_0_, bf16[256,3200]{1,0:T(8,128)(2,1)} %collective-permute-done.12.refs_1_, f32[8,128]{1,0:T(8,128)S(1)} %get-tuple-element.31.refs_2_.refs_3_), custom_call_target="tpu_custom_call" | custom-call | tf_op jit(solution)/shard_map/weighted/pallas_call | solution.py:292
  104.3 3.7 %collective-permute-start.14 = (bf16[512,384]{1,0:T(8,128)(2,1)S(1)}, bf16[512,384]{1,0:T(8,128)(2,1)S(1)}, u32[]{:S(2)}, u32[]{:S(2)}) collective-permute-start(bf16[512,384]{1,0:T(8,128)(2,1)S(1)} %weighted.5.left), channel_id=1, source_target_pairs={{0,8},{8,0},{32,40},{40,32},{64,72},{72,64},{96,104},{104,96},{4,1... | collective-permute-start | bytes 1179656 | tf_op jit(solution)/shard_map/ppermute | solution.py:211
  108.0 4.1 %partial_own.4 = (f32[384,3072]{1,0:T(8,128)S(1)}, f32[8,128]{1,0:T(8,128)S(1)}) custom-call(bf16[512,384]{1,0:T(8,128)(2,1)S(1)} %weighted.5.left, bf16[256,3200]{1,0:T(8,128)(2,1)} %collective-permute-done.11.refs_0_, bf16[256,3200]{1,0:T(8,128)(2,1)} %collective-permute-done.12.refs_1_, ...), custom_call_target="tpu_custom_call", output_to_operand_aliasing={{0}: (3, {})} | custom-call | flops 1207959552 | bytes 12582912 | tf_op jit(solution)/shard_map/partial_own/pallas_call | solution.py:350
  112.1 4.1 %partial_other.4 = (f32[384,3072]{1,0:T(8,128)S(1)}, f32[8,128]{1,0:T(8,128)S(1)}) custom-call(bf16[512,384]{1,0:T(8,128)(2,1)S(1)} %collective-permute-done.14.left, bf16[256,3200]{1,0:T(8,128)(2,1)} %collective-permute-done.11.refs_0_, bf16[256,3200]{1,0:T(8,128)(2,1)} %collective-permute-done.12.refs_1_, ...), custom_call_target="tpu_custom_call", output_to_operand_aliasing={{0}: (3, {})} | custom-call | flops 1207959552 | bytes 12582912 | tf_op jit(solution)/shard_map/partial_other/pallas_call | solution.py:350
  117.3 1.7 %collective-permute-done.10.refs_1_ = bf16[256,3200]{1,0:T(8,128)(2,1)S(1)} collective-permute-done((bf16[256,3200]{1,0:T(8,128)(2,1)}, bf16[256,3200]{1,0:T(8,128)(2,1)S(1)}, u32[]{:S(2)}, u32[]{:S(2)}) %collective-permute-start.10) | collective-permute-done | bytes 1638432 | tf_op jit(solution)/shard_map/ppermute | solution.py:211
  119.8 3.9 %collective-permute-start.15 = (bf16[512,384]{1,0:T(8,128)(2,1)S(1)}, bf16[512,384]{1,0:T(8,128)(2,1)S(1)}, u32[]{:S(2)}, u32[]{:S(2)}) collective-permute-start(bf16[512,384]{1,0:T(8,128)(2,1)S(1)} %weighted.6.left), channel_id=1, source_target_pairs={{0,8},{8,0},{32,40},{40,32},{64,72},{72,64},{96,104},{104,96},{4,1... | collective-permute-start | bytes 1179656 | tf_op jit(solution)/shard_map/ppermute | solution.py:211
  123.7 2.2 %partial_own.5 = (f32[384,3072]{1,0:T(8,128)S(1)}, f32[8,128]{1,0:T(8,128)S(1)}) custom-call(bf16[512,384]{1,0:T(8,128)(2,1)S(1)} %weighted.6.left, bf16[256,3200]{1,0:T(8,128)(2,1)S(1)} %collective-permute-done.9.refs_0_, bf16[256,3200]{1,0:T(8,128)(2,1)S(1)} %collective-permute-done.10.refs_1_, ...), custom_call_target="tpu_custom_call", output_to_operand_aliasing={{0}: (3, {})} | custom-call | flops 1207959552 | bytes 12582912 | tf_op jit(solution)/shard_map/partial_own/pallas_call | solution.py:350
  125.9 2.2 %partial_other.5 = (f32[384,3072]{1,0:T(8,128)S(1)}, f32[8,128]{1,0:T(8,128)S(1)}) custom-call(bf16[512,384]{1,0:T(8,128)(2,1)S(1)} %collective-permute-done.15.left, bf16[256,3200]{1,0:T(8,128)(2,1)S(1)} %collective-permute-done.9.refs_0_, bf16[256,3200]{1,0:T(8,128)(2,1)S(1)} %collective-permute-done.10.refs_1_, ...), custom_call_target="tpu_custom_call", output_to_operand_aliasing={{0}: (3, {})} | custom-call | flops 1207959552 | bytes 12582912 | tf_op jit(solution)/shard_map/partial_other/pallas_call | solution.py:350
  129.1 2.1 %own_rows.2 = (f32[384,6144]{1,0:T(8,128)}, f32[8,128]{1,0:T(8,128)S(1)}) custom-call(s32[1]{0:T(128)} %bitcast.core, bf16[512,384]{1,0:T(8,128)(2,1)S(1)} %weighted.7.left, bf16[512,3200]{1,0:T(8,128)(2,1)S(1)} %collective-permute-done.8.refs_0_, f32[384,3072]{1,0:T(8,128)S(1)} %get-tuple-element.41.refs_1_, f32[8,128]{1,0:T(8,128)S(1)} %get-tuple-element.39.refs_1_.refs_2_), custom_call_target="tpu_custom_call" | custom-call | flops 603979776 | bytes 6291456 | tf_op jit(solution)/shard_map/own_rows/pallas_call | solution.py:386
  133.9 2.6 %own_rows.3 = (f32[384,6144]{1,0:T(8,128)}, f32[8,128]{1,0:T(8,128)}) custom-call(s32[1]{0:T(128)} %bitcast.core, bf16[512,384]{1,0:T(8,128)(2,1)S(1)} %weighted.7.left, bf16[512,3200]{1,0:T(8,128)(2,1)S(1)} %collective-permute-done.8.refs_0_, f32[384,3072]{1,0:T(8,128)S(1)} %get-tuple-element.41.refs_1_, ...), custom_call_target="tpu_custom_call", output_to_operand_aliasing={{0}: (4, {})} | custom-call | flops 603979776 | bytes 6291456 | tf_op jit(solution)/shard_map/own_rows/pallas_call | solution.py:386
  136.9 2.3 %finish.1 = f32[384,6144]{1,0:T(8,128)} custom-call(s32[1]{0:T(128)} %bitcast.core, bf16[384,1536]{1,0:T(8,128)(2,1)S(1)} %collective-permute-done.17.r0, bf16[384,1536]{1,0:T(8,128)(2,1)S(1)} %collective-permute-done.18.r1, f32[384,6144]{1,0:T(8,128)} %get-tuple-element.44._), custom_call_target="tpu_custom_call", output_to_operand_aliasing={{}: (3, {})} | custom-call | tf_op jit(solution)/shard_map/finish/pallas_call | solution.py:440
  (57 shorter events, 21.9 us)
Async XLA Ops:
  0.0 0.9 copy-start
  1.0 0.7 copy-start.5
  2.5 17.5 %all-to-all-start = ((bf16[8,24,1024]{2,1,0:T(8,128)(2,1)}), bf16[8,24,1024]{2,1,0:T(8,128)(2,1)S(1)}, u32[]{:S(2)}, u32[]{:S(2)}) async-start(bf16[8,24,1024]{2,1,0:T(8,128)(2,1)} %payload.1), calls=%async_computation | async-start | bytes 786432 | tf_op jit(solution)/shard_map/all_to_all | solution.py:461
  20.0 3.5 %collective-permute-start = (bf16[8,24,1024]{2,1,0:T(8,128)(2,1)S(1)}, bf16[8,24,1024]{2,1,0:T(8,128)(2,1)S(1)}, u32[]{:S(2)}, u32[]{:S(2)}) collective-permute-start(bf16[8,24,1024]{2,1,0:T(8,128)(2,1)S(1)} %all-to-all-done.mine), channel_id=1, source_target_pairs={{0,8},{8,0},{32,40},{40,32},{64,72},{72,64},{96,104},{104,96},{4,1... | collective-permute-start | bytes 1179656 | tf_op jit(solution)/shard_map/ppermute | solution.py:211
  23.5 0.9 copy-start.1
  24.4 0.9 copy-start.2
  25.4 0.9 copy-start.3
  26.3 0.9 copy-start.4
  31.9 50.7 %copy-start.6 = (f32[8]{0:T(128)S(1)}, f32[8]{0:T(128)}, u32[]{:S(2)}) copy-start(f32[8]{0:T(128)} %param.16) | copy-start | bytes 100
  31.9 2.7 %collective-permute-start.1 = (bf16[16,3200]{1,0:T(8,128)(2,1)S(1)}, bf16[16,3200]{1,0:T(8,128)(2,1)S(1)}, u32[]{:S(2)}, u32[]{:S(2)}) collective-permute-start(bf16[16,3200]{1,0:T(8,128)(2,1)S(1)} %get-tuple-element.26), channel_id=1, source_target_pairs={{0,8},{8,0},{32,40},{40,32},{64,72},{72,64},{96,104},{104,96},{4,1... | collective-permute-start | bytes 307208 | tf_op jit(solution)/shard_map/ppermute | solution.py:211
  34.7 12.9 %collective-permute-start.2 = (bf16[32,3200]{1,0:T(8,128)(2,1)S(1)}, bf16[32,3200]{1,0:T(8,128)(2,1)S(1)}, u32[]{:S(2)}, u32[]{:S(2)}) collective-permute-start(bf16[32,3200]{1,0:T(8,128)(2,1)S(1)} %join.2.refs_0_), channel_id=1, source_target_pairs={{0,82},{8,90},{32,114},{40,122},{64,18},{72,26},{96,50},{104,58},{... | collective-permute-start | bytes 614408 | tf_op jit(solution)/shard_map/ppermute | solution.py:211
  37.9 12.1 %collective-permute-start.3 = (bf16[32,3200]{1,0:T(8,128)(2,1)S(1)}, bf16[32,3200]{1,0:T(8,128)(2,1)S(1)}, u32[]{:S(2)}, u32[]{:S(2)}) collective-permute-start(bf16[32,3200]{1,0:T(8,128)(2,1)S(1)} %join.2.refs_0_), channel_id=1, source_target_pairs={{0,37},{8,127},{32,69},{40,31},{64,101},{72,63},{96,5},{104,95},{4... | collective-permute-start | bytes 614408 | tf_op jit(solution)/shard_map/ppermute | solution.py:211
  42.4 10.0 %collective-permute-start.4 = (bf16[32,3200]{1,0:T(8,128)(2,1)S(1)}, bf16[32,3200]{1,0:T(8,128)(2,1)S(1)}, u32[]{:S(2)}, u32[]{:S(2)}) collective-permute-start(bf16[32,3200]{1,0:T(8,128)(2,1)S(1)} %join.2.refs_0_), channel_id=1, source_target_pairs={{0,119},{8,45},{32,23},{40,77},{64,55},{72,109},{96,87},{104,13},{... | collective-permute-start | bytes 614408 | tf_op jit(solution)/shard_map/ppermute | solution.py:211
  52.5 21.8 %collective-permute-start.5 = (bf16[128,3200]{1,0:T(8,128)(2,1)S(1)}, bf16[128,3200]{1,0:T(8,128)(2,1)S(1)}, u32[]{:S(2)}, u32[]{:S(2)}) collective-permute-start(bf16[128,3200]{1,0:T(8,128)(2,1)S(1)} %join.3.b0), channel_id=1, source_target_pairs={{0,2},{8,10},{32,34},{40,42},{64,66},{72,74},{96,98},{104,106},{4,... | collective-permute-start | bytes 2457608 | tf_op jit(solution)/shard_map/ppermute | solution.py:211
  55.1 20.9 %collective-permute-start.6 = (bf16[128,3200]{1,0:T(8,128)(2,1)S(1)}, bf16[128,3200]{1,0:T(8,128)(2,1)S(1)}, u32[]{:S(2)}, u32[]{:S(2)}) collective-permute-start(bf16[128,3200]{1,0:T(8,128)(2,1)S(1)} %join.3.b0), channel_id=1, source_target_pairs={{0,16},{8,24},{32,48},{40,56},{64,80},{72,88},{96,112},{104,120},{... | collective-permute-start | bytes 2457608 | tf_op jit(solution)/shard_map/ppermute | solution.py:211
  55.8 20.2 %collective-permute-start.7 = (bf16[128,3200]{1,0:T(8,128)(2,1)S(1)}, bf16[128,3200]{1,0:T(8,128)(2,1)S(1)}, u32[]{:S(2)}, u32[]{:S(2)}) collective-permute-start(bf16[128,3200]{1,0:T(8,128)(2,1)S(1)} %join.3.b0), channel_id=1, source_target_pairs={{0,64},{8,72},{32,96},{40,104},{64,0},{72,8},{96,32},{104,40},{4,6... | collective-permute-start | bytes 2457608 | tf_op jit(solution)/shard_map/ppermute | solution.py:211
  79.2 48.9 %collective-permute-start.8 = (bf16[512,3200]{1,0:T(8,128)(2,1)}, bf16[512,3200]{1,0:T(8,128)(2,1)S(1)}, u32[]{:S(2)}, u32[]{:S(2)}) collective-permute-start(bf16[512,3200]{1,0:T(8,128)(2,1)} %get-tuple-element.27), channel_id=1, source_target_pairs={{0,32},{8,104},{32,64},{40,8},{64,96},{72,40},{96,0},{104,72},{4,3... | collective-permute-start | bytes 9830408 | tf_op jit(solution)/shard_map/ppermute | solution.py:211
  79.2 20.6 %collective-permute-start.11 = (bf16[256,3200]{1,0:T(8,128)(2,1)}, bf16[256,3200]{1,0:T(8,128)(2,1)}, u32[]{:S(2)}, u32[]{:S(2)}) collective-permute-start(bf16[256,3200]{1,0:T(8,128)(2,1)} %get-tuple-element.29.refs_0_), channel_id=1, source_target_pairs={{0,1},{8,11},{32,33},{40,43},{64,65},{72,75},{96,97},{104,107},{4,... | collective-permute-start | bytes 4915208 | tf_op jit(solution)/shard_map/ppermute | solution.py:211
  80.9 20.6 %collective-permute-start.12 = (bf16[256,3200]{1,0:T(8,128)(2,1)}, bf16[256,3200]{1,0:T(8,128)(2,1)}, u32[]{:S(2)}, u32[]{:S(2)}) collective-permute-start(bf16[256,3200]{1,0:T(8,128)(2,1)} %get-tuple-element.29.refs_0_), channel_id=1, source_target_pairs={{0,4},{8,28},{32,36},{40,60},{64,68},{72,92},{96,100},{104,124},{4... | collective-permute-start | bytes 4915208 | tf_op jit(solution)/shard_map/ppermute | solution.py:211
  86.1 2.6 %collective-permute-start.13 = (bf16[512,384]{1,0:T(8,128)(2,1)S(1)}, bf16[512,384]{1,0:T(8,128)(2,1)S(1)}, u32[]{:S(2)}, u32[]{:S(2)}) collective-permute-start(bf16[512,384]{1,0:T(8,128)(2,1)S(1)} %weighted.4.left), channel_id=1, source_target_pairs={{0,8},{8,0},{32,40},{40,32},{64,72},{72,64},{96,104},{104,96},{4,1... | collective-permute-start | bytes 1179656 | tf_op jit(solution)/shard_map/ppermute | solution.py:211
  86.1 31.1 %collective-permute-start.9 = (bf16[256,3200]{1,0:T(8,128)(2,1)}, bf16[256,3200]{1,0:T(8,128)(2,1)S(1)}, u32[]{:S(2)}, u32[]{:S(2)}) collective-permute-start(bf16[256,3200]{1,0:T(8,128)(2,1)} %get-tuple-element.28.refs_1_), channel_id=1, source_target_pairs={{0,1},{8,11},{32,33},{40,43},{64,65},{72,75},{96,97},{104,107},{4,... | collective-permute-start | bytes 4915208 | tf_op jit(solution)/shard_map/ppermute | solution.py:211
  88.7 30.3 %collective-permute-start.10 = (bf16[256,3200]{1,0:T(8,128)(2,1)}, bf16[256,3200]{1,0:T(8,128)(2,1)S(1)}, u32[]{:S(2)}, u32[]{:S(2)}) collective-permute-start(bf16[256,3200]{1,0:T(8,128)(2,1)} %get-tuple-element.28.refs_1_), channel_id=1, source_target_pairs={{0,4},{8,28},{32,36},{40,60},{64,68},{72,92},{96,100},{104,124},{4... | collective-permute-start | bytes 4915208 | tf_op jit(solution)/shard_map/ppermute | solution.py:211
  104.3 7.8 %collective-permute-start.14 = (bf16[512,384]{1,0:T(8,128)(2,1)S(1)}, bf16[512,384]{1,0:T(8,128)(2,1)S(1)}, u32[]{:S(2)}, u32[]{:S(2)}) collective-permute-start(bf16[512,384]{1,0:T(8,128)(2,1)S(1)} %weighted.5.left), channel_id=1, source_target_pairs={{0,8},{8,0},{32,40},{40,32},{64,72},{72,64},{96,104},{104,96},{4,1... | collective-permute-start | bytes 1179656 | tf_op jit(solution)/shard_map/ppermute | solution.py:211
  119.8 6.1 %collective-permute-start.15 = (bf16[512,384]{1,0:T(8,128)(2,1)S(1)}, bf16[512,384]{1,0:T(8,128)(2,1)S(1)}, u32[]{:S(2)}, u32[]{:S(2)}) collective-permute-start(bf16[512,384]{1,0:T(8,128)(2,1)S(1)} %weighted.6.left), channel_id=1, source_target_pairs={{0,8},{8,0},{32,40},{40,32},{64,72},{72,64},{96,104},{104,96},{4,1... | collective-permute-start | bytes 1179656 | tf_op jit(solution)/shard_map/ppermute | solution.py:211
  129.0 2.2 %collective-permute-start.16 = (bf16[512,384]{1,0:T(8,128)(2,1)S(1)}, bf16[512,384]{1,0:T(8,128)(2,1)S(1)}, u32[]{:S(2)}, u32[]{:S(2)}) collective-permute-start(bf16[512,384]{1,0:T(8,128)(2,1)S(1)} %weighted.7.left), channel_id=1, source_target_pairs={{0,8},{8,0},{32,40},{40,32},{64,72},{72,64},{96,104},{104,96},{4,1... | collective-permute-start | bytes 1179656 | tf_op jit(solution)/shard_map/ppermute | solution.py:211
  132.2 4.3 %collective-permute-start.17 = (bf16[384,1536]{1,0:T(8,128)(2,1)S(1)}, bf16[384,1536]{1,0:T(8,128)(2,1)S(1)}, u32[]{:S(2)}, u32[]{:S(2)}) collective-permute-start(bf16[384,1536]{1,0:T(8,128)(2,1)S(1)} %other_rows.2), channel_id=1, source_target_pairs={{0,8},{8,0},{32,40},{40,32},{64,72},{72,64},{96,104},{104,96},{4,1... | collective-permute-start | bytes 3538952 | tf_op jit(solution)/shard_map/ppermute | solution.py:211
  133.8 3.1 %collective-permute-start.18 = (bf16[384,1536]{1,0:T(8,128)(2,1)S(1)}, bf16[384,1536]{1,0:T(8,128)(2,1)S(1)}, u32[]{:S(2)}, u32[]{:S(2)}) collective-permute-start(bf16[384,1536]{1,0:T(8,128)(2,1)S(1)} %other_rows.3), channel_id=1, source_target_pairs={{0,8},{8,0},{32,40},{40,32},{64,72},{72,64},{96,104},{104,96},{4,1... | collective-permute-start | bytes 3538952 | tf_op jit(solution)/shard_map/ppermute | solution.py:211

commit v9 on v8

--- a/solution.py
+++ b/solution.py
@@ -58,14 +58,13 @@
     return np.stack(first), tcos, tsin, np.concatenate([sh, sl], 1)
 
 
-def payload_kernel(val, con, out, val_here, con_here, sem):
-    copies = [
-        pltpu.make_async_copy(val, val_here, sem.at[0]),
-        pltpu.make_async_copy(con, con_here, sem.at[1]),
-    ]
+def payload_kernel(val, con, first, tcos, tsin, second, out, *refs):
+    here, (val_here, con_here, sem) = refs[:4], refs[4:]
+    pairs = [(val, val_here), (con, con_here), *zip((first, tcos, tsin, second), here)]
+    copies = [pltpu.make_async_copy(src, dst, sem.at[i]) for i, (src, dst) in enumerate(pairs)]
     for copy in copies:
         copy.start()
-    for copy in copies:
+    for copy in copies[:2]:
         copy.wait()
     v = val_here[...].astype(jnp.float32)
     values = jnp.concatenate([v[:, :1024], v[:, 1024:]], 0)
@@ -73,22 +72,27 @@
         c = con_here[chip * 8 : chip * 8 + 8, :].astype(jnp.float32)
         rows = jnp.concatenate([c[:, :1024], c[:, 1024:], values], 0)
         out[chip] = rows.astype(jnp.bfloat16)
+    for copy in copies[2:]:
+        copy.wait()
 
 
 def payload(val, con):
+    constants = [jnp.asarray(c) for c in dft_constants()]
+    operands = [pltpu.with_memory_space_constraint(a, pltpu.HBM) for a in (val, con, *constants)]
     return pl.pallas_call(
         payload_kernel,
-        out_shape=jax.ShapeDtypeStruct((8, 24, 1024), jnp.bfloat16),
-        in_specs=[HBM] * 2,
-        out_specs=VM,
+        out_shape=[pltpu.VMEM((8, 24, 1024), jnp.bfloat16)]
+        + [pltpu.VMEM(c.shape, c.dtype) for c in constants],
+        in_specs=[HBM] * 6,
+        out_specs=[VM] * 5,
         scratch_shapes=[
             pltpu.VMEM(val.shape, val.dtype),
             pltpu.VMEM(con.shape, con.dtype),
-            pltpu.SemaphoreType.DMA((2,)),
+            pltpu.SemaphoreType.DMA((6,)),
         ],
         compiler_params=PARAMS,
         name="payload",
-    )(val, con)
+    )(*operands)
 
 
 def transform(core, mine, others, first, tcos, tsin, second, spec, high, low, grid):
@@ -160,12 +164,12 @@
     pick(spec, gidx, meta, out)
 
 
-def rho_spectrum(core, mine, others, gidx, meta):
+def rho_spectrum(core, mine, others, gidx, meta, constants):
     return pl.pallas_call(
         transform_kernel,
         out_shape=[
-            jax.ShapeDtypeStruct((PAIRS * 64, 256), jnp.bfloat16),
-            jax.ShapeDtypeStruct((PAIRS, WIDE), jnp.bfloat16),
+            pltpu.VMEM((PAIRS * 64, 256), jnp.bfloat16),
+            pltpu.VMEM((PAIRS, WIDE), jnp.bfloat16),
         ],
         in_specs=[SM] + [VM] * 8,
         out_specs=[VM] * 2,
@@ -173,13 +177,13 @@
         + [pltpu.VMEM((2, 8, 8 * 24, LANES), jnp.float32)],
         compiler_params=PARAMS,
         name="rho_spectrum",
-    )(core, mine, others, gidx, meta, *(jnp.asarray(c) for c in dft_constants()))
+    )(core, mine, others, gidx, meta, *constants)
 
 
 def rho_pick(spec, gidx, meta):
     return pl.pallas_call(
         pick,
-        out_shape=jax.ShapeDtypeStruct((PAIRS, WIDE), jnp.bfloat16),
+        out_shape=pltpu.VMEM((PAIRS, WIDE), jnp.bfloat16),
         in_specs=[VM] * 3,
         out_specs=VM,
         compiler_params=PARAMS,
@@ -227,7 +231,7 @@
     rows = sum(b.shape[0] for b in blocks)
     return pl.pallas_call(
         functools.partial(join_kernel, len(blocks)),
-        out_shape=jax.ShapeDtypeStruct((rows, WIDE), jnp.bfloat16),
+        out_shape=pltpu.VMEM((rows, WIDE), jnp.bfloat16),
         in_specs=[VM] * len(blocks),
         out_specs=VM,
         compiler_params=PARAMS,
@@ -246,7 +250,7 @@
 def deal(blocks):
     return pl.pallas_call(
         deal_kernel,
-        out_shape=[jax.ShapeDtypeStruct((rows, WIDE), jnp.bfloat16) for rows in (256, 256, 512)],
+        out_shape=[pltpu.VMEM((rows, WIDE), jnp.bfloat16) for rows in (256, 256, 512)],
         in_specs=[VM] * 4,
         out_specs=[VM] * 3,
         compiler_params=PARAMS,
@@ -291,7 +295,7 @@
 def weighted(place, omega, pieces, tie):
     return pl.pallas_call(
         weighted_kernel,
-        out_shape=jax.ShapeDtypeStruct((sum(p.shape[0] for p in pieces), ROWS), jnp.bfloat16),
+        out_shape=pltpu.VMEM((sum(p.shape[0] for p in pieces), ROWS), jnp.bfloat16),
         in_specs=[SM, SM] + [VM] * (len(pieces) + 1),
         out_specs=VM,
         compiler_params=PARAMS,
@@ -349,7 +353,7 @@
     before = [] if before is None else [before]
     return pl.pallas_call(
         functools.partial(partial_kernel, names, len(pieces), other),
-        out_shape=[jax.ShapeDtypeStruct((ROWS, HALF), jnp.float32), TIE],
+        out_shape=[pltpu.VMEM((ROWS, HALF), jnp.float32), TIE],
         in_specs=[VM] * (2 + len(pieces) + len(before)),
         out_specs=[VM] * 2,
         input_output_aliases={1 + len(pieces): 0} if before else {},
@@ -411,7 +415,7 @@
 def other_rows(names, start, left, pieces, before, tie):
     return pl.pallas_call(
         functools.partial(other_kernel, names, len(pieces), start),
-        out_shape=jax.ShapeDtypeStruct((ROWS, HALF // 2), jnp.bfloat16),
+        out_shape=pltpu.VMEM((ROWS, HALF // 2), jnp.bfloat16),
         in_specs=[VM] * (len(pieces) + 3),
         out_specs=VM,
         compiler_params=PARAMS,
@@ -458,7 +462,8 @@
     ba = lax.axis_index("ba")
     core = lax.rem(ga, 2).astype(jnp.int32)
     kinds = [[2 * i + c for i in range(8)] for c in range(2)]
-    psi = lax.all_to_all(payload(psi_val, psi_con), "ga", 0, 0, tiled=True, axis_index_groups=kinds)
+    rows, *constants = payload(psi_val, psi_con)
+    psi = lax.all_to_all(rows, "ga", 0, 0, tiled=True, axis_index_groups=kinds)
     psi_other = send(psi, core_pairs())
 
     delta = (lax.dynamic_slice(e_con, (ga * 4,), (4,))[None, :] - e_val[:, None]).reshape(PAIRS)
@@ -472,7 +477,7 @@
     kinds_of_rows = g_index.reshape(8, 2, ROWS).transpose(1, 0, 2).reshape(2, HALF)
     kept = lax.dynamic_slice(kinds_of_rows, (core, 0), (1, HALF))
     given = lax.dynamic_slice(kinds_of_rows, (1 - core, 0), (1, HALF))
-    spec, give = rho_spectrum(core.reshape(1), psi, psi_other, given, meta)
+    spec, give = rho_spectrum(core.reshape(1), psi, psi_other, given, meta, constants)
     swapped = send(give, core_pairs())
     keep = rho_pick(spec, kept, meta)
 

time: 140 us -> 136 us (0.971)
  local copies, waits for them, and re-layouts: 7.85 us -> 2.53 us
    unnamed x14 -> x2, local copies, waits for them, and re-layouts: 5.38 us -> 0.01 us
  transfers between devices with their start and end apart: 20 -> 20, of which waited for: 12 -> 13; matrix products, arithmetic and copies ran while one was open for 3% -> 3% of each run, Pallas kernels for 25% -> 26%
where the time goes in v9:
time: 136 us; the launch traced here: 135 us
  Pallas kernels  49.2 us (36%)
  waiting for transfers between devices  42.2 us (31%)
  starting transfers between devices  39.3 us (29%)
  local copies, waits for them, and re-layouts  2.53 us (2%)
  other arithmetic  1.41 us (1%)
    ppermute x19, waiting for transfers between devices, send(): return lax.ppermute(a, ('ga', 'ba'), pairs)  36.4 us
    ppermute x19, starting transfers between devices, send(): return lax.ppermute(a, ('ga', 'ba'), pairs)  30.8 us
    pallas_call x6, Pallas kernels, partial_rows(): pl.pallas_call(functools.partial(partial_kernel, names, len(pieces), othe...  20.4 us
    all_to_all x1, starting transfers between devices, on_device(): psi = lax.all_to_all(rows, 'ga', 0, 0, tiled=True, axis_index_groups=kinds)  8.51 us
    pallas_call x4, Pallas kernels, weighted(): pl.pallas_call(weighted_kernel, out_shape=pltpu.VMEM((sum((p.shape[0] for...  7.65 us
    all_to_all x1, waiting for transfers between devices, on_device(): psi = lax.all_to_all(rows, 'ga', 0, 0, tiled=True, axis_index_groups=kinds)  5.85 us
    pallas_call x2, Pallas kernels, own_rows(): pl.pallas_call(functools.partial(own_kernel, names, len(pieces), start),...  4.7 us
    pallas_call x1, Pallas kernels, rho_spectrum(): pl.pallas_call(transform_kernel, out_shape=[pltpu.VMEM((PAIRS * 64, 256),...  4.58 us
  transfers between devices with their start and end apart: 20, of which 13 were waited for; matrix products, arithmetic and copies ran while one was open for 3% of the time, Pallas kernels for 26%

profile of v9, /device:TPU:1, one launch (start us, length us, event | category | flops | bytes accessed | tf_op | source)
XLA Modules:
  0.0 135.1 jit_solution(2997431830142125766)
XLA Ops:
  0.0 2.0 %payload.1 = (bf16[8,24,1024]{2,1,0:T(8,128)(2,1)}, bf16[2,256,256]{2,1,0:T(8,128)(2,1)S(1)}, f32[128,256]{1,0:T(8,128)S(1)}, f32[128,256]{1,0:T(8,128)S(1)}, bf16[512,256]{1,0:T(8,128)(2,1)S(1)}) custom-call(bf16[4,2048]{1,0:T(4,128)(2,1)} %val.1, bf16[64,2048]{1,0:T(8,128)(2,1)} %con.1, bf16[2,256,256]{2,1,0:T(8,128)(2,1)} %constant.39.clone.first, ...), custom_call_target="tpu_custom_call" | custom-call | tf_op jit(solution)/shard_map/payload/pallas_call | solution.py:82
  2.0 8.5 %all-to-all-start = ((bf16[8,24,1024]{2,1,0:T(8,128)(2,1)}), bf16[8,24,1024]{2,1,0:T(8,128)(2,1)S(1)}, u32[]{:S(2)}, u32[]{:S(2)}) async-start(bf16[8,24,1024]{2,1,0:T(8,128)(2,1)} %get-tuple-element.30), calls=%async_computation | async-start | bytes 786432 | tf_op jit(solution)/shard_map/all_to_all | solution.py:466
  13.6 5.8 %all-to-all-done.mine = bf16[8,24,1024]{2,1,0:T(8,128)(2,1)S(1)} async-done(((bf16[8,24,1024]{2,1,0:T(8,128)(2,1)}), bf16[8,24,1024]{2,1,0:T(8,128)(2,1)S(1)}, u32[]{:S(2)}, u32[]{:S(2)}) %all-to-all-start) | async-done | bytes 393248 | tf_op jit(solution)/shard_map/all_to_all | solution.py:466
  19.5 2.2 %collective-permute-start = (bf16[8,24,1024]{2,1,0:T(8,128)(2,1)S(1)}, bf16[8,24,1024]{2,1,0:T(8,128)(2,1)S(1)}, u32[]{:S(2)}, u32[]{:S(2)}) collective-permute-start(bf16[8,24,1024]{2,1,0:T(8,128)(2,1)S(1)} %all-to-all-done.mine), channel_id=1, source_target_pairs={{0,8},{8,0},{32,40},{40,32},{64,72},{72,64},{96,104},{104,96},{4,1... | collective-permute-start | bytes 1179656 | tf_op jit(solution)/shard_map/ppermute | solution.py:215
  23.0 4.6 %rho_spectrum.1 = (bf16[1024,256]{1,0:T(8,128)(2,1)S(1)}, bf16[16,3200]{1,0:T(8,128)(2,1)S(1)}) custom-call(s32[1]{0:T(128)} %bitcast.core, bf16[8,24,1024]{2,1,0:T(8,128)(2,1)S(1)} %all-to-all-done.mine, bf16[8,24,1024]{2,1,0:T(8,128)(2,1)S(1)} %collective-permute-done.others, s32[1,3072]{1,0:T(1,128)S(1)} %get-tuple-element.56.gidx, ...), custom_call_target="tpu_custom_call" | custom-call | tf_op jit(solution)/shard_map/rho_spectrum/pallas_call | solution.py:168
  28.0 2.3 %rho_pick.1.refs_0_ = bf16[16,3200]{1,0:T(8,128)(2,1)S(1)} custom-call(bf16[1024,256]{1,0:T(8,128)(2,1)S(1)} %get-tuple-element.35.spec, s32[1,3072]{1,0:T(1,128)S(1)} %get-tuple-element.55.gidx, bf16[16,128]{1,0:T(8,128)(2,1)S(1)} %pad.4.meta), custom_call_target="tpu_custom_call" | custom-call | tf_op jit(solution)/shard_map/rho_pick/pallas_call | solution.py:184
  30.4 3.2 %collective-permute-start.2 = (bf16[32,3200]{1,0:T(8,128)(2,1)S(1)}, bf16[32,3200]{1,0:T(8,128)(2,1)S(1)}, u32[]{:S(2)}, u32[]{:S(2)}) collective-permute-start(bf16[32,3200]{1,0:T(8,128)(2,1)S(1)} %join.2.refs_0_), channel_id=1, source_target_pairs={{0,82},{8,90},{32,114},{40,122},{64,18},{72,26},{96,50},{104,58},{... | collective-permute-start | bytes 614408 | tf_op jit(solution)/shard_map/ppermute | solution.py:215
  33.6 4.4 %collective-permute-start.3 = (bf16[32,3200]{1,0:T(8,128)(2,1)S(1)}, bf16[32,3200]{1,0:T(8,128)(2,1)S(1)}, u32[]{:S(2)}, u32[]{:S(2)}) collective-permute-start(bf16[32,3200]{1,0:T(8,128)(2,1)S(1)} %join.2.refs_0_), channel_id=1, source_target_pairs={{0,37},{8,127},{32,69},{40,31},{64,101},{72,63},{96,5},{104,95},{4... | collective-permute-start | bytes 614408 | tf_op jit(solution)/shard_map/ppermute | solution.py:215
  38.0 5.2 %collective-permute-done.2.refs_1_ = bf16[32,3200]{1,0:T(8,128)(2,1)S(1)} collective-permute-done((bf16[32,3200]{1,0:T(8,128)(2,1)S(1)}, bf16[32,3200]{1,0:T(8,128)(2,1)S(1)}, u32[]{:S(2)}, u32[]{:S(2)}) %collective-permute-start.2) | collective-permute-done | bytes 204832 | tf_op jit(solution)/shard_map/ppermute | solution.py:215
  43.3 2.5 %collective-permute-done.3.refs_2_ = bf16[32,3200]{1,0:T(8,128)(2,1)S(1)} collective-permute-done((bf16[32,3200]{1,0:T(8,128)(2,1)S(1)}, bf16[32,3200]{1,0:T(8,128)(2,1)S(1)}, u32[]{:S(2)}, u32[]{:S(2)}) %collective-permute-start.3) | collective-permute-done | bytes 204832 | tf_op jit(solution)/shard_map/ppermute | solution.py:215
  45.8 2.3 %collective-permute-done.4.refs_3_ = bf16[32,3200]{1,0:T(8,128)(2,1)S(1)} collective-permute-done((bf16[32,3200]{1,0:T(8,128)(2,1)S(1)}, bf16[32,3200]{1,0:T(8,128)(2,1)S(1)}, u32[]{:S(2)}, u32[]{:S(2)}) %collective-permute-start.4) | collective-permute-done | bytes 204832 | tf_op jit(solution)/shard_map/ppermute | solution.py:215
  48.1 2.7 %collective-permute-start.5 = (bf16[128,3200]{1,0:T(8,128)(2,1)S(1)}, bf16[128,3200]{1,0:T(8,128)(2,1)S(1)}, u32[]{:S(2)}, u32[]{:S(2)}) collective-permute-start(bf16[128,3200]{1,0:T(8,128)(2,1)S(1)} %join.3.b0), channel_id=1, source_target_pairs={{0,2},{8,10},{32,34},{40,42},{64,66},{72,74},{96,98},{104,106},{4,... | collective-permute-start | bytes 2457608 | tf_op jit(solution)/shard_map/ppermute | solution.py:215
  52.2 17.8 %collective-permute-done.5.b1 = bf16[128,3200]{1,0:T(8,128)(2,1)S(1)} collective-permute-done((bf16[128,3200]{1,0:T(8,128)(2,1)S(1)}, bf16[128,3200]{1,0:T(8,128)(2,1)S(1)}, u32[]{:S(2)}, u32[]{:S(2)}) %collective-permute-start.5) | collective-permute-done | bytes 819232 | tf_op jit(solution)/shard_map/ppermute | solution.py:215
  70.0 1.7 %collective-permute-done.6.b2 = bf16[128,3200]{1,0:T(8,128)(2,1)S(1)} collective-permute-done((bf16[128,3200]{1,0:T(8,128)(2,1)S(1)}, bf16[128,3200]{1,0:T(8,128)(2,1)S(1)}, u32[]{:S(2)}, u32[]{:S(2)}) %collective-permute-start.6) | collective-permute-done | bytes 819232 | tf_op jit(solution)/shard_map/ppermute | solution.py:215
  71.7 3.2 %deal.1 = (bf16[256,3200]{1,0:T(8,128)(2,1)}, bf16[256,3200]{1,0:T(8,128)(2,1)}, bf16[512,3200]{1,0:T(8,128)(2,1)}) custom-call(bf16[128,3200]{1,0:T(8,128)(2,1)S(1)} %join.3.b0, bf16[128,3200]{1,0:T(8,128)(2,1)S(1)} %collective-permute-done.5.b1, bf16[128,3200]{1,0:T(8,128)(2,1)S(1)} %collective-permute-done.6.b2, ...), custom_call_target="tpu_custom_call" | custom-call | tf_op jit(solution)/shard_map/deal/pallas_call | solution.py:251
  75.0 1.6 %collective-permute-start.11 = (bf16[256,3200]{1,0:T(8,128)(2,1)}, bf16[256,3200]{1,0:T(8,128)(2,1)}, u32[]{:S(2)}, u32[]{:S(2)}) collective-permute-start(bf16[256,3200]{1,0:T(8,128)(2,1)} %get-tuple-element.39.refs_0_), channel_id=1, source_target_pairs={{0,1},{8,11},{32,33},{40,43},{64,65},{72,75},{96,97},{104,107},{4,... | collective-permute-start | bytes 4915208 | tf_op jit(solution)/shard_map/ppermute | solution.py:215
  76.6 1.7 %collective-permute-start.12 = (bf16[256,3200]{1,0:T(8,128)(2,1)}, bf16[256,3200]{1,0:T(8,128)(2,1)}, u32[]{:S(2)}, u32[]{:S(2)}) collective-permute-start(bf16[256,3200]{1,0:T(8,128)(2,1)} %get-tuple-element.39.refs_0_), channel_id=1, source_target_pairs={{0,4},{8,28},{32,36},{40,60},{64,68},{72,92},{96,100},{104,124},{4... | collective-permute-start | bytes 4915208 | tf_op jit(solution)/shard_map/ppermute | solution.py:215
  79.0 2.9 %weighted.4.left = bf16[512,384]{1,0:T(8,128)(2,1)S(1)} custom-call(s32[1]{0:T(128)} %bitcast.1.place, f32[1]{0:T(128)} %dynamic_slice.12.omega, bf16[256,3200]{1,0:T(8,128)(2,1)} %get-tuple-element.39.refs_0_, bf16[256,3200]{1,0:T(8,128)(2,1)} %get-tuple-element.38.refs_1_, f32[8,128]{1,0:T(8,128)S(1)} %broadcast_in_dim.7.refs_2_), custom_call_target="tpu_custom_call" | custom-call | tf_op jit(solution)/shard_map/weighted/pallas_call | solution.py:296
  82.0 2.5 %collective-permute-start.9 = (bf16[256,3200]{1,0:T(8,128)(2,1)}, bf16[256,3200]{1,0:T(8,128)(2,1)S(1)}, u32[]{:S(2)}, u32[]{:S(2)}) collective-permute-start(bf16[256,3200]{1,0:T(8,128)(2,1)} %get-tuple-element.38.refs_1_), channel_id=1, source_target_pairs={{0,1},{8,11},{32,33},{40,43},{64,65},{72,75},{96,97},{104,107},{4,... | collective-permute-start | bytes 4915208 | tf_op jit(solution)/shard_map/ppermute | solution.py:215
  84.5 2.3 %collective-permute-start.10 = (bf16[256,3200]{1,0:T(8,128)(2,1)}, bf16[256,3200]{1,0:T(8,128)(2,1)S(1)}, u32[]{:S(2)}, u32[]{:S(2)}) collective-permute-start(bf16[256,3200]{1,0:T(8,128)(2,1)} %get-tuple-element.38.refs_1_), channel_id=1, source_target_pairs={{0,4},{8,28},{32,36},{40,60},{64,68},{72,92},{96,100},{104,124},{4... | collective-permute-start | bytes 4915208 | tf_op jit(solution)/shard_map/ppermute | solution.py:215
  86.8 3.9 %partial_own.3 = (f32[384,3072]{1,0:T(8,128)S(1)}, f32[8,128]{1,0:T(8,128)S(1)}) custom-call(bf16[512,384]{1,0:T(8,128)(2,1)S(1)} %weighted.4.left, bf16[256,3200]{1,0:T(8,128)(2,1)} %get-tuple-element.39.refs_0_, bf16[256,3200]{1,0:T(8,128)(2,1)} %get-tuple-element.38.refs_1_, f32[8,128]{1,0:T(8,128)S(1)} %broadcast_in_dim.7.refs_2_), custom_call_target="tpu_custom_call" | custom-call | flops 1207959552 | bytes 12582912 | tf_op jit(solution)/shard_map/partial_own/pallas_call | solution.py:354
  90.7 3.9 %partial_other.3 = (f32[384,3072]{1,0:T(8,128)S(1)}, f32[8,128]{1,0:T(8,128)S(1)}) custom-call(bf16[512,384]{1,0:T(8,128)(2,1)S(1)} %collective-permute-done.13.left, bf16[256,3200]{1,0:T(8,128)(2,1)} %get-tuple-element.39.refs_0_, bf16[256,3200]{1,0:T(8,128)(2,1)} %get-tuple-element.38.refs_1_, f32[8,128]{1,0:T(8,128)S(1)} %get-tuple-element.40.refs_2_), custom_call_target="tpu_custom_call" | custom-call | flops 1207959552 | bytes 12582912 | tf_op jit(solution)/shard_map/partial_other/pallas_call | solution.py:354
  97.2 2.9 %weighted.5.left = bf16[512,384]{1,0:T(8,128)(2,1)S(1)} custom-call(s32[1]{0:T(128)} %bitcast.1.place, f32[1]{0:T(128)} %dynamic_slice.12.omega, bf16[256,3200]{1,0:T(8,128)(2,1)} %collective-permute-done.11.refs_0_, bf16[256,3200]{1,0:T(8,128)(2,1)} %collective-permute-done.12.refs_1_, f32[8,128]{1,0:T(8,128)S(1)} %get-tuple-element.41.refs_2_.refs_3_), custom_call_target="tpu_custom_call" | custom-call | tf_op jit(solution)/shard_map/weighted/pallas_call | solution.py:296
  100.1 3.6 %collective-permute-start.14 = (bf16[512,384]{1,0:T(8,128)(2,1)S(1)}, bf16[512,384]{1,0:T(8,128)(2,1)S(1)}, u32[]{:S(2)}, u32[]{:S(2)}) collective-permute-start(bf16[512,384]{1,0:T(8,128)(2,1)S(1)} %weighted.5.left), channel_id=1, source_target_pairs={{0,8},{8,0},{32,40},{40,32},{64,72},{72,64},{96,104},{104,96},{4,1... | collective-permute-start | bytes 1179656 | tf_op jit(solution)/shard_map/ppermute | solution.py:215
  103.7 4.1 %partial_own.4 = (f32[384,3072]{1,0:T(8,128)S(1)}, f32[8,128]{1,0:T(8,128)S(1)}) custom-call(bf16[512,384]{1,0:T(8,128)(2,1)S(1)} %weighted.5.left, bf16[256,3200]{1,0:T(8,128)(2,1)} %collective-permute-done.11.refs_0_, bf16[256,3200]{1,0:T(8,128)(2,1)} %collective-permute-done.12.refs_1_, ...), custom_call_target="tpu_custom_call", output_to_operand_aliasing={{0}: (3, {})} | custom-call | flops 1207959552 | bytes 12582912 | tf_op jit(solution)/shard_map/partial_own/pallas_call | solution.py:354
  107.8 4.1 %partial_other.4 = (f32[384,3072]{1,0:T(8,128)S(1)}, f32[8,128]{1,0:T(8,128)S(1)}) custom-call(bf16[512,384]{1,0:T(8,128)(2,1)S(1)} %collective-permute-done.14.left, bf16[256,3200]{1,0:T(8,128)(2,1)} %collective-permute-done.11.refs_0_, bf16[256,3200]{1,0:T(8,128)(2,1)} %collective-permute-done.12.refs_1_, ...), custom_call_target="tpu_custom_call", output_to_operand_aliasing={{0}: (3, {})} | custom-call | flops 1207959552 | bytes 12582912 | tf_op jit(solution)/shard_map/partial_other/pallas_call | solution.py:354
  115.6 3.8 %collective-permute-start.15 = (bf16[512,384]{1,0:T(8,128)(2,1)S(1)}, bf16[512,384]{1,0:T(8,128)(2,1)S(1)}, u32[]{:S(2)}, u32[]{:S(2)}) collective-permute-start(bf16[512,384]{1,0:T(8,128)(2,1)S(1)} %weighted.6.left), channel_id=1, source_target_pairs={{0,8},{8,0},{32,40},{40,32},{64,72},{72,64},{96,104},{104,96},{4,1... | collective-permute-start | bytes 1179656 | tf_op jit(solution)/shard_map/ppermute | solution.py:215
  119.4 2.2 %partial_own.5 = (f32[384,3072]{1,0:T(8,128)S(1)}, f32[8,128]{1,0:T(8,128)S(1)}) custom-call(bf16[512,384]{1,0:T(8,128)(2,1)S(1)} %weighted.6.left, bf16[256,3200]{1,0:T(8,128)(2,1)S(1)} %collective-permute-done.9.refs_0_, bf16[256,3200]{1,0:T(8,128)(2,1)S(1)} %collective-permute-done.10.refs_1_, ...), custom_call_target="tpu_custom_call", output_to_operand_aliasing={{0}: (3, {})} | custom-call | flops 1207959552 | bytes 12582912 | tf_op jit(solution)/shard_map/partial_own/pallas_call | solution.py:354
  121.6 2.2 %partial_other.5 = (f32[384,3072]{1,0:T(8,128)S(1)}, f32[8,128]{1,0:T(8,128)S(1)}) custom-call(bf16[512,384]{1,0:T(8,128)(2,1)S(1)} %collective-permute-done.15.left, bf16[256,3200]{1,0:T(8,128)(2,1)S(1)} %collective-permute-done.9.refs_0_, bf16[256,3200]{1,0:T(8,128)(2,1)S(1)} %collective-permute-done.10.refs_1_, ...), custom_call_target="tpu_custom_call", output_to_operand_aliasing={{0}: (3, {})} | custom-call | flops 1207959552 | bytes 12582912 | tf_op jit(solution)/shard_map/partial_other/pallas_call | solution.py:354
  124.8 2.1 %own_rows.2 = (f32[384,6144]{1,0:T(8,128)}, f32[8,128]{1,0:T(8,128)S(1)}) custom-call(s32[1]{0:T(128)} %bitcast.core, bf16[512,384]{1,0:T(8,128)(2,1)S(1)} %weighted.7.left, bf16[512,3200]{1,0:T(8,128)(2,1)S(1)} %collective-permute-done.8.refs_0_, f32[384,3072]{1,0:T(8,128)S(1)} %get-tuple-element.51.refs_1_, f32[8,128]{1,0:T(8,128)S(1)} %get-tuple-element.49.refs_1_.refs_2_), custom_call_target="tpu_custom_call" | custom-call | flops 603979776 | bytes 6291456 | tf_op jit(solution)/shard_map/own_rows/pallas_call | solution.py:390
  129.6 2.6 %own_rows.3 = (f32[384,6144]{1,0:T(8,128)}, f32[8,128]{1,0:T(8,128)}) custom-call(s32[1]{0:T(128)} %bitcast.core, bf16[512,384]{1,0:T(8,128)(2,1)S(1)} %weighted.7.left, bf16[512,3200]{1,0:T(8,128)(2,1)S(1)} %collective-permute-done.8.refs_0_, f32[384,3072]{1,0:T(8,128)S(1)} %get-tuple-element.51.refs_1_, ...), custom_call_target="tpu_custom_call", output_to_operand_aliasing={{0}: (4, {})} | custom-call | flops 603979776 | bytes 6291456 | tf_op jit(solution)/shard_map/own_rows/pallas_call | solution.py:390
  132.7 2.3 %finish.1 = f32[384,6144]{1,0:T(8,128)} custom-call(s32[1]{0:T(128)} %bitcast.core, bf16[384,1536]{1,0:T(8,128)(2,1)S(1)} %collective-permute-done.17.r0, bf16[384,1536]{1,0:T(8,128)(2,1)S(1)} %collective-permute-done.18.r1, f32[384,6144]{1,0:T(8,128)} %get-tuple-element.54._), custom_call_target="tpu_custom_call", output_to_operand_aliasing={{}: (3, {})} | custom-call | tf_op jit(solution)/shard_map/finish/pallas_call | solution.py:444
  (45 shorter events, 17.5 us)
Async XLA Ops:
  2.0 17.5 %all-to-all-start = ((bf16[8,24,1024]{2,1,0:T(8,128)(2,1)}), bf16[8,24,1024]{2,1,0:T(8,128)(2,1)S(1)}, u32[]{:S(2)}, u32[]{:S(2)}) async-start(bf16[8,24,1024]{2,1,0:T(8,128)(2,1)} %get-tuple-element.30), calls=%async_computation | async-start | bytes 786432 | tf_op jit(solution)/shard_map/all_to_all | solution.py:466
  19.5 3.5 %collective-permute-start = (bf16[8,24,1024]{2,1,0:T(8,128)(2,1)S(1)}, bf16[8,24,1024]{2,1,0:T(8,128)(2,1)S(1)}, u32[]{:S(2)}, u32[]{:S(2)}) collective-permute-start(bf16[8,24,1024]{2,1,0:T(8,128)(2,1)S(1)} %all-to-all-done.mine), channel_id=1, source_target_pairs={{0,8},{8,0},{32,40},{40,32},{64,72},{72,64},{96,104},{104,96},{4,1... | collective-permute-start | bytes 1179656 | tf_op jit(solution)/shard_map/ppermute | solution.py:215
  27.6 50.7 %copy-start = (f32[8]{0:T(128)S(1)}, f32[8]{0:T(128)}, u32[]{:S(2)}) copy-start(f32[8]{0:T(128)} %param.16) | copy-start | bytes 100
  27.6 2.7 %collective-permute-start.1 = (bf16[16,3200]{1,0:T(8,128)(2,1)S(1)}, bf16[16,3200]{1,0:T(8,128)(2,1)S(1)}, u32[]{:S(2)}, u32[]{:S(2)}) collective-permute-start(bf16[16,3200]{1,0:T(8,128)(2,1)S(1)} %get-tuple-element.36), channel_id=1, source_target_pairs={{0,8},{8,0},{32,40},{40,32},{64,72},{72,64},{96,104},{104,96},{4,1... | collective-permute-start | bytes 307208 | tf_op jit(solution)/shard_map/ppermute | solution.py:215
  30.4 12.9 %collective-permute-start.2 = (bf16[32,3200]{1,0:T(8,128)(2,1)S(1)}, bf16[32,3200]{1,0:T(8,128)(2,1)S(1)}, u32[]{:S(2)}, u32[]{:S(2)}) collective-permute-start(bf16[32,3200]{1,0:T(8,128)(2,1)S(1)} %join.2.refs_0_), channel_id=1, source_target_pairs={{0,82},{8,90},{32,114},{40,122},{64,18},{72,26},{96,50},{104,58},{... | collective-permute-start | bytes 614408 | tf_op jit(solution)/shard_map/ppermute | solution.py:215
  33.6 12.2 %collective-permute-start.3 = (bf16[32,3200]{1,0:T(8,128)(2,1)S(1)}, bf16[32,3200]{1,0:T(8,128)(2,1)S(1)}, u32[]{:S(2)}, u32[]{:S(2)}) collective-permute-start(bf16[32,3200]{1,0:T(8,128)(2,1)S(1)} %join.2.refs_0_), channel_id=1, source_target_pairs={{0,37},{8,127},{32,69},{40,31},{64,101},{72,63},{96,5},{104,95},{4... | collective-permute-start | bytes 614408 | tf_op jit(solution)/shard_map/ppermute | solution.py:215
  38.0 10.0 %collective-permute-start.4 = (bf16[32,3200]{1,0:T(8,128)(2,1)S(1)}, bf16[32,3200]{1,0:T(8,128)(2,1)S(1)}, u32[]{:S(2)}, u32[]{:S(2)}) collective-permute-start(bf16[32,3200]{1,0:T(8,128)(2,1)S(1)} %join.2.refs_0_), channel_id=1, source_target_pairs={{0,119},{8,45},{32,23},{40,77},{64,55},{72,109},{96,87},{104,13},{... | collective-permute-start | bytes 614408 | tf_op jit(solution)/shard_map/ppermute | solution.py:215
  48.1 21.8 %collective-permute-start.5 = (bf16[128,3200]{1,0:T(8,128)(2,1)S(1)}, bf16[128,3200]{1,0:T(8,128)(2,1)S(1)}, u32[]{:S(2)}, u32[]{:S(2)}) collective-permute-start(bf16[128,3200]{1,0:T(8,128)(2,1)S(1)} %join.3.b0), channel_id=1, source_target_pairs={{0,2},{8,10},{32,34},{40,42},{64,66},{72,74},{96,98},{104,106},{4,... | collective-permute-start | bytes 2457608 | tf_op jit(solution)/shard_map/ppermute | solution.py:215
  50.8 20.8 %collective-permute-start.6 = (bf16[128,3200]{1,0:T(8,128)(2,1)S(1)}, bf16[128,3200]{1,0:T(8,128)(2,1)S(1)}, u32[]{:S(2)}, u32[]{:S(2)}) collective-permute-start(bf16[128,3200]{1,0:T(8,128)(2,1)S(1)} %join.3.b0), channel_id=1, source_target_pairs={{0,16},{8,24},{32,48},{40,56},{64,80},{72,88},{96,112},{104,120},{... | collective-permute-start | bytes 2457608 | tf_op jit(solution)/shard_map/ppermute | solution.py:215
  51.6 20.2 %collective-permute-start.7 = (bf16[128,3200]{1,0:T(8,128)(2,1)S(1)}, bf16[128,3200]{1,0:T(8,128)(2,1)S(1)}, u32[]{:S(2)}, u32[]{:S(2)}) collective-permute-start(bf16[128,3200]{1,0:T(8,128)(2,1)S(1)} %join.3.b0), channel_id=1, source_target_pairs={{0,64},{8,72},{32,96},{40,104},{64,0},{72,8},{96,32},{104,40},{4,6... | collective-permute-start | bytes 2457608 | tf_op jit(solution)/shard_map/ppermute | solution.py:215
  75.0 48.8 %collective-permute-start.8 = (bf16[512,3200]{1,0:T(8,128)(2,1)}, bf16[512,3200]{1,0:T(8,128)(2,1)S(1)}, u32[]{:S(2)}, u32[]{:S(2)}) collective-permute-start(bf16[512,3200]{1,0:T(8,128)(2,1)} %get-tuple-element.37), channel_id=1, source_target_pairs={{0,32},{8,104},{32,64},{40,8},{64,96},{72,40},{96,0},{104,72},{4,3... | collective-permute-start | bytes 9830408 | tf_op jit(solution)/shard_map/ppermute | solution.py:215
  75.0 20.6 %collective-permute-start.11 = (bf16[256,3200]{1,0:T(8,128)(2,1)}, bf16[256,3200]{1,0:T(8,128)(2,1)}, u32[]{:S(2)}, u32[]{:S(2)}) collective-permute-start(bf16[256,3200]{1,0:T(8,128)(2,1)} %get-tuple-element.39.refs_0_), channel_id=1, source_target_pairs={{0,1},{8,11},{32,33},{40,43},{64,65},{72,75},{96,97},{104,107},{4,... | collective-permute-start | bytes 4915208 | tf_op jit(solution)/shard_map/ppermute | solution.py:215
  76.6 20.6 %collective-permute-start.12 = (bf16[256,3200]{1,0:T(8,128)(2,1)}, bf16[256,3200]{1,0:T(8,128)(2,1)}, u32[]{:S(2)}, u32[]{:S(2)}) collective-permute-start(bf16[256,3200]{1,0:T(8,128)(2,1)} %get-tuple-element.39.refs_0_), channel_id=1, source_target_pairs={{0,4},{8,28},{32,36},{40,60},{64,68},{72,92},{96,100},{104,124},{4... | collective-permute-start | bytes 4915208 | tf_op jit(solution)/shard_map/ppermute | solution.py:215
  81.9 2.6 %collective-permute-start.13 = (bf16[512,384]{1,0:T(8,128)(2,1)S(1)}, bf16[512,384]{1,0:T(8,128)(2,1)S(1)}, u32[]{:S(2)}, u32[]{:S(2)}) collective-permute-start(bf16[512,384]{1,0:T(8,128)(2,1)S(1)} %weighted.4.left), channel_id=1, source_target_pairs={{0,8},{8,0},{32,40},{40,32},{64,72},{72,64},{96,104},{104,96},{4,1... | collective-permute-start | bytes 1179656 | tf_op jit(solution)/shard_map/ppermute | solution.py:215
  82.0 31.0 %collective-permute-start.9 = (bf16[256,3200]{1,0:T(8,128)(2,1)}, bf16[256,3200]{1,0:T(8,128)(2,1)S(1)}, u32[]{:S(2)}, u32[]{:S(2)}) collective-permute-start(bf16[256,3200]{1,0:T(8,128)(2,1)} %get-tuple-element.38.refs_1_), channel_id=1, source_target_pairs={{0,1},{8,11},{32,33},{40,43},{64,65},{72,75},{96,97},{104,107},{4,... | collective-permute-start | bytes 4915208 | tf_op jit(solution)/shard_map/ppermute | solution.py:215
  84.5 30.2 %collective-permute-start.10 = (bf16[256,3200]{1,0:T(8,128)(2,1)}, bf16[256,3200]{1,0:T(8,128)(2,1)S(1)}, u32[]{:S(2)}, u32[]{:S(2)}) collective-permute-start(bf16[256,3200]{1,0:T(8,128)(2,1)} %get-tuple-element.38.refs_1_), channel_id=1, source_target_pairs={{0,4},{8,28},{32,36},{40,60},{64,68},{72,92},{96,100},{104,124},{4... | collective-permute-start | bytes 4915208 | tf_op jit(solution)/shard_map/ppermute | solution.py:215
  100.1 7.8 %collective-permute-start.14 = (bf16[512,384]{1,0:T(8,128)(2,1)S(1)}, bf16[512,384]{1,0:T(8,128)(2,1)S(1)}, u32[]{:S(2)}, u32[]{:S(2)}) collective-permute-start(bf16[512,384]{1,0:T(8,128)(2,1)S(1)} %weighted.5.left), channel_id=1, source_target_pairs={{0,8},{8,0},{32,40},{40,32},{64,72},{72,64},{96,104},{104,96},{4,1... | collective-permute-start | bytes 1179656 | tf_op jit(solution)/shard_map/ppermute | solution.py:215
  115.6 6.0 %collective-permute-start.15 = (bf16[512,384]{1,0:T(8,128)(2,1)S(1)}, bf16[512,384]{1,0:T(8,128)(2,1)S(1)}, u32[]{:S(2)}, u32[]{:S(2)}) collective-permute-start(bf16[512,384]{1,0:T(8,128)(2,1)S(1)} %weighted.6.left), channel_id=1, source_target_pairs={{0,8},{8,0},{32,40},{40,32},{64,72},{72,64},{96,104},{104,96},{4,1... | collective-permute-start | bytes 1179656 | tf_op jit(solution)/shard_map/ppermute | solution.py:215
  124.7 2.2 %collective-permute-start.16 = (bf16[512,384]{1,0:T(8,128)(2,1)S(1)}, bf16[512,384]{1,0:T(8,128)(2,1)S(1)}, u32[]{:S(2)}, u32[]{:S(2)}) collective-permute-start(bf16[512,384]{1,0:T(8,128)(2,1)S(1)} %weighted.7.left), channel_id=1, source_target_pairs={{0,8},{8,0},{32,40},{40,32},{64,72},{72,64},{96,104},{104,96},{4,1... | collective-permute-start | bytes 1179656 | tf_op jit(solution)/shard_map/ppermute | solution.py:215
  128.0 4.3 %collective-permute-start.17 = (bf16[384,1536]{1,0:T(8,128)(2,1)S(1)}, bf16[384,1536]{1,0:T(8,128)(2,1)S(1)}, u32[]{:S(2)}, u32[]{:S(2)}) collective-permute-start(bf16[384,1536]{1,0:T(8,128)(2,1)S(1)} %other_rows.2), channel_id=1, source_target_pairs={{0,8},{8,0},{32,40},{40,32},{64,72},{72,64},{96,104},{104,96},{4,1... | collective-permute-start | bytes 3538952 | tf_op jit(solution)/shard_map/ppermute | solution.py:215
  129.5 3.2 %collective-permute-start.18 = (bf16[384,1536]{1,0:T(8,128)(2,1)S(1)}, bf16[384,1536]{1,0:T(8,128)(2,1)S(1)}, u32[]{:S(2)}, u32[]{:S(2)}) collective-permute-start(bf16[384,1536]{1,0:T(8,128)(2,1)S(1)} %other_rows.3), channel_id=1, source_target_pairs={{0,8},{8,0},{32,40},{40,32},{64,72},{72,64},{96,104},{104,96},{4,1... | collective-permute-start | bytes 3538952 | tf_op jit(solution)/shard_map/ppermute | solution.py:215

commit v10 on v9

--- a/solution.py
+++ b/solution.py
@@ -220,7 +220,7 @@
 
 
 def join_kernel(n, *refs):
-    out = refs[n]
+    out = refs[-1]
     row = 0
     for ref in refs[:n]:
         out[row : row + ref.shape[0], :] = ref[...]
@@ -239,20 +239,18 @@
     )(*blocks)
 
 
-def deal_kernel(b0, b1, b2, b3, out0, out1, both):
+def deal_kernel(b0, b1, b2, b3, out0, out1):
     for i, ref in enumerate((b0, b1, b2, b3)):
-        for half, out in enumerate((out0, out1)):
-            rows = ref[half * 64 : half * 64 + 64, :]
-            out[i * 64 : i * 64 + 64, :] = rows
-            both[half * 256 + i * 64 : half * 256 + i * 64 + 64, :] = rows
+        out0[i * 64 : i * 64 + 64, :] = ref[0:64, :]
+        out1[i * 64 : i * 64 + 64, :] = ref[64:128, :]
 
 
 def deal(blocks):
     return pl.pallas_call(
         deal_kernel,
-        out_shape=[pltpu.VMEM((rows, WIDE), jnp.bfloat16) for rows in (256, 256, 512)],
+        out_shape=[pltpu.VMEM((256, WIDE), jnp.bfloat16)] * 2,
         in_specs=[VM] * 4,
-        out_specs=[VM] * 3,
+        out_specs=[VM] * 2,
         compiler_params=PARAMS,
         name="deal",
     )(*blocks)
@@ -482,21 +480,21 @@
     keep = rho_pick(spec, kept, meta)
 
     a = join(level(join([keep, swapped]), NEAR))
-    *sources, both = deal(level(a, EVEN))
+    sources = deal(level(a, EVEN))
     got = {(h, 0): m for h, m in enumerate(sources)}
     for h in range(2):
         for s in (1, 2):
             got[h, s] = send(sources[h], offset_pairs(STEP[s]))
-    got["z"] = send(both, offset_pairs(STEP[3]))
+    got["z"] = send(join(sources), offset_pairs(STEP[3]))
 
     place = lax.div(ga, 2).astype(jnp.int32).reshape(1)
     mine_omega = lax.dynamic_slice(omega, (ba,), (1,))
     core = core.reshape(1)
     own = other = None
     tie = jnp.zeros(TIE.shape, TIE.dtype)
-    groups = (((0, 0), (1, 0)), ((0, 1), (0, 2)), ((1, 1), (1, 2)), ((0, 3), (1, 3)))
+    groups = (((0, 0), (1, 0)), ((0, 1), (0, 2)), ((0, 3), (1, 3)), ((1, 1), (1, 2)))
     for names in groups:
-        pieces = [in_vmem(got[name]) for name in (("z",) if names is groups[-1] else names)]
+        pieces = [in_vmem(got[name]) for name in (("z",) if (0, 3) in names else names)]
         left = weighted(place, mine_omega, pieces, tie)
         mirror = send(left, core_pairs())
         if names is not groups[-1]:

time: 136 us -> 137 us (level)
  Pallas kernels: 49.2 us -> 51.8 us
  waiting for transfers between devices: 42.2 us -> 40.6 us
    pallas_call x2 -> x3, Pallas kernels: 0.07 us -> 3.93 us  [join(): pl.pallas_call(functools.partial(join_kernel, len(blocks)), out_shape=plt...]
    ppermute x19, waiting for transfers between devices: 36.4 us -> 34.7 us  [send(): return lax.ppermute(a, ('ga', 'ba'), pairs)]
  transfers between devices with their start and end apart: 20 -> 20, of which waited for: 13 -> 11; matrix products, arithmetic and copies ran while one was open for 3% -> 3% of each run, Pallas kernels for 26% -> 26%
where the time goes in v10:
time: 137 us
  Pallas kernels  51.8 us (38%)
  waiting for transfers between devices  40.6 us (30%)
  starting transfers between devices  39.8 us (29%)
  local copies, waits for them, and re-layouts  2.52 us (2%)
  other arithmetic  1.41 us (1%)
    ppermute x19, waiting for transfers between devices, send(): return lax.ppermute(a, ('ga', 'ba'), pairs)  34.7 us
    ppermute x19, starting transfers between devices, send(): return lax.ppermute(a, ('ga', 'ba'), pairs)  31.3 us
    pallas_call x6, Pallas kernels, partial_rows(): pl.pallas_call(functools.partial(partial_kernel, names, len(pieces), othe...  20.4 us
    all_to_all x1, starting transfers between devices, on_device(): psi = lax.all_to_all(rows, 'ga', 0, 0, tiled=True, axis_index_groups=kinds)  8.51 us
    pallas_call x4, Pallas kernels, weighted(): pl.pallas_call(weighted_kernel, out_shape=pltpu.VMEM((sum((p.shape[0] for...  7.65 us
    all_to_all x1, waiting for transfers between devices, on_device(): psi = lax.all_to_all(rows, 'ga', 0, 0, tiled=True, axis_index_groups=kinds)  5.85 us
    pallas_call x2, Pallas kernels, own_rows(): pl.pallas_call(functools.partial(own_kernel, names, len(pieces), start),...  4.7 us
    pallas_call x1, Pallas kernels, rho_spectrum(): pl.pallas_call(transform_kernel, out_shape=[pltpu.VMEM((PAIRS * 64, 256),...  4.58 us
  transfers between devices with their start and end apart: 20, of which 11 were waited for; matrix products, arithmetic and copies ran while one was open for 3% of the time, Pallas kernels for 26%

profile of v10, /device:TPU:1, one launch (start us, length us, event | category | flops | bytes accessed | tf_op | source)
XLA Modules:
  0.0 136.5 jit_solution(17968587788942953411)
XLA Ops:
  0.0 2.0 %payload.1 = (bf16[8,24,1024]{2,1,0:T(8,128)(2,1)}, bf16[2,256,256]{2,1,0:T(8,128)(2,1)S(1)}, f32[128,256]{1,0:T(8,128)S(1)}, f32[128,256]{1,0:T(8,128)S(1)}, bf16[512,256]{1,0:T(8,128)(2,1)S(1)}) custom-call(bf16[4,2048]{1,0:T(4,128)(2,1)} %val.1, bf16[64,2048]{1,0:T(8,128)(2,1)} %con.1, bf16[2,256,256]{2,1,0:T(8,128)(2,1)} %constant.39.clone.first, ...), custom_call_target="tpu_custom_call" | custom-call | tf_op jit(solution)/shard_map/payload/pallas_call | solution.py:82
  2.0 8.5 %all-to-all-start = ((bf16[8,24,1024]{2,1,0:T(8,128)(2,1)}), bf16[8,24,1024]{2,1,0:T(8,128)(2,1)S(1)}, u32[]{:S(2)}, u32[]{:S(2)}) async-start(bf16[8,24,1024]{2,1,0:T(8,128)(2,1)} %get-tuple-element.29), calls=%async_computation | async-start | bytes 786432 | tf_op jit(solution)/shard_map/all_to_all | solution.py:464
  13.6 5.8 %all-to-all-done.mine = bf16[8,24,1024]{2,1,0:T(8,128)(2,1)S(1)} async-done(((bf16[8,24,1024]{2,1,0:T(8,128)(2,1)}), bf16[8,24,1024]{2,1,0:T(8,128)(2,1)S(1)}, u32[]{:S(2)}, u32[]{:S(2)}) %all-to-all-start) | async-done | bytes 393248 | tf_op jit(solution)/shard_map/all_to_all | solution.py:464
  19.5 2.2 %collective-permute-start = (bf16[8,24,1024]{2,1,0:T(8,128)(2,1)S(1)}, bf16[8,24,1024]{2,1,0:T(8,128)(2,1)S(1)}, u32[]{:S(2)}, u32[]{:S(2)}) collective-permute-start(bf16[8,24,1024]{2,1,0:T(8,128)(2,1)S(1)} %all-to-all-done.mine), channel_id=1, source_target_pairs={{0,8},{8,0},{32,40},{40,32},{64,72},{72,64},{96,104},{104,96},{4,1... | collective-permute-start | bytes 1179656 | tf_op jit(solution)/shard_map/ppermute | solution.py:215
  23.0 4.6 %rho_spectrum.1 = (bf16[1024,256]{1,0:T(8,128)(2,1)S(1)}, bf16[16,3200]{1,0:T(8,128)(2,1)S(1)}) custom-call(s32[1]{0:T(128)} %bitcast.core, bf16[8,24,1024]{2,1,0:T(8,128)(2,1)S(1)} %all-to-all-done.mine, bf16[8,24,1024]{2,1,0:T(8,128)(2,1)S(1)} %collective-permute-done.others, s32[1,3072]{1,0:T(1,128)S(1)} %get-tuple-element.54.gidx, ...), custom_call_target="tpu_custom_call" | custom-call | tf_op jit(solution)/shard_map/rho_spectrum/pallas_call | solution.py:168
  28.0 2.3 %rho_pick.1.refs_0_ = bf16[16,3200]{1,0:T(8,128)(2,1)S(1)} custom-call(bf16[1024,256]{1,0:T(8,128)(2,1)S(1)} %get-tuple-element.34.spec, s32[1,3072]{1,0:T(1,128)S(1)} %get-tuple-element.53.gidx, bf16[16,128]{1,0:T(8,128)(2,1)S(1)} %pad.4.meta), custom_call_target="tpu_custom_call" | custom-call | tf_op jit(solution)/shard_map/rho_pick/pallas_call | solution.py:184
  30.3 3.2 %collective-permute-start.2 = (bf16[32,3200]{1,0:T(8,128)(2,1)S(1)}, bf16[32,3200]{1,0:T(8,128)(2,1)S(1)}, u32[]{:S(2)}, u32[]{:S(2)}) collective-permute-start(bf16[32,3200]{1,0:T(8,128)(2,1)S(1)} %join.3.refs_0_), channel_id=1, source_target_pairs={{0,82},{8,90},{32,114},{40,122},{64,18},{72,26},{96,50},{104,58},{... | collective-permute-start | bytes 614408 | tf_op jit(solution)/shard_map/ppermute | solution.py:215
  33.6 4.4 %collective-permute-start.3 = (bf16[32,3200]{1,0:T(8,128)(2,1)S(1)}, bf16[32,3200]{1,0:T(8,128)(2,1)S(1)}, u32[]{:S(2)}, u32[]{:S(2)}) collective-permute-start(bf16[32,3200]{1,0:T(8,128)(2,1)S(1)} %join.3.refs_0_), channel_id=1, source_target_pairs={{0,37},{8,127},{32,69},{40,31},{64,101},{72,63},{96,5},{104,95},{4... | collective-permute-start | bytes 614408 | tf_op jit(solution)/shard_map/ppermute | solution.py:215
  38.0 5.2 %collective-permute-done.2.refs_1_ = bf16[32,3200]{1,0:T(8,128)(2,1)S(1)} collective-permute-done((bf16[32,3200]{1,0:T(8,128)(2,1)S(1)}, bf16[32,3200]{1,0:T(8,128)(2,1)S(1)}, u32[]{:S(2)}, u32[]{:S(2)}) %collective-permute-start.2) | collective-permute-done | bytes 204832 | tf_op jit(solution)/shard_map/ppermute | solution.py:215
  43.3 2.5 %collective-permute-done.3.refs_2_ = bf16[32,3200]{1,0:T(8,128)(2,1)S(1)} collective-permute-done((bf16[32,3200]{1,0:T(8,128)(2,1)S(1)}, bf16[32,3200]{1,0:T(8,128)(2,1)S(1)}, u32[]{:S(2)}, u32[]{:S(2)}) %collective-permute-start.3) | collective-permute-done | bytes 204832 | tf_op jit(solution)/shard_map/ppermute | solution.py:215
  45.8 2.3 %collective-permute-done.4.refs_3_ = bf16[32,3200]{1,0:T(8,128)(2,1)S(1)} collective-permute-done((bf16[32,3200]{1,0:T(8,128)(2,1)S(1)}, bf16[32,3200]{1,0:T(8,128)(2,1)S(1)}, u32[]{:S(2)}, u32[]{:S(2)}) %collective-permute-start.4) | collective-permute-done | bytes 204832 | tf_op jit(solution)/shard_map/ppermute | solution.py:215
  48.1 2.7 %collective-permute-start.5 = (bf16[128,3200]{1,0:T(8,128)(2,1)S(1)}, bf16[128,3200]{1,0:T(8,128)(2,1)S(1)}, u32[]{:S(2)}, u32[]{:S(2)}) collective-permute-start(bf16[128,3200]{1,0:T(8,128)(2,1)S(1)} %join.4.b0), channel_id=1, source_target_pairs={{0,2},{8,10},{32,34},{40,42},{64,66},{72,74},{96,98},{104,106},{4,... | collective-permute-start | bytes 2457608 | tf_op jit(solution)/shard_map/ppermute | solution.py:215
  52.1 17.8 %collective-permute-done.5.b1 = bf16[128,3200]{1,0:T(8,128)(2,1)S(1)} collective-permute-done((bf16[128,3200]{1,0:T(8,128)(2,1)S(1)}, bf16[128,3200]{1,0:T(8,128)(2,1)S(1)}, u32[]{:S(2)}, u32[]{:S(2)}) %collective-permute-start.5) | collective-permute-done | bytes 819232 | tf_op jit(solution)/shard_map/ppermute | solution.py:215
  70.0 1.7 %collective-permute-done.6.b2 = bf16[128,3200]{1,0:T(8,128)(2,1)S(1)} collective-permute-done((bf16[128,3200]{1,0:T(8,128)(2,1)S(1)}, bf16[128,3200]{1,0:T(8,128)(2,1)S(1)}, u32[]{:S(2)}, u32[]{:S(2)}) %collective-permute-start.6) | collective-permute-done | bytes 819232 | tf_op jit(solution)/shard_map/ppermute | solution.py:215
  71.7 1.9 %deal.1 = (bf16[256,3200]{1,0:T(8,128)(2,1)}, bf16[256,3200]{1,0:T(8,128)(2,1)}) custom-call(bf16[128,3200]{1,0:T(8,128)(2,1)S(1)} %join.4.b0, bf16[128,3200]{1,0:T(8,128)(2,1)S(1)} %collective-permute-done.5.b1, bf16[128,3200]{1,0:T(8,128)(2,1)S(1)} %collective-permute-done.6.b2, bf16[128,3200]{1,0:T(8,128)(2,1)S(1)} %collective-permute-done.7.b3), custom_call_target="tpu_custom_call" | custom-call | tf_op jit(solution)/shard_map/deal/pallas_call | solution.py:249
  73.6 3.9 %join.5 = bf16[512,3200]{1,0:T(8,128)(2,1)} custom-call(bf16[256,3200]{1,0:T(8,128)(2,1)} %get-tuple-element.37.refs_0_, bf16[256,3200]{1,0:T(8,128)(2,1)} %get-tuple-element.36.refs_1_), custom_call_target="tpu_custom_call" | custom-call | tf_op jit(solution)/shard_map/join/pallas_call | solution.py:232
  79.2 1.7 %collective-permute-start.12 = (bf16[256,3200]{1,0:T(8,128)(2,1)}, bf16[256,3200]{1,0:T(8,128)(2,1)}, u32[]{:S(2)}, u32[]{:S(2)}) collective-permute-start(bf16[256,3200]{1,0:T(8,128)(2,1)} %get-tuple-element.37.refs_0_), channel_id=1, source_target_pairs={{0,4},{8,28},{32,36},{40,60},{64,68},{72,92},{96,100},{104,124},{4... | collective-permute-start | bytes 4915208 | tf_op jit(solution)/shard_map/ppermute | solution.py:215
  81.6 2.9 %weighted.4.left = bf16[512,384]{1,0:T(8,128)(2,1)S(1)} custom-call(s32[1]{0:T(128)} %bitcast.1.place, f32[1]{0:T(128)} %dynamic_slice.12.omega, bf16[256,3200]{1,0:T(8,128)(2,1)} %get-tuple-element.37.refs_0_, bf16[256,3200]{1,0:T(8,128)(2,1)} %get-tuple-element.36.refs_1_, f32[8,128]{1,0:T(8,128)S(1)} %broadcast_in_dim.7.refs_2_), custom_call_target="tpu_custom_call" | custom-call | tf_op jit(solution)/shard_map/weighted/pallas_call | solution.py:294
  84.5 2.5 %collective-permute-start.8 = (bf16[256,3200]{1,0:T(8,128)(2,1)}, bf16[256,3200]{1,0:T(8,128)(2,1)S(1)}, u32[]{:S(2)}, u32[]{:S(2)}) collective-permute-start(bf16[256,3200]{1,0:T(8,128)(2,1)} %get-tuple-element.36.refs_1_), channel_id=1, source_target_pairs={{0,1},{8,11},{32,33},{40,43},{64,65},{72,75},{96,97},{104,107},{4,... | collective-permute-start | bytes 4915208 | tf_op jit(solution)/shard_map/ppermute | solution.py:215
  87.0 2.3 %collective-permute-start.9 = (bf16[256,3200]{1,0:T(8,128)(2,1)}, bf16[256,3200]{1,0:T(8,128)(2,1)S(1)}, u32[]{:S(2)}, u32[]{:S(2)}) collective-permute-start(bf16[256,3200]{1,0:T(8,128)(2,1)} %get-tuple-element.36.refs_1_), channel_id=1, source_target_pairs={{0,4},{8,28},{32,36},{40,60},{64,68},{72,92},{96,100},{104,124},{4... | collective-permute-start | bytes 4915208 | tf_op jit(solution)/shard_map/ppermute | solution.py:215
  89.3 3.9 %partial_own.3 = (f32[384,3072]{1,0:T(8,128)S(1)}, f32[8,128]{1,0:T(8,128)S(1)}) custom-call(bf16[512,384]{1,0:T(8,128)(2,1)S(1)} %weighted.4.left, bf16[256,3200]{1,0:T(8,128)(2,1)} %get-tuple-element.37.refs_0_, bf16[256,3200]{1,0:T(8,128)(2,1)} %get-tuple-element.36.refs_1_, f32[8,128]{1,0:T(8,128)S(1)} %broadcast_in_dim.7.refs_2_), custom_call_target="tpu_custom_call" | custom-call | flops 1207959552 | bytes 12582912 | tf_op jit(solution)/shard_map/partial_own/pallas_call | solution.py:352
  93.2 3.9 %partial_other.3 = (f32[384,3072]{1,0:T(8,128)S(1)}, f32[8,128]{1,0:T(8,128)S(1)}) custom-call(bf16[512,384]{1,0:T(8,128)(2,1)S(1)} %collective-permute-done.13.left, bf16[256,3200]{1,0:T(8,128)(2,1)} %get-tuple-element.37.refs_0_, bf16[256,3200]{1,0:T(8,128)(2,1)} %get-tuple-element.36.refs_1_, f32[8,128]{1,0:T(8,128)S(1)} %get-tuple-element.38.refs_2_), custom_call_target="tpu_custom_call" | custom-call | flops 1207959552 | bytes 12582912 | tf_op jit(solution)/shard_map/partial_other/pallas_call | solution.py:352
  99.7 2.9 %weighted.5.left = bf16[512,384]{1,0:T(8,128)(2,1)S(1)} custom-call(s32[1]{0:T(128)} %bitcast.1.place, f32[1]{0:T(128)} %dynamic_slice.12.omega, bf16[256,3200]{1,0:T(8,128)(2,1)} %collective-permute-done.11.refs_0_, bf16[256,3200]{1,0:T(8,128)(2,1)} %collective-permute-done.12.refs_1_, f32[8,128]{1,0:T(8,128)S(1)} %get-tuple-element.39.refs_2_.refs_3_), custom_call_target="tpu_custom_call" | custom-call | tf_op jit(solution)/shard_map/weighted/pallas_call | solution.py:294
  102.6 3.7 %collective-permute-start.14 = (bf16[512,384]{1,0:T(8,128)(2,1)S(1)}, bf16[512,384]{1,0:T(8,128)(2,1)S(1)}, u32[]{:S(2)}, u32[]{:S(2)}) collective-permute-start(bf16[512,384]{1,0:T(8,128)(2,1)S(1)} %weighted.5.left), channel_id=1, source_target_pairs={{0,8},{8,0},{32,40},{40,32},{64,72},{72,64},{96,104},{104,96},{4,1... | collective-permute-start | bytes 1179656 | tf_op jit(solution)/shard_map/ppermute | solution.py:215
  106.3 4.1 %partial_own.4 = (f32[384,3072]{1,0:T(8,128)S(1)}, f32[8,128]{1,0:T(8,128)S(1)}) custom-call(bf16[512,384]{1,0:T(8,128)(2,1)S(1)} %weighted.5.left, bf16[256,3200]{1,0:T(8,128)(2,1)} %collective-permute-done.11.refs_0_, bf16[256,3200]{1,0:T(8,128)(2,1)} %collective-permute-done.12.refs_1_, ...), custom_call_target="tpu_custom_call", output_to_operand_aliasing={{0}: (3, {})} | custom-call | flops 1207959552 | bytes 12582912 | tf_op jit(solution)/shard_map/partial_own/pallas_call | solution.py:352
  110.4 4.1 %partial_other.4 = (f32[384,3072]{1,0:T(8,128)S(1)}, f32[8,128]{1,0:T(8,128)S(1)}) custom-call(bf16[512,384]{1,0:T(8,128)(2,1)S(1)} %collective-permute-done.14.left, bf16[256,3200]{1,0:T(8,128)(2,1)} %collective-permute-done.11.refs_0_, bf16[256,3200]{1,0:T(8,128)(2,1)} %collective-permute-done.12.refs_1_, ...), custom_call_target="tpu_custom_call", output_to_operand_aliasing={{0}: (3, {})} | custom-call | flops 1207959552 | bytes 12582912 | tf_op jit(solution)/shard_map/partial_other/pallas_call | solution.py:352
  116.5 4.3 %collective-permute-start.15 = (bf16[512,384]{1,0:T(8,128)(2,1)S(1)}, bf16[512,384]{1,0:T(8,128)(2,1)S(1)}, u32[]{:S(2)}, u32[]{:S(2)}) collective-permute-start(bf16[512,384]{1,0:T(8,128)(2,1)S(1)} %weighted.6.left), channel_id=1, source_target_pairs={{0,8},{8,0},{32,40},{40,32},{64,72},{72,64},{96,104},{104,96},{4,1... | collective-permute-start | bytes 1179656 | tf_op jit(solution)/shard_map/ppermute | solution.py:215
  120.8 2.2 %partial_own.5 = (f32[384,3072]{1,0:T(8,128)S(1)}, f32[8,128]{1,0:T(8,128)S(1)}) custom-call(bf16[512,384]{1,0:T(8,128)(2,1)S(1)} %weighted.6.left, bf16[512,3200]{1,0:T(8,128)(2,1)S(1)} %collective-permute-done.10.refs_0_, f32[384,3072]{1,0:T(8,128)S(1)} %get-tuple-element.45.refs_1_, ...), custom_call_target="tpu_custom_call", output_to_operand_aliasing={{0}: (2, {})} | custom-call | flops 1207959552 | bytes 12582912 | tf_op jit(solution)/shard_map/partial_own/pallas_call | solution.py:352
  123.0 2.2 %partial_other.5 = (f32[384,3072]{1,0:T(8,128)S(1)}, f32[8,128]{1,0:T(8,128)S(1)}) custom-call(bf16[512,384]{1,0:T(8,128)(2,1)S(1)} %collective-permute-done.15.left, bf16[512,3200]{1,0:T(8,128)(2,1)S(1)} %collective-permute-done.10.refs_0_, f32[384,3072]{1,0:T(8,128)S(1)} %get-tuple-element.44.refs_1_, ...), custom_call_target="tpu_custom_call", output_to_operand_aliasing={{0}: (2, {})} | custom-call | flops 1207959552 | bytes 12582912 | tf_op jit(solution)/shard_map/partial_other/pallas_call | solution.py:352
  126.3 2.1 %own_rows.2 = (f32[384,6144]{1,0:T(8,128)}, f32[8,128]{1,0:T(8,128)S(1)}) custom-call(s32[1]{0:T(128)} %bitcast.core, bf16[512,384]{1,0:T(8,128)(2,1)S(1)} %weighted.7.left, bf16[256,3200]{1,0:T(8,128)(2,1)S(1)} %collective-permute-done.8.refs_0_, bf16[256,3200]{1,0:T(8,128)(2,1)S(1)} %collective-permute-done.9.refs_1_, ...), custom_call_target="tpu_custom_call" | custom-call | flops 603979776 | bytes 6291456 | tf_op jit(solution)/shard_map/own_rows/pallas_call | solution.py:388
  131.0 2.6 %own_rows.3 = (f32[384,6144]{1,0:T(8,128)}, f32[8,128]{1,0:T(8,128)}) custom-call(s32[1]{0:T(128)} %bitcast.core, bf16[512,384]{1,0:T(8,128)(2,1)S(1)} %weighted.7.left, bf16[256,3200]{1,0:T(8,128)(2,1)S(1)} %collective-permute-done.8.refs_0_, bf16[256,3200]{1,0:T(8,128)(2,1)S(1)} %collective-permute-done.9.refs_1_, ...), custom_call_target="tpu_custom_call", output_to_operand_aliasing={{0}: (5, {})} | custom-call | flops 603979776 | bytes 6291456 | tf_op jit(solution)/shard_map/own_rows/pallas_call | solution.py:388
  134.1 2.3 %finish.1 = f32[384,6144]{1,0:T(8,128)} custom-call(s32[1]{0:T(128)} %bitcast.core, bf16[384,1536]{1,0:T(8,128)(2,1)S(1)} %collective-permute-done.17.r0, bf16[384,1536]{1,0:T(8,128)(2,1)S(1)} %collective-permute-done.18.r1, f32[384,6144]{1,0:T(8,128)} %get-tuple-element.52._), custom_call_target="tpu_custom_call", output_to_operand_aliasing={{}: (3, {})} | custom-call | tf_op jit(solution)/shard_map/finish/pallas_call | solution.py:442
  (46 shorter events, 17.4 us)
Async XLA Ops:
  2.0 17.5 %all-to-all-start = ((bf16[8,24,1024]{2,1,0:T(8,128)(2,1)}), bf16[8,24,1024]{2,1,0:T(8,128)(2,1)S(1)}, u32[]{:S(2)}, u32[]{:S(2)}) async-start(bf16[8,24,1024]{2,1,0:T(8,128)(2,1)} %get-tuple-element.29), calls=%async_computation | async-start | bytes 786432 | tf_op jit(solution)/shard_map/all_to_all | solution.py:464
  19.5 3.5 %collective-permute-start = (bf16[8,24,1024]{2,1,0:T(8,128)(2,1)S(1)}, bf16[8,24,1024]{2,1,0:T(8,128)(2,1)S(1)}, u32[]{:S(2)}, u32[]{:S(2)}) collective-permute-start(bf16[8,24,1024]{2,1,0:T(8,128)(2,1)S(1)} %all-to-all-done.mine), channel_id=1, source_target_pairs={{0,8},{8,0},{32,40},{40,32},{64,72},{72,64},{96,104},{104,96},{4,1... | collective-permute-start | bytes 1179656 | tf_op jit(solution)/shard_map/ppermute | solution.py:215
  27.6 2.7 %collective-permute-start.1 = (bf16[16,3200]{1,0:T(8,128)(2,1)S(1)}, bf16[16,3200]{1,0:T(8,128)(2,1)S(1)}, u32[]{:S(2)}, u32[]{:S(2)}) collective-permute-start(bf16[16,3200]{1,0:T(8,128)(2,1)S(1)} %get-tuple-element.35), channel_id=1, source_target_pairs={{0,8},{8,0},{32,40},{40,32},{64,72},{72,64},{96,104},{104,96},{4,1... | collective-permute-start | bytes 307208 | tf_op jit(solution)/shard_map/ppermute | solution.py:215
  30.3 12.9 %collective-permute-start.2 = (bf16[32,3200]{1,0:T(8,128)(2,1)S(1)}, bf16[32,3200]{1,0:T(8,128)(2,1)S(1)}, u32[]{:S(2)}, u32[]{:S(2)}) collective-permute-start(bf16[32,3200]{1,0:T(8,128)(2,1)S(1)} %join.3.refs_0_), channel_id=1, source_target_pairs={{0,82},{8,90},{32,114},{40,122},{64,18},{72,26},{96,50},{104,58},{... | collective-permute-start | bytes 614408 | tf_op jit(solution)/shard_map/ppermute | solution.py:215
  33.6 12.2 %collective-permute-start.3 = (bf16[32,3200]{1,0:T(8,128)(2,1)S(1)}, bf16[32,3200]{1,0:T(8,128)(2,1)S(1)}, u32[]{:S(2)}, u32[]{:S(2)}) collective-permute-start(bf16[32,3200]{1,0:T(8,128)(2,1)S(1)} %join.3.refs_0_), channel_id=1, source_target_pairs={{0,37},{8,127},{32,69},{40,31},{64,101},{72,63},{96,5},{104,95},{4... | collective-permute-start | bytes 614408 | tf_op jit(solution)/shard_map/ppermute | solution.py:215
  38.0 10.0 %collective-permute-start.4 = (bf16[32,3200]{1,0:T(8,128)(2,1)S(1)}, bf16[32,3200]{1,0:T(8,128)(2,1)S(1)}, u32[]{:S(2)}, u32[]{:S(2)}) collective-permute-start(bf16[32,3200]{1,0:T(8,128)(2,1)S(1)} %join.3.refs_0_), channel_id=1, source_target_pairs={{0,119},{8,45},{32,23},{40,77},{64,55},{72,109},{96,87},{104,13},{... | collective-permute-start | bytes 614408 | tf_op jit(solution)/shard_map/ppermute | solution.py:215
  48.1 21.8 %collective-permute-start.5 = (bf16[128,3200]{1,0:T(8,128)(2,1)S(1)}, bf16[128,3200]{1,0:T(8,128)(2,1)S(1)}, u32[]{:S(2)}, u32[]{:S(2)}) collective-permute-start(bf16[128,3200]{1,0:T(8,128)(2,1)S(1)} %join.4.b0), channel_id=1, source_target_pairs={{0,2},{8,10},{32,34},{40,42},{64,66},{72,74},{96,98},{104,106},{4,... | collective-permute-start | bytes 2457608 | tf_op jit(solution)/shard_map/ppermute | solution.py:215
  50.8 20.8 %collective-permute-start.6 = (bf16[128,3200]{1,0:T(8,128)(2,1)S(1)}, bf16[128,3200]{1,0:T(8,128)(2,1)S(1)}, u32[]{:S(2)}, u32[]{:S(2)}) collective-permute-start(bf16[128,3200]{1,0:T(8,128)(2,1)S(1)} %join.4.b0), channel_id=1, source_target_pairs={{0,16},{8,24},{32,48},{40,56},{64,80},{72,88},{96,112},{104,120},{... | collective-permute-start | bytes 2457608 | tf_op jit(solution)/shard_map/ppermute | solution.py:215
  51.5 20.2 %collective-permute-start.7 = (bf16[128,3200]{1,0:T(8,128)(2,1)S(1)}, bf16[128,3200]{1,0:T(8,128)(2,1)S(1)}, u32[]{:S(2)}, u32[]{:S(2)}) collective-permute-start(bf16[128,3200]{1,0:T(8,128)(2,1)S(1)} %join.4.b0), channel_id=1, source_target_pairs={{0,64},{8,72},{32,96},{40,104},{64,0},{72,8},{96,32},{104,40},{4,6... | collective-permute-start | bytes 2457608 | tf_op jit(solution)/shard_map/ppermute | solution.py:215
  73.6 7.3 %copy-start = (f32[8]{0:T(128)S(1)}, f32[8]{0:T(128)}, u32[]{:S(2)}) copy-start(f32[8]{0:T(128)} %param.16) | copy-start | bytes 100
  77.5 38.0 %collective-permute-start.10 = (bf16[512,3200]{1,0:T(8,128)(2,1)}, bf16[512,3200]{1,0:T(8,128)(2,1)S(1)}, u32[]{:S(2)}, u32[]{:S(2)}) collective-permute-start(bf16[512,3200]{1,0:T(8,128)(2,1)} %join.5), channel_id=1, source_target_pairs={{0,32},{8,104},{32,64},{40,8},{64,96},{72,40},{96,0},{104,72},{4,3... | collective-permute-start | bytes 9830408 | tf_op jit(solution)/shard_map/ppermute | solution.py:215
  77.5 20.6 %collective-permute-start.11 = (bf16[256,3200]{1,0:T(8,128)(2,1)}, bf16[256,3200]{1,0:T(8,128)(2,1)}, u32[]{:S(2)}, u32[]{:S(2)}) collective-permute-start(bf16[256,3200]{1,0:T(8,128)(2,1)} %get-tuple-element.37.refs_0_), channel_id=1, source_target_pairs={{0,1},{8,11},{32,33},{40,43},{64,65},{72,75},{96,97},{104,107},{4,... | collective-permute-start | bytes 4915208 | tf_op jit(solution)/shard_map/ppermute | solution.py:215
  79.2 20.6 %collective-permute-start.12 = (bf16[256,3200]{1,0:T(8,128)(2,1)}, bf16[256,3200]{1,0:T(8,128)(2,1)}, u32[]{:S(2)}, u32[]{:S(2)}) collective-permute-start(bf16[256,3200]{1,0:T(8,128)(2,1)} %get-tuple-element.37.refs_0_), channel_id=1, source_target_pairs={{0,4},{8,28},{32,36},{40,60},{64,68},{72,92},{96,100},{104,124},{4... | collective-permute-start | bytes 4915208 | tf_op jit(solution)/shard_map/ppermute | solution.py:215
  84.5 2.6 %collective-permute-start.13 = (bf16[512,384]{1,0:T(8,128)(2,1)S(1)}, bf16[512,384]{1,0:T(8,128)(2,1)S(1)}, u32[]{:S(2)}, u32[]{:S(2)}) collective-permute-start(bf16[512,384]{1,0:T(8,128)(2,1)S(1)} %weighted.4.left), channel_id=1, source_target_pairs={{0,8},{8,0},{32,40},{40,32},{64,72},{72,64},{96,104},{104,96},{4,1... | collective-permute-start | bytes 1179656 | tf_op jit(solution)/shard_map/ppermute | solution.py:215
  84.5 40.6 %collective-permute-start.8 = (bf16[256,3200]{1,0:T(8,128)(2,1)}, bf16[256,3200]{1,0:T(8,128)(2,1)S(1)}, u32[]{:S(2)}, u32[]{:S(2)}) collective-permute-start(bf16[256,3200]{1,0:T(8,128)(2,1)} %get-tuple-element.36.refs_1_), channel_id=1, source_target_pairs={{0,1},{8,11},{32,33},{40,43},{64,65},{72,75},{96,97},{104,107},{4,... | collective-permute-start | bytes 4915208 | tf_op jit(solution)/shard_map/ppermute | solution.py:215
  87.0 38.2 %collective-permute-start.9 = (bf16[256,3200]{1,0:T(8,128)(2,1)}, bf16[256,3200]{1,0:T(8,128)(2,1)S(1)}, u32[]{:S(2)}, u32[]{:S(2)}) collective-permute-start(bf16[256,3200]{1,0:T(8,128)(2,1)} %get-tuple-element.36.refs_1_), channel_id=1, source_target_pairs={{0,4},{8,28},{32,36},{40,60},{64,68},{72,92},{96,100},{104,124},{4... | collective-permute-start | bytes 4915208 | tf_op jit(solution)/shard_map/ppermute | solution.py:215
  102.6 7.8 %collective-permute-start.14 = (bf16[512,384]{1,0:T(8,128)(2,1)S(1)}, bf16[512,384]{1,0:T(8,128)(2,1)S(1)}, u32[]{:S(2)}, u32[]{:S(2)}) collective-permute-start(bf16[512,384]{1,0:T(8,128)(2,1)S(1)} %weighted.5.left), channel_id=1, source_target_pairs={{0,8},{8,0},{32,40},{40,32},{64,72},{72,64},{96,104},{104,96},{4,1... | collective-permute-start | bytes 1179656 | tf_op jit(solution)/shard_map/ppermute | solution.py:215
  116.5 6.5 %collective-permute-start.15 = (bf16[512,384]{1,0:T(8,128)(2,1)S(1)}, bf16[512,384]{1,0:T(8,128)(2,1)S(1)}, u32[]{:S(2)}, u32[]{:S(2)}) collective-permute-start(bf16[512,384]{1,0:T(8,128)(2,1)S(1)} %weighted.6.left), channel_id=1, source_target_pairs={{0,8},{8,0},{32,40},{40,32},{64,72},{72,64},{96,104},{104,96},{4,1... | collective-permute-start | bytes 1179656 | tf_op jit(solution)/shard_map/ppermute | solution.py:215
  126.2 2.2 %collective-permute-start.16 = (bf16[512,384]{1,0:T(8,128)(2,1)S(1)}, bf16[512,384]{1,0:T(8,128)(2,1)S(1)}, u32[]{:S(2)}, u32[]{:S(2)}) collective-permute-start(bf16[512,384]{1,0:T(8,128)(2,1)S(1)} %weighted.7.left), channel_id=1, source_target_pairs={{0,8},{8,0},{32,40},{40,32},{64,72},{72,64},{96,104},{104,96},{4,1... | collective-permute-start | bytes 1179656 | tf_op jit(solution)/shard_map/ppermute | solution.py:215
  129.4 4.3 %collective-permute-start.17 = (bf16[384,1536]{1,0:T(8,128)(2,1)S(1)}, bf16[384,1536]{1,0:T(8,128)(2,1)S(1)}, u32[]{:S(2)}, u32[]{:S(2)}) collective-permute-start(bf16[384,1536]{1,0:T(8,128)(2,1)S(1)} %other_rows.2), channel_id=1, source_target_pairs={{0,8},{8,0},{32,40},{40,32},{64,72},{72,64},{96,104},{104,96},{4,1... | collective-permute-start | bytes 3538952 | tf_op jit(solution)/shard_map/ppermute | solution.py:215
  130.9 3.2 %collective-permute-start.18 = (bf16[384,1536]{1,0:T(8,128)(2,1)S(1)}, bf16[384,1536]{1,0:T(8,128)(2,1)S(1)}, u32[]{:S(2)}, u32[]{:S(2)}) collective-permute-start(bf16[384,1536]{1,0:T(8,128)(2,1)S(1)} %other_rows.3), channel_id=1, source_target_pairs={{0,8},{8,0},{32,40},{40,32},{64,72},{72,64},{96,104},{104,96},{4,1... | collective-permute-start | bytes 3538952 | tf_op jit(solution)/shard_map/ppermute | solution.py:215

commit v11 on v10

--- a/solution.py
+++ b/solution.py
@@ -272,8 +272,10 @@
     return [places.index(tuple(-v % 4 for v in p)) for p in places]
 
 
-def weighted_kernel(place, omega, *refs):
-    pieces, left = halves(refs[:-2]), refs[-1]
+def weighted_kernel(n, place, omega, *refs):
+    pieces, left = halves(refs[:n]), refs[n + 1]
+    if len(refs) > n + 2:
+        refs[-1][...] = pieces[0][:, :HALF]
     w2 = omega[0] * omega[0]
     row = lax.broadcasted_iota(jnp.int32, (LANES, 2 * LANES), 0)
     lane = lax.broadcasted_iota(jnp.int32, (LANES, 2 * LANES), 1)
@@ -290,12 +292,15 @@
             ).astype(jnp.bfloat16)
 
 
-def weighted(place, omega, pieces, tie):
-    return pl.pallas_call(
-        weighted_kernel,
-        out_shape=pltpu.VMEM((sum(p.shape[0] for p in pieces), ROWS), jnp.bfloat16),
+def weighted(place, omega, pieces, tie, copied=False):
+    shapes = [pltpu.VMEM((sum(p.shape[0] for p in pieces), ROWS), jnp.bfloat16)]
+    if copied:
+        shapes.append(pltpu.VMEM((pieces[0].shape[0], HALF), jnp.bfloat16))
+    return pl.pallas_call(
+        functools.partial(weighted_kernel, len(pieces)),
+        out_shape=shapes,
         in_specs=[SM, SM] + [VM] * (len(pieces) + 1),
-        out_specs=VM,
+        out_specs=[VM] * len(shapes),
         compiler_params=PARAMS,
         name="weighted",
     )(place, omega, *pieces, tie)
@@ -361,20 +366,24 @@
     )(left, *pieces, *before, tie)
 
 
-def own_kernel(names, n, start, core, left, *refs):
-    pieces = halves(refs[:n])
-    before, _, out, tie, wide, sem = refs[n:]
-    tie[...] = jnp.zeros_like(tie)
+def last_kernel(names, other, core, left, piece, *refs):
+    n = 2 if other else 1
+    before = refs[:n]
+    out, wide, sem = refs[-3:]
+    half = 1 - core[0] if other else core[0]
     copies = []
-    for i in range(2):
-        cols = slice(start + i * CHUNK, start + (i + 1) * CHUNK)
-        wide[:, i * CHUNK : (i + 1) * CHUNK] = product(names, False, left, pieces, cols) + before[:, cols]
+    for i in range(4):
+        cols = slice(i * CHUNK, (i + 1) * CHUNK)
+        if other:
+            sofar = before[i // 2][:, (i % 2) * CHUNK : (i % 2 + 1) * CHUNK].astype(jnp.float32)
+        else:
+            sofar = before[0][:, cols]
+        wide[:, cols] = product(names, other, left, [piece], cols) + sofar
         for j in (2 * i, 2 * i + 1):
-            block = (start // ROWS + j) * 2 + core[0]
             copies.append(
                 pltpu.make_async_copy(
                     wide.at[:, pl.ds(j * ROWS, ROWS)],
-                    out.at[:, pl.ds(pl.multiple_of(block * ROWS, LANES), ROWS)],
+                    out.at[:, pl.ds(pl.multiple_of((j * 2 + half) * ROWS, LANES), ROWS)],
                     sem.at[j],
                 )
             )
@@ -383,19 +392,19 @@
         copy.wait()
 
 
-def own_rows(names, start, core, left, pieces, before, after):
-    grows = after.shape == (ROWS, NG)
-    return pl.pallas_call(
-        functools.partial(own_kernel, names, len(pieces), start),
-        out_shape=[jax.ShapeDtypeStruct((ROWS, NG), jnp.float32), TIE],
-        in_specs=[SM, VM] + [VM] * (len(pieces) + 1) + [HBM if grows else VM],
-        out_specs=[HBM, VM],
-        scratch_shapes=[pltpu.VMEM((ROWS, HALF // 2), jnp.float32), pltpu.SemaphoreType.DMA((4,))],
-        input_output_aliases={3 + len(pieces): 0} if grows else {},
-        compiler_params=PARAMS,
-        cost_estimate=cost(names, HALF // 2),
-        name="own_rows",
-    )(core, left, *pieces, before, after)
+def last_rows(names, other, core, left, piece, before, out):
+    out = [] if out is None else [out]
+    return pl.pallas_call(
+        functools.partial(last_kernel, names, other),
+        out_shape=jax.ShapeDtypeStruct((ROWS, NG), jnp.float32),
+        in_specs=[SM, VM, VM] + [VM] * len(before) + [HBM] * len(out),
+        out_specs=HBM,
+        scratch_shapes=[pltpu.VMEM((ROWS, HALF), jnp.float32), pltpu.SemaphoreType.DMA((8,))],
+        input_output_aliases={3 + len(before): 0} if out else {},
+        compiler_params=PARAMS,
+        cost_estimate=cost(names, HALF),
+        name="last_other" if other else "last_own",
+    )(core, left, piece, *before, *out)
 
 
 def other_kernel(names, n, start, left, *refs):
@@ -420,35 +429,6 @@
         cost_estimate=cost(names, HALF // 2),
         name="other_rows",
     )(left, *pieces, before, tie)
-
-
-def finish_kernel(core, r0, r1, _, out, wide, sem):
-    def copy(i):
-        return pltpu.make_async_copy(
-            wide.at[:, pl.ds(i * ROWS, ROWS)],
-            out.at[:, pl.ds(pl.multiple_of((i * 2 + 1 - core[0]) * ROWS, LANES), ROWS)],
-            sem.at[i],
-        )
-
-    for i in range(8):
-        src = (r0, r1)[i // 4]
-        wide[:, i * ROWS : (i + 1) * ROWS] = src[:, (i % 4) * ROWS : (i % 4 + 1) * ROWS].astype(jnp.float32)
-        copy(i).start()
-    for i in range(8):
-        copy(i).wait()
-
-
-def finish(core, rows, out):
-    return pl.pallas_call(
-        finish_kernel,
-        out_shape=jax.ShapeDtypeStruct((ROWS, NG), jnp.float32),
-        in_specs=[SM, VM, VM, HBM],
-        out_specs=HBM,
-        scratch_shapes=[pltpu.VMEM((ROWS, HALF), jnp.float32), pltpu.SemaphoreType.DMA((8,))],
-        input_output_aliases={3: 0},
-        compiler_params=PARAMS,
-        name="finish",
-    )(core, *rows, out)
 
 
 def in_vmem(a):
@@ -483,27 +463,33 @@
     sources = deal(level(a, EVEN))
     got = {(h, 0): m for h, m in enumerate(sources)}
     for h in range(2):
-        for s in (1, 2):
+        for s in (1, 2, 3):
             got[h, s] = send(sources[h], offset_pairs(STEP[s]))
-    got["z"] = send(join(sources), offset_pairs(STEP[3]))
 
     place = lax.div(ga, 2).astype(jnp.int32).reshape(1)
     mine_omega = lax.dynamic_slice(omega, (ba,), (1,))
     core = core.reshape(1)
     own = other = None
     tie = jnp.zeros(TIE.shape, TIE.dtype)
-    groups = (((0, 0), (1, 0)), ((0, 1), (0, 2)), ((0, 3), (1, 3)), ((1, 1), (1, 2)))
+    groups = (((0, 0), (1, 0), (0, 1), (0, 2), (0, 3)), ((1, 1), (1, 2)))
     for names in groups:
-        pieces = [in_vmem(got[name]) for name in (("z",) if (0, 3) in names else names)]
-        left = weighted(place, mine_omega, pieces, tie)
+        pieces = [in_vmem(got[name]) for name in names]
+        (left,) = weighted(place, mine_omega, pieces, tie)
         mirror = send(left, core_pairs())
-        if names is not groups[-1]:
-            own, tie = partial_rows(names, False, left, pieces, own, tie)
+        own, tie = partial_rows(names, False, left, pieces, own, tie)
+        if names is groups[0]:
             other, tie = partial_rows(names, True, mirror, pieces, other, tie)
-    out, tie = own_rows(names, 0, core, left, pieces, own, tie)
-    rows = [send(other_rows(names, s, mirror, pieces, other, tie), core_pairs()) for s in (0, HALF // 2)]
-    out, _ = own_rows(names, HALF // 2, core, left, pieces, own, out)
-    return finish(core, rows, out)[None]
+    rows = []
+    for s in (0, HALF // 2):
+        rows.append(other_rows(names, s, mirror, pieces, other, rows[0] if rows else tie))
+    swapped = [send(row, core_pairs()) for row in rows]
+
+    names = ((1, 3),)
+    piece = got[1, 3]
+    left, copy = weighted(place, mine_omega, [piece], rows[1], True)
+    theirs = send(copy, core_pairs())
+    out = last_rows(names, False, core, left, piece, [own], None)
+    return last_rows(names, True, core, left, theirs, swapped, out)[None]
 
 
 def solution(mesh):

time: 137 us -> 137 us (level)
  waiting for transfers between devices: 40.6 us -> 61.1 us
  Pallas kernels: 51.8 us -> 41.6 us
  starting transfers between devices: 39.8 us -> 32.8 us
    ppermute x19, waiting for transfers between devices: 34.7 us -> 52.6 us  [send(): return lax.ppermute(a, ('ga', 'ba'), pairs)]
    ppermute x19, starting transfers between devices: 31.3 us -> 24.3 us  [send(): return lax.ppermute(a, ('ga', 'ba'), pairs)]
    pallas_call x3 -> x2, Pallas kernels: 3.93 us -> 0.07 us  [join(): pl.pallas_call(functools.partial(join_kernel, len(blocks)), out_shape=plt...]
    pallas_call x6 -> x3, Pallas kernels: 20.4 us -> 16.8 us  [partial_rows(): pl.pallas_call(functools.partial(partial_kernel, names, len(pieces), othe...]
    pallas_call x7 -> x5, Pallas kernels: 14.6 us -> 11.8 us  [the longest x3 6.47 us: weighted(): pl.pallas_call(functools.partial(weighted_kernel, len(pieces)), out_shape...]
    all_to_all x1, waiting for transfers between devices: 5.85 us -> 8.52 us  [on_device(): psi = lax.all_to_all(rows, 'ga', 0, 0, tiled=True, axis_index_groups=kinds)]
  transfers between devices with their start and end apart: 20 -> 20, of which waited for: 11 -> 14; matrix products, arithmetic and copies ran while one was open for 3% -> 1% of each run, Pallas kernels for 26% -> 21%
where the time goes in v11:
time: 137 us
  waiting for transfers between devices  61.1 us (45%)
  Pallas kernels  41.6 us (30%)
  starting transfers between devices  32.8 us (24%)
    ppermute x19, waiting for transfers between devices, send(): return lax.ppermute(a, ('ga', 'ba'), pairs)  52.6 us
    ppermute x19, starting transfers between devices, send(): return lax.ppermute(a, ('ga', 'ba'), pairs)  24.3 us
    pallas_call x3, Pallas kernels, partial_rows(): pl.pallas_call(functools.partial(partial_kernel, names, len(pieces), othe...  16.8 us
    all_to_all x1, waiting for transfers between devices, on_device(): psi = lax.all_to_all(rows, 'ga', 0, 0, tiled=True, axis_index_groups=kinds)  8.52 us
    all_to_all x1, starting transfers between devices, on_device(): psi = lax.all_to_all(rows, 'ga', 0, 0, tiled=True, axis_index_groups=kinds)  8.51 us
    pallas_call x3, Pallas kernels, weighted(): pl.pallas_call(functools.partial(weighted_kernel, len(pieces)), out_shape...  6.47 us
    pallas_call x2, Pallas kernels, last_rows(): pl.pallas_call(functools.partial(last_kernel, names, other), out_shape=ja...  5.35 us
    pallas_call x1, Pallas kernels, rho_spectrum(): pl.pallas_call(transform_kernel, out_shape=[pltpu.VMEM((PAIRS * 64, 256),...  4.58 us
  transfers between devices with their start and end apart: 20, of which 14 were waited for; matrix products, arithmetic and copies ran while one was open for 1% of the time, Pallas kernels for 21%

profile of v11, /device:TPU:1, one launch (start us, length us, event | category | flops | bytes accessed | tf_op | source)
XLA Modules:
  0.0 137.1 jit_solution(6493060320641747112)
XLA Ops:
  0.0 2.0 %payload.1 = (bf16[8,24,1024]{2,1,0:T(8,128)(2,1)}, bf16[2,256,256]{2,1,0:T(8,128)(2,1)S(1)}, f32[128,256]{1,0:T(8,128)S(1)}, f32[128,256]{1,0:T(8,128)S(1)}, bf16[512,256]{1,0:T(8,128)(2,1)S(1)}) custom-call(bf16[4,2048]{1,0:T(4,128)(2,1)} %val.1, bf16[64,2048]{1,0:T(8,128)(2,1)} %con.1, bf16[2,256,256]{2,1,0:T(8,128)(2,1)} %constant.39.clone.first, ...), custom_call_target="tpu_custom_call" | custom-call | tf_op jit(solution)/shard_map/payload/pallas_call | solution.py:82
  2.1 8.5 %all-to-all-start = ((bf16[8,24,1024]{2,1,0:T(8,128)(2,1)}), bf16[8,24,1024]{2,1,0:T(8,128)(2,1)S(1)}, u32[]{:S(2)}, u32[]{:S(2)}) async-start(bf16[8,24,1024]{2,1,0:T(8,128)(2,1)} %get-tuple-element.22), calls=%async_computation | async-start | bytes 786432 | tf_op jit(solution)/shard_map/all_to_all | solution.py:444
  11.0 8.5 %all-to-all-done.mine = bf16[8,24,1024]{2,1,0:T(8,128)(2,1)S(1)} async-done(((bf16[8,24,1024]{2,1,0:T(8,128)(2,1)}), bf16[8,24,1024]{2,1,0:T(8,128)(2,1)S(1)}, u32[]{:S(2)}, u32[]{:S(2)}) %all-to-all-start) | async-done | bytes 393248 | tf_op jit(solution)/shard_map/all_to_all | solution.py:444
  19.6 2.2 %collective-permute-start = (bf16[8,24,1024]{2,1,0:T(8,128)(2,1)S(1)}, bf16[8,24,1024]{2,1,0:T(8,128)(2,1)S(1)}, u32[]{:S(2)}, u32[]{:S(2)}) collective-permute-start(bf16[8,24,1024]{2,1,0:T(8,128)(2,1)S(1)} %all-to-all-done.mine), channel_id=1, source_target_pairs={{0,8},{8,0},{32,40},{40,32},{64,72},{72,64},{96,104},{104,96},{4,1... | collective-permute-start | bytes 1179656 | tf_op jit(solution)/shard_map/ppermute | solution.py:215
  21.9 1.2 collective-permute-done.others
  23.1 4.6 %rho_spectrum.1 = (bf16[1024,256]{1,0:T(8,128)(2,1)S(1)}, bf16[16,3200]{1,0:T(8,128)(2,1)S(1)}) custom-call(s32[1]{0:T(128)} %bitcast.core, bf16[8,24,1024]{2,1,0:T(8,128)(2,1)S(1)} %all-to-all-done.mine, bf16[8,24,1024]{2,1,0:T(8,128)(2,1)S(1)} %collective-permute-done.others, s32[1,3072]{1,0:T(1,128)S(1)} %get-tuple-element.40.gidx, ...), custom_call_target="tpu_custom_call" | custom-call | tf_op jit(solution)/shard_map/rho_spectrum/pallas_call | solution.py:168
  28.1 2.3 %rho_pick.1.refs_0_ = bf16[16,3200]{1,0:T(8,128)(2,1)S(1)} custom-call(bf16[1024,256]{1,0:T(8,128)(2,1)S(1)} %get-tuple-element.27.spec, s32[1,3072]{1,0:T(1,128)S(1)} %get-tuple-element.39.gidx, bf16[16,128]{1,0:T(8,128)(2,1)S(1)} %pad.4.meta), custom_call_target="tpu_custom_call" | custom-call | tf_op jit(solution)/shard_map/rho_pick/pallas_call | solution.py:184
  30.4 3.2 %collective-permute-start.2 = (bf16[32,3200]{1,0:T(8,128)(2,1)S(1)}, bf16[32,3200]{1,0:T(8,128)(2,1)S(1)}, u32[]{:S(2)}, u32[]{:S(2)}) collective-permute-start(bf16[32,3200]{1,0:T(8,128)(2,1)S(1)} %join.2.refs_0_), channel_id=1, source_target_pairs={{0,82},{8,90},{32,114},{40,122},{64,18},{72,26},{96,50},{104,58},{... | collective-permute-start | bytes 614408 | tf_op jit(solution)/shard_map/ppermute | solution.py:215
  33.6 4.5 %collective-permute-start.3 = (bf16[32,3200]{1,0:T(8,128)(2,1)S(1)}, bf16[32,3200]{1,0:T(8,128)(2,1)S(1)}, u32[]{:S(2)}, u32[]{:S(2)}) collective-permute-start(bf16[32,3200]{1,0:T(8,128)(2,1)S(1)} %join.2.refs_0_), channel_id=1, source_target_pairs={{0,37},{8,127},{32,69},{40,31},{64,101},{72,63},{96,5},{104,95},{4... | collective-permute-start | bytes 614408 | tf_op jit(solution)/shard_map/ppermute | solution.py:215
  38.1 5.2 %collective-permute-done.2.refs_1_ = bf16[32,3200]{1,0:T(8,128)(2,1)S(1)} collective-permute-done((bf16[32,3200]{1,0:T(8,128)(2,1)S(1)}, bf16[32,3200]{1,0:T(8,128)(2,1)S(1)}, u32[]{:S(2)}, u32[]{:S(2)}) %collective-permute-start.2) | collective-permute-done | bytes 204832 | tf_op jit(solution)/shard_map/ppermute | solution.py:215
  43.3 2.5 %collective-permute-done.3.refs_2_ = bf16[32,3200]{1,0:T(8,128)(2,1)S(1)} collective-permute-done((bf16[32,3200]{1,0:T(8,128)(2,1)S(1)}, bf16[32,3200]{1,0:T(8,128)(2,1)S(1)}, u32[]{:S(2)}, u32[]{:S(2)}) %collective-permute-start.3) | collective-permute-done | bytes 204832 | tf_op jit(solution)/shard_map/ppermute | solution.py:215
  45.8 2.4 %collective-permute-done.4.refs_3_ = bf16[32,3200]{1,0:T(8,128)(2,1)S(1)} collective-permute-done((bf16[32,3200]{1,0:T(8,128)(2,1)S(1)}, bf16[32,3200]{1,0:T(8,128)(2,1)S(1)}, u32[]{:S(2)}, u32[]{:S(2)}) %collective-permute-start.4) | collective-permute-done | bytes 204832 | tf_op jit(solution)/shard_map/ppermute | solution.py:215
  48.2 2.7 %collective-permute-start.5 = (bf16[128,3200]{1,0:T(8,128)(2,1)S(1)}, bf16[128,3200]{1,0:T(8,128)(2,1)S(1)}, u32[]{:S(2)}, u32[]{:S(2)}) collective-permute-start(bf16[128,3200]{1,0:T(8,128)(2,1)S(1)} %join.3.b0), channel_id=1, source_target_pairs={{0,2},{8,10},{32,34},{40,42},{64,66},{72,74},{96,98},{104,106},{4,... | collective-permute-start | bytes 2457608 | tf_op jit(solution)/shard_map/ppermute | solution.py:215
  52.3 17.8 %collective-permute-done.5.b1 = bf16[128,3200]{1,0:T(8,128)(2,1)S(1)} collective-permute-done((bf16[128,3200]{1,0:T(8,128)(2,1)S(1)}, bf16[128,3200]{1,0:T(8,128)(2,1)S(1)}, u32[]{:S(2)}, u32[]{:S(2)}) %collective-permute-start.5) | collective-permute-done | bytes 819232 | tf_op jit(solution)/shard_map/ppermute | solution.py:215
  70.1 1.6 %collective-permute-done.6.b2 = bf16[128,3200]{1,0:T(8,128)(2,1)S(1)} collective-permute-done((bf16[128,3200]{1,0:T(8,128)(2,1)S(1)}, bf16[128,3200]{1,0:T(8,128)(2,1)S(1)}, u32[]{:S(2)}, u32[]{:S(2)}) %collective-permute-start.6) | collective-permute-done | bytes 819232 | tf_op jit(solution)/shard_map/ppermute | solution.py:215
  71.8 2.0 %deal.1 = (bf16[256,3200]{1,0:T(8,128)(2,1)}, bf16[256,3200]{1,0:T(8,128)(2,1)}) custom-call(bf16[128,3200]{1,0:T(8,128)(2,1)S(1)} %join.3.b0, bf16[128,3200]{1,0:T(8,128)(2,1)S(1)} %collective-permute-done.5.b1, bf16[128,3200]{1,0:T(8,128)(2,1)S(1)} %collective-permute-done.6.b2, bf16[128,3200]{1,0:T(8,128)(2,1)S(1)} %collective-permute-done.7.b3), custom_call_target="tpu_custom_call" | custom-call | tf_op jit(solution)/shard_map/deal/pallas_call | solution.py:249
  73.7 1.7 %collective-permute-start.11 = (bf16[256,3200]{1,0:T(8,128)(2,1)}, bf16[256,3200]{1,0:T(8,128)(2,1)}, u32[]{:S(2)}, u32[]{:S(2)}) collective-permute-start(bf16[256,3200]{1,0:T(8,128)(2,1)} %get-tuple-element.30.refs_0_), channel_id=1, source_target_pairs={{0,1},{8,11},{32,33},{40,43},{64,65},{72,75},{96,97},{104,107},{4,... | collective-permute-start | bytes 4915208 | tf_op jit(solution)/shard_map/ppermute | solution.py:215
  75.4 1.5 %collective-permute-start.12 = (bf16[256,3200]{1,0:T(8,128)(2,1)}, bf16[256,3200]{1,0:T(8,128)(2,1)}, u32[]{:S(2)}, u32[]{:S(2)}) collective-permute-start(bf16[256,3200]{1,0:T(8,128)(2,1)} %get-tuple-element.30.refs_0_), channel_id=1, source_target_pairs={{0,4},{8,28},{32,36},{40,60},{64,68},{72,92},{96,100},{104,124},{4... | collective-permute-start | bytes 4915208 | tf_op jit(solution)/shard_map/ppermute | solution.py:215
  77.2 1.2 collective-permute-start.10
  79.1 15.2 %collective-permute-done.11.refs_2_ = bf16[256,3200]{1,0:T(8,128)(2,1)} collective-permute-done((bf16[256,3200]{1,0:T(8,128)(2,1)}, bf16[256,3200]{1,0:T(8,128)(2,1)}, u32[]{:S(2)}, u32[]{:S(2)}) %collective-permute-start.11) | collective-permute-done | bytes 1638432 | tf_op jit(solution)/shard_map/ppermute | solution.py:215
  94.3 1.7 %collective-permute-done.12.refs_3_ = bf16[256,3200]{1,0:T(8,128)(2,1)} collective-permute-done((bf16[256,3200]{1,0:T(8,128)(2,1)}, bf16[256,3200]{1,0:T(8,128)(2,1)}, u32[]{:S(2)}, u32[]{:S(2)}) %collective-permute-start.12) | collective-permute-done | bytes 1638432 | tf_op jit(solution)/shard_map/ppermute | solution.py:215
  96.0 1.5 %collective-permute-done.13.refs_4_ = bf16[256,3200]{1,0:T(8,128)(2,1)} collective-permute-done((bf16[256,3200]{1,0:T(8,128)(2,1)}, bf16[256,3200]{1,0:T(8,128)(2,1)}, u32[]{:S(2)}, u32[]{:S(2)}) %collective-permute-start.13) | collective-permute-done | bytes 1638432 | tf_op jit(solution)/shard_map/ppermute | solution.py:215
  97.5 4.5 %weighted.3.left = bf16[1280,384]{1,0:T(8,128)(2,1)S(1)} custom-call(s32[1]{0:T(128)} %bitcast.1.place, f32[1]{0:T(128)} %dynamic_slice.12.omega, bf16[256,3200]{1,0:T(8,128)(2,1)} %get-tuple-element.30.refs_0_, bf16[256,3200]{1,0:T(8,128)(2,1)} %get-tuple-element.29.refs_1_, bf16[256,3200]{1,0:T(8,128)(2,1)} %collective-permute-done.11.refs_2_, ...), custom_call_target="tpu_custom_call" | custom-call | tf_op jit(solution)/shard_map/weighted/pallas_call | solution.py:299
  102.1 2.1 %collective-permute-start.14 = (bf16[1280,384]{1,0:T(8,128)(2,1)S(1)}, bf16[1280,384]{1,0:T(8,128)(2,1)S(1)}, u32[]{:S(2)}, u32[]{:S(2)}) collective-permute-start(bf16[1280,384]{1,0:T(8,128)(2,1)S(1)} %weighted.3.left), channel_id=1, source_target_pairs={{0,8},{8,0},{32,40},{40,32},{64,72},{72,64},{96,104},{104,96},{4,1... | collective-permute-start | bytes 2949128 | tf_op jit(solution)/shard_map/ppermute | solution.py:215
  104.2 7.3 %partial_own.2 = (f32[384,3072]{1,0:T(8,128)S(1)}, f32[8,128]{1,0:T(8,128)S(1)}) custom-call(bf16[1280,384]{1,0:T(8,128)(2,1)S(1)} %weighted.3.left, bf16[256,3200]{1,0:T(8,128)(2,1)} %get-tuple-element.30.refs_0_, bf16[256,3200]{1,0:T(8,128)(2,1)} %get-tuple-element.29.refs_1_, bf16[256,3200]{1,0:T(8,128)(2,1)} %collective-permute-done.11.refs_2_, ...), custom_call_target="tpu_custom_call" | custom-call | flops 3019898880 | bytes 17301504 | tf_op jit(solution)/shard_map/partial_own/pallas_call | solution.py:357
  111.5 7.3 %partial_other.1 = (f32[384,3072]{1,0:T(8,128)S(1)}, f32[8,128]{1,0:T(8,128)S(1)}) custom-call(bf16[1280,384]{1,0:T(8,128)(2,1)S(1)} %collective-permute-done.14.left, bf16[256,3200]{1,0:T(8,128)(2,1)} %get-tuple-element.30.refs_0_, bf16[256,3200]{1,0:T(8,128)(2,1)} %get-tuple-element.29.refs_1_, bf16[256,3200]{1,0:T(8,128)(2,1)} %collective-permute-done.11.refs_2_, ...), custom_call_target="tpu_custom_call" | custom-call | flops 3019898880 | bytes 17301504 | tf_op jit(solution)/shard_map/partial_other/pallas_call | solution.py:357
  120.2 2.2 %partial_own.3 = (f32[384,3072]{1,0:T(8,128)S(1)}, f32[8,128]{1,0:T(8,128)S(1)}) custom-call(bf16[512,384]{1,0:T(8,128)(2,1)S(1)} %weighted.4.left, bf16[256,3200]{1,0:T(8,128)(2,1)S(1)} %collective-permute-done.9.refs_0_, bf16[256,3200]{1,0:T(8,128)(2,1)S(1)} %collective-permute-done.10.refs_1_, ...), custom_call_target="tpu_custom_call", output_to_operand_aliasing={{0}: (3, {})} | custom-call | flops 1207959552 | bytes 12582912 | tf_op jit(solution)/shard_map/partial_own/pallas_call | solution.py:357
  125.6 2.2 %collective-permute-start.16 = (bf16[256,3072]{1,0:T(8,128)(2,1)S(1)}, bf16[256,3072]{1,0:T(8,128)(2,1)S(1)}, u32[]{:S(2)}, u32[]{:S(2)}) collective-permute-start(bf16[256,3072]{1,0:T(8,128)(2,1)S(1)} %get-tuple-element.37), channel_id=1, source_target_pairs={{0,8},{8,0},{32,40},{40,32},{64,72},{72,64},{96,104},{104,96},{4,1... | collective-permute-start | bytes 4718600 | tf_op jit(solution)/shard_map/ppermute | solution.py:215
  128.4 2.7 %last_own.1.refs_2_ = f32[384,6144]{1,0:T(8,128)} custom-call(s32[1]{0:T(128)} %bitcast.core, bf16[256,384]{1,0:T(8,128)(2,1)S(1)} %get-tuple-element.36.left, bf16[256,3200]{1,0:T(8,128)(2,1)S(1)} %collective-permute-done.8.refs_0_.piece, f32[384,3072]{1,0:T(8,128)S(1)} %get-tuple-element.38.refs_0_), custom_call_target="tpu_custom_call" | custom-call | flops 603979776 | bytes 11010048 | tf_op jit(solution)/shard_map/last_own/pallas_call | solution.py:397
  131.1 1.5 %collective-permute-done.18.refs_1_ = bf16[384,1536]{1,0:T(8,128)(2,1)S(1)} collective-permute-done((bf16[384,1536]{1,0:T(8,128)(2,1)S(1)}, bf16[384,1536]{1,0:T(8,128)(2,1)S(1)}, u32[]{:S(2)}, u32[]{:S(2)}) %collective-permute-start.18) | collective-permute-done | bytes 1179680 | tf_op jit(solution)/shard_map/ppermute | solution.py:215
  132.6 1.7 %collective-permute-done.17.refs_0_ = bf16[384,1536]{1,0:T(8,128)(2,1)S(1)} collective-permute-done((bf16[384,1536]{1,0:T(8,128)(2,1)S(1)}, bf16[384,1536]{1,0:T(8,128)(2,1)S(1)}, u32[]{:S(2)}, u32[]{:S(2)}) %collective-permute-start.17) | collective-permute-done | bytes 1179680 | tf_op jit(solution)/shard_map/ppermute | solution.py:215
  134.3 2.7 %last_other.1 = f32[384,6144]{1,0:T(8,128)} custom-call(s32[1]{0:T(128)} %bitcast.core, bf16[256,384]{1,0:T(8,128)(2,1)S(1)} %get-tuple-element.36.left, bf16[256,3072]{1,0:T(8,128)(2,1)S(1)} %collective-permute-done.16.piece, bf16[384,1536]{1,0:T(8,128)(2,1)S(1)} %collective-permute-done.17.refs_0_, ...), custom_call_target="tpu_custom_call", output_to_operand_aliasing={{}: (5, {})} | custom-call | flops 603979776 | bytes 11010048 | tf_op jit(solution)/shard_map/last_other/pallas_call | solution.py:397
  (48 shorter events, 8.6 us)
Async XLA Ops:
  0.0 10.6 %copy-start = (s32[6144]{0:T(1024)S(1)}, s32[6144]{0:T(1024)}, u32[]{:S(2)}) copy-start(s32[6144]{0:T(1024)} %param.17) | copy-start | bytes 73732
  0.0 10.6 %copy-start.2 = (f32[64]{0:T(128)S(1)}, f32[64]{0:T(128)}, u32[]{:S(2)}) copy-start(f32[64]{0:T(128)} %param.14) | copy-start | bytes 772
  0.0 10.7 %copy-start.1 = (f32[4]{0:T(128)S(1)}, f32[4]{0:T(128)}, u32[]{:S(2)}) copy-start(f32[4]{0:T(128)} %param.13) | copy-start | bytes 52
  0.0 10.8 %copy-start.3 = (s32[4]{0:T(128)S(1)}, s32[4]{0:T(128)}, u32[]{:S(2)}) copy-start(s32[4]{0:T(128)} %param.15) | copy-start | bytes 52
  2.1 17.5 %all-to-all-start = ((bf16[8,24,1024]{2,1,0:T(8,128)(2,1)}), bf16[8,24,1024]{2,1,0:T(8,128)(2,1)S(1)}, u32[]{:S(2)}, u32[]{:S(2)}) async-start(bf16[8,24,1024]{2,1,0:T(8,128)(2,1)} %get-tuple-element.22), calls=%async_computation | async-start | bytes 786432 | tf_op jit(solution)/shard_map/all_to_all | solution.py:444
  19.6 3.5 %collective-permute-start = (bf16[8,24,1024]{2,1,0:T(8,128)(2,1)S(1)}, bf16[8,24,1024]{2,1,0:T(8,128)(2,1)S(1)}, u32[]{:S(2)}, u32[]{:S(2)}) collective-permute-start(bf16[8,24,1024]{2,1,0:T(8,128)(2,1)S(1)} %all-to-all-done.mine), channel_id=1, source_target_pairs={{0,8},{8,0},{32,40},{40,32},{64,72},{72,64},{96,104},{104,96},{4,1... | collective-permute-start | bytes 1179656 | tf_op jit(solution)/shard_map/ppermute | solution.py:215
  27.6 2.7 %collective-permute-start.1 = (bf16[16,3200]{1,0:T(8,128)(2,1)S(1)}, bf16[16,3200]{1,0:T(8,128)(2,1)S(1)}, u32[]{:S(2)}, u32[]{:S(2)}) collective-permute-start(bf16[16,3200]{1,0:T(8,128)(2,1)S(1)} %get-tuple-element.28), channel_id=1, source_target_pairs={{0,8},{8,0},{32,40},{40,32},{64,72},{72,64},{96,104},{104,96},{4,1... | collective-permute-start | bytes 307208 | tf_op jit(solution)/shard_map/ppermute | solution.py:215
  30.4 12.9 %collective-permute-start.2 = (bf16[32,3200]{1,0:T(8,128)(2,1)S(1)}, bf16[32,3200]{1,0:T(8,128)(2,1)S(1)}, u32[]{:S(2)}, u32[]{:S(2)}) collective-permute-start(bf16[32,3200]{1,0:T(8,128)(2,1)S(1)} %join.2.refs_0_), channel_id=1, source_target_pairs={{0,82},{8,90},{32,114},{40,122},{64,18},{72,26},{96,50},{104,58},{... | collective-permute-start | bytes 614408 | tf_op jit(solution)/shard_map/ppermute | solution.py:215
  33.6 12.1 %collective-permute-start.3 = (bf16[32,3200]{1,0:T(8,128)(2,1)S(1)}, bf16[32,3200]{1,0:T(8,128)(2,1)S(1)}, u32[]{:S(2)}, u32[]{:S(2)}) collective-permute-start(bf16[32,3200]{1,0:T(8,128)(2,1)S(1)} %join.2.refs_0_), channel_id=1, source_target_pairs={{0,37},{8,127},{32,69},{40,31},{64,101},{72,63},{96,5},{104,95},{4... | collective-permute-start | bytes 614408 | tf_op jit(solution)/shard_map/ppermute | solution.py:215
  38.1 10.0 %collective-permute-start.4 = (bf16[32,3200]{1,0:T(8,128)(2,1)S(1)}, bf16[32,3200]{1,0:T(8,128)(2,1)S(1)}, u32[]{:S(2)}, u32[]{:S(2)}) collective-permute-start(bf16[32,3200]{1,0:T(8,128)(2,1)S(1)} %join.2.refs_0_), channel_id=1, source_target_pairs={{0,119},{8,45},{32,23},{40,77},{64,55},{72,109},{96,87},{104,13},{... | collective-permute-start | bytes 614408 | tf_op jit(solution)/shard_map/ppermute | solution.py:215
  48.2 30.3 %copy-start.4 = (f32[8]{0:T(128)S(1)}, f32[8]{0:T(128)}, u32[]{:S(2)}) copy-start(f32[8]{0:T(128)} %param.16) | copy-start | bytes 100
  48.2 21.8 %collective-permute-start.5 = (bf16[128,3200]{1,0:T(8,128)(2,1)S(1)}, bf16[128,3200]{1,0:T(8,128)(2,1)S(1)}, u32[]{:S(2)}, u32[]{:S(2)}) collective-permute-start(bf16[128,3200]{1,0:T(8,128)(2,1)S(1)} %join.3.b0), channel_id=1, source_target_pairs={{0,2},{8,10},{32,34},{40,42},{64,66},{72,74},{96,98},{104,106},{4,... | collective-permute-start | bytes 2457608 | tf_op jit(solution)/shard_map/ppermute | solution.py:215
  50.9 20.8 %collective-permute-start.6 = (bf16[128,3200]{1,0:T(8,128)(2,1)S(1)}, bf16[128,3200]{1,0:T(8,128)(2,1)S(1)}, u32[]{:S(2)}, u32[]{:S(2)}) collective-permute-start(bf16[128,3200]{1,0:T(8,128)(2,1)S(1)} %join.3.b0), channel_id=1, source_target_pairs={{0,16},{8,24},{32,48},{40,56},{64,80},{72,88},{96,112},{104,120},{... | collective-permute-start | bytes 2457608 | tf_op jit(solution)/shard_map/ppermute | solution.py:215
  51.6 20.2 %collective-permute-start.7 = (bf16[128,3200]{1,0:T(8,128)(2,1)S(1)}, bf16[128,3200]{1,0:T(8,128)(2,1)S(1)}, u32[]{:S(2)}, u32[]{:S(2)}) collective-permute-start(bf16[128,3200]{1,0:T(8,128)(2,1)S(1)} %join.3.b0), channel_id=1, source_target_pairs={{0,64},{8,72},{32,96},{40,104},{64,0},{72,8},{96,32},{104,40},{4,6... | collective-permute-start | bytes 2457608 | tf_op jit(solution)/shard_map/ppermute | solution.py:215
  73.7 20.6 %collective-permute-start.11 = (bf16[256,3200]{1,0:T(8,128)(2,1)}, bf16[256,3200]{1,0:T(8,128)(2,1)}, u32[]{:S(2)}, u32[]{:S(2)}) collective-permute-start(bf16[256,3200]{1,0:T(8,128)(2,1)} %get-tuple-element.30.refs_0_), channel_id=1, source_target_pairs={{0,1},{8,11},{32,33},{40,43},{64,65},{72,75},{96,97},{104,107},{4,... | collective-permute-start | bytes 4915208 | tf_op jit(solution)/shard_map/ppermute | solution.py:215
  75.4 20.6 %collective-permute-start.12 = (bf16[256,3200]{1,0:T(8,128)(2,1)}, bf16[256,3200]{1,0:T(8,128)(2,1)}, u32[]{:S(2)}, u32[]{:S(2)}) collective-permute-start(bf16[256,3200]{1,0:T(8,128)(2,1)} %get-tuple-element.30.refs_0_), channel_id=1, source_target_pairs={{0,4},{8,28},{32,36},{40,60},{64,68},{72,92},{96,100},{104,124},{4... | collective-permute-start | bytes 4915208 | tf_op jit(solution)/shard_map/ppermute | solution.py:215
  76.9 20.6 %collective-permute-start.13 = (bf16[256,3200]{1,0:T(8,128)(2,1)}, bf16[256,3200]{1,0:T(8,128)(2,1)}, u32[]{:S(2)}, u32[]{:S(2)}) collective-permute-start(bf16[256,3200]{1,0:T(8,128)(2,1)} %get-tuple-element.30.refs_0_), channel_id=1, source_target_pairs={{0,32},{8,104},{32,64},{40,8},{64,96},{72,40},{96,0},{104,72},{4,3... | collective-permute-start | bytes 4915208 | tf_op jit(solution)/shard_map/ppermute | solution.py:215
  77.2 41.6 %collective-permute-start.10 = (bf16[256,3200]{1,0:T(8,128)(2,1)}, bf16[256,3200]{1,0:T(8,128)(2,1)S(1)}, u32[]{:S(2)}, u32[]{:S(2)}) collective-permute-start(bf16[256,3200]{1,0:T(8,128)(2,1)} %get-tuple-element.29.refs_1_), channel_id=1, source_target_pairs={{0,4},{8,28},{32,36},{40,60},{64,68},{72,92},{96,100},{104,124},{4... | collective-permute-start | bytes 4915208 | tf_op jit(solution)/shard_map/ppermute | solution.py:215
  78.5 40.4 %collective-permute-start.9 = (bf16[256,3200]{1,0:T(8,128)(2,1)}, bf16[256,3200]{1,0:T(8,128)(2,1)S(1)}, u32[]{:S(2)}, u32[]{:S(2)}) collective-permute-start(bf16[256,3200]{1,0:T(8,128)(2,1)} %get-tuple-element.29.refs_1_), channel_id=1, source_target_pairs={{0,1},{8,11},{32,33},{40,43},{64,65},{72,75},{96,97},{104,107},{4,... | collective-permute-start | bytes 4915208 | tf_op jit(solution)/shard_map/ppermute | solution.py:215
  102.1 9.4 %collective-permute-start.14 = (bf16[1280,384]{1,0:T(8,128)(2,1)S(1)}, bf16[1280,384]{1,0:T(8,128)(2,1)S(1)}, u32[]{:S(2)}, u32[]{:S(2)}) collective-permute-start(bf16[1280,384]{1,0:T(8,128)(2,1)S(1)} %weighted.3.left), channel_id=1, source_target_pairs={{0,8},{8,0},{32,40},{40,32},{64,72},{72,64},{96,104},{104,96},{4,1... | collective-permute-start | bytes 2949128 | tf_op jit(solution)/shard_map/ppermute | solution.py:215
  104.2 20.5 %collective-permute-start.8 = (bf16[256,3200]{1,0:T(8,128)(2,1)}, bf16[256,3200]{1,0:T(8,128)(2,1)S(1)}, u32[]{:S(2)}, u32[]{:S(2)}) collective-permute-start(bf16[256,3200]{1,0:T(8,128)(2,1)} %get-tuple-element.29.refs_1_), channel_id=1, source_target_pairs={{0,32},{8,104},{32,64},{40,8},{64,96},{72,40},{96,0},{104,72},{4,3... | collective-permute-start | bytes 4915208 | tf_op jit(solution)/shard_map/ppermute | solution.py:215
  119.8 2.6 %collective-permute-start.15 = (bf16[512,384]{1,0:T(8,128)(2,1)S(1)}, bf16[512,384]{1,0:T(8,128)(2,1)S(1)}, u32[]{:S(2)}, u32[]{:S(2)}) collective-permute-start(bf16[512,384]{1,0:T(8,128)(2,1)S(1)} %weighted.4.left), channel_id=1, source_target_pairs={{0,8},{8,0},{32,40},{40,32},{64,72},{72,64},{96,104},{104,96},{4,1... | collective-permute-start | bytes 1179656 | tf_op jit(solution)/shard_map/ppermute | solution.py:215
  125.6 8.6 %collective-permute-start.16 = (bf16[256,3072]{1,0:T(8,128)(2,1)S(1)}, bf16[256,3072]{1,0:T(8,128)(2,1)S(1)}, u32[]{:S(2)}, u32[]{:S(2)}) collective-permute-start(bf16[256,3072]{1,0:T(8,128)(2,1)S(1)} %get-tuple-element.37), channel_id=1, source_target_pairs={{0,8},{8,0},{32,40},{40,32},{64,72},{72,64},{96,104},{104,96},{4,1... | collective-permute-start | bytes 4718600 | tf_op jit(solution)/shard_map/ppermute | solution.py:215
  127.9 4.7 %collective-permute-start.18 = (bf16[384,1536]{1,0:T(8,128)(2,1)S(1)}, bf16[384,1536]{1,0:T(8,128)(2,1)S(1)}, u32[]{:S(2)}, u32[]{:S(2)}) collective-permute-start(bf16[384,1536]{1,0:T(8,128)(2,1)S(1)} %other_rows.3.refs_1_), channel_id=1, source_target_pairs={{0,8},{8,0},{32,40},{40,32},{64,72},{72,64},{96,104},{104,96},{4,1... | collective-permute-start | bytes 3538952 | tf_op jit(solution)/shard_map/ppermute | solution.py:215
  128.0 6.3 %collective-permute-start.17 = (bf16[384,1536]{1,0:T(8,128)(2,1)S(1)}, bf16[384,1536]{1,0:T(8,128)(2,1)S(1)}, u32[]{:S(2)}, u32[]{:S(2)}) collective-permute-start(bf16[384,1536]{1,0:T(8,128)(2,1)S(1)} %other_rows.2.refs_3_), channel_id=1, source_target_pairs={{0,8},{8,0},{32,40},{40,32},{64,72},{72,64},{96,104},{104,96},{4,1... | collective-permute-start | bytes 3538952 | tf_op jit(solution)/shard_map/ppermute | solution.py:215

commit v12 on v9

--- a/solution.py
+++ b/solution.py
@@ -494,9 +494,10 @@
     core = core.reshape(1)
     own = other = None
     tie = jnp.zeros(TIE.shape, TIE.dtype)
-    groups = (((0, 0), (1, 0)), ((0, 1), (0, 2)), ((1, 1), (1, 2)), ((0, 3), (1, 3)))
+    groups = (((0, 0), (1, 0)), ((0, 1), (0, 2)), ((1, 1), (1, 2), (0, 3), (1, 3)))
     for names in groups:
-        pieces = [in_vmem(got[name]) for name in (("z",) if names is groups[-1] else names)]
+        held = names if names is not groups[-1] else (*names[:2], "z")
+        pieces = [in_vmem(got[name]) for name in held]
         left = weighted(place, mine_omega, pieces, tie)
         mirror = send(left, core_pairs())
         if names is not groups[-1]:

time: 136 us -> 133 us (0.978)
  waiting for transfers between devices: 42.2 us -> 44.8 us
  Pallas kernels: 49.2 us -> 47.1 us
  local copies, waits for them, and re-layouts: 2.53 us -> 1.1 us
    pallas_call x6 -> x4, Pallas kernels: 20.4 us -> 16.1 us  [partial_rows(): pl.pallas_call(functools.partial(partial_kernel, names, len(pieces), othe...]
    all_to_all x1, waiting for transfers between devices: 5.85 us -> 8.52 us  [on_device(): psi = lax.all_to_all(rows, 'ga', 0, 0, tiled=True, axis_index_groups=kinds)]
    pallas_call x2, Pallas kernels: 4.7 us -> 6.55 us  [own_rows(): pl.pallas_call(functools.partial(own_kernel, names, len(pieces), start),...]
    pallas_call x4 -> x3, Pallas kernels: 7.65 us -> 6.59 us  [weighted(): pl.pallas_call(weighted_kernel, out_shape=pltpu.VMEM((sum((p.shape[0] for...]
    ppermute x19 -> x18, waiting for transfers between devices: 36.4 us -> 36.3 us  [send(): return lax.ppermute(a, ('ga', 'ba'), pairs)]
    ppermute x19 -> x18, starting transfers between devices: 30.8 us -> 30.7 us  [send(): return lax.ppermute(a, ('ga', 'ba'), pairs)]
  transfers between devices with their start and end apart: 20 -> 19, of which waited for: 13 -> 12; matrix products, arithmetic and copies ran while one was open for 3% -> 1% of each run, Pallas kernels for 26% -> 24%
where the time goes in v12:
time: 133 us
  Pallas kernels  47.1 us (35%)
  waiting for transfers between devices  44.8 us (34%)
  starting transfers between devices  39.2 us (29%)
    ppermute x18, waiting for transfers between devices, send(): return lax.ppermute(a, ('ga', 'ba'), pairs)  36.3 us
    ppermute x18, starting transfers between devices, send(): return lax.ppermute(a, ('ga', 'ba'), pairs)  30.7 us
    pallas_call x4, Pallas kernels, partial_rows(): pl.pallas_call(functools.partial(partial_kernel, names, len(pieces), othe...  16.1 us
    all_to_all x1, waiting for transfers between devices, on_device(): psi = lax.all_to_all(rows, 'ga', 0, 0, tiled=True, axis_index_groups=kinds)  8.52 us
    all_to_all x1, starting transfers between devices, on_device(): psi = lax.all_to_all(rows, 'ga', 0, 0, tiled=True, axis_index_groups=kinds)  8.51 us
    pallas_call x3, Pallas kernels, weighted(): pl.pallas_call(weighted_kernel, out_shape=pltpu.VMEM((sum((p.shape[0] for...  6.59 us
    pallas_call x2, Pallas kernels, own_rows(): pl.pallas_call(functools.partial(own_kernel, names, len(pieces), start),...  6.55 us
    pallas_call x1, Pallas kernels, rho_spectrum(): pl.pallas_call(transform_kernel, out_shape=[pltpu.VMEM((PAIRS * 64, 256),...  4.58 us
  transfers between devices with their start and end apart: 19, of which 12 were waited for; matrix products, arithmetic and copies ran while one was open for 1% of the time, Pallas kernels for 24%

profile of v12, /device:TPU:1, one launch (start us, length us, event | category | flops | bytes accessed | tf_op | source)
XLA Modules:
  0.0 132.7 jit_solution(3405860089349804352)
XLA Ops:
  0.0 2.0 %payload.1 = (bf16[8,24,1024]{2,1,0:T(8,128)(2,1)}, bf16[2,256,256]{2,1,0:T(8,128)(2,1)S(1)}, f32[128,256]{1,0:T(8,128)S(1)}, f32[128,256]{1,0:T(8,128)S(1)}, bf16[512,256]{1,0:T(8,128)(2,1)S(1)}) custom-call(bf16[4,2048]{1,0:T(4,128)(2,1)} %val.1, bf16[64,2048]{1,0:T(8,128)(2,1)} %con.1, bf16[2,256,256]{2,1,0:T(8,128)(2,1)} %constant.39.clone.first, ...), custom_call_target="tpu_custom_call" | custom-call | tf_op jit(solution)/shard_map/payload/pallas_call | solution.py:82
  2.1 8.5 %all-to-all-start = ((bf16[8,24,1024]{2,1,0:T(8,128)(2,1)}), bf16[8,24,1024]{2,1,0:T(8,128)(2,1)S(1)}, u32[]{:S(2)}, u32[]{:S(2)}) async-start(bf16[8,24,1024]{2,1,0:T(8,128)(2,1)} %get-tuple-element.26), calls=%async_computation | async-start | bytes 786432 | tf_op jit(solution)/shard_map/all_to_all | solution.py:466
  11.0 8.5 %all-to-all-done.mine = bf16[8,24,1024]{2,1,0:T(8,128)(2,1)S(1)} async-done(((bf16[8,24,1024]{2,1,0:T(8,128)(2,1)}), bf16[8,24,1024]{2,1,0:T(8,128)(2,1)S(1)}, u32[]{:S(2)}, u32[]{:S(2)}) %all-to-all-start) | async-done | bytes 393248 | tf_op jit(solution)/shard_map/all_to_all | solution.py:466
  19.6 2.2 %collective-permute-start = (bf16[8,24,1024]{2,1,0:T(8,128)(2,1)S(1)}, bf16[8,24,1024]{2,1,0:T(8,128)(2,1)S(1)}, u32[]{:S(2)}, u32[]{:S(2)}) collective-permute-start(bf16[8,24,1024]{2,1,0:T(8,128)(2,1)S(1)} %all-to-all-done.mine), channel_id=1, source_target_pairs={{0,8},{8,0},{32,40},{40,32},{64,72},{72,64},{96,104},{104,96},{4,1... | collective-permute-start | bytes 1179656 | tf_op jit(solution)/shard_map/ppermute | solution.py:215
  23.1 4.6 %rho_spectrum.1 = (bf16[1024,256]{1,0:T(8,128)(2,1)S(1)}, bf16[16,3200]{1,0:T(8,128)(2,1)S(1)}) custom-call(s32[1]{0:T(128)} %bitcast.core, bf16[8,24,1024]{2,1,0:T(8,128)(2,1)S(1)} %all-to-all-done.mine, bf16[8,24,1024]{2,1,0:T(8,128)(2,1)S(1)} %collective-permute-done.others, s32[1,3072]{1,0:T(1,128)S(1)} %get-tuple-element.48.gidx, ...), custom_call_target="tpu_custom_call" | custom-call | tf_op jit(solution)/shard_map/rho_spectrum/pallas_call | solution.py:168
  28.1 2.3 %rho_pick.1.refs_0_ = bf16[16,3200]{1,0:T(8,128)(2,1)S(1)} custom-call(bf16[1024,256]{1,0:T(8,128)(2,1)S(1)} %get-tuple-element.31.spec, s32[1,3072]{1,0:T(1,128)S(1)} %get-tuple-element.47.gidx, bf16[16,128]{1,0:T(8,128)(2,1)S(1)} %pad.4.meta), custom_call_target="tpu_custom_call" | custom-call | tf_op jit(solution)/shard_map/rho_pick/pallas_call | solution.py:184
  30.4 3.2 %collective-permute-start.2 = (bf16[32,3200]{1,0:T(8,128)(2,1)S(1)}, bf16[32,3200]{1,0:T(8,128)(2,1)S(1)}, u32[]{:S(2)}, u32[]{:S(2)}) collective-permute-start(bf16[32,3200]{1,0:T(8,128)(2,1)S(1)} %join.2.refs_0_), channel_id=1, source_target_pairs={{0,82},{8,90},{32,114},{40,122},{64,18},{72,26},{96,50},{104,58},{... | collective-permute-start | bytes 614408 | tf_op jit(solution)/shard_map/ppermute | solution.py:215
  33.6 4.5 %collective-permute-start.3 = (bf16[32,3200]{1,0:T(8,128)(2,1)S(1)}, bf16[32,3200]{1,0:T(8,128)(2,1)S(1)}, u32[]{:S(2)}, u32[]{:S(2)}) collective-permute-start(bf16[32,3200]{1,0:T(8,128)(2,1)S(1)} %join.2.refs_0_), channel_id=1, source_target_pairs={{0,37},{8,127},{32,69},{40,31},{64,101},{72,63},{96,5},{104,95},{4... | collective-permute-start | bytes 614408 | tf_op jit(solution)/shard_map/ppermute | solution.py:215
  38.1 5.2 %collective-permute-done.2.refs_1_ = bf16[32,3200]{1,0:T(8,128)(2,1)S(1)} collective-permute-done((bf16[32,3200]{1,0:T(8,128)(2,1)S(1)}, bf16[32,3200]{1,0:T(8,128)(2,1)S(1)}, u32[]{:S(2)}, u32[]{:S(2)}) %collective-permute-start.2) | collective-permute-done | bytes 204832 | tf_op jit(solution)/shard_map/ppermute | solution.py:215
  43.3 2.5 %collective-permute-done.3.refs_2_ = bf16[32,3200]{1,0:T(8,128)(2,1)S(1)} collective-permute-done((bf16[32,3200]{1,0:T(8,128)(2,1)S(1)}, bf16[32,3200]{1,0:T(8,128)(2,1)S(1)}, u32[]{:S(2)}, u32[]{:S(2)}) %collective-permute-start.3) | collective-permute-done | bytes 204832 | tf_op jit(solution)/shard_map/ppermute | solution.py:215
  45.8 2.4 %collective-permute-done.4.refs_3_ = bf16[32,3200]{1,0:T(8,128)(2,1)S(1)} collective-permute-done((bf16[32,3200]{1,0:T(8,128)(2,1)S(1)}, bf16[32,3200]{1,0:T(8,128)(2,1)S(1)}, u32[]{:S(2)}, u32[]{:S(2)}) %collective-permute-start.4) | collective-permute-done | bytes 204832 | tf_op jit(solution)/shard_map/ppermute | solution.py:215
  48.2 2.7 %collective-permute-start.5 = (bf16[128,3200]{1,0:T(8,128)(2,1)S(1)}, bf16[128,3200]{1,0:T(8,128)(2,1)S(1)}, u32[]{:S(2)}, u32[]{:S(2)}) collective-permute-start(bf16[128,3200]{1,0:T(8,128)(2,1)S(1)} %join.3.b0), channel_id=1, source_target_pairs={{0,2},{8,10},{32,34},{40,42},{64,66},{72,74},{96,98},{104,106},{4,... | collective-permute-start | bytes 2457608 | tf_op jit(solution)/shard_map/ppermute | solution.py:215
  52.3 17.8 %collective-permute-done.5.b1 = bf16[128,3200]{1,0:T(8,128)(2,1)S(1)} collective-permute-done((bf16[128,3200]{1,0:T(8,128)(2,1)S(1)}, bf16[128,3200]{1,0:T(8,128)(2,1)S(1)}, u32[]{:S(2)}, u32[]{:S(2)}) %collective-permute-start.5) | collective-permute-done | bytes 819232 | tf_op jit(solution)/shard_map/ppermute | solution.py:215
  71.8 3.2 %deal.1 = (bf16[256,3200]{1,0:T(8,128)(2,1)}, bf16[256,3200]{1,0:T(8,128)(2,1)}, bf16[512,3200]{1,0:T(8,128)(2,1)}) custom-call(bf16[128,3200]{1,0:T(8,128)(2,1)S(1)} %join.3.b0, bf16[128,3200]{1,0:T(8,128)(2,1)S(1)} %collective-permute-done.5.b1, bf16[128,3200]{1,0:T(8,128)(2,1)S(1)} %collective-permute-done.6.b2, ...), custom_call_target="tpu_custom_call" | custom-call | tf_op jit(solution)/shard_map/deal/pallas_call | solution.py:251
  75.0 1.7 %collective-permute-start.11 = (bf16[256,3200]{1,0:T(8,128)(2,1)}, bf16[256,3200]{1,0:T(8,128)(2,1)}, u32[]{:S(2)}, u32[]{:S(2)}) collective-permute-start(bf16[256,3200]{1,0:T(8,128)(2,1)} %get-tuple-element.35.refs_0_), channel_id=1, source_target_pairs={{0,1},{8,11},{32,33},{40,43},{64,65},{72,75},{96,97},{104,107},{4,... | collective-permute-start | bytes 4915208 | tf_op jit(solution)/shard_map/ppermute | solution.py:215
  76.7 1.8 %collective-permute-start.12 = (bf16[256,3200]{1,0:T(8,128)(2,1)}, bf16[256,3200]{1,0:T(8,128)(2,1)}, u32[]{:S(2)}, u32[]{:S(2)}) collective-permute-start(bf16[256,3200]{1,0:T(8,128)(2,1)} %get-tuple-element.35.refs_0_), channel_id=1, source_target_pairs={{0,4},{8,28},{32,36},{40,60},{64,68},{72,92},{96,100},{104,124},{4... | collective-permute-start | bytes 4915208 | tf_op jit(solution)/shard_map/ppermute | solution.py:215
  79.1 2.8 %weighted.3.left = bf16[512,384]{1,0:T(8,128)(2,1)S(1)} custom-call(s32[1]{0:T(128)} %bitcast.1.place, f32[1]{0:T(128)} %dynamic_slice.12.omega, bf16[256,3200]{1,0:T(8,128)(2,1)} %get-tuple-element.35.refs_0_, bf16[256,3200]{1,0:T(8,128)(2,1)} %get-tuple-element.33.refs_1_, f32[8,128]{1,0:T(8,128)S(1)} %broadcast_in_dim.7.refs_2_), custom_call_target="tpu_custom_call" | custom-call | tf_op jit(solution)/shard_map/weighted/pallas_call | solution.py:296
  82.0 2.4 %collective-permute-start.8 = (bf16[256,3200]{1,0:T(8,128)(2,1)}, bf16[256,3200]{1,0:T(8,128)(2,1)S(1)}, u32[]{:S(2)}, u32[]{:S(2)}) collective-permute-start(bf16[256,3200]{1,0:T(8,128)(2,1)} %get-tuple-element.33.refs_1_), channel_id=1, source_target_pairs={{0,1},{8,11},{32,33},{40,43},{64,65},{72,75},{96,97},{104,107},{4,... | collective-permute-start | bytes 4915208 | tf_op jit(solution)/shard_map/ppermute | solution.py:215
  84.4 2.2 %collective-permute-start.9 = (bf16[256,3200]{1,0:T(8,128)(2,1)}, bf16[256,3200]{1,0:T(8,128)(2,1)S(1)}, u32[]{:S(2)}, u32[]{:S(2)}) collective-permute-start(bf16[256,3200]{1,0:T(8,128)(2,1)} %get-tuple-element.33.refs_1_), channel_id=1, source_target_pairs={{0,4},{8,28},{32,36},{40,60},{64,68},{72,92},{96,100},{104,124},{4... | collective-permute-start | bytes 4915208 | tf_op jit(solution)/shard_map/ppermute | solution.py:215
  86.6 3.9 %partial_own.2 = (f32[384,3072]{1,0:T(8,128)S(1)}, f32[8,128]{1,0:T(8,128)S(1)}) custom-call(bf16[512,384]{1,0:T(8,128)(2,1)S(1)} %weighted.3.left, bf16[256,3200]{1,0:T(8,128)(2,1)} %get-tuple-element.35.refs_0_, bf16[256,3200]{1,0:T(8,128)(2,1)} %get-tuple-element.33.refs_1_, f32[8,128]{1,0:T(8,128)S(1)} %broadcast_in_dim.7.refs_2_), custom_call_target="tpu_custom_call" | custom-call | flops 1207959552 | bytes 12582912 | tf_op jit(solution)/shard_map/partial_own/pallas_call | solution.py:354
  90.6 3.9 %partial_other.2 = (f32[384,3072]{1,0:T(8,128)S(1)}, f32[8,128]{1,0:T(8,128)S(1)}) custom-call(bf16[512,384]{1,0:T(8,128)(2,1)S(1)} %collective-permute-done.13.left, bf16[256,3200]{1,0:T(8,128)(2,1)} %get-tuple-element.35.refs_0_, bf16[256,3200]{1,0:T(8,128)(2,1)} %get-tuple-element.33.refs_1_, f32[8,128]{1,0:T(8,128)S(1)} %get-tuple-element.36.refs_2_), custom_call_target="tpu_custom_call" | custom-call | flops 1207959552 | bytes 12582912 | tf_op jit(solution)/shard_map/partial_other/pallas_call | solution.py:354
  95.6 1.7 %collective-permute-done.12.refs_1_ = bf16[256,3200]{1,0:T(8,128)(2,1)} collective-permute-done((bf16[256,3200]{1,0:T(8,128)(2,1)}, bf16[256,3200]{1,0:T(8,128)(2,1)}, u32[]{:S(2)}, u32[]{:S(2)}) %collective-permute-start.12) | collective-permute-done | bytes 1638432 | tf_op jit(solution)/shard_map/ppermute | solution.py:215
  97.3 2.8 %weighted.4.left = bf16[512,384]{1,0:T(8,128)(2,1)S(1)} custom-call(s32[1]{0:T(128)} %bitcast.1.place, f32[1]{0:T(128)} %dynamic_slice.12.omega, bf16[256,3200]{1,0:T(8,128)(2,1)} %collective-permute-done.11.refs_0_, bf16[256,3200]{1,0:T(8,128)(2,1)} %collective-permute-done.12.refs_1_, f32[8,128]{1,0:T(8,128)S(1)} %get-tuple-element.37.refs_2_.refs_3_), custom_call_target="tpu_custom_call" | custom-call | tf_op jit(solution)/shard_map/weighted/pallas_call | solution.py:296
  100.1 3.7 %collective-permute-start.14 = (bf16[512,384]{1,0:T(8,128)(2,1)S(1)}, bf16[512,384]{1,0:T(8,128)(2,1)S(1)}, u32[]{:S(2)}, u32[]{:S(2)}) collective-permute-start(bf16[512,384]{1,0:T(8,128)(2,1)S(1)} %weighted.4.left), channel_id=1, source_target_pairs={{0,8},{8,0},{32,40},{40,32},{64,72},{72,64},{96,104},{104,96},{4,1... | collective-permute-start | bytes 1179656 | tf_op jit(solution)/shard_map/ppermute | solution.py:215
  103.7 4.1 %partial_own.3 = (f32[384,3072]{1,0:T(8,128)S(1)}, f32[8,128]{1,0:T(8,128)S(1)}) custom-call(bf16[512,384]{1,0:T(8,128)(2,1)S(1)} %weighted.4.left, bf16[256,3200]{1,0:T(8,128)(2,1)} %collective-permute-done.11.refs_0_, bf16[256,3200]{1,0:T(8,128)(2,1)} %collective-permute-done.12.refs_1_, ...), custom_call_target="tpu_custom_call", output_to_operand_aliasing={{0}: (3, {})} | custom-call | flops 1207959552 | bytes 12582912 | tf_op jit(solution)/shard_map/partial_own/pallas_call | solution.py:354
  107.9 4.1 %partial_other.3 = (f32[384,3072]{1,0:T(8,128)S(1)}, f32[8,128]{1,0:T(8,128)S(1)}) custom-call(bf16[512,384]{1,0:T(8,128)(2,1)S(1)} %collective-permute-done.14.left, bf16[256,3200]{1,0:T(8,128)(2,1)} %collective-permute-done.11.refs_0_, bf16[256,3200]{1,0:T(8,128)(2,1)} %collective-permute-done.12.refs_1_, ...), custom_call_target="tpu_custom_call", output_to_operand_aliasing={{0}: (3, {})} | custom-call | flops 1207959552 | bytes 12582912 | tf_op jit(solution)/shard_map/partial_other/pallas_call | solution.py:354
  113.0 1.7 %collective-permute-done.9.refs_1_ = bf16[256,3200]{1,0:T(8,128)(2,1)S(1)} collective-permute-done((bf16[256,3200]{1,0:T(8,128)(2,1)}, bf16[256,3200]{1,0:T(8,128)(2,1)S(1)}, u32[]{:S(2)}, u32[]{:S(2)}) %collective-permute-start.9) | collective-permute-done | bytes 1638432 | tf_op jit(solution)/shard_map/ppermute | solution.py:215
  115.8 3.8 %collective-permute-start.15 = (bf16[1024,384]{1,0:T(8,128)(2,1)S(1)}, bf16[1024,384]{1,0:T(8,128)(2,1)S(1)}, u32[]{:S(2)}, u32[]{:S(2)}) collective-permute-start(bf16[1024,384]{1,0:T(8,128)(2,1)S(1)} %weighted.5.left), channel_id=1, source_target_pairs={{0,8},{8,0},{32,40},{40,32},{64,72},{72,64},{96,104},{104,96},{4,1... | collective-permute-start | bytes 2359304 | tf_op jit(solution)/shard_map/ppermute | solution.py:215
  119.6 3.0 %own_rows.2 = (f32[384,6144]{1,0:T(8,128)}, f32[8,128]{1,0:T(8,128)S(1)}) custom-call(s32[1]{0:T(128)} %bitcast.core, bf16[1024,384]{1,0:T(8,128)(2,1)S(1)} %weighted.5.left, bf16[256,3200]{1,0:T(8,128)(2,1)S(1)} %collective-permute-done.8.refs_0_, bf16[256,3200]{1,0:T(8,128)(2,1)S(1)} %collective-permute-done.9.refs_1_, ...), custom_call_target="tpu_custom_call" | custom-call | flops 1207959552 | bytes 7864320 | tf_op jit(solution)/shard_map/own_rows/pallas_call | solution.py:390
  122.6 1.7 %other_rows.2 = bf16[384,1536]{1,0:T(8,128)(2,1)S(1)} custom-call(bf16[1024,384]{1,0:T(8,128)(2,1)S(1)} %collective-permute-done.15.left, bf16[256,3200]{1,0:T(8,128)(2,1)S(1)} %collective-permute-done.8.refs_0_, bf16[256,3200]{1,0:T(8,128)(2,1)S(1)} %collective-permute-done.9.refs_1_, bf16[512,3200]{1,0:T(8,128)(2,1)S(1)} %collective-permute-done.10.refs_2_, ...), custom_call_target="tpu_custom_call" | custom-call | flops 1207959552 | bytes 7864320 | tf_op jit(solution)/shard_map/other_rows/pallas_call | solution.py:416
  126.7 3.6 %own_rows.3 = (f32[384,6144]{1,0:T(8,128)}, f32[8,128]{1,0:T(8,128)}) custom-call(s32[1]{0:T(128)} %bitcast.core, bf16[1024,384]{1,0:T(8,128)(2,1)S(1)} %weighted.5.left, bf16[256,3200]{1,0:T(8,128)(2,1)S(1)} %collective-permute-done.8.refs_0_, bf16[256,3200]{1,0:T(8,128)(2,1)S(1)} %collective-permute-done.9.refs_1_, ...), custom_call_target="tpu_custom_call", output_to_operand_aliasing={{0}: (6, {})} | custom-call | flops 1207959552 | bytes 7864320 | tf_op jit(solution)/shard_map/own_rows/pallas_call | solution.py:390
  130.3 2.3 %finish.1 = f32[384,6144]{1,0:T(8,128)} custom-call(s32[1]{0:T(128)} %bitcast.core, bf16[384,1536]{1,0:T(8,128)(2,1)S(1)} %collective-permute-done.16.r0, bf16[384,1536]{1,0:T(8,128)(2,1)S(1)} %collective-permute-done.17.r1, f32[384,6144]{1,0:T(8,128)} %get-tuple-element.46._), custom_call_target="tpu_custom_call", output_to_operand_aliasing={{}: (3, {})} | custom-call | tf_op jit(solution)/shard_map/finish/pallas_call | solution.py:444
  (48 shorter events, 11.6 us)
Async XLA Ops:
  0.0 10.6 %copy-start = (s32[6144]{0:T(1024)S(1)}, s32[6144]{0:T(1024)}, u32[]{:S(2)}) copy-start(s32[6144]{0:T(1024)} %param.17) | copy-start | bytes 73732
  0.0 10.6 %copy-start.2 = (s32[4]{0:T(128)S(1)}, s32[4]{0:T(128)}, u32[]{:S(2)}) copy-start(s32[4]{0:T(128)} %param.15) | copy-start | bytes 52
  0.0 10.8 %copy-start.3 = (f32[64]{0:T(128)S(1)}, f32[64]{0:T(128)}, u32[]{:S(2)}) copy-start(f32[64]{0:T(128)} %param.14) | copy-start | bytes 772
  0.0 10.9 %copy-start.1 = (f32[4]{0:T(128)S(1)}, f32[4]{0:T(128)}, u32[]{:S(2)}) copy-start(f32[4]{0:T(128)} %param.13) | copy-start | bytes 52
  2.1 17.5 %all-to-all-start = ((bf16[8,24,1024]{2,1,0:T(8,128)(2,1)}), bf16[8,24,1024]{2,1,0:T(8,128)(2,1)S(1)}, u32[]{:S(2)}, u32[]{:S(2)}) async-start(bf16[8,24,1024]{2,1,0:T(8,128)(2,1)} %get-tuple-element.26), calls=%async_computation | async-start | bytes 786432 | tf_op jit(solution)/shard_map/all_to_all | solution.py:466
  19.6 3.5 %collective-permute-start = (bf16[8,24,1024]{2,1,0:T(8,128)(2,1)S(1)}, bf16[8,24,1024]{2,1,0:T(8,128)(2,1)S(1)}, u32[]{:S(2)}, u32[]{:S(2)}) collective-permute-start(bf16[8,24,1024]{2,1,0:T(8,128)(2,1)S(1)} %all-to-all-done.mine), channel_id=1, source_target_pairs={{0,8},{8,0},{32,40},{40,32},{64,72},{72,64},{96,104},{104,96},{4,1... | collective-permute-start | bytes 1179656 | tf_op jit(solution)/shard_map/ppermute | solution.py:215
  27.6 2.7 %collective-permute-start.1 = (bf16[16,3200]{1,0:T(8,128)(2,1)S(1)}, bf16[16,3200]{1,0:T(8,128)(2,1)S(1)}, u32[]{:S(2)}, u32[]{:S(2)}) collective-permute-start(bf16[16,3200]{1,0:T(8,128)(2,1)S(1)} %get-tuple-element.32), channel_id=1, source_target_pairs={{0,8},{8,0},{32,40},{40,32},{64,72},{72,64},{96,104},{104,96},{4,1... | collective-permute-start | bytes 307208 | tf_op jit(solution)/shard_map/ppermute | solution.py:215
  30.4 12.9 %collective-permute-start.2 = (bf16[32,3200]{1,0:T(8,128)(2,1)S(1)}, bf16[32,3200]{1,0:T(8,128)(2,1)S(1)}, u32[]{:S(2)}, u32[]{:S(2)}) collective-permute-start(bf16[32,3200]{1,0:T(8,128)(2,1)S(1)} %join.2.refs_0_), channel_id=1, source_target_pairs={{0,82},{8,90},{32,114},{40,122},{64,18},{72,26},{96,50},{104,58},{... | collective-permute-start | bytes 614408 | tf_op jit(solution)/shard_map/ppermute | solution.py:215
  33.6 12.1 %collective-permute-start.3 = (bf16[32,3200]{1,0:T(8,128)(2,1)S(1)}, bf16[32,3200]{1,0:T(8,128)(2,1)S(1)}, u32[]{:S(2)}, u32[]{:S(2)}) collective-permute-start(bf16[32,3200]{1,0:T(8,128)(2,1)S(1)} %join.2.refs_0_), channel_id=1, source_target_pairs={{0,37},{8,127},{32,69},{40,31},{64,101},{72,63},{96,5},{104,95},{4... | collective-permute-start | bytes 614408 | tf_op jit(solution)/shard_map/ppermute | solution.py:215
  38.1 10.0 %collective-permute-start.4 = (bf16[32,3200]{1,0:T(8,128)(2,1)S(1)}, bf16[32,3200]{1,0:T(8,128)(2,1)S(1)}, u32[]{:S(2)}, u32[]{:S(2)}) collective-permute-start(bf16[32,3200]{1,0:T(8,128)(2,1)S(1)} %join.2.refs_0_), channel_id=1, source_target_pairs={{0,119},{8,45},{32,23},{40,77},{64,55},{72,109},{96,87},{104,13},{... | collective-permute-start | bytes 614408 | tf_op jit(solution)/shard_map/ppermute | solution.py:215
  48.2 30.3 %copy-start.4 = (f32[8]{0:T(128)S(1)}, f32[8]{0:T(128)}, u32[]{:S(2)}) copy-start(f32[8]{0:T(128)} %param.16) | copy-start | bytes 100
  48.2 21.8 %collective-permute-start.5 = (bf16[128,3200]{1,0:T(8,128)(2,1)S(1)}, bf16[128,3200]{1,0:T(8,128)(2,1)S(1)}, u32[]{:S(2)}, u32[]{:S(2)}) collective-permute-start(bf16[128,3200]{1,0:T(8,128)(2,1)S(1)} %join.3.b0), channel_id=1, source_target_pairs={{0,2},{8,10},{32,34},{40,42},{64,66},{72,74},{96,98},{104,106},{4,... | collective-permute-start | bytes 2457608 | tf_op jit(solution)/shard_map/ppermute | solution.py:215
  50.9 20.8 %collective-permute-start.6 = (bf16[128,3200]{1,0:T(8,128)(2,1)S(1)}, bf16[128,3200]{1,0:T(8,128)(2,1)S(1)}, u32[]{:S(2)}, u32[]{:S(2)}) collective-permute-start(bf16[128,3200]{1,0:T(8,128)(2,1)S(1)} %join.3.b0), channel_id=1, source_target_pairs={{0,16},{8,24},{32,48},{40,56},{64,80},{72,88},{96,112},{104,120},{... | collective-permute-start | bytes 2457608 | tf_op jit(solution)/shard_map/ppermute | solution.py:215
  51.6 20.2 %collective-permute-start.7 = (bf16[128,3200]{1,0:T(8,128)(2,1)S(1)}, bf16[128,3200]{1,0:T(8,128)(2,1)S(1)}, u32[]{:S(2)}, u32[]{:S(2)}) collective-permute-start(bf16[128,3200]{1,0:T(8,128)(2,1)S(1)} %join.3.b0), channel_id=1, source_target_pairs={{0,64},{8,72},{32,96},{40,104},{64,0},{72,8},{96,32},{104,40},{4,6... | collective-permute-start | bytes 2457608 | tf_op jit(solution)/shard_map/ppermute | solution.py:215
  75.0 39.7 %collective-permute-start.10 = (bf16[512,3200]{1,0:T(8,128)(2,1)}, bf16[512,3200]{1,0:T(8,128)(2,1)S(1)}, u32[]{:S(2)}, u32[]{:S(2)}) collective-permute-start(bf16[512,3200]{1,0:T(8,128)(2,1)} %get-tuple-element.34), channel_id=1, source_target_pairs={{0,32},{8,104},{32,64},{40,8},{64,96},{72,40},{96,0},{104,72},{4,3... | collective-permute-start | bytes 9830408 | tf_op jit(solution)/shard_map/ppermute | solution.py:215
  75.0 20.6 %collective-permute-start.11 = (bf16[256,3200]{1,0:T(8,128)(2,1)}, bf16[256,3200]{1,0:T(8,128)(2,1)}, u32[]{:S(2)}, u32[]{:S(2)}) collective-permute-start(bf16[256,3200]{1,0:T(8,128)(2,1)} %get-tuple-element.35.refs_0_), channel_id=1, source_target_pairs={{0,1},{8,11},{32,33},{40,43},{64,65},{72,75},{96,97},{104,107},{4,... | collective-permute-start | bytes 4915208 | tf_op jit(solution)/shard_map/ppermute | solution.py:215
  76.7 20.6 %collective-permute-start.12 = (bf16[256,3200]{1,0:T(8,128)(2,1)}, bf16[256,3200]{1,0:T(8,128)(2,1)}, u32[]{:S(2)}, u32[]{:S(2)}) collective-permute-start(bf16[256,3200]{1,0:T(8,128)(2,1)} %get-tuple-element.35.refs_0_), channel_id=1, source_target_pairs={{0,4},{8,28},{32,36},{40,60},{64,68},{72,92},{96,100},{104,124},{4... | collective-permute-start | bytes 4915208 | tf_op jit(solution)/shard_map/ppermute | solution.py:215
  81.9 2.5 %collective-permute-start.13 = (bf16[512,384]{1,0:T(8,128)(2,1)S(1)}, bf16[512,384]{1,0:T(8,128)(2,1)S(1)}, u32[]{:S(2)}, u32[]{:S(2)}) collective-permute-start(bf16[512,384]{1,0:T(8,128)(2,1)S(1)} %weighted.3.left), channel_id=1, source_target_pairs={{0,8},{8,0},{32,40},{40,32},{64,72},{72,64},{96,104},{104,96},{4,1... | collective-permute-start | bytes 1179656 | tf_op jit(solution)/shard_map/ppermute | solution.py:215
  82.0 31.0 %collective-permute-start.8 = (bf16[256,3200]{1,0:T(8,128)(2,1)}, bf16[256,3200]{1,0:T(8,128)(2,1)S(1)}, u32[]{:S(2)}, u32[]{:S(2)}) collective-permute-start(bf16[256,3200]{1,0:T(8,128)(2,1)} %get-tuple-element.33.refs_1_), channel_id=1, source_target_pairs={{0,1},{8,11},{32,33},{40,43},{64,65},{72,75},{96,97},{104,107},{4,... | collective-permute-start | bytes 4915208 | tf_op jit(solution)/shard_map/ppermute | solution.py:215
  84.4 30.3 %collective-permute-start.9 = (bf16[256,3200]{1,0:T(8,128)(2,1)}, bf16[256,3200]{1,0:T(8,128)(2,1)S(1)}, u32[]{:S(2)}, u32[]{:S(2)}) collective-permute-start(bf16[256,3200]{1,0:T(8,128)(2,1)} %get-tuple-element.33.refs_1_), channel_id=1, source_target_pairs={{0,4},{8,28},{32,36},{40,60},{64,68},{72,92},{96,100},{104,124},{4... | collective-permute-start | bytes 4915208 | tf_op jit(solution)/shard_map/ppermute | solution.py:215
  100.1 7.8 %collective-permute-start.14 = (bf16[512,384]{1,0:T(8,128)(2,1)S(1)}, bf16[512,384]{1,0:T(8,128)(2,1)S(1)}, u32[]{:S(2)}, u32[]{:S(2)}) collective-permute-start(bf16[512,384]{1,0:T(8,128)(2,1)S(1)} %weighted.4.left), channel_id=1, source_target_pairs={{0,8},{8,0},{32,40},{40,32},{64,72},{72,64},{96,104},{104,96},{4,1... | collective-permute-start | bytes 1179656 | tf_op jit(solution)/shard_map/ppermute | solution.py:215
  115.8 6.8 %collective-permute-start.15 = (bf16[1024,384]{1,0:T(8,128)(2,1)S(1)}, bf16[1024,384]{1,0:T(8,128)(2,1)S(1)}, u32[]{:S(2)}, u32[]{:S(2)}) collective-permute-start(bf16[1024,384]{1,0:T(8,128)(2,1)S(1)} %weighted.5.left), channel_id=1, source_target_pairs={{0,8},{8,0},{32,40},{40,32},{64,72},{72,64},{96,104},{104,96},{4,1... | collective-permute-start | bytes 2359304 | tf_op jit(solution)/shard_map/ppermute | solution.py:215
  124.3 6.0 %collective-permute-start.16 = (bf16[384,1536]{1,0:T(8,128)(2,1)S(1)}, bf16[384,1536]{1,0:T(8,128)(2,1)S(1)}, u32[]{:S(2)}, u32[]{:S(2)}) collective-permute-start(bf16[384,1536]{1,0:T(8,128)(2,1)S(1)} %other_rows.2), channel_id=1, source_target_pairs={{0,8},{8,0},{32,40},{40,32},{64,72},{72,64},{96,104},{104,96},{4,1... | collective-permute-start | bytes 3538952 | tf_op jit(solution)/shard_map/ppermute | solution.py:215
  126.1 4.2 %collective-permute-start.17 = (bf16[384,1536]{1,0:T(8,128)(2,1)S(1)}, bf16[384,1536]{1,0:T(8,128)(2,1)S(1)}, u32[]{:S(2)}, u32[]{:S(2)}) collective-permute-start(bf16[384,1536]{1,0:T(8,128)(2,1)S(1)} %other_rows.3), channel_id=1, source_target_pairs={{0,8},{8,0},{32,40},{40,32},{64,72},{72,64},{96,104},{104,96},{4,1... | collective-permute-start | bytes 3538952 | tf_op jit(solution)/shard_map/ppermute | solution.py:215

commit v13 on v12

--- a/solution.py
+++ b/solution.py
@@ -365,39 +365,47 @@
 
 def own_kernel(names, n, start, core, left, *refs):
     pieces = halves(refs[:n])
-    before, _, out, tie, wide, sem = refs[n:]
+    before, *swapped = refs[n:-6]
+    out, tie, wide, sem, wide_swapped = refs[-5:]
     tie[...] = jnp.zeros_like(tie)
     copies = []
+
+    def write(src, block, half, s):
+        at = pl.multiple_of((block * 2 + half) * ROWS, LANES)
+        copies.append(pltpu.make_async_copy(src, out.at[:, pl.ds(at, ROWS)], s))
+        copies[-1].start()
+
+    for row in swapped:
+        for j in range(4):
+            at = slice(j * ROWS, (j + 1) * ROWS)
+            wide_swapped[:, at] = row[:, at].astype(jnp.float32)
+            write(wide_swapped.at[:, pl.ds(j * ROWS, ROWS)], j, 1 - core[0], sem.at[4 + j])
     for i in range(2):
         cols = slice(start + i * CHUNK, start + (i + 1) * CHUNK)
         wide[:, i * CHUNK : (i + 1) * CHUNK] = product(names, False, left, pieces, cols) + before[:, cols]
         for j in (2 * i, 2 * i + 1):
-            block = (start // ROWS + j) * 2 + core[0]
-            copies.append(
-                pltpu.make_async_copy(
-                    wide.at[:, pl.ds(j * ROWS, ROWS)],
-                    out.at[:, pl.ds(pl.multiple_of(block * ROWS, LANES), ROWS)],
-                    sem.at[j],
-                )
-            )
-            copies[-1].start()
+            write(wide.at[:, pl.ds(j * ROWS, ROWS)], start // ROWS + j, core[0], sem.at[j])
     for copy in copies:
         copy.wait()
 
 
-def own_rows(names, start, core, left, pieces, before, after):
+def own_rows(names, start, core, left, pieces, before, swapped, after):
     grows = after.shape == (ROWS, NG)
     return pl.pallas_call(
         functools.partial(own_kernel, names, len(pieces), start),
         out_shape=[jax.ShapeDtypeStruct((ROWS, NG), jnp.float32), TIE],
-        in_specs=[SM, VM] + [VM] * (len(pieces) + 1) + [HBM if grows else VM],
+        in_specs=[SM, VM] + [VM] * (len(pieces) + 1 + len(swapped)) + [HBM if grows else VM],
         out_specs=[HBM, VM],
-        scratch_shapes=[pltpu.VMEM((ROWS, HALF // 2), jnp.float32), pltpu.SemaphoreType.DMA((4,))],
-        input_output_aliases={3 + len(pieces): 0} if grows else {},
+        scratch_shapes=[
+            pltpu.VMEM((ROWS, HALF // 2), jnp.float32),
+            pltpu.SemaphoreType.DMA((8,)),
+            pltpu.VMEM((ROWS, HALF // 2) if swapped else (8, LANES), jnp.float32),
+        ],
+        input_output_aliases={3 + len(pieces) + len(swapped): 0} if grows else {},
         compiler_params=PARAMS,
         cost_estimate=cost(names, HALF // 2),
         name="own_rows",
-    )(core, left, *pieces, before, after)
+    )(core, left, *pieces, before, *swapped, after)
 
 
 def other_kernel(names, n, start, left, *refs):
@@ -424,33 +432,32 @@
     )(left, *pieces, before, tie)
 
 
-def finish_kernel(core, r0, r1, _, out, wide, sem):
-    def copy(i):
+def finish_kernel(core, row, _, out, wide, sem):
+    def copy(j):
+        at = pl.multiple_of(((4 + j) * 2 + 1 - core[0]) * ROWS, LANES)
         return pltpu.make_async_copy(
-            wide.at[:, pl.ds(i * ROWS, ROWS)],
-            out.at[:, pl.ds(pl.multiple_of((i * 2 + 1 - core[0]) * ROWS, LANES), ROWS)],
-            sem.at[i],
+            wide.at[:, pl.ds(j * ROWS, ROWS)], out.at[:, pl.ds(at, ROWS)], sem.at[j]
         )
 
-    for i in range(8):
-        src = (r0, r1)[i // 4]
-        wide[:, i * ROWS : (i + 1) * ROWS] = src[:, (i % 4) * ROWS : (i % 4 + 1) * ROWS].astype(jnp.float32)
-        copy(i).start()
-    for i in range(8):
-        copy(i).wait()
-
-
-def finish(core, rows, out):
+    for j in range(4):
+        at = slice(j * ROWS, (j + 1) * ROWS)
+        wide[:, at] = row[:, at].astype(jnp.float32)
+        copy(j).start()
+    for j in range(4):
+        copy(j).wait()
+
+
+def finish(core, row, out):
     return pl.pallas_call(
         finish_kernel,
         out_shape=jax.ShapeDtypeStruct((ROWS, NG), jnp.float32),
-        in_specs=[SM, VM, VM, HBM],
+        in_specs=[SM, VM, HBM],
         out_specs=HBM,
-        scratch_shapes=[pltpu.VMEM((ROWS, HALF), jnp.float32), pltpu.SemaphoreType.DMA((8,))],
-        input_output_aliases={3: 0},
+        scratch_shapes=[pltpu.VMEM((ROWS, HALF // 2), jnp.float32), pltpu.SemaphoreType.DMA((4,))],
+        input_output_aliases={2: 0},
         compiler_params=PARAMS,
         name="finish",
-    )(core, *rows, out)
+    )(core, row, out)
 
 
 def in_vmem(a):
@@ -503,10 +510,10 @@
         if names is not groups[-1]:
             own, tie = partial_rows(names, False, left, pieces, own, tie)
             other, tie = partial_rows(names, True, mirror, pieces, other, tie)
-    out, tie = own_rows(names, 0, core, left, pieces, own, tie)
+    out, tie = own_rows(names, 0, core, left, pieces, own, [], tie)
     rows = [send(other_rows(names, s, mirror, pieces, other, tie), core_pairs()) for s in (0, HALF // 2)]
-    out, _ = own_rows(names, HALF // 2, core, left, pieces, own, out)
-    return finish(core, rows, out)[None]
+    out, _ = own_rows(names, HALF // 2, core, left, pieces, own, rows[:1], out)
+    return finish(core, rows[1], out)[None]
 
 
 def solution(mesh):

time: 133 us -> 133 us (level)
  starting transfers between devices: 39.2 us -> 37 us
  waiting for transfers between devices: 44.8 us -> 46.4 us
    ppermute x18, starting transfers between devices: 30.7 us -> 28.5 us  [send(): return lax.ppermute(a, ('ga', 'ba'), pairs)]
    ppermute x18, waiting for transfers between devices: 36.3 us -> 37.8 us  [send(): return lax.ppermute(a, ('ga', 'ba'), pairs)]
  transfers between devices with their start and end apart: 19 -> 19, of which waited for: 12 -> 12; matrix products, arithmetic and copies ran while one was open for 1% -> 1% of each run, Pallas kernels for 24% -> 25%
where the time goes in v13:
time: 133 us; the launch traced here: 132 us
  Pallas kernels  47.1 us (35%)
  waiting for transfers between devices  46.4 us (35%)
  starting transfers between devices  37 us (28%)
    ppermute x18, waiting for transfers between devices, send(): return lax.ppermute(a, ('ga', 'ba'), pairs)  37.8 us
    ppermute x18, starting transfers between devices, send(): return lax.ppermute(a, ('ga', 'ba'), pairs)  28.5 us
    pallas_call x4, Pallas kernels, partial_rows(): pl.pallas_call(functools.partial(partial_kernel, names, len(pieces), othe...  16.1 us
    all_to_all x1, waiting for transfers between devices, on_device(): psi = lax.all_to_all(rows, 'ga', 0, 0, tiled=True, axis_index_groups=kinds)  8.55 us
    all_to_all x1, starting transfers between devices, on_device(): psi = lax.all_to_all(rows, 'ga', 0, 0, tiled=True, axis_index_groups=kinds)  8.51 us
    pallas_call x2, Pallas kernels, own_rows(): pl.pallas_call(functools.partial(own_kernel, names, len(pieces), start),...  7.36 us
    pallas_call x3, Pallas kernels, weighted(): pl.pallas_call(weighted_kernel, out_shape=pltpu.VMEM((sum((p.shape[0] for...  6.59 us
    pallas_call x1, Pallas kernels, rho_spectrum(): pl.pallas_call(transform_kernel, out_shape=[pltpu.VMEM((PAIRS * 64, 256),...  4.58 us
  transfers between devices with their start and end apart: 19, of which 12 were waited for; matrix products, arithmetic and copies ran while one was open for 1% of the time, Pallas kernels for 25%

profile of v13, /device:TPU:1, one launch (start us, length us, event | category | flops | bytes accessed | tf_op | source)
XLA Modules:
  0.0 132.1 jit_solution(5567396762473250108)
XLA Ops:
  0.0 2.0 %payload.1 = (bf16[8,24,1024]{2,1,0:T(8,128)(2,1)}, bf16[2,256,256]{2,1,0:T(8,128)(2,1)S(1)}, f32[128,256]{1,0:T(8,128)S(1)}, f32[128,256]{1,0:T(8,128)S(1)}, bf16[512,256]{1,0:T(8,128)(2,1)S(1)}) custom-call(bf16[4,2048]{1,0:T(4,128)(2,1)} %val.1, bf16[64,2048]{1,0:T(8,128)(2,1)} %con.1, bf16[2,256,256]{2,1,0:T(8,128)(2,1)} %constant.39.clone.first, ...), custom_call_target="tpu_custom_call" | custom-call | tf_op jit(solution)/shard_map/payload/pallas_call | solution.py:82
  2.1 8.5 %all-to-all-start = ((bf16[8,24,1024]{2,1,0:T(8,128)(2,1)}), bf16[8,24,1024]{2,1,0:T(8,128)(2,1)S(1)}, u32[]{:S(2)}, u32[]{:S(2)}) async-start(bf16[8,24,1024]{2,1,0:T(8,128)(2,1)} %get-tuple-element.26), calls=%async_computation | async-start | bytes 786432 | tf_op jit(solution)/shard_map/all_to_all | solution.py:473
  11.0 8.6 %all-to-all-done.mine = bf16[8,24,1024]{2,1,0:T(8,128)(2,1)S(1)} async-done(((bf16[8,24,1024]{2,1,0:T(8,128)(2,1)}), bf16[8,24,1024]{2,1,0:T(8,128)(2,1)S(1)}, u32[]{:S(2)}, u32[]{:S(2)}) %all-to-all-start) | async-done | bytes 393248 | tf_op jit(solution)/shard_map/all_to_all | solution.py:473
  19.6 2.2 %collective-permute-start = (bf16[8,24,1024]{2,1,0:T(8,128)(2,1)S(1)}, bf16[8,24,1024]{2,1,0:T(8,128)(2,1)S(1)}, u32[]{:S(2)}, u32[]{:S(2)}) collective-permute-start(bf16[8,24,1024]{2,1,0:T(8,128)(2,1)S(1)} %all-to-all-done.mine), channel_id=1, source_target_pairs={{0,8},{8,0},{32,40},{40,32},{64,72},{72,64},{96,104},{104,96},{4,1... | collective-permute-start | bytes 1179656 | tf_op jit(solution)/shard_map/ppermute | solution.py:215
  23.1 4.6 %rho_spectrum.1 = (bf16[1024,256]{1,0:T(8,128)(2,1)S(1)}, bf16[16,3200]{1,0:T(8,128)(2,1)S(1)}) custom-call(s32[1]{0:T(128)} %bitcast.core, bf16[8,24,1024]{2,1,0:T(8,128)(2,1)S(1)} %all-to-all-done.mine, bf16[8,24,1024]{2,1,0:T(8,128)(2,1)S(1)} %collective-permute-done.others, s32[1,3072]{1,0:T(1,128)S(1)} %get-tuple-element.48.gidx, ...), custom_call_target="tpu_custom_call" | custom-call | tf_op jit(solution)/shard_map/rho_spectrum/pallas_call | solution.py:168
  28.1 2.3 %rho_pick.1.refs_0_ = bf16[16,3200]{1,0:T(8,128)(2,1)S(1)} custom-call(bf16[1024,256]{1,0:T(8,128)(2,1)S(1)} %get-tuple-element.31.spec, s32[1,3072]{1,0:T(1,128)S(1)} %get-tuple-element.47.gidx, bf16[16,128]{1,0:T(8,128)(2,1)S(1)} %pad.4.meta), custom_call_target="tpu_custom_call" | custom-call | tf_op jit(solution)/shard_map/rho_pick/pallas_call | solution.py:184
  31.5 5.9 %collective-permute-start.3 = (bf16[32,3200]{1,0:T(8,128)(2,1)S(1)}, bf16[32,3200]{1,0:T(8,128)(2,1)S(1)}, u32[]{:S(2)}, u32[]{:S(2)}) collective-permute-start(bf16[32,3200]{1,0:T(8,128)(2,1)S(1)} %join.2.refs_0_), channel_id=1, source_target_pairs={{0,37},{8,127},{32,69},{40,31},{64,101},{72,63},{96,5},{104,95},{4... | collective-permute-start | bytes 614408 | tf_op jit(solution)/shard_map/ppermute | solution.py:215
  37.4 3.1 %collective-permute-done.4.refs_3_ = bf16[32,3200]{1,0:T(8,128)(2,1)S(1)} collective-permute-done((bf16[32,3200]{1,0:T(8,128)(2,1)S(1)}, bf16[32,3200]{1,0:T(8,128)(2,1)S(1)}, u32[]{:S(2)}, u32[]{:S(2)}) %collective-permute-start.4) | collective-permute-done | bytes 204832 | tf_op jit(solution)/shard_map/ppermute | solution.py:215
  40.5 8.1 %collective-permute-done.2.refs_1_ = bf16[32,3200]{1,0:T(8,128)(2,1)S(1)} collective-permute-done((bf16[32,3200]{1,0:T(8,128)(2,1)S(1)}, bf16[32,3200]{1,0:T(8,128)(2,1)S(1)}, u32[]{:S(2)}, u32[]{:S(2)}) %collective-permute-start.2) | collective-permute-done | bytes 204832 | tf_op jit(solution)/shard_map/ppermute | solution.py:215
  50.7 1.2 collective-permute-start.5
  51.8 16.8 %collective-permute-done.7.b3 = bf16[128,3200]{1,0:T(8,128)(2,1)S(1)} collective-permute-done((bf16[128,3200]{1,0:T(8,128)(2,1)S(1)}, bf16[128,3200]{1,0:T(8,128)(2,1)S(1)}, u32[]{:S(2)}, u32[]{:S(2)}) %collective-permute-start.7) | collective-permute-done | bytes 819232 | tf_op jit(solution)/shard_map/ppermute | solution.py:215
  68.7 1.2 collective-permute-done.6.b2
  69.9 3.2 %deal.1 = (bf16[256,3200]{1,0:T(8,128)(2,1)}, bf16[256,3200]{1,0:T(8,128)(2,1)}, bf16[512,3200]{1,0:T(8,128)(2,1)}) custom-call(bf16[128,3200]{1,0:T(8,128)(2,1)S(1)} %join.3.b0, bf16[128,3200]{1,0:T(8,128)(2,1)S(1)} %collective-permute-done.5.b1, bf16[128,3200]{1,0:T(8,128)(2,1)S(1)} %collective-permute-done.6.b2, ...), custom_call_target="tpu_custom_call" | custom-call | tf_op jit(solution)/shard_map/deal/pallas_call | solution.py:251
  73.1 2.4 %collective-permute-start.10 = (bf16[512,3200]{1,0:T(8,128)(2,1)}, bf16[512,3200]{1,0:T(8,128)(2,1)S(1)}, u32[]{:S(2)}, u32[]{:S(2)}) collective-permute-start(bf16[512,3200]{1,0:T(8,128)(2,1)} %get-tuple-element.34), channel_id=1, source_target_pairs={{0,32},{8,104},{32,64},{40,8},{64,96},{72,40},{96,0},{104,72},{4,3... | collective-permute-start | bytes 9830408 | tf_op jit(solution)/shard_map/ppermute | solution.py:215
  77.3 2.8 %weighted.3.left = bf16[512,384]{1,0:T(8,128)(2,1)S(1)} custom-call(s32[1]{0:T(128)} %bitcast.1.place, f32[1]{0:T(128)} %dynamic_slice.12.omega, bf16[256,3200]{1,0:T(8,128)(2,1)} %get-tuple-element.35.refs_0_, bf16[256,3200]{1,0:T(8,128)(2,1)} %get-tuple-element.33.refs_1_, f32[8,128]{1,0:T(8,128)S(1)} %broadcast_in_dim.7.refs_2_), custom_call_target="tpu_custom_call" | custom-call | tf_op jit(solution)/shard_map/weighted/pallas_call | solution.py:296
  80.1 1.2 collective-permute-start.13
  81.3 2.7 %collective-permute-start.9 = (bf16[256,3200]{1,0:T(8,128)(2,1)}, bf16[256,3200]{1,0:T(8,128)(2,1)S(1)}, u32[]{:S(2)}, u32[]{:S(2)}) collective-permute-start(bf16[256,3200]{1,0:T(8,128)(2,1)} %get-tuple-element.33.refs_1_), channel_id=1, source_target_pairs={{0,4},{8,28},{32,36},{40,60},{64,68},{72,92},{96,100},{104,124},{4... | collective-permute-start | bytes 4915208 | tf_op jit(solution)/shard_map/ppermute | solution.py:215
  84.1 2.4 %collective-permute-start.8 = (bf16[256,3200]{1,0:T(8,128)(2,1)}, bf16[256,3200]{1,0:T(8,128)(2,1)S(1)}, u32[]{:S(2)}, u32[]{:S(2)}) collective-permute-start(bf16[256,3200]{1,0:T(8,128)(2,1)} %get-tuple-element.33.refs_1_), channel_id=1, source_target_pairs={{0,1},{8,11},{32,33},{40,43},{64,65},{72,75},{96,97},{104,107},{4,... | collective-permute-start | bytes 4915208 | tf_op jit(solution)/shard_map/ppermute | solution.py:215
  86.5 3.9 %partial_own.2 = (f32[384,3072]{1,0:T(8,128)S(1)}, f32[8,128]{1,0:T(8,128)S(1)}) custom-call(bf16[512,384]{1,0:T(8,128)(2,1)S(1)} %weighted.3.left, bf16[256,3200]{1,0:T(8,128)(2,1)} %get-tuple-element.35.refs_0_, bf16[256,3200]{1,0:T(8,128)(2,1)} %get-tuple-element.33.refs_1_, f32[8,128]{1,0:T(8,128)S(1)} %broadcast_in_dim.7.refs_2_), custom_call_target="tpu_custom_call" | custom-call | flops 1207959552 | bytes 12582912 | tf_op jit(solution)/shard_map/partial_own/pallas_call | solution.py:354
  90.4 3.9 %partial_other.2 = (f32[384,3072]{1,0:T(8,128)S(1)}, f32[8,128]{1,0:T(8,128)S(1)}) custom-call(bf16[512,384]{1,0:T(8,128)(2,1)S(1)} %collective-permute-done.13.left, bf16[256,3200]{1,0:T(8,128)(2,1)} %get-tuple-element.35.refs_0_, bf16[256,3200]{1,0:T(8,128)(2,1)} %get-tuple-element.33.refs_1_, f32[8,128]{1,0:T(8,128)S(1)} %get-tuple-element.36.refs_2_), custom_call_target="tpu_custom_call" | custom-call | flops 1207959552 | bytes 12582912 | tf_op jit(solution)/shard_map/partial_other/pallas_call | solution.py:354
  94.4 1.7 %collective-permute-done.12.refs_1_ = bf16[256,3200]{1,0:T(8,128)(2,1)} collective-permute-done((bf16[256,3200]{1,0:T(8,128)(2,1)}, bf16[256,3200]{1,0:T(8,128)(2,1)}, u32[]{:S(2)}, u32[]{:S(2)}) %collective-permute-start.12) | collective-permute-done | bytes 1638432 | tf_op jit(solution)/shard_map/ppermute | solution.py:215
  97.3 2.8 %weighted.4.left = bf16[512,384]{1,0:T(8,128)(2,1)S(1)} custom-call(s32[1]{0:T(128)} %bitcast.1.place, f32[1]{0:T(128)} %dynamic_slice.12.omega, bf16[256,3200]{1,0:T(8,128)(2,1)} %collective-permute-done.11.refs_0_, bf16[256,3200]{1,0:T(8,128)(2,1)} %collective-permute-done.12.refs_1_, f32[8,128]{1,0:T(8,128)S(1)} %get-tuple-element.37.refs_2_.refs_3_), custom_call_target="tpu_custom_call" | custom-call | tf_op jit(solution)/shard_map/weighted/pallas_call | solution.py:296
  100.1 2.5 %collective-permute-start.14 = (bf16[512,384]{1,0:T(8,128)(2,1)S(1)}, bf16[512,384]{1,0:T(8,128)(2,1)S(1)}, u32[]{:S(2)}, u32[]{:S(2)}) collective-permute-start(bf16[512,384]{1,0:T(8,128)(2,1)S(1)} %weighted.4.left), channel_id=1, source_target_pairs={{0,8},{8,0},{32,40},{40,32},{64,72},{72,64},{96,104},{104,96},{4,1... | collective-permute-start | bytes 1179656 | tf_op jit(solution)/shard_map/ppermute | solution.py:215
  102.6 4.1 %partial_own.3 = (f32[384,3072]{1,0:T(8,128)S(1)}, f32[8,128]{1,0:T(8,128)S(1)}) custom-call(bf16[512,384]{1,0:T(8,128)(2,1)S(1)} %weighted.4.left, bf16[256,3200]{1,0:T(8,128)(2,1)} %collective-permute-done.11.refs_0_, bf16[256,3200]{1,0:T(8,128)(2,1)} %collective-permute-done.12.refs_1_, ...), custom_call_target="tpu_custom_call", output_to_operand_aliasing={{0}: (3, {})} | custom-call | flops 1207959552 | bytes 12582912 | tf_op jit(solution)/shard_map/partial_own/pallas_call | solution.py:354
  106.7 4.1 %partial_other.3 = (f32[384,3072]{1,0:T(8,128)S(1)}, f32[8,128]{1,0:T(8,128)S(1)}) custom-call(bf16[512,384]{1,0:T(8,128)(2,1)S(1)} %collective-permute-done.14.left, bf16[256,3200]{1,0:T(8,128)(2,1)} %collective-permute-done.11.refs_0_, bf16[256,3200]{1,0:T(8,128)(2,1)} %collective-permute-done.12.refs_1_, ...), custom_call_target="tpu_custom_call", output_to_operand_aliasing={{0}: (3, {})} | custom-call | flops 1207959552 | bytes 12582912 | tf_op jit(solution)/shard_map/partial_other/pallas_call | solution.py:354
  110.8 2.7 %collective-permute-done.9.refs_1_ = bf16[256,3200]{1,0:T(8,128)(2,1)S(1)} collective-permute-done((bf16[256,3200]{1,0:T(8,128)(2,1)}, bf16[256,3200]{1,0:T(8,128)(2,1)S(1)}, u32[]{:S(2)}, u32[]{:S(2)}) %collective-permute-start.9) | collective-permute-done | bytes 1638432 | tf_op jit(solution)/shard_map/ppermute | solution.py:215
  115.7 2.7 %collective-permute-start.15 = (bf16[1024,384]{1,0:T(8,128)(2,1)S(1)}, bf16[1024,384]{1,0:T(8,128)(2,1)S(1)}, u32[]{:S(2)}, u32[]{:S(2)}) collective-permute-start(bf16[1024,384]{1,0:T(8,128)(2,1)S(1)} %weighted.5.left), channel_id=1, source_target_pairs={{0,8},{8,0},{32,40},{40,32},{64,72},{72,64},{96,104},{104,96},{4,1... | collective-permute-start | bytes 2359304 | tf_op jit(solution)/shard_map/ppermute | solution.py:215
  118.5 3.0 %own_rows.2 = (f32[384,6144]{1,0:T(8,128)}, f32[8,128]{1,0:T(8,128)S(1)}) custom-call(s32[1]{0:T(128)} %bitcast.core, bf16[1024,384]{1,0:T(8,128)(2,1)S(1)} %weighted.5.left, bf16[256,3200]{1,0:T(8,128)(2,1)S(1)} %collective-permute-done.8.refs_0_, bf16[256,3200]{1,0:T(8,128)(2,1)S(1)} %collective-permute-done.9.refs_1_, ...), custom_call_target="tpu_custom_call" | custom-call | flops 1207959552 | bytes 7864320 | tf_op jit(solution)/shard_map/own_rows/pallas_call | solution.py:394
  121.5 1.7 %other_rows.3 = bf16[384,1536]{1,0:T(8,128)(2,1)S(1)} custom-call(bf16[1024,384]{1,0:T(8,128)(2,1)S(1)} %collective-permute-done.15.left, bf16[256,3200]{1,0:T(8,128)(2,1)S(1)} %collective-permute-done.8.refs_0_, bf16[256,3200]{1,0:T(8,128)(2,1)S(1)} %collective-permute-done.9.refs_1_, bf16[512,3200]{1,0:T(8,128)(2,1)S(1)} %collective-permute-done.10.refs_2_, ...), custom_call_target="tpu_custom_call" | custom-call | flops 1207959552 | bytes 7864320 | tf_op jit(solution)/shard_map/other_rows/pallas_call | solution.py:424
  123.3 1.7 %other_rows.2 = bf16[384,1536]{1,0:T(8,128)(2,1)S(1)} custom-call(bf16[1024,384]{1,0:T(8,128)(2,1)S(1)} %collective-permute-done.15.left, bf16[256,3200]{1,0:T(8,128)(2,1)S(1)} %collective-permute-done.8.refs_0_, bf16[256,3200]{1,0:T(8,128)(2,1)S(1)} %collective-permute-done.9.refs_1_, bf16[512,3200]{1,0:T(8,128)(2,1)S(1)} %collective-permute-done.10.refs_2_, ...), custom_call_target="tpu_custom_call" | custom-call | flops 1207959552 | bytes 7864320 | tf_op jit(solution)/shard_map/other_rows/pallas_call | solution.py:424
  126.1 4.3 %own_rows.3 = (f32[384,6144]{1,0:T(8,128)}, f32[8,128]{1,0:T(8,128)}) custom-call(s32[1]{0:T(128)} %bitcast.core, bf16[1024,384]{1,0:T(8,128)(2,1)S(1)} %weighted.5.left, bf16[256,3200]{1,0:T(8,128)(2,1)S(1)} %collective-permute-done.8.refs_0_, bf16[256,3200]{1,0:T(8,128)(2,1)S(1)} %collective-permute-done.9.refs_1_, ...), custom_call_target="tpu_custom_call", output_to_operand_aliasing={{0}: (7, {})} | custom-call | flops 1207959552 | bytes 7864320 | tf_op jit(solution)/shard_map/own_rows/pallas_call | solution.py:394
  130.5 1.5 %finish.1 = f32[384,6144]{1,0:T(8,128)} custom-call(s32[1]{0:T(128)} %bitcast.core, bf16[384,1536]{1,0:T(8,128)(2,1)S(1)} %collective-permute-done.16.row, f32[384,6144]{1,0:T(8,128)} %get-tuple-element.46._), custom_call_target="tpu_custom_call", output_to_operand_aliasing={{}: (2, {})} | custom-call | tf_op jit(solution)/shard_map/finish/pallas_call | solution.py:451
  (48 shorter events, 11.7 us)
Async XLA Ops:
  0.0 10.6 %copy-start.2 = (s32[4]{0:T(128)S(1)}, s32[4]{0:T(128)}, u32[]{:S(2)}) copy-start(s32[4]{0:T(128)} %param.15) | copy-start | bytes 52
  0.0 10.8 %copy-start.3 = (f32[64]{0:T(128)S(1)}, f32[64]{0:T(128)}, u32[]{:S(2)}) copy-start(f32[64]{0:T(128)} %param.14) | copy-start | bytes 772
  0.0 10.8 %copy-start.1 = (f32[4]{0:T(128)S(1)}, f32[4]{0:T(128)}, u32[]{:S(2)}) copy-start(f32[4]{0:T(128)} %param.13) | copy-start | bytes 52
  0.0 21.8 %copy-start = (s32[6144]{0:T(1024)S(1)}, s32[6144]{0:T(1024)}, u32[]{:S(2)}) copy-start(s32[6144]{0:T(1024)} %param.17) | copy-start | bytes 73732
  2.1 17.5 %all-to-all-start = ((bf16[8,24,1024]{2,1,0:T(8,128)(2,1)}), bf16[8,24,1024]{2,1,0:T(8,128)(2,1)S(1)}, u32[]{:S(2)}, u32[]{:S(2)}) async-start(bf16[8,24,1024]{2,1,0:T(8,128)(2,1)} %get-tuple-element.26), calls=%async_computation | async-start | bytes 786432 | tf_op jit(solution)/shard_map/all_to_all | solution.py:473
  19.6 3.5 %collective-permute-start = (bf16[8,24,1024]{2,1,0:T(8,128)(2,1)S(1)}, bf16[8,24,1024]{2,1,0:T(8,128)(2,1)S(1)}, u32[]{:S(2)}, u32[]{:S(2)}) collective-permute-start(bf16[8,24,1024]{2,1,0:T(8,128)(2,1)S(1)} %all-to-all-done.mine), channel_id=1, source_target_pairs={{0,8},{8,0},{32,40},{40,32},{64,72},{72,64},{96,104},{104,96},{4,1... | collective-permute-start | bytes 1179656 | tf_op jit(solution)/shard_map/ppermute | solution.py:215
  27.6 2.7 %collective-permute-start.1 = (bf16[16,3200]{1,0:T(8,128)(2,1)S(1)}, bf16[16,3200]{1,0:T(8,128)(2,1)S(1)}, u32[]{:S(2)}, u32[]{:S(2)}) collective-permute-start(bf16[16,3200]{1,0:T(8,128)(2,1)S(1)} %get-tuple-element.32), channel_id=1, source_target_pairs={{0,8},{8,0},{32,40},{40,32},{64,72},{72,64},{96,104},{104,96},{4,1... | collective-permute-start | bytes 307208 | tf_op jit(solution)/shard_map/ppermute | solution.py:215
  30.4 10.1 %collective-permute-start.4 = (bf16[32,3200]{1,0:T(8,128)(2,1)S(1)}, bf16[32,3200]{1,0:T(8,128)(2,1)S(1)}, u32[]{:S(2)}, u32[]{:S(2)}) collective-permute-start(bf16[32,3200]{1,0:T(8,128)(2,1)S(1)} %join.2.refs_0_), channel_id=1, source_target_pairs={{0,119},{8,45},{32,23},{40,77},{64,55},{72,109},{96,87},{104,13},{... | collective-permute-start | bytes 614408 | tf_op jit(solution)/shard_map/ppermute | solution.py:215
  31.5 9.0 %collective-permute-start.3 = (bf16[32,3200]{1,0:T(8,128)(2,1)S(1)}, bf16[32,3200]{1,0:T(8,128)(2,1)S(1)}, u32[]{:S(2)}, u32[]{:S(2)}) collective-permute-start(bf16[32,3200]{1,0:T(8,128)(2,1)S(1)} %join.2.refs_0_), channel_id=1, source_target_pairs={{0,37},{8,127},{32,69},{40,31},{64,101},{72,63},{96,5},{104,95},{4... | collective-permute-start | bytes 614408 | tf_op jit(solution)/shard_map/ppermute | solution.py:215
  37.4 11.3 %collective-permute-start.2 = (bf16[32,3200]{1,0:T(8,128)(2,1)S(1)}, bf16[32,3200]{1,0:T(8,128)(2,1)S(1)}, u32[]{:S(2)}, u32[]{:S(2)}) collective-permute-start(bf16[32,3200]{1,0:T(8,128)(2,1)S(1)} %join.2.refs_0_), channel_id=1, source_target_pairs={{0,82},{8,90},{32,114},{40,122},{64,18},{72,26},{96,50},{104,58},{... | collective-permute-start | bytes 614408 | tf_op jit(solution)/shard_map/ppermute | solution.py:215
  48.7 28.0 %copy-start.4 = (f32[8]{0:T(128)S(1)}, f32[8]{0:T(128)}, u32[]{:S(2)}) copy-start(f32[8]{0:T(128)} %param.16) | copy-start | bytes 100
  48.7 19.9 %collective-permute-start.7 = (bf16[128,3200]{1,0:T(8,128)(2,1)S(1)}, bf16[128,3200]{1,0:T(8,128)(2,1)S(1)}, u32[]{:S(2)}, u32[]{:S(2)}) collective-permute-start(bf16[128,3200]{1,0:T(8,128)(2,1)S(1)} %join.3.b0), channel_id=1, source_target_pairs={{0,64},{8,72},{32,96},{40,104},{64,0},{72,8},{96,32},{104,40},{4,6... | collective-permute-start | bytes 2457608 | tf_op jit(solution)/shard_map/ppermute | solution.py:215
  49.9 20.0 %collective-permute-start.6 = (bf16[128,3200]{1,0:T(8,128)(2,1)S(1)}, bf16[128,3200]{1,0:T(8,128)(2,1)S(1)}, u32[]{:S(2)}, u32[]{:S(2)}) collective-permute-start(bf16[128,3200]{1,0:T(8,128)(2,1)S(1)} %join.3.b0), channel_id=1, source_target_pairs={{0,16},{8,24},{32,48},{40,56},{64,80},{72,88},{96,112},{104,120},{... | collective-permute-start | bytes 2457608 | tf_op jit(solution)/shard_map/ppermute | solution.py:215
  50.7 19.3 %collective-permute-start.5 = (bf16[128,3200]{1,0:T(8,128)(2,1)S(1)}, bf16[128,3200]{1,0:T(8,128)(2,1)S(1)}, u32[]{:S(2)}, u32[]{:S(2)}) collective-permute-start(bf16[128,3200]{1,0:T(8,128)(2,1)S(1)} %join.3.b0), channel_id=1, source_target_pairs={{0,2},{8,10},{32,34},{40,42},{64,66},{72,74},{96,98},{104,106},{4,... | collective-permute-start | bytes 2457608 | tf_op jit(solution)/shard_map/ppermute | solution.py:215
  73.1 41.6 %collective-permute-start.10 = (bf16[512,3200]{1,0:T(8,128)(2,1)}, bf16[512,3200]{1,0:T(8,128)(2,1)S(1)}, u32[]{:S(2)}, u32[]{:S(2)}) collective-permute-start(bf16[512,3200]{1,0:T(8,128)(2,1)} %get-tuple-element.34), channel_id=1, source_target_pairs={{0,32},{8,104},{32,64},{40,8},{64,96},{72,40},{96,0},{104,72},{4,3... | collective-permute-start | bytes 9830408 | tf_op jit(solution)/shard_map/ppermute | solution.py:215
  75.5 20.6 %collective-permute-start.12 = (bf16[256,3200]{1,0:T(8,128)(2,1)}, bf16[256,3200]{1,0:T(8,128)(2,1)}, u32[]{:S(2)}, u32[]{:S(2)}) collective-permute-start(bf16[256,3200]{1,0:T(8,128)(2,1)} %get-tuple-element.35.refs_0_), channel_id=1, source_target_pairs={{0,4},{8,28},{32,36},{40,60},{64,68},{72,92},{96,100},{104,124},{4... | collective-permute-start | bytes 4915208 | tf_op jit(solution)/shard_map/ppermute | solution.py:215
  76.7 20.6 %collective-permute-start.11 = (bf16[256,3200]{1,0:T(8,128)(2,1)}, bf16[256,3200]{1,0:T(8,128)(2,1)}, u32[]{:S(2)}, u32[]{:S(2)}) collective-permute-start(bf16[256,3200]{1,0:T(8,128)(2,1)} %get-tuple-element.35.refs_0_), channel_id=1, source_target_pairs={{0,1},{8,11},{32,33},{40,43},{64,65},{72,75},{96,97},{104,107},{4,... | collective-permute-start | bytes 4915208 | tf_op jit(solution)/shard_map/ppermute | solution.py:215
  80.1 4.0 %collective-permute-start.13 = (bf16[512,384]{1,0:T(8,128)(2,1)S(1)}, bf16[512,384]{1,0:T(8,128)(2,1)S(1)}, u32[]{:S(2)}, u32[]{:S(2)}) collective-permute-start(bf16[512,384]{1,0:T(8,128)(2,1)S(1)} %weighted.3.left), channel_id=1, source_target_pairs={{0,8},{8,0},{32,40},{40,32},{64,72},{72,64},{96,104},{104,96},{4,1... | collective-permute-start | bytes 1179656 | tf_op jit(solution)/shard_map/ppermute | solution.py:215
  81.3 32.2 %collective-permute-start.9 = (bf16[256,3200]{1,0:T(8,128)(2,1)}, bf16[256,3200]{1,0:T(8,128)(2,1)S(1)}, u32[]{:S(2)}, u32[]{:S(2)}) collective-permute-start(bf16[256,3200]{1,0:T(8,128)(2,1)} %get-tuple-element.33.refs_1_), channel_id=1, source_target_pairs={{0,4},{8,28},{32,36},{40,60},{64,68},{72,92},{96,100},{104,124},{4... | collective-permute-start | bytes 4915208 | tf_op jit(solution)/shard_map/ppermute | solution.py:215
  84.1 30.7 %collective-permute-start.8 = (bf16[256,3200]{1,0:T(8,128)(2,1)}, bf16[256,3200]{1,0:T(8,128)(2,1)S(1)}, u32[]{:S(2)}, u32[]{:S(2)}) collective-permute-start(bf16[256,3200]{1,0:T(8,128)(2,1)} %get-tuple-element.33.refs_1_), channel_id=1, source_target_pairs={{0,1},{8,11},{32,33},{40,43},{64,65},{72,75},{96,97},{104,107},{4,... | collective-permute-start | bytes 4915208 | tf_op jit(solution)/shard_map/ppermute | solution.py:215
  100.1 6.7 %collective-permute-start.14 = (bf16[512,384]{1,0:T(8,128)(2,1)S(1)}, bf16[512,384]{1,0:T(8,128)(2,1)S(1)}, u32[]{:S(2)}, u32[]{:S(2)}) collective-permute-start(bf16[512,384]{1,0:T(8,128)(2,1)S(1)} %weighted.4.left), channel_id=1, source_target_pairs={{0,8},{8,0},{32,40},{40,32},{64,72},{72,64},{96,104},{104,96},{4,1... | collective-permute-start | bytes 1179656 | tf_op jit(solution)/shard_map/ppermute | solution.py:215
  115.7 5.7 %collective-permute-start.15 = (bf16[1024,384]{1,0:T(8,128)(2,1)S(1)}, bf16[1024,384]{1,0:T(8,128)(2,1)S(1)}, u32[]{:S(2)}, u32[]{:S(2)}) collective-permute-start(bf16[1024,384]{1,0:T(8,128)(2,1)S(1)} %weighted.5.left), channel_id=1, source_target_pairs={{0,8},{8,0},{32,40},{40,32},{64,72},{72,64},{96,104},{104,96},{4,1... | collective-permute-start | bytes 2359304 | tf_op jit(solution)/shard_map/ppermute | solution.py:215
  123.2 2.9 %collective-permute-start.17 = (bf16[384,1536]{1,0:T(8,128)(2,1)S(1)}, bf16[384,1536]{1,0:T(8,128)(2,1)S(1)}, u32[]{:S(2)}, u32[]{:S(2)}) collective-permute-start(bf16[384,1536]{1,0:T(8,128)(2,1)S(1)} %other_rows.3), channel_id=1, source_target_pairs={{0,8},{8,0},{32,40},{40,32},{64,72},{72,64},{96,104},{104,96},{4,1... | collective-permute-start | bytes 3538952 | tf_op jit(solution)/shard_map/ppermute | solution.py:215
  125.0 5.5 %collective-permute-start.16 = (bf16[384,1536]{1,0:T(8,128)(2,1)S(1)}, bf16[384,1536]{1,0:T(8,128)(2,1)S(1)}, u32[]{:S(2)}, u32[]{:S(2)}) collective-permute-start(bf16[384,1536]{1,0:T(8,128)(2,1)S(1)} %other_rows.2), channel_id=1, source_target_pairs={{0,8},{8,0},{32,40},{40,32},{64,72},{72,64},{96,104},{104,96},{4,1... | collective-permute-start | bytes 3538952 | tf_op jit(solution)/shard_map/ppermute | solution.py:215
